TPU v7x, 128 devices: a whole 4x4x4 slice. The times are simulated.
128 devices in a mesh: section: 2 (over y_lo), ctx: 16 (over x, y_hi, core), fsdp: 4 (over z).
Axes of the slice: x: 4, y: 4 (y_hi: 2, y_lo: 2; y = y_hi * 2 + y_lo), z: 4, core: 2. Of those that a mesh axis runs over, the one named last changes fastest.
Arguments:
- inputs: bfloat16 [4, 4, 1024, 768], P(None, 'fsdp', 'ctx'), may hold values from -6 to 6
- cotangent: bfloat16 [4, 4, 1024, 768], P(None, 'fsdp', 'ctx'), may hold values from -6 to 6
- plan: int32 [4], replicated, may hold values from 0 to 3, each once
- block_table: int32 [32], replicated, may hold values from 0 to 31, each once
- attn_in: bfloat16 [2, 768, 2304], P('section', 'fsdp'), may hold values from -0.21875 to 0.21875
- attn_out: bfloat16 [2, 768, 768], P('section', 'fsdp'), may hold values from -1.25 to 1.25
- mlp_in: bfloat16 [2, 768, 3072], P('section', 'fsdp'), may hold values from -0.21875 to 0.21875
- mlp_out: bfloat16 [2, 3072, 768], P('section', 'fsdp'), may hold values from -0.15625 to 0.15625
- norm_gains: bfloat16 [2, 2, 768], P('section', None, 'fsdp'), may hold values from 0.5 to 1.5
- biases: bfloat16 [2, 6, 768], P('section', None, 'fsdp'), may hold values from -3 to 3
- mlp_bias: bfloat16 [2, 3072], P('section', 'fsdp'), may hold values from -3 to 3
Outputs:
- layer_out: bfloat16 [2, 4, 4, 1024, 768], P('section', None, 'fsdp', 'ctx')
- input_grad: bfloat16 [2, 4, 4, 1024, 768], P('section', None, 'fsdp', 'ctx')
- grad_attn_in: float32 [2, 768, 2304], P('section', 'fsdp')
- grad_attn_out: float32 [2, 768, 768], P('section', 'fsdp')
- grad_mlp_in: float32 [2, 768, 3072], P('section', 'fsdp')
- grad_mlp_out: float32 [2, 3072, 768], P('section', 'fsdp')
- grad_gains: float32 [2, 2, 768], P('section', None, 'fsdp')
- grad_biases: float32 [2, 6, 768], P('section', None, 'fsdp')
- grad_mlp_bias: float32 [2, 3072], P('section', 'fsdp')
Inputs may be any that keep to these rules, and one draw needn't show every extreme that they name: `plan`: every micro-batch is taken at exactly one step. `block_table`: every block number occurs exactly once.
All inputs are finite; a program needn't handle non-finite values.
Results may differ from a plain program's by a relative error of at most 0.02.
Values may be sent and summed in bfloat16 or wider, within the bound.
No kernel may reach another device: no remote copies, remote signals or barrier semaphores. Data moves between devices by JAX's collectives and lax.ppermute only.
A program may use at most 256 MiB of HBM per device.

v0:
```python
import jax
import jax.numpy as jnp
from jax import lax
from jax.experimental import pallas as pl
from jax.experimental.pallas import tpu as pltpu
from jax.sharding import Mesh
from jax.sharding import PartitionSpec as P

HEADS = 12
HDIM = 64
GROUPS = 4
GROUP_HEADS = HEADS // GROUPS
WIDTH = GROUP_HEADS * HDIM
QUERY_BLOCK = 256
EXTRA = 32
JOINT_ROWS = 112
CTX = ("x", "yh", "core")

epsilon = 1e-05
neg_fill = -1e30


def dot(left_side, right_side, left_dim, right_dim):
    return lax.dot_general(
        left_side,
        right_side,
        (((left_dim,), (right_dim,)), ((), ())),
        preferred_element_type=jnp.float32,
    )


def head_columns(part, head):
    start = part * WIDTH + head * HDIM
    return slice(start, start + HDIM)


def whole(*shape):
    return pl.BlockSpec(shape, lambda i, *unused: (0,) * len(shape))


def sort_rows(target, source, table, back):
    blocks = table.shape[0]
    size = source.shape[0] // blocks
    for block in range(blocks):
        fixed = slice(block * size, (block + 1) * size)
        moved = pl.ds(pl.multiple_of(table[block] * size, size), size)
        if back:
            target[fixed, :] = source[moved, :]
        else:
            target[moved, :] = source[fixed, :]


def place_weight(target, members, ids):
    count, rows = len(members), members[0].shape[0]
    for shift, member in enumerate(members):
        place = lax.rem(ids[1] + shift - 2 * ids[0] + count, count)
        target[pl.ds(pl.multiple_of(place * rows, rows), rows), :] = member[...]


def mask_scores(scores):
    count = scores.shape[0] - QUERY_BLOCK
    tile = (QUERY_BLOCK, QUERY_BLOCK)
    visible = lax.broadcasted_iota(jnp.int32, tile, 0) <= lax.broadcasted_iota(jnp.int32, tile, 1)
    masked = jnp.where(visible, scores[count:], neg_fill)
    return jnp.concatenate([scores[:count], masked], 0) if count else masked


def attend_body(
    table, ids, own, other, w0, w1, w2, w3, bias, joined, mixed, log_total, weight, scratch, sorted_out
):
    step = pl.program_id(0)
    half = own.shape[1]

    @pl.when(step == 0)
    def _():
        place_weight(weight, (w0, w1, w2, w3), ids)
        product = dot(own[...], weight[:half, :], 1, 0) + dot(other[...], weight[half:, :], 1, 0)
        scratch[...] = (product + bias[...]).astype(jnp.bfloat16)
        sort_rows(joined, scratch, table, False)

    def block(index):
        rows = slice(index * QUERY_BLOCK, (index + 1) * QUERY_BLOCK)
        seen = slice(0, (index + 1) * QUERY_BLOCK)
        parts = []
        for head in range(GROUP_HEADS):
            queries = joined[rows, head_columns(0, head)] * jnp.bfloat16(HDIM ** (-0.5))
            keys = joined[seen, head_columns(1, head)]
            values = joined[seen, head_columns(2, head)]
            scores = mask_scores(dot(keys, queries, 1, 1))
            top = jnp.max(scores, 0, keepdims=True)
            powers = jnp.exp(scores - top)
            total = jnp.sum(powers, 0, keepdims=True)
            parts.append(dot(values, powers.astype(jnp.bfloat16), 0, 0) / total)
            log_total[head : head + 1, rows] = top + jnp.log(total)
        sorted_out[rows, :] = jnp.concatenate(parts, 0).T.astype(jnp.bfloat16)

    for index in range(own.shape[0] // QUERY_BLOCK):
        pl.when(step == index)(lambda index=index: block(index))

    @pl.when(step == pl.num_programs(0) - 1)
    def _():
        sort_rows(mixed, sorted_out, table, True)


def attend(table, ids, own, other, weights, bias):
    count, half = own.shape
    return pl.pallas_call(
        attend_body,
        grid_spec=pltpu.PrefetchScalarGridSpec(
            num_scalar_prefetch=2,
            grid=(count // QUERY_BLOCK,),
            in_specs=[whole(count, half)] * 2
            + [whole(*weight.shape) for weight in weights]
            + [whole(1, 3 * WIDTH)],
            out_specs=[whole(count, 3 * WIDTH), whole(count, WIDTH), whole(8, count)],
            scratch_shapes=[
                pltpu.VMEM((2 * half, 3 * WIDTH), jnp.bfloat16),
                pltpu.VMEM((count, 3 * WIDTH), jnp.bfloat16),
                pltpu.VMEM((count, WIDTH), jnp.bfloat16),
            ],
        ),
        out_shape=[
            jax.ShapeDtypeStruct((count, 3 * WIDTH), jnp.bfloat16),
            jax.ShapeDtypeStruct((count, WIDTH), jnp.bfloat16),
            jax.ShapeDtypeStruct((8, count), jnp.float32),
        ],
        compiler_params=pltpu.CompilerParams(vmem_limit_bytes=48 << 20),
        cost_estimate=pl.CostEstimate(
            flops=4 * count * count * WIDTH,
            bytes_accessed=8 * count * WIDTH,
            transcendentals=count * count * GROUP_HEADS,
        ),
    )(table, ids, own, other, *weights, bias)


def attend_back_body(
    table,
    ids,
    joined,
    grad_mixed,
    log_total,
    w0,
    w1,
    w2,
    w3,
    grad_joined,
    grad_own,
    grad_other,
    weight,
    sorted_grads,
    sorted_out,
    key_sums,
    value_sums,
):
    step = pl.program_id(0)
    half = grad_own.shape[1]

    @pl.when(step == 0)
    def _():
        place_weight(weight, (w0, w1, w2, w3), ids)
        sort_rows(sorted_grads, grad_mixed, table, False)
        key_sums[...] = jnp.zeros_like(key_sums)
        value_sums[...] = jnp.zeros_like(value_sums)

    def block(index):
        rows = slice(index * QUERY_BLOCK, (index + 1) * QUERY_BLOCK)
        seen = slice(0, (index + 1) * QUERY_BLOCK)
        parts = []
        for head in range(GROUP_HEADS):
            queries = joined[rows, head_columns(0, head)] * jnp.bfloat16(HDIM ** (-0.5))
            keys = joined[seen, head_columns(1, head)]
            values = joined[seen, head_columns(2, head)]
            grads = sorted_grads[rows, head_columns(0, head)]
            scores = mask_scores(dot(keys, queries, 1, 1))
            weights = jnp.exp(scores - log_total[head : head + 1, rows])
            grad_weights = dot(values, grads, 1, 1)
            inner_sum = jnp.sum(weights * grad_weights, 0, keepdims=True)
            grad_scores = (weights * (grad_weights - inner_sum)).astype(jnp.bfloat16)
            value_sums[head, seen, :] += dot(weights.astype(jnp.bfloat16), grads, 1, 0)
            key_sums[head, seen, :] += dot(grad_scores, queries, 1, 0)
            parts.append(dot(keys, grad_scores, 0, 0) * (HDIM ** (-0.5)))
        sorted_out[rows, :WIDTH] = jnp.concatenate(parts, 0).T.astype(jnp.bfloat16)

    for index in range(joined.shape[0] // QUERY_BLOCK):
        pl.when(step == index)(lambda index=index: block(index))

    @pl.when(step == pl.num_programs(0) - 1)
    def _():
        for head in range(GROUP_HEADS):
            sorted_out[:, head_columns(1, head)] = key_sums[head].astype(jnp.bfloat16)
            sorted_out[:, head_columns(2, head)] = value_sums[head].astype(jnp.bfloat16)
        sort_rows(grad_joined, sorted_out, table, True)
        grad_own[...] = dot(grad_joined[...], weight[:half, :], 1, 1).astype(jnp.bfloat16)
        grad_other[...] = dot(grad_joined[...], weight[half:, :], 1, 1).astype(jnp.bfloat16)


def attend_back(table, ids, joined, grad_mixed, log_total, weights):
    count = joined.shape[0]
    half = len(weights) * weights[0].shape[0] // 2
    return pl.pallas_call(
        attend_back_body,
        grid_spec=pltpu.PrefetchScalarGridSpec(
            num_scalar_prefetch=2,
            grid=(count // QUERY_BLOCK,),
            in_specs=[whole(count, 3 * WIDTH), whole(count, WIDTH), whole(8, count)]
            + [whole(*weight.shape) for weight in weights],
            out_specs=[whole(count, 3 * WIDTH), whole(count, half), whole(count, half)],
            scratch_shapes=[
                pltpu.VMEM((2 * half, 3 * WIDTH), jnp.bfloat16),
                pltpu.VMEM((count, WIDTH), jnp.bfloat16),
                pltpu.VMEM((count, 3 * WIDTH), jnp.bfloat16),
                pltpu.VMEM((GROUP_HEADS, count, HDIM), jnp.float32),
                pltpu.VMEM((GROUP_HEADS, count, HDIM), jnp.float32),
            ],
        ),
        out_shape=[
            jax.ShapeDtypeStruct((count, 3 * WIDTH), jnp.bfloat16),
            jax.ShapeDtypeStruct((count, half), jnp.bfloat16),
            jax.ShapeDtypeStruct((count, half), jnp.bfloat16),
        ],
        compiler_params=pltpu.CompilerParams(vmem_limit_bytes=48 << 20),
        cost_estimate=pl.CostEstimate(
            flops=10 * count * count * WIDTH,
            bytes_accessed=16 * count * WIDTH,
            transcendentals=count * count * GROUP_HEADS,
        ),
    )(table, ids, joined, grad_mixed, log_total, *weights)


def weight_grads_body(
    core_id,
    active,
    active_other,
    grad_low,
    grad_low_other,
    normed_two,
    normed_two_other,
    grad_hidden,
    grad_hidden_other,
    mixed,
    mixed_other,
    grad_attn,
    grad_attn_other,
    joint,
):
    down_rows, up_rows = active.shape[1], normed_two.shape[0]
    width = grad_low.shape[1]
    product = dot(active[...], grad_low[...], 0, 0)
    product += dot(active_other[...], grad_low_other[...], 0, 0)
    joint[0, :down_rows, :] = product.astype(jnp.bfloat16)
    place = down_rows
    for panel in range(grad_hidden.shape[1] // width):
        columns = slice(panel * width, (panel + 1) * width)
        product = dot(normed_two[...], grad_hidden[:, columns], 1, 0)
        product += dot(normed_two_other[...], grad_hidden_other[:, columns], 1, 0)
        joint[0, place : place + up_rows, :] = product.astype(jnp.bfloat16)
        place += up_rows
    product = dot(mixed[...], grad_attn[...], 1, 0)
    product += dot(mixed_other[...], grad_attn_other[...], 1, 0)
    joint[0, place : place + up_rows, :] = product.astype(jnp.bfloat16)
    place += up_rows
    joint[0, place:, :] = jnp.zeros_like(joint[0, place:, :])


def weight_grads(core_id, pairs, members):
    rows, hidden_width = pairs[0][0].shape
    width = pairs[1][0].shape[1]
    down_rows, up_rows = hidden_width // members // 2, width // members // 2
    out_rows = 2 * down_rows + up_rows + EXTRA
    flat = pl.BlockSpec((rows, width), lambda i, core: (0, 0))
    tall = pl.BlockSpec((up_rows, rows), lambda i, core: (2 * i + core[0], 0))
    specs = [
        pl.BlockSpec((rows, down_rows), lambda i, core: (0, 2 * i + core[0])),
        flat,
        tall,
        pl.BlockSpec((rows, hidden_width), lambda i, core: (0, 0)),
        tall,
        flat,
    ]
    return pl.pallas_call(
        weight_grads_body,
        grid_spec=pltpu.PrefetchScalarGridSpec(
            num_scalar_prefetch=1,
            grid=(members,),
            in_specs=[spec for spec in specs for _ in range(2)],
            out_specs=pl.BlockSpec((1, out_rows, width), lambda i, core: (i, 0, 0)),
        ),
        out_shape=jax.ShapeDtypeStruct((members, out_rows, width), jnp.bfloat16),
        compiler_params=pltpu.CompilerParams(vmem_limit_bytes=48 << 20),
        cost_estimate=pl.CostEstimate(
            flops=2 * rows * width * (2 * hidden_width + width),
            bytes_accessed=2 * members * out_rows * width,
            transcendentals=0,
        ),
    )(core_id, *[value for pair in pairs for value in pair])


def feed_forward_body(mixed, entering, packed, vectors, up_bias, result):
    members, width = packed.shape[0], packed.shape[2]
    panels = up_bias.shape[0]
    up_rows = width // members
    down_rows = panels * up_rows
    micro_count = mixed.shape[0] // GROUPS

    def weight_panel(start):
        return jnp.concatenate(
            [packed[member, start : start + up_rows, :] for member in range(members)], 0
        )

    w_out = weight_panel(2 * down_rows)
    middle = entering[...].astype(jnp.float32) + vectors[5:6, :]
    for group in range(GROUPS):
        part = jnp.concatenate([mixed[m * GROUPS + group] for m in range(micro_count)], 0)
        middle += dot(part, w_out[group * WIDTH : (group + 1) * WIDTH, :], 1, 0)
    normed, _, _ = normalize(middle, vectors[1:2, :], vectors[6:7, :])
    normed = normed.astype(jnp.bfloat16)
    parts = []
    for panel in range(panels):
        hidden = dot(normed, weight_panel(down_rows + panel * up_rows), 1, 0)
        hidden = hidden + up_bias[panel : panel + 1, :]
        parts.append(jax.nn.gelu(hidden).astype(jnp.bfloat16))
    active = jnp.concatenate(parts, 1)
    total = middle + vectors[7:8, :]
    for member in range(members):
        columns = slice(member * down_rows, (member + 1) * down_rows)
        total += dot(active[:, columns], packed[member, :down_rows, :], 1, 0)
    result[...] = total.astype(jnp.bfloat16)


def feed_forward(mixed, entering, packed, vectors, up_bias):
    rows, width = entering.shape
    return pl.pallas_call(
        feed_forward_body,
        in_specs=[pl.BlockSpec(memory_space=pltpu.VMEM)] * 5,
        out_specs=pl.BlockSpec(memory_space=pltpu.VMEM),
        out_shape=jax.ShapeDtypeStruct((rows, width), jnp.bfloat16),
        compiler_params=pltpu.CompilerParams(vmem_limit_bytes=48 << 20),
        cost_estimate=pl.CostEstimate(
            flops=18 * rows * width * width,
            bytes_accessed=18 * width * width,
            transcendentals=4 * rows * width,
        ),
    )(mixed, entering, packed, vectors, up_bias)


def qkv_grads_body(ids, own, other, grad_joined, *outs):
    pieces, sums, both = outs[:-2], outs[-2], outs[-1]
    first_core = ids[0] == 0
    grads = grad_joined[...]
    half = own.shape[1]
    own_grads = dot(own[...], grads, 0, 0).astype(jnp.bfloat16)
    other_grads = dot(other[...], grads, 0, 0).astype(jnp.bfloat16)
    both[:half, :] = jnp.where(first_core, own_grads, other_grads)
    both[half:, :] = jnp.where(first_core, other_grads, own_grads)
    count, piece_rows = len(pieces), pieces[0].shape[0]
    for shift in range(count):
        start = lax.rem(ids[1] + shift, count) * piece_rows
        pieces[shift][...] = both[pl.ds(pl.multiple_of(start, piece_rows), piece_rows), :]
    sums[...] = jnp.sum(grads.astype(jnp.float32), 0, keepdims=True)


def qkv_grads(ids, own, other, grad_joined, count):
    rows, half = own.shape
    width = grad_joined.shape[1]
    piece = jax.ShapeDtypeStruct((2 * half // count, width), jnp.bfloat16)
    return pl.pallas_call(
        qkv_grads_body,
        in_specs=[pl.BlockSpec(memory_space=pltpu.SMEM)]
        + [pl.BlockSpec(memory_space=pltpu.VMEM)] * 3,
        out_specs=[pl.BlockSpec(memory_space=pltpu.VMEM)] * (count + 1),
        out_shape=[piece] * count + [jax.ShapeDtypeStruct((1, width), jnp.float32)],
        scratch_shapes=[pltpu.VMEM((2 * half, width), jnp.bfloat16)],
        compiler_params=pltpu.CompilerParams(vmem_limit_bytes=48 << 20),
        cost_estimate=pl.CostEstimate(
            flops=4 * rows * half * width, bytes_accessed=6 * rows * half, transcendentals=0
        ),
    )(ids, own, other, grad_joined)


def unpack_body(core_id, own, other, g_qkv, g_out, g_up, g_down, vectors):
    first_core = core_id[0] == 0
    count = own.shape[0]
    width = own.shape[2]
    joint_rows = JOINT_ROWS
    piece_rows = own.shape[1] - joint_rows - 16
    up_rows = g_up.shape[0] // 2
    down_rows = g_down.shape[0] // 2
    sums = jnp.zeros(vectors.shape, jnp.float32)
    for core in range(2):
        pick = first_core if core == 0 else jnp.logical_not(first_core)
        joint = jnp.concatenate(
            [
                jnp.where(pick, own[i, :joint_rows, :], other[i, :joint_rows, :])
                for i in range(count)
            ],
            0,
        ).astype(jnp.float32)
        g_down[core * down_rows : (core + 1) * down_rows, :] = joint[:down_rows]
        place = down_rows
        for panel in range(g_up.shape[1] // width):
            g_up[core * up_rows : (core + 1) * up_rows, panel * width : (panel + 1) * width] = (
                joint[place : place + up_rows]
            )
            place += up_rows
        g_out[core * up_rows : (core + 1) * up_rows, :] = joint[place : place + up_rows]
        for i in range(count):
            x_id, group = i // 2, (i % 2) * 2 + core
            piece = jnp.where(pick, own[i, joint_rows:, :], other[i, joint_rows:, :])
            piece = piece.astype(jnp.float32)
            for part in range(3):
                start = part * width + group * WIDTH
                g_qkv[x_id * piece_rows : (x_id + 1) * piece_rows, start : start + WIDTH] = piece[
                    :piece_rows, part * WIDTH : (part + 1) * WIDTH
                ]
            sums += piece[piece_rows : piece_rows + 4, :]
    vectors[...] = sums


def unpack(core_id, own, other, shard, hidden_width, hidden_shard):
    width = own.shape[2]
    return pl.pallas_call(
        unpack_body,
        in_specs=[pl.BlockSpec(memory_space=pltpu.SMEM)]
        + [pl.BlockSpec(memory_space=pltpu.VMEM)] * 2,
        out_specs=[pl.BlockSpec(memory_space=pltpu.VMEM)] * 5,
        out_shape=[
            jax.ShapeDtypeStruct((shard, 3 * width), jnp.float32),
            jax.ShapeDtypeStruct((shard, width), jnp.float32),
            jax.ShapeDtypeStruct((shard, hidden_width), jnp.float32),
            jax.ShapeDtypeStruct((hidden_shard, width), jnp.float32),
            jax.ShapeDtypeStruct((4, width), jnp.float32),
        ],
        compiler_params=pltpu.CompilerParams(vmem_limit_bytes=48 << 20),
        cost_estimate=pl.CostEstimate(flops=0, bytes_accessed=12 << 20, transcendentals=0),
    )(core_id, own, other)


def cross(left_side, right_side, pattern):
    return jnp.einsum(pattern, left_side, right_side, preferred_element_type=jnp.float32)


def normalize(values, gain_row, shift_row):
    center = values - jnp.mean(values, -1, keepdims=True)
    spread = lax.rsqrt(jnp.mean(center * center, -1, keepdims=True) + epsilon)
    unit_rows = center * spread
    return (unit_rows * gain_row + shift_row, unit_rows, spread)


def normalize_back(grad_out, unit_rows, spread, gain_row):
    grad_unit = grad_out * gain_row
    grad_in = spread * (
        grad_unit
        - jnp.mean(grad_unit, -1, keepdims=True)
        - unit_rows * jnp.mean(grad_unit * unit_rows, -1, keepdims=True)
    )
    return (grad_in, jnp.sum(grad_out * unit_rows, 0), jnp.sum(grad_out, 0))


def exchange(value, axes):
    return lax.all_to_all(value, axes, 0, 0, tiled=True)


def swap(value):
    return lax.ppermute(value, "core", [(0, 1), (1, 0)])


def in_order(own, other):
    first = lax.axis_index("core") == 0
    return jnp.where(first, own, other), jnp.where(first, other, own)


def gather_weights(attn_out, mlp_in, mlp_out):
    core_id = lax.axis_index("core")
    width = attn_out.shape[2]
    out_half, up_half, down_half = (
        lax.dynamic_slice_in_dim(
            weight[0], core_id * (weight.shape[1] // 2), weight.shape[1] // 2, 0
        )
        for weight in (attn_out, mlp_in, mlp_out)
    )
    panels = [up_half[:, start : start + width] for start in range(0, mlp_in.shape[2], width)]
    packed = jnp.concatenate([down_half] + panels + [out_half], 0)
    everyone = lax.all_gather(packed, ("fsdp", "core"), axis=0)
    down_rows, up_rows = down_half.shape[0], up_half.shape[0]
    w_down = everyone[:, :down_rows].reshape(-1, width)
    w_up = jnp.concatenate(
        [
            everyone[:, start : start + up_rows].reshape(-1, width)
            for start in range(down_rows, 2 * down_rows, up_rows)
        ],
        1,
    )
    w_out = everyone[:, 2 * down_rows :].reshape(-1, width)
    return everyone, w_out, w_up, w_down


def ring_pairs(axis, shift):
    count = lax.axis_size(axis)
    return [(source, (source + shift) % count) for source in range(count)]


def gather_ring(value, axis):
    return [value] + [
        lax.ppermute(value, axis, ring_pairs(axis, -shift))
        for shift in range(1, lax.axis_size(axis))
    ]


def sum_pieces(pieces, axis):
    total = pieces[0].astype(jnp.float32)
    for shift in range(1, len(pieces)):
        received = lax.ppermute(pieces[shift], axis, ring_pairs(axis, shift))
        total = total + received.astype(jnp.float32)
    return total.astype(jnp.bfloat16)


def sum_low(value):
    return jnp.sum(value.astype(jnp.float32), 0).astype(jnp.bfloat16)


def spread(value, axes):
    count = lax.axis_size(axes)
    return exchange(jnp.broadcast_to(value[None], (count,) + value.shape), axes)


def shards(
    inputs,
    cotangent,
    plan,
    block_table,
    attn_in,
    attn_out,
    mlp_in,
    mlp_out,
    norm_gains,
    biases,
    mlp_bias,
):
    shard = norm_gains.shape[2]
    core_id = lax.axis_index("core")
    group_id = lax.axis_index("yh") * 2 + core_id
    fsdp_id = lax.axis_index("fsdp")
    section_id = lax.axis_index("section")
    sections = lax.axis_size("section")
    fsdp_count = lax.axis_size("fsdp")

    small = jnp.concatenate([norm_gains[0], biases[0], mlp_bias.reshape(-1, shard)], 0)
    small = small.reshape(-1, 3 * WIDTH)
    own_columns = lax.dynamic_index_in_dim(
        attn_in[0].reshape(shard, 3, GROUPS, WIDTH), group_id, 2, keepdims=False
    ).reshape(shard, 3 * WIDTH)
    small_all = spread(small, "fsdp").reshape(fsdp_count, -1, shard).astype(jnp.float32)
    own_columns, small_all = lax.optimization_barrier((own_columns, small_all))
    w_group = gather_ring(own_columns, "fsdp")
    packed, w_out, w_up, w_down = gather_weights(attn_out, mlp_in, mlp_out)
    model_width = w_out.shape[0]
    half = model_width // 2
    w_out_groups = w_out.reshape(GROUPS, WIDTH, model_width)
    vector_rows = small_all[:, :8].transpose(1, 0, 2).reshape(8, model_width)
    gain_rows, bias_rows = vector_rows[:2], vector_rows[2:]
    up_bias = small_all[:, 8:].reshape(-1)
    own_bias = lax.dynamic_index_in_dim(small_all, group_id, 0, keepdims=False)
    group_bias = jnp.concatenate([own_bias[3], jnp.zeros_like(own_bias[3]), own_bias[4]])[None]

    micro_count, _, local_rows, _ = inputs.shape
    rows = micro_count * local_rows
    fresh = jnp.stack(
        [lax.dynamic_index_in_dim(inputs, plan[step], 0, keepdims=False) for step in range(micro_count)]
    ).reshape(rows, model_width)
    top_grad = cotangent.reshape(rows, model_width)
    core_number = core_id.astype(jnp.int32)[None]
    numbers = jnp.stack([core_id, fsdp_id]).astype(jnp.int32)
    head_shape = (micro_count, GROUPS, local_rows, WIDTH)

    def forward(entering, last):
        stream = entering.astype(jnp.float32)
        normed, unit_one, spread_one = normalize(stream, gain_rows[0], bias_rows[0])
        halves = normed.astype(jnp.bfloat16).reshape(micro_count, 1, local_rows, 2, half)
        halves = jnp.broadcast_to(
            halves.transpose(0, 1, 3, 2, 4), (micro_count, 2, 2, local_rows, half)
        )
        own = exchange(halves.reshape(-1, local_rows, half), CTX).reshape(-1, half)
        other = swap(own)
        joined, mixed_heads, log_total = attend(
            block_table, numbers, own, other, w_group, group_bias
        )
        mixed = exchange(mixed_heads.reshape(-1, local_rows, WIDTH), CTX)
        if not last:
            return feed_forward(
                mixed, entering, packed, vector_rows, up_bias.reshape(-1, model_width)
            )
        mixed = mixed.reshape(head_shape)
        attended = cross(mixed, w_out_groups, "mgtd,gde->mte").reshape(rows, model_width)
        middle = stream + (attended + bias_rows[3])
        normed_two, unit_two, spread_two = normalize(middle, gain_rows[1], bias_rows[4])
        normed_two_low = normed_two.astype(jnp.bfloat16)
        hidden_pre = cross(normed_two_low, w_up, "td,df->tf") + up_bias
        active_low = jax.nn.gelu(hidden_pre).astype(jnp.bfloat16)
        result = (middle + (cross(active_low, w_down, "tf,fd->td") + bias_rows[5])).astype(
            jnp.bfloat16
        )
        saved = (
            unit_one,
            spread_one,
            own,
            other,
            joined,
            log_total,
            mixed,
            unit_two,
            spread_two,
            normed_two_low,
            hidden_pre,
            active_low,
        )
        return result, saved

    def backward(grad_low, saved, last):
        (
            unit_one,
            spread_one,
            own,
            other,
            joined,
            log_total,
            mixed,
            unit_two,
            spread_two,
            normed_two_low,
            hidden_pre,
            active_low,
        ) = saved
        grad_top = grad_low.astype(jnp.float32)
        grad_active = cross(grad_low, w_down, "td,fd->tf")
        _, gelu_pull = jax.vjp(jax.nn.gelu, hidden_pre)
        grad_hidden = gelu_pull(grad_active)[0].astype(jnp.bfloat16)
        grad_normed_two = cross(grad_hidden, w_up, "tf,df->td")
        grad_norm_two, d_gain_two, d_shift_two = normalize_back(
            grad_normed_two, unit_two, spread_two, gain_rows[1]
        )
        grad_middle = grad_top + grad_norm_two
        grad_attn = grad_middle.astype(jnp.bfloat16)
        attn_parts = grad_attn.reshape(micro_count, local_rows, model_width)
        grad_mixed = cross(attn_parts, w_out_groups, "mte,gde->mgtd").astype(jnp.bfloat16)
        share = None
        grad_heads = exchange(grad_mixed.reshape(-1, local_rows, WIDTH), CTX).reshape(-1, WIDTH)
        if last:
            normed_tall = normed_two_low.T
            mixed_tall = mixed.transpose(1, 3, 0, 2).reshape(model_width, rows)
            members = (active_low, grad_low, normed_tall, grad_hidden, mixed_tall, grad_attn)
            joint = weight_grads(
                core_number, [(value, swap(value)) for value in members], fsdp_count
            )
            grad_heads, joint = lax.optimization_barrier((grad_heads, joint))
            share = lax.psum_scatter(
                joint.reshape(-1, model_width),
                "fsdp",
                scatter_dimension=0,
                tiled=True,
            )
        grad_joined, grad_own, grad_other = attend_back(
            block_table, numbers, joined, grad_heads, log_total, w_group
        )
        received = swap(grad_other)
        summed = (grad_own.astype(jnp.float32) + received.astype(jnp.float32)).astype(jnp.bfloat16)
        returned = exchange(summed.reshape(-1, local_rows, half), CTX)
        returned = returned.reshape(micro_count, 2, 2, local_rows, half).astype(jnp.float32)
        grad_normed = (returned[:, 0] + returned[:, 1]).transpose(0, 2, 1, 3)
        grad_normed = grad_normed.reshape(rows, model_width)
        grad_norm_one, d_gain_one, d_shift_one = normalize_back(
            grad_normed, unit_one, spread_one, gain_rows[0]
        )
        grad_in = (grad_middle + grad_norm_one).astype(jnp.bfloat16)
        if not last:
            return grad_in
        *pieces, joined_sums = qkv_grads(numbers, own, other, grad_joined, fsdp_count)
        joined_sums = joined_sums[0]
        qkv_share = sum_pieces(pieces, "fsdp")
        x_count = lax.axis_size("x")
        piece_rows = shard // x_count
        x_pieces = [
            lax.dynamic_slice_in_dim(
                qkv_share, (lax.axis_index("x") + shift) % x_count * piece_rows, piece_rows, 0
            )
            for shift in range(x_count)
        ]
        qkv_piece = sum_pieces(x_pieces, "x")
        vectors = jnp.stack(
            [
                d_gain_one,
                d_gain_two,
                d_shift_one,
                jnp.sum(grad_attn.astype(jnp.float32), 0),
                d_shift_two,
                jnp.sum(grad_top, 0),
            ]
        )
        d_up_bias = jnp.sum(grad_hidden.astype(jnp.float32), 0)
        return grad_in, share, qkv_piece, joined_sums, vectors, d_up_bias

    forward_pairs = [(i, i + 1) for i in range(sections - 1)]
    entering = fresh
    for _ in range(sections - 1):
        result = forward(entering, False)
        received = lax.ppermute(result, "section", forward_pairs)
        entering = jnp.where(section_id == 0, fresh, received)
    layer_out, saved = forward(entering, True)

    back_pairs = [(i + 1, i) for i in range(sections - 1)]
    grad_low = top_grad
    for _ in range(sections - 1):
        result = backward(grad_low, saved, False)
        received = lax.ppermute(result, "section", back_pairs)
        grad_low = jnp.where(section_id == sections - 1, top_grad, received)
    input_grad, share, qkv_piece, joined_sums, vectors, d_up_bias = backward(grad_low, saved, True)

    ours = jnp.arange(fsdp_count)[:, None] == group_id
    vector_parts = jnp.concatenate(
        [
            vectors.reshape(6, -1, shard).transpose(1, 0, 2).reshape(-1, 6 * shard),
            jnp.where(ours, joined_sums[None, :WIDTH], 0.0),
            jnp.where(ours, joined_sums[None, 2 * WIDTH :], 0.0),
            d_up_bias.reshape(fsdp_count, -1),
        ],
        1,
    )
    vector_parts = vector_parts.astype(jnp.bfloat16).reshape(fsdp_count, 4, 3 * WIDTH)
    vector_share = sum_low(exchange(vector_parts, "fsdp"))
    vector_share = jnp.pad(vector_share, ((0, 12), (0, 0)))
    qkv_piece = jnp.concatenate([qkv_piece, vector_share], 0)
    qkv_piece = jnp.pad(qkv_piece, ((0, 0), (0, model_width - 3 * WIDTH)))
    share, qkv_piece = lax.optimization_barrier((share, qkv_piece))
    joint_piece = sum_low(exchange(share.reshape(8, -1, model_width), ("x", "yh")))
    joint_piece, layer_out = lax.optimization_barrier((joint_piece, layer_out))
    both = spread(jnp.concatenate([joint_piece, qkv_piece], 0), ("x", "yh"))
    g_qkv, g_out, g_up, g_down, vector_sum = unpack(
        core_number, both, swap(both), shard, mlp_in.shape[2], mlp_out.shape[1]
    )
    vector_sum = vector_sum[:, : 3 * WIDTH].reshape(-1)
    own_vectors = vector_sum[: 8 * shard].reshape(8, shard)
    own_up_bias = vector_sum[8 * shard :]
    order = (2, 6, 7, 3, 4, 5)
    g_biases = jnp.stack([own_vectors[place] for place in order])
    out_shape = (1, micro_count, 1, local_rows, model_width)
    return (
        layer_out.reshape(out_shape),
        input_grad.reshape(out_shape),
        g_qkv[None],
        g_out[None],
        g_up[None],
        g_down[None],
        own_vectors[None, :2],
        g_biases[None],
        own_up_bias[None],
    )


def solution(mesh):
    fine = Mesh(
        mesh.devices.reshape(2, 4, 2, 2, 4), ("section", "x", "yh", "core", "fsdp")
    )
    rows = P(None, "fsdp", CTX, None)
    weight = P("section", "fsdp", None)
    vector = P("section", None, "fsdp")
    row = P("section", "fsdp")
    out_rows = P("section", None, "fsdp", CTX, None)
    return jax.shard_map(
        shards,
        mesh=fine,
        in_specs=(rows, rows, P(), P(), weight, weight, weight, weight, vector, vector, row),
        out_specs=(out_rows, out_rows, weight, weight, weight, weight, vector, vector, row),
        check_vma=False,
    )
```

profile of v0, /device:TPU:1, one launch (start us, length us, event | category | flops | bytes accessed | tf_op | source)
XLA Modules:
  0.0 448.8 jit_solution(10885889323482432970)
XLA Ops:
  11.7 5.9 %all-to-all-start = ((bf16[4,4,576]{2,1,0:T(4,128)(2,1)}), bf16[4,4,576]{2,1,0:T(4,128)(2,1)S(1)}, u32[]{:S(2)}, u32[]{:S(2)}) async-start(bf16[4,4,576]{2,1,0:T(4,128)(2,1)} %broadcast_in_dim.104), calls=%async_computation | async-start | bytes 40960 | tf_op jit(solution)/shard_map/all_to_all | solution.py:460
  31.3 22.2 %all_to_all.60 = bf16[16,64,384]{2,1,0:T(8,128)(2,1)S(1)} all-to-all(bf16[16,64,384]{2,1,0:T(8,128)(2,1)S(1)} %bitcast.182), channel_id=1, replica_groups=mesh['section'=2,'x'=4,'yh'=2,'core'=2,'fsdp'=4] {'x','yh','core'}, dimensions={0} | all-to-all | bytes 1572864 | tf_op jit(solution)/shard_map/all_to_all | solution.py:460
  54.2 1.9 collective-permute-start.3
  56.1 2.4 collective-permute-start.2
  60.7 8.3 %collective-permute-done.3.w3 = bf16[192,576]{1,0:T(8,128)(2,1)S(1)} collective-permute-done((bf16[192,576]{1,0:T(8,128)(2,1)S(1)}, bf16[192,576]{1,0:T(8,128)(2,1)S(1)}, u32[]{:S(2)}, u32[]{:S(2)}) %collective-permute-start.3) | collective-permute-done | bytes 221216 | tf_op jit(solution)/shard_map/ppermute | solution.py:504
  69.0 11.6 %collective-permute-done.2.w2 = bf16[192,576]{1,0:T(8,128)(2,1)S(1)} collective-permute-done((bf16[192,576]{1,0:T(8,128)(2,1)S(1)}, bf16[192,576]{1,0:T(8,128)(2,1)S(1)}, u32[]{:S(2)}, u32[]{:S(2)}) %collective-permute-start.2) | collective-permute-done | bytes 221216 | tf_op jit(solution)/shard_map/ppermute | solution.py:504
  80.6 10.3 %shard_map.178 = (bf16[1024,576]{1,0:T(8,128)(2,1)}, bf16[1024,192]{1,0:T(8,128)(2,1)}, f32[8,1024]{1,0:T(8,128)}) custom-call(s32[32]{0:T(128)S(1)} %copy-done.15, s32[2]{0:T(128)S(1)} %pad_add_fusion.ids, bf16[1024,384]{1,0:T(8,128)(2,1)S(1)} %bitcast.167, bf16[1024,384]{1,0:T(8,128)(2,1)S(1)} %collective-permute-done.other, ...), custom_call_target="tpu_custom_call" | custom-call | flops 805306368 | bytes 1572864 | tf_op jit(solution)/shard_map/pallas_call | solution.py:107
  90.9 4.3 all-to-all-start.2
  96.2 10.2 %all-to-all-done.2.mixed = bf16[16,64,192]{2,1,0:T(8,128)(2,1)S(1)} async-done(((bf16[16,64,192]{2,1,0:T(8,128)(2,1)}), bf16[16,64,192]{2,1,0:T(8,128)(2,1)S(1)}, u32[]{:S(2)}, u32[]{:S(2)}) %all-to-all-start.2) | async-done | bytes 393248 | tf_op jit(solution)/shard_map/all_to_all | solution.py:460
  106.4 8.5 %shard_map.179 = bf16[256,768]{1,0:T(8,128)(2,1)S(1)} custom-call(bf16[16,64,192]{2,1,0:T(8,128)(2,1)S(1)} %all-to-all-done.2.mixed, bf16[256,768]{1,0:T(8,128)(2,1)S(1)} %bitcast.161, bf16[8,864,768]{2,1,0:T(8,128)(2,1)} %bitcast.169, f32[8,768]{1,0:T(8,128)S(1)} %reshape.446.vectors, f32[4,768]{1,0:T(4,128)S(1)} %reshape_reshape.7.up_bias), custom_call_target="tpu_custom_call" | custom-call | flops 2717908992 | bytes 10616832 | tf_op jit(solution)/shard_map/pallas_call | solution.py:332
  114.9 2.3 collective-permute-start.4
  117.4 6.8 %collective-permute-done.4 = bf16[256,768]{1,0:T(8,128)(2,1)S(1)} collective-permute-done((bf16[256,768]{1,0:T(8,128)(2,1)S(1)}, bf16[256,768]{1,0:T(8,128)(2,1)S(1)}, u32[]{:S(2)}, u32[]{:S(2)}) %collective-permute-start.4) | collective-permute-done | bytes 393248 | tf_op jit(solution)/shard_map/ppermute | solution.py:705
  125.3 20.6 %all_to_all.61 = bf16[16,64,384]{2,1,0:T(8,128)(2,1)S(1)} all-to-all(bf16[16,64,384]{2,1,0:T(8,128)(2,1)S(1)} %bitcast.183), channel_id=1, replica_groups=mesh['section'=2,'x'=4,'yh'=2,'core'=2,'fsdp'=4] {'x','yh','core'}, dimensions={0} | all-to-all | bytes 1572864 | tf_op jit(solution)/shard_map/all_to_all | solution.py:460
  147.6 4.8 %slice.228 = bf16[8,384,768]{2,1,0:T(8,128)(2,1)} slice(bf16[8,864,768]{2,1,0:T(8,128)(2,1)} %bitcast.170), slice={[0:8], [0:384], [0:768]} | slice | bytes 9437184 | tf_op jit(solution)/shard_map/slice | solution.py:485
  152.4 9.8 %shard_map.180 = (bf16[1024,576]{1,0:T(8,128)(2,1)S(1)}, bf16[1024,192]{1,0:T(8,128)(2,1)}, f32[8,1024]{1,0:T(8,128)S(1)}) custom-call(s32[32]{0:T(128)S(1)} %copy-done.15, s32[2]{0:T(128)S(1)} %pad_add_fusion.ids, bf16[1024,384]{1,0:T(8,128)(2,1)S(1)} %bitcast.164, bf16[1024,384]{1,0:T(8,128)(2,1)S(1)} %collective-permute-done.5.other, ...), custom_call_target="tpu_custom_call" | custom-call | flops 805306368 | bytes 1572864 | tf_op jit(solution)/shard_map/pallas_call | solution.py:107
  163.3 3.5 all-to-all-start.4
  166.8 5.3 %fusion.61 = (bf16[8,96,768]{2,1,0:T(8,128)(2,1)}, bf16[8,96,768]{2,1,0:T(8,128)(2,1)}, bf16[8,96,768]{2,1,0:T(8,128)(2,1)}, bf16[8,96,768]{2,1,0:T(8,128)(2,1)}, bf16[8,96,768]{2,1,0:T(8,128)(2,1)}) fusion(bf16[8,864,768]{2,1,0:T(8,128)(2,1)} %bitcast.171), kind=kLoop, calls=%fused_computation.151 | loop fusion | bytes 11796480 | tf_op jit(solution)/shard_map/slice | solution.py:488
  172.1 5.8 %all-to-all-done.4 = bf16[16,64,192]{2,1,0:T(8,128)(2,1)S(1)} async-done(((bf16[16,64,192]{2,1,0:T(8,128)(2,1)}), bf16[16,64,192]{2,1,0:T(8,128)(2,1)S(1)}, u32[]{:S(2)}, u32[]{:S(2)}) %all-to-all-start.4) | async-done | bytes 393248 | tf_op jit(solution)/shard_map/all_to_all | solution.py:460
  178.1 2.1 fusion.65
  180.9 3.6 multiply_convert_fusion
  184.5 10.6 %fusion.54 = (f32[256]{0:T(256)}, f32[256]{0:T(256)}, f32[256,768]{1,0:T(8,128)}) fusion(f32[256]{0:T(256)S(1)} %add_rsqrt_fusion.1, f32[256,768]{1,0:T(8,128)S(1)} %get-tuple-element.152, f32[256]{0:T(256)S(1)} %broadcast_multiply_fusion.9, f32[768]{0:T(1024)S(1)} %mul.300, bf16[768,768]{1,0:T(8,128)(2,1)} %bitcast.198, bf16[768,768]{1,0:T(8,128)(2,1)} %bitcast.201, ...), kind=kOutput, calls=%fused_computation.146 | convolution fusion | flops 2451701248 | bytes 14556160 | tf_op jit(solution)/shard_map/tf,df->td/dot_general | solution.py:439
  195.9 2.7 fusion.60
  199.2 15.1 %all_to_all.62 = bf16[16,64,192]{2,1,0:T(8,128)(2,1)S(1)} all-to-all(bf16[16,64,192]{2,1,0:T(8,128)(2,1)S(1)} %bitcast.188), channel_id=1, replica_groups=mesh['section'=2,'x'=4,'yh'=2,'core'=2,'fsdp'=4] {'x','yh','core'}, dimensions={0} | all-to-all | bytes 786432 | tf_op jit(solution)/shard_map/all_to_all | solution.py:460
  214.4 12.1 %shard_map.181 = (bf16[1024,576]{1,0:T(8,128)(2,1)}, bf16[1024,384]{1,0:T(8,128)(2,1)S(1)}, bf16[1024,384]{1,0:T(8,128)(2,1)S(1)}) custom-call(s32[32]{0:T(128)S(1)} %copy-done.15, s32[2]{0:T(128)S(1)} %pad_add_fusion.ids, bf16[1024,576]{1,0:T(8,128)(2,1)S(1)} %copy-done.19, bf16[1024,192]{1,0:T(8,128)(2,1)S(1)} %bitcast.168, ...), custom_call_target="tpu_custom_call" | custom-call | flops 2013265920 | bytes 3145728 | tf_op jit(solution)/shard_map/pallas_call | solution.py:200
  227.9 1.9 collective-permute-done.6
  230.0 17.4 %all_to_all.63 = bf16[16,64,384]{2,1,0:T(8,128)(2,1)S(1)} all-to-all(bf16[16,64,384]{2,1,0:T(8,128)(2,1)S(1)} %bitcast.187), channel_id=1, replica_groups=mesh['section'=2,'x'=4,'yh'=2,'core'=2,'fsdp'=4] {'x','yh','core'}, dimensions={0} | all-to-all | bytes 1572864 | tf_op jit(solution)/shard_map/all_to_all | solution.py:460
  250.8 2.2 fusion.32
  256.1 9.3 %collective-permute-done.7 = bf16[256,768]{1,0:T(8,128)(2,1)} collective-permute-done((bf16[256,768]{1,0:T(8,128)(2,1)}, bf16[256,768]{1,0:T(8,128)(2,1)}, u32[]{:S(2)}, u32[]{:S(2)}) %collective-permute-start.7) | collective-permute-done | bytes 393248 | tf_op jit(solution)/shard_map/ppermute | solution.py:713
  267.3 8.4 %fusion.55 = (bf16[3072]{0:T(1024)(128)(2,1)}, bf16[256,3072]{1,0:T(8,128)(2,1)}) fusion(f32[256,3072]{1,0:T(8,128)} %get-tuple-element.155, bf16[256,768]{1,0:T(8,128)(2,1)S(1)} %get-tuple-element.109.grad_low, bf16[3072,768]{1,0:T(8,128)(2,1)} %bitcast.178), kind=kOutput, calls=%fused_computation.147 | convolution fusion | flops 1224471552 | bytes 9836544 | tf_op jit(solution)/shard_map/td,fd->tf/dot_general | solution.py:439
  277.0 2.9 fusion.53
  284.9 4.4 all-to-all-start.7
  292.1 8.1 %shard_map.182 = bf16[4,896,768]{2,1,0:T(8,128)(2,1)} custom-call(s32[1]{0:T(128)} %bitcast.13.core_id, bf16[256,3072]{1,0:T(8,128)(2,1)S(1)} %get-tuple-element.154.active, bf16[256,3072]{1,0:T(8,128)(2,1)} %collective-permute-done.8.active_other, bf16[256,768]{1,0:T(8,128)(2,1)S(1)} %get-tuple-element.109.grad_low, ...), custom_call_target="tpu_custom_call" | custom-call | flops 2717908992 | bytes 5505024 | tf_op jit(solution)/shard_map/pallas_call | solution.py:280
  305.3 13.0 %shard_map.183 = (bf16[1024,576]{1,0:T(8,128)(2,1)S(1)}, bf16[1024,384]{1,0:T(8,128)(2,1)S(1)}, bf16[1024,384]{1,0:T(8,128)(2,1)}) custom-call(s32[32]{0:T(128)S(1)} %copy-done.15, s32[2]{0:T(128)S(1)} %pad_add_fusion.ids, bf16[1024,576]{1,0:T(8,128)(2,1)S(1)} %copy-done.20, bf16[1024,192]{1,0:T(8,128)(2,1)} %bitcast.58.grad_mixed, ...), custom_call_target="tpu_custom_call" | custom-call | flops 2013265920 | bytes 3145728 | tf_op jit(solution)/shard_map/pallas_call | solution.py:200
  325.4 3.0 shard_map.184
  328.4 2.6 collective-permute-start.15
  331.0 2.1 collective-permute-start.16
  333.1 2.2 add_convert_fusion.2
  335.3 7.5 %all-to-all-start.8 = ((bf16[16,64,384]{2,1,0:T(8,128)(2,1)}), bf16[16,64,384]{2,1,0:T(8,128)(2,1)S(1)}, u32[]{:S(2)}, u32[]{:S(2)}) async-start(bf16[16,64,384]{2,1,0:T(8,128)(2,1)} %bitcast.186), calls=%async_computation.9 | async-start | bytes 1572864 | tf_op jit(solution)/shard_map/all_to_all | solution.py:460
  343.2 10.5 %collective-permute-done.15 = bf16[192,576]{1,0:T(8,128)(2,1)} collective-permute-done((bf16[192,576]{1,0:T(8,128)(2,1)}, bf16[192,576]{1,0:T(8,128)(2,1)}, u32[]{:S(2)}, u32[]{:S(2)}) %collective-permute-start.15) | collective-permute-done | bytes 221216 | tf_op jit(solution)/shard_map/ppermute | solution.py:512
  362.7 3.9 all-to-all-start.9
  366.7 4.2 all-to-all-done.9
  371.0 5.1 %all-to-all-start.10 = ((bf16[8,112,768]{2,1,0:T(8,128)(2,1)}), bf16[8,112,768]{2,1,0:T(8,128)(2,1)}, u32[]{:S(2)}, u32[]{:S(2)}) async-start(bf16[8,112,768]{2,1,0:T(8,128)(2,1)} %bitcast.191), calls=%async_computation.11 | async-start | bytes 2752512 | tf_op jit(solution)/shard_map/all_to_all | solution.py:460
  376.2 4.5 fusion.15
  380.6 12.4 %all-to-all-done.10 = bf16[8,112,768]{2,1,0:T(8,128)(2,1)} async-done(((bf16[8,112,768]{2,1,0:T(8,128)(2,1)}), bf16[8,112,768]{2,1,0:T(8,128)(2,1)}, u32[]{:S(2)}, u32[]{:S(2)}) %all-to-all-start.10) | async-done | bytes 1376288 | tf_op jit(solution)/shard_map/all_to_all | solution.py:460
  394.8 33.2 %all_to_all.64.own = bf16[8,176,768]{2,1,0:T(8,128)(2,1)S(1)} all-to-all(bf16[8,176,768]{2,1,0:T(8,128)(2,1)S(1)} %broadcast_in_dim.117), channel_id=1, replica_groups=mesh['section'=2,'x'=4,'yh'=2,'core'=2,'fsdp'=4] {'x','yh'}, dimensions={0} | all-to-all | bytes 4325376 | tf_op jit(solution)/shard_map/all_to_all | solution.py:460
  428.0 2.9 collective-permute-start.21
  431.0 2.6 fusion.38
  434.9 4.8 %shard_map.185 = (f32[192,2304]{1,0:T(8,128)}, f32[192,768]{1,0:T(8,128)}, f32[192,3072]{1,0:T(8,128)}, f32[768,768]{1,0:T(8,128)}, f32[4,768]{1,0:T(4,128)S(1)}) custom-call(s32[1]{0:T(128)} %bitcast.13.core_id, bf16[8,176,768]{2,1,0:T(8,128)(2,1)S(1)} %all_to_all.64.own, bf16[8,176,768]{2,1,0:T(8,128)(2,1)} %collective-permute-done.21.other), custom_call_target="tpu_custom_call" | custom-call | bytes 12582912 | tf_op jit(solution)/shard_map/pallas_call | solution.py:421
  (337 shorter events, 65.9 us)
Async XLA Ops:
  7.3 99.1 %all-gather.3.cloned.1.call-start = ((), (), s32[]{:S(2)}) async-start(), calls=%async_computation.14 | async-start | bytes 11943936 | tf_op jit(solution)/shard_map/all_gather | solution.py:483
  11.7 17.7 %all-to-all-start = ((bf16[4,4,576]{2,1,0:T(4,128)(2,1)}), bf16[4,4,576]{2,1,0:T(4,128)(2,1)S(1)}, u32[]{:S(2)}, u32[]{:S(2)}) async-start(bf16[4,4,576]{2,1,0:T(4,128)(2,1)} %broadcast_in_dim.104), calls=%async_computation | async-start | bytes 40960 | tf_op jit(solution)/shard_map/all_to_all | solution.py:460
  28.6 52.0 %copy-start.15 = (s32[32]{0:T(128)S(1)}, s32[32]{0:T(128)}, u32[]{:S(2)}) copy-start(s32[32]{0:T(128)} %table.7) | copy-start | bytes 388
  29.6 24.6 %copy-start.48 = (f32[4,12,192]{2,1,0:T(8,128)}, f32[4,12,192]{2,1,0:T(8,128)S(1)}, u32[]{:S(2)}) copy-start(f32[4,12,192]{2,1,0:T(8,128)S(1)} %reshape.476) | copy-start | bytes 110596
  30.3 23.7 %copy-start.55 = (f32[4,192]{1,0:T(4,128)}, f32[4,192]{1,0:T(4,128)S(1)}, u32[]{:S(2)}) copy-start(f32[4,192]{1,0:T(4,128)S(1)} %get-tuple-element.105) | copy-start | bytes 9220
  30.3 60.6 %copy-start.50 = (f32[2,384]{1,0:T(2,128)}, f32[2,384]{1,0:T(2,128)S(1)}, u32[]{:S(2)}) copy-start(f32[2,384]{1,0:T(2,128)S(1)} %mul.288) | copy-start | bytes 9220
  53.6 27.0 %collective-permute-start = (bf16[1024,384]{1,0:T(8,128)(2,1)S(1)}, bf16[1024,384]{1,0:T(8,128)(2,1)S(1)}, u32[]{:S(2)}, u32[]{:S(2)}) collective-permute-start(bf16[1024,384]{1,0:T(8,128)(2,1)S(1)} %bitcast.166), channel_id=1, source_target_pairs={{0,4},{4,0},{1,5},{5,1},{2,6},{6,2},{3,7},{7,3},{8,12},{12,8},{9,1... | collective-permute-start | bytes 2359304 | tf_op jit(solution)/shard_map/ppermute | solution.py:464
  54.2 160.1 %copy-start.4 = (bf16[192,576]{1,0:T(8,128)(2,1)}, bf16[192,576]{1,0:T(8,128)(2,1)S(1)}, u32[]{:S(2)}) copy-start(bf16[192,576]{1,0:T(8,128)(2,1)S(1)} %copy.61.w0) | copy-start | bytes 663556
  54.2 14.8 %collective-permute-start.3 = (bf16[192,576]{1,0:T(8,128)(2,1)S(1)}, bf16[192,576]{1,0:T(8,128)(2,1)S(1)}, u32[]{:S(2)}, u32[]{:S(2)}) collective-permute-start(bf16[192,576]{1,0:T(8,128)(2,1)S(1)} %copy.61.w0), channel_id=1, source_target_pairs={{0,1},{1,2},{2,3},{3,0},{4,5},{5,6},{6,7},{7,4},{8,9},{9,10},{10,1... | collective-permute-start | bytes 663560 | tf_op jit(solution)/shard_map/ppermute | solution.py:504
  56.1 24.5 %collective-permute-start.2 = (bf16[192,576]{1,0:T(8,128)(2,1)S(1)}, bf16[192,576]{1,0:T(8,128)(2,1)S(1)}, u32[]{:S(2)}, u32[]{:S(2)}) collective-permute-start(bf16[192,576]{1,0:T(8,128)(2,1)S(1)} %copy.61.w0), channel_id=1, source_target_pairs={{0,2},{1,3},{2,0},{3,1},{4,6},{5,7},{6,4},{7,5},{8,10},{9,11},{10,... | collective-permute-start | bytes 663560 | tf_op jit(solution)/shard_map/ppermute | solution.py:504
  58.5 22.1 %collective-permute-start.1 = (bf16[192,576]{1,0:T(8,128)(2,1)S(1)}, bf16[192,576]{1,0:T(8,128)(2,1)S(1)}, u32[]{:S(2)}, u32[]{:S(2)}) collective-permute-start(bf16[192,576]{1,0:T(8,128)(2,1)S(1)} %copy.61.w0), channel_id=1, source_target_pairs={{0,3},{1,0},{2,1},{3,2},{4,7},{5,4},{6,5},{7,6},{8,11},{9,8},{10,9... | collective-permute-start | bytes 663560 | tf_op jit(solution)/shard_map/ppermute | solution.py:504
  69.0 145.3 %copy-start.8 = (bf16[192,576]{1,0:T(8,128)(2,1)}, bf16[192,576]{1,0:T(8,128)(2,1)S(1)}, u32[]{:S(2)}) copy-start(bf16[192,576]{1,0:T(8,128)(2,1)S(1)} %collective-permute-done.3.w3) | copy-start | bytes 663556
  80.6 133.7 %copy-start.10 = (bf16[192,576]{1,0:T(8,128)(2,1)}, bf16[192,576]{1,0:T(8,128)(2,1)S(1)}, u32[]{:S(2)}) copy-start(bf16[192,576]{1,0:T(8,128)(2,1)S(1)} %collective-permute-done.2.w2) | copy-start | bytes 663556
  80.6 71.8 %copy-start.12 = (bf16[192,576]{1,0:T(8,128)(2,1)}, bf16[192,576]{1,0:T(8,128)(2,1)S(1)}, u32[]{:S(2)}) copy-start(bf16[192,576]{1,0:T(8,128)(2,1)S(1)} %collective-permute-done.1.w1) | copy-start | bytes 663556
  90.9 15.5 %all-to-all-start.2 = ((bf16[16,64,192]{2,1,0:T(8,128)(2,1)}), bf16[16,64,192]{2,1,0:T(8,128)(2,1)S(1)}, u32[]{:S(2)}, u32[]{:S(2)}) async-start(bf16[16,64,192]{2,1,0:T(8,128)(2,1)} %bitcast.25), calls=%async_computation.2 | async-start | bytes 1048576 | tf_op jit(solution)/shard_map/all_to_all | solution.py:460
  114.9 9.4 %collective-permute-start.4 = (bf16[256,768]{1,0:T(8,128)(2,1)S(1)}, bf16[256,768]{1,0:T(8,128)(2,1)S(1)}, u32[]{:S(2)}, u32[]{:S(2)}) collective-permute-start(bf16[256,768]{1,0:T(8,128)(2,1)S(1)} %shard_map.179), channel_id=1, source_target_pairs={{0,64},{1,65},{2,66},{3,67},{4,68},{5,69},{6,70},{7,71},{8,72},{9,... | collective-permute-start | bytes 1179656 | tf_op jit(solution)/shard_map/ppermute | solution.py:705
  117.4 29.9 %copy-start.70 = (f32[4,192]{1,0:T(4,128)S(1)}, f32[4,192]{1,0:T(4,128)}, u32[]{:S(2)}) copy-start(f32[4,192]{1,0:T(4,128)} %get-tuple-element.102) | copy-start | bytes 9220
  117.4 30.0 %copy-start.69 = (f32[4,192]{1,0:T(4,128)S(1)}, f32[4,192]{1,0:T(4,128)}, u32[]{:S(2)}) copy-start(f32[4,192]{1,0:T(4,128)} %get-tuple-element.101) | copy-start | bytes 9220
  117.4 30.1 %copy-start.68 = (f32[4,192]{1,0:T(4,128)S(1)}, f32[4,192]{1,0:T(4,128)}, u32[]{:S(2)}) copy-start(f32[4,192]{1,0:T(4,128)} %get-tuple-element.103) | copy-start | bytes 9220
  124.5 53.6 %copy-start.23 = (bf16[256,768]{1,0:T(8,128)(2,1)}, bf16[256,768]{1,0:T(8,128)(2,1)S(1)}, u32[]{:S(2)}) copy-start(bf16[256,768]{1,0:T(8,128)(2,1)S(1)} %get-tuple-element.119) | copy-start | bytes 1179652
  124.7 27.6 %copy-start.57 = (f32[256]{0:T(256)}, f32[256]{0:T(256)S(1)}, u32[]{:S(2)}) copy-start(f32[256]{0:T(256)S(1)} %add_rsqrt_fusion.2) | copy-start | bytes 3076
  145.9 6.5 %collective-permute-start.5 = (bf16[1024,384]{1,0:T(8,128)(2,1)S(1)}, bf16[1024,384]{1,0:T(8,128)(2,1)S(1)}, u32[]{:S(2)}, u32[]{:S(2)}) collective-permute-start(bf16[1024,384]{1,0:T(8,128)(2,1)S(1)} %bitcast.163), channel_id=1, source_target_pairs={{0,4},{4,0},{1,5},{5,1},{2,6},{6,2},{3,7},{7,3},{8,12},{12,8},{9,1... | collective-permute-start | bytes 2359304 | tf_op jit(solution)/shard_map/ppermute | solution.py:464
  147.4 37.1 %copy-start.53 = (f32[768]{0:T(1024)}, f32[768]{0:T(1024)S(1)}, u32[]{:S(2)}) copy-start(f32[768]{0:T(1024)S(1)} %mul.300) | copy-start | bytes 9220
  147.5 32.9 %copy-start.65 = (f32[768]{0:T(1024)}, f32[768]{0:T(1024)S(1)}, u32[]{:S(2)}) copy-start(f32[768]{0:T(1024)S(1)} %add.247) | copy-start | bytes 9220
  163.3 51.0 %copy-start.21 = (f32[8,1024]{1,0:T(8,128)}, f32[8,1024]{1,0:T(8,128)S(1)}, u32[]{:S(2)}) copy-start(f32[8,1024]{1,0:T(8,128)S(1)} %get-tuple-element.41.log_total) | copy-start | bytes 98308
  163.3 14.7 %all-to-all-start.4 = ((bf16[16,64,192]{2,1,0:T(8,128)(2,1)}), bf16[16,64,192]{2,1,0:T(8,128)(2,1)S(1)}, u32[]{:S(2)}, u32[]{:S(2)}) async-start(bf16[16,64,192]{2,1,0:T(8,128)(2,1)} %bitcast.30), calls=%async_computation.4 | async-start | bytes 1048576 | tf_op jit(solution)/shard_map/all_to_all | solution.py:460
  226.5 3.3 collective-permute-start.6
  253.0 12.5 %collective-permute-start.7 = (bf16[256,768]{1,0:T(8,128)(2,1)}, bf16[256,768]{1,0:T(8,128)(2,1)}, u32[]{:S(2)}, u32[]{:S(2)}) collective-permute-start(bf16[256,768]{1,0:T(8,128)(2,1)} %fusion.32), channel_id=1, source_target_pairs={{64,0},{65,1},{66,2},{67,3},{68,4},{69,5},{70,6},{71,7},{72,8},{73... | collective-permute-start | bytes 1179656 | tf_op jit(solution)/shard_map/ppermute | solution.py:713
  255.5 36.5 %collective-permute-start.12 = (bf16[768,256]{1,0:T(8,128)(2,1)S(1)}, bf16[768,256]{1,0:T(8,128)(2,1)}, u32[]{:S(2)}, u32[]{:S(2)}) collective-permute-start(bf16[768,256]{1,0:T(8,128)(2,1)S(1)} %reshape.484.mixed), channel_id=1, source_target_pairs={{0,4},{4,0},{1,5},{5,1},{2,6},{6,2},{3,7},{7,3},{8,12},{12,8},{9,1... | collective-permute-start | bytes 1179656 | tf_op jit(solution)/shard_map/ppermute | solution.py:464
  256.1 36.0 %collective-permute-start.8 = (bf16[256,3072]{1,0:T(8,128)(2,1)S(1)}, bf16[256,3072]{1,0:T(8,128)(2,1)}, u32[]{:S(2)}, u32[]{:S(2)}) collective-permute-start(bf16[256,3072]{1,0:T(8,128)(2,1)S(1)} %get-tuple-element.154.active), channel_id=1, source_target_pairs={{0,4},{4,0},{1,5},{5,1},{2,6},{6,2},{3,7},{7,3},{8,12},{12,8},{9,1... | collective-permute-start | bytes 4718600 | tf_op jit(solution)/shard_map/ppermute | solution.py:464
  275.6 16.4 %collective-permute-start.11 = (bf16[256,3072]{1,0:T(8,128)(2,1)}, bf16[256,3072]{1,0:T(8,128)(2,1)}, u32[]{:S(2)}, u32[]{:S(2)}) collective-permute-start(bf16[256,3072]{1,0:T(8,128)(2,1)} %get-tuple-element.107.grad_hidden), channel_id=1, source_target_pairs={{0,4},{4,0},{1,5},{5,1},{2,6},{6,2},{3,7},{7,3},{8,12},{12,8},{9,1... | collective-permute-start | bytes 4718600 | tf_op jit(solution)/shard_map/ppermute | solution.py:464
  281.0 2.3 collective-permute-start.10
  282.9 9.1 %collective-permute-start.13 = (bf16[256,768]{1,0:T(8,128)(2,1)S(1)}, bf16[256,768]{1,0:T(8,128)(2,1)}, u32[]{:S(2)}, u32[]{:S(2)}) collective-permute-start(bf16[256,768]{1,0:T(8,128)(2,1)S(1)} %get-tuple-element.111.grad_attn), channel_id=1, source_target_pairs={{0,4},{4,0},{1,5},{5,1},{2,6},{6,2},{3,7},{7,3},{8,12},{12,8},{9,1... | collective-permute-start | bytes 1179656 | tf_op jit(solution)/shard_map/ppermute | solution.py:464
  283.3 8.7 %collective-permute-start.9 = (bf16[256,768]{1,0:T(8,128)(2,1)S(1)}, bf16[256,768]{1,0:T(8,128)(2,1)}, u32[]{:S(2)}, u32[]{:S(2)}) collective-permute-start(bf16[256,768]{1,0:T(8,128)(2,1)S(1)} %get-tuple-element.109.grad_low), channel_id=1, source_target_pairs={{0,4},{4,0},{1,5},{5,1},{2,6},{6,2},{3,7},{7,3},{8,12},{12,8},{9,1... | collective-permute-start | bytes 1179656 | tf_op jit(solution)/shard_map/ppermute | solution.py:464
  284.9 15.7 %all-to-all-start.7 = ((bf16[16,64,192]{2,1,0:T(8,128)(2,1)}), bf16[16,64,192]{2,1,0:T(8,128)(2,1)}, u32[]{:S(2)}, u32[]{:S(2)}) async-start(bf16[16,64,192]{2,1,0:T(8,128)(2,1)} %bitcast.57), calls=%async_computation.7 | async-start | bytes 1048576 | tf_op jit(solution)/shard_map/all_to_all | solution.py:460
  289.3 81.7 %reduce-scatter.2.cloned.1.call-start = ((), (), s32[]{:S(2)}) async-start(), calls=%async_computation.13 | async-start | bytes 6881280 | tf_op jit(solution)/shard_map/reduce_scatter | solution.py:655
  319.4 13.7 %collective-permute-start.20 = (bf16[1024,384]{1,0:T(8,128)(2,1)}, bf16[1024,384]{1,0:T(8,128)(2,1)}, u32[]{:S(2)}, u32[]{:S(2)}) collective-permute-start(bf16[1024,384]{1,0:T(8,128)(2,1)} %get-tuple-element.52), channel_id=1, source_target_pairs={{0,4},{4,0},{1,5},{5,1},{2,6},{6,2},{3,7},{7,3},{8,12},{12,8},{9,1... | collective-permute-start | bytes 2359304 | tf_op jit(solution)/shard_map/ppermute | solution.py:464
  328.4 14.8 %collective-permute-start.14 = (bf16[192,576]{1,0:T(8,128)(2,1)}, bf16[192,576]{1,0:T(8,128)(2,1)}, u32[]{:S(2)}, u32[]{:S(2)}) collective-permute-start(bf16[192,576]{1,0:T(8,128)(2,1)} %get-tuple-element.48), channel_id=1, source_target_pairs={{0,1},{1,2},{2,3},{3,0},{4,5},{5,6},{6,7},{7,4},{8,9},{9,10},{10,1... | collective-permute-start | bytes 663560 | tf_op jit(solution)/shard_map/ppermute | solution.py:512
  328.4 25.3 %collective-permute-start.15 = (bf16[192,576]{1,0:T(8,128)(2,1)}, bf16[192,576]{1,0:T(8,128)(2,1)}, u32[]{:S(2)}, u32[]{:S(2)}) collective-permute-start(bf16[192,576]{1,0:T(8,128)(2,1)} %get-tuple-element.49), channel_id=1, source_target_pairs={{0,2},{1,3},{2,0},{3,1},{4,6},{5,7},{6,4},{7,5},{8,10},{9,11},{10,... | collective-permute-start | bytes 663560 | tf_op jit(solution)/shard_map/ppermute | solution.py:512
  331.0 23.3 %collective-permute-start.16 = (bf16[192,576]{1,0:T(8,128)(2,1)}, bf16[192,576]{1,0:T(8,128)(2,1)}, u32[]{:S(2)}, u32[]{:S(2)}) collective-permute-start(bf16[192,576]{1,0:T(8,128)(2,1)} %get-tuple-element.50), channel_id=1, source_target_pairs={{0,3},{1,0},{2,1},{3,2},{4,7},{5,4},{6,5},{7,6},{8,11},{9,8},{10,9... | collective-permute-start | bytes 663560 | tf_op jit(solution)/shard_map/ppermute | solution.py:512
  335.3 24.4 %copy-start.52 = (f32[2,384]{1,0:T(2,128)S(1)}, f32[2,384]{1,0:T(2,128)}, u32[]{:S(2)}) copy-start(f32[2,384]{1,0:T(2,128)} %copy-done.50) | copy-start | bytes 9220
  335.3 24.3 %all-to-all-start.8 = ((bf16[16,64,384]{2,1,0:T(8,128)(2,1)}), bf16[16,64,384]{2,1,0:T(8,128)(2,1)S(1)}, u32[]{:S(2)}, u32[]{:S(2)}) async-start(bf16[16,64,384]{2,1,0:T(8,128)(2,1)} %bitcast.186), calls=%async_computation.9 | async-start | bytes 1572864 | tf_op jit(solution)/shard_map/all_to_all | solution.py:460
  355.6 11.0 %collective-permute-start.17 = (bf16[48,576]{1,0:T(8,128)(2,1)S(1)}, bf16[48,576]{1,0:T(8,128)(2,1)S(1)}, u32[]{:S(2)}, u32[]{:S(2)}) collective-permute-start(bf16[48,576]{1,0:T(8,128)(2,1)S(1)} %get-tuple-element.132), channel_id=1, source_target_pairs={{0,16},{16,32},{32,48},{48,0},{1,17},{17,33},{33,49},{49,1},{2,18}... | collective-permute-start | bytes 165896 | tf_op jit(solution)/shard_map/ppermute | solution.py:512
  356.5 10.1 %collective-permute-start.19 = (bf16[48,576]{1,0:T(8,128)(2,1)S(1)}, bf16[48,576]{1,0:T(8,128)(2,1)S(1)}, u32[]{:S(2)}, u32[]{:S(2)}) collective-permute-start(bf16[48,576]{1,0:T(8,128)(2,1)S(1)} %get-tuple-element.133), channel_id=1, source_target_pairs={{0,48},{16,0},{32,16},{48,32},{1,49},{17,1},{33,17},{49,33},{2,50}... | collective-permute-start | bytes 165896 | tf_op jit(solution)/shard_map/ppermute | solution.py:512
  358.3 8.3 %collective-permute-start.18 = (bf16[48,576]{1,0:T(8,128)(2,1)S(1)}, bf16[48,576]{1,0:T(8,128)(2,1)S(1)}, u32[]{:S(2)}, u32[]{:S(2)}) collective-permute-start(bf16[48,576]{1,0:T(8,128)(2,1)S(1)} %get-tuple-element.134), channel_id=1, source_target_pairs={{0,32},{16,48},{32,0},{48,16},{1,33},{17,49},{33,1},{49,17},{2,34}... | collective-permute-start | bytes 165896 | tf_op jit(solution)/shard_map/ppermute | solution.py:512
  362.7 8.1 %all-to-all-start.9 = ((bf16[4,4,576]{2,1,0:T(4,128)(2,1)}), bf16[4,4,576]{2,1,0:T(4,128)(2,1)S(1)}, u32[]{:S(2)}, u32[]{:S(2)}) async-start(bf16[4,4,576]{2,1,0:T(4,128)(2,1)} %convert_element_type.215), calls=%async_computation.10 | async-start | bytes 40960 | tf_op jit(solution)/shard_map/all_to_all | solution.py:460
  371.0 22.1 %all-to-all-start.10 = ((bf16[8,112,768]{2,1,0:T(8,128)(2,1)}), bf16[8,112,768]{2,1,0:T(8,128)(2,1)}, u32[]{:S(2)}, u32[]{:S(2)}) async-start(bf16[8,112,768]{2,1,0:T(8,128)(2,1)} %bitcast.191), calls=%async_computation.11 | async-start | bytes 2752512 | tf_op jit(solution)/shard_map/all_to_all | solution.py:460
  428.0 6.9 %collective-permute-start.21 = (bf16[8,176,768]{2,1,0:T(8,128)(2,1)S(1)}, bf16[8,176,768]{2,1,0:T(8,128)(2,1)}, u32[]{:S(2)}, u32[]{:S(2)}) collective-permute-start(bf16[8,176,768]{2,1,0:T(8,128)(2,1)S(1)} %all_to_all.64.own), channel_id=1, source_target_pairs={{0,4},{4,0},{1,5},{5,1},{2,6},{6,2},{3,7},{7,3},{8,12},{12,8},{9,1... | collective-permute-start | bytes 6488072 | tf_op jit(solution)/shard_map/ppermute | solution.py:464
  (67 other events, 443.8 us)
Sparse Core Ops, SparseCore 0:
  11.0 73.4 all-gather.2
  300.7 68.7 reduce-scatter.1
where the time goes:
time: 455 us; the launch traced here: 449 us
  blocking collectives  108 us (24%)
  waiting for transfers between devices  83.7 us (18%)
  Pallas kernels  69.7 us (15%)
  starting transfers between devices  62 us (14%)
  local copies, waits for them, and re-layouts  45.7 us (10%)
  matrix products  33.1 us (7%)
  between operations  23.2 us (5%)
  other arithmetic  22.8 us (5%)
    all_to_all x5, blocking collectives, exchange(): return lax.all_to_all(value, axes, 0, 0, tiled=True)  108 us
    all_to_all x7, starting transfers between devices, exchange(): return lax.all_to_all(value, axes, 0, 0, tiled=True)  34.5 us
    dot_general x8, matrix products, cross(): jnp.einsum(pattern, left_side, right_side, preferred_element_type=jnp.flo...  33.1 us
    all_to_all x7, waiting for transfers between devices, exchange(): return lax.all_to_all(value, axes, 0, 0, tiled=True)  33.1 us
    pallas_call x2, Pallas kernels, attend_back(): pl.pallas_call(attend_back_body, grid_spec=pltpu.PrefetchScalarGridSpec(n...  25.2 us
    pallas_call x2, Pallas kernels, attend(): pl.pallas_call(attend_body, grid_spec=pltpu.PrefetchScalarGridSpec(num_sc...  20.1 us
    ppermute x3, waiting for transfers between devices, gather_ring(): lax.ppermute(value, axis, ring_pairs(axis, -shift))  19.9 us
    unnamed x181, local copies, waits for them, and re-layouts  14.9 us
  transfers between devices with their start and end apart: 31, of which 14 were waited for; matrix products, arithmetic and copies ran while one was open for 13% of the time, Pallas kernels for 8%

commit v1 on v0

--- a/solution.py
+++ b/solution.py
@@ -18,6 +18,8 @@
 
 epsilon = 1e-05
 neg_fill = -1e30
+GELU_SCALE = (2.0 / 3.141592653589793) ** 0.5
+GELU_CUBE = 0.044715
 
 
 def dot(left_side, right_side, left_dim, right_dim):
@@ -295,28 +297,36 @@
     )(core_id, *[value for pair in pairs for value in pair])
 
 
+def weight_panel(packed, start):
+    members, width = packed.shape[0], packed.shape[2]
+    rows = width // members
+    return jnp.concatenate([packed[i, start : start + rows, :] for i in range(members)], 0)
+
+
+def join_groups(mixed, group):
+    micro_count = mixed.shape[0] // GROUPS
+    return jnp.concatenate([mixed[m * GROUPS + group] for m in range(micro_count)], 0)
+
+
+def attend_out(mixed, entering, packed, vectors, w_out):
+    middle = entering[...].astype(jnp.float32) + vectors[5:6, :]
+    for group in range(GROUPS):
+        rows = slice(group * WIDTH, (group + 1) * WIDTH)
+        middle += dot(join_groups(mixed, group), w_out[rows, :], 1, 0)
+    return middle
+
+
 def feed_forward_body(mixed, entering, packed, vectors, up_bias, result):
     members, width = packed.shape[0], packed.shape[2]
     panels = up_bias.shape[0]
     up_rows = width // members
     down_rows = panels * up_rows
-    micro_count = mixed.shape[0] // GROUPS
-
-    def weight_panel(start):
-        return jnp.concatenate(
-            [packed[member, start : start + up_rows, :] for member in range(members)], 0
-        )
-
-    w_out = weight_panel(2 * down_rows)
-    middle = entering[...].astype(jnp.float32) + vectors[5:6, :]
-    for group in range(GROUPS):
-        part = jnp.concatenate([mixed[m * GROUPS + group] for m in range(micro_count)], 0)
-        middle += dot(part, w_out[group * WIDTH : (group + 1) * WIDTH, :], 1, 0)
+    middle = attend_out(mixed, entering, packed, vectors, weight_panel(packed, 2 * down_rows))
     normed, _, _ = normalize(middle, vectors[1:2, :], vectors[6:7, :])
     normed = normed.astype(jnp.bfloat16)
     parts = []
     for panel in range(panels):
-        hidden = dot(normed, weight_panel(down_rows + panel * up_rows), 1, 0)
+        hidden = dot(normed, weight_panel(packed, down_rows + panel * up_rows), 1, 0)
         hidden = hidden + up_bias[panel : panel + 1, :]
         parts.append(jax.nn.gelu(hidden).astype(jnp.bfloat16))
     active = jnp.concatenate(parts, 1)
@@ -341,6 +351,92 @@
             transcendentals=4 * rows * width,
         ),
     )(mixed, entering, packed, vectors, up_bias)
+
+
+def feed_back_body(mixed, entering, packed, vectors, up_bias, grad_low, *outs):
+    last = len(outs) == 6
+    grad_mixed, grad_middle = outs[:2]
+    members, width = packed.shape[0], packed.shape[2]
+    panels = up_bias.shape[0]
+    up_rows = width // members
+    down_rows = panels * up_rows
+    micro_count = mixed.shape[0] // GROUPS
+    local_rows = mixed.shape[1]
+    w_out = weight_panel(packed, 2 * down_rows)
+    middle = attend_out(mixed, entering, packed, vectors, w_out)
+    normed, unit, spread_two = normalize(middle, vectors[1:2, :], vectors[6:7, :])
+    normed = normed.astype(jnp.bfloat16)
+    grads = grad_low[...]
+    grad_normed = jnp.zeros(middle.shape, jnp.float32)
+    per_panel = members // panels
+    for panel in range(panels):
+        columns = slice(panel * width, (panel + 1) * width)
+        w_up = weight_panel(packed, down_rows + panel * up_rows)
+        hidden = dot(normed, w_up, 1, 0) + up_bias[panel : panel + 1, :]
+        square = hidden * hidden
+        bend = jnp.tanh(GELU_SCALE * (hidden + GELU_CUBE * (square * hidden)))
+        slope = 0.5 * (1.0 + bend) + 0.5 * hidden * (1.0 - bend * bend) * (
+            GELU_SCALE * (1.0 + 3.0 * GELU_CUBE * square)
+        )
+        w_down = jnp.concatenate(
+            [packed[i, :down_rows, :] for i in range(panel * per_panel, (panel + 1) * per_panel)],
+            0,
+        )
+        grad_hidden = (dot(grads, w_down, 1, 1) * slope).astype(jnp.bfloat16)
+        grad_normed += dot(grad_hidden, w_up, 1, 1)
+        if last:
+            outs[2][:, columns] = grad_hidden
+            outs[5][panel : panel + 1, :] = jnp.sum(
+                grad_hidden.astype(jnp.float32), 0, keepdims=True
+            )
+        else:
+            outs[2][:, columns] = (0.5 * hidden * (1.0 + bend)).astype(jnp.bfloat16)
+    grad_top = grads.astype(jnp.float32)
+    grad_norm, d_gain, d_shift = normalize_back(grad_normed, unit, spread_two, vectors[1:2, :])
+    grad_sum = grad_top + grad_norm
+    grad_middle[...] = grad_sum
+    grad_attn = grad_sum.astype(jnp.bfloat16)
+    for group in range(GROUPS):
+        part = dot(grad_attn, w_out[group * WIDTH : (group + 1) * WIDTH, :], 1, 1)
+        part = part.astype(jnp.bfloat16)
+        for m in range(micro_count):
+            grad_mixed[m * GROUPS + group] = part[m * local_rows : (m + 1) * local_rows]
+    if last:
+        outs[3][...] = grad_attn
+        sums = outs[4]
+        sums[0:1, :] = d_gain[None]
+        sums[1:2, :] = d_shift[None]
+        sums[2:3, :] = jnp.sum(grad_attn.astype(jnp.float32), 0, keepdims=True)
+        sums[3:4, :] = jnp.sum(grad_top, 0, keepdims=True)
+    else:
+        outs[3][...] = normed.astype(jnp.float32).T.astype(jnp.bfloat16)
+        for group in range(GROUPS):
+            part = join_groups(mixed, group).astype(jnp.float32).T.astype(jnp.bfloat16)
+            outs[4][group * WIDTH : (group + 1) * WIDTH, :] = part
+
+
+def feed_back(mixed, entering, packed, vectors, up_bias, grad_low, last):
+    rows, width = entering.shape
+    hidden_width = up_bias.size
+    shapes = [(mixed.shape, jnp.bfloat16), ((rows, width), jnp.float32)]
+    shapes.append(((rows, hidden_width), jnp.bfloat16))
+    if last:
+        shapes.append(((rows, width), jnp.bfloat16))
+        shapes += [((4, width), jnp.float32), (up_bias.shape, jnp.float32)]
+    else:
+        shapes += [((width, rows), jnp.bfloat16)] * 2
+    return pl.pallas_call(
+        feed_back_body,
+        in_specs=[pl.BlockSpec(memory_space=pltpu.VMEM)] * 6,
+        out_specs=[pl.BlockSpec(memory_space=pltpu.VMEM)] * len(shapes),
+        out_shape=[jax.ShapeDtypeStruct(*shape) for shape in shapes],
+        compiler_params=pltpu.CompilerParams(vmem_limit_bytes=56 << 20),
+        cost_estimate=pl.CostEstimate(
+            flops=28 * rows * width * width,
+            bytes_accessed=24 * width * width,
+            transcendentals=4 * rows * width,
+        ),
+    )(mixed, entering, packed, vectors, up_bias, grad_low)
 
 
 def qkv_grads_body(ids, own, other, grad_joined, *outs):
@@ -435,10 +531,6 @@
     )(core_id, own, other)
 
 
-def cross(left_side, right_side, pattern):
-    return jnp.einsum(pattern, left_side, right_side, preferred_element_type=jnp.float32)
-
-
 def normalize(values, gain_row, shift_row):
     center = values - jnp.mean(values, -1, keepdims=True)
     spread = lax.rsqrt(jnp.mean(center * center, -1, keepdims=True) + epsilon)
@@ -480,18 +572,7 @@
     )
     panels = [up_half[:, start : start + width] for start in range(0, mlp_in.shape[2], width)]
     packed = jnp.concatenate([down_half] + panels + [out_half], 0)
-    everyone = lax.all_gather(packed, ("fsdp", "core"), axis=0)
-    down_rows, up_rows = down_half.shape[0], up_half.shape[0]
-    w_down = everyone[:, :down_rows].reshape(-1, width)
-    w_up = jnp.concatenate(
-        [
-            everyone[:, start : start + up_rows].reshape(-1, width)
-            for start in range(down_rows, 2 * down_rows, up_rows)
-        ],
-        1,
-    )
-    w_out = everyone[:, 2 * down_rows :].reshape(-1, width)
-    return everyone, w_out, w_up, w_down
+    return lax.all_gather(packed, ("fsdp", "core"), axis=0)
 
 
 def ring_pairs(axis, shift):
@@ -550,15 +631,13 @@
         attn_in[0].reshape(shard, 3, GROUPS, WIDTH), group_id, 2, keepdims=False
     ).reshape(shard, 3 * WIDTH)
     small_all = spread(small, "fsdp").reshape(fsdp_count, -1, shard).astype(jnp.float32)
-    own_columns, small_all = lax.optimization_barrier((own_columns, small_all))
     w_group = gather_ring(own_columns, "fsdp")
-    packed, w_out, w_up, w_down = gather_weights(attn_out, mlp_in, mlp_out)
-    model_width = w_out.shape[0]
+    packed = gather_weights(attn_out, mlp_in, mlp_out)
+    model_width = attn_out.shape[2]
     half = model_width // 2
-    w_out_groups = w_out.reshape(GROUPS, WIDTH, model_width)
     vector_rows = small_all[:, :8].transpose(1, 0, 2).reshape(8, model_width)
     gain_rows, bias_rows = vector_rows[:2], vector_rows[2:]
-    up_bias = small_all[:, 8:].reshape(-1)
+    up_rows = small_all[:, 8:].reshape(-1, model_width)
     own_bias = lax.dynamic_index_in_dim(small_all, group_id, 0, keepdims=False)
     group_bias = jnp.concatenate([own_bias[3], jnp.zeros_like(own_bias[3]), own_bias[4]])[None]
 
@@ -570,9 +649,8 @@
     top_grad = cotangent.reshape(rows, model_width)
     core_number = core_id.astype(jnp.int32)[None]
     numbers = jnp.stack([core_id, fsdp_id]).astype(jnp.int32)
-    head_shape = (micro_count, GROUPS, local_rows, WIDTH)
-
-    def forward(entering, last):
+
+    def forward(entering):
         stream = entering.astype(jnp.float32)
         normed, unit_one, spread_one = normalize(stream, gain_rows[0], bias_rows[0])
         halves = normed.astype(jnp.bfloat16).reshape(micro_count, 1, local_rows, 2, half)
@@ -585,68 +663,19 @@
             block_table, numbers, own, other, w_group, group_bias
         )
         mixed = exchange(mixed_heads.reshape(-1, local_rows, WIDTH), CTX)
-        if not last:
-            return feed_forward(
-                mixed, entering, packed, vector_rows, up_bias.reshape(-1, model_width)
-            )
-        mixed = mixed.reshape(head_shape)
-        attended = cross(mixed, w_out_groups, "mgtd,gde->mte").reshape(rows, model_width)
-        middle = stream + (attended + bias_rows[3])
-        normed_two, unit_two, spread_two = normalize(middle, gain_rows[1], bias_rows[4])
-        normed_two_low = normed_two.astype(jnp.bfloat16)
-        hidden_pre = cross(normed_two_low, w_up, "td,df->tf") + up_bias
-        active_low = jax.nn.gelu(hidden_pre).astype(jnp.bfloat16)
-        result = (middle + (cross(active_low, w_down, "tf,fd->td") + bias_rows[5])).astype(
-            jnp.bfloat16
+        result = feed_forward(mixed, entering, packed, vector_rows, up_rows)
+        return result, (entering, unit_one, spread_one, own, other, joined, log_total, mixed)
+
+    def backward(grad_low, saved, kept):
+        entering, unit_one, spread_one, own, other, joined, log_total, mixed = saved
+        last = kept is not None
+        grad_mixed, grad_middle, *extra = feed_back(
+            mixed, entering, packed, vector_rows, up_rows, grad_low, last
         )
-        saved = (
-            unit_one,
-            spread_one,
-            own,
-            other,
-            joined,
-            log_total,
-            mixed,
-            unit_two,
-            spread_two,
-            normed_two_low,
-            hidden_pre,
-            active_low,
-        )
-        return result, saved
-
-    def backward(grad_low, saved, last):
-        (
-            unit_one,
-            spread_one,
-            own,
-            other,
-            joined,
-            log_total,
-            mixed,
-            unit_two,
-            spread_two,
-            normed_two_low,
-            hidden_pre,
-            active_low,
-        ) = saved
-        grad_top = grad_low.astype(jnp.float32)
-        grad_active = cross(grad_low, w_down, "td,fd->tf")
-        _, gelu_pull = jax.vjp(jax.nn.gelu, hidden_pre)
-        grad_hidden = gelu_pull(grad_active)[0].astype(jnp.bfloat16)
-        grad_normed_two = cross(grad_hidden, w_up, "tf,df->td")
-        grad_norm_two, d_gain_two, d_shift_two = normalize_back(
-            grad_normed_two, unit_two, spread_two, gain_rows[1]
-        )
-        grad_middle = grad_top + grad_norm_two
-        grad_attn = grad_middle.astype(jnp.bfloat16)
-        attn_parts = grad_attn.reshape(micro_count, local_rows, model_width)
-        grad_mixed = cross(attn_parts, w_out_groups, "mte,gde->mgtd").astype(jnp.bfloat16)
-        share = None
         grad_heads = exchange(grad_mixed.reshape(-1, local_rows, WIDTH), CTX).reshape(-1, WIDTH)
         if last:
-            normed_tall = normed_two_low.T
-            mixed_tall = mixed.transpose(1, 3, 0, 2).reshape(model_width, rows)
+            grad_hidden, grad_attn, sums, up_sums = extra
+            active_low, normed_tall, mixed_tall = kept
             members = (active_low, grad_low, normed_tall, grad_hidden, mixed_tall, grad_attn)
             joint = weight_grads(
                 core_number, [(value, swap(value)) for value in members], fsdp_count
@@ -672,7 +701,7 @@
         )
         grad_in = (grad_middle + grad_norm_one).astype(jnp.bfloat16)
         if not last:
-            return grad_in
+            return grad_in, extra
         *pieces, joined_sums = qkv_grads(numbers, own, other, grad_joined, fsdp_count)
         joined_sums = joined_sums[0]
         qkv_share = sum_pieces(pieces, "fsdp")
@@ -685,34 +714,25 @@
             for shift in range(x_count)
         ]
         qkv_piece = sum_pieces(x_pieces, "x")
-        vectors = jnp.stack(
-            [
-                d_gain_one,
-                d_gain_two,
-                d_shift_one,
-                jnp.sum(grad_attn.astype(jnp.float32), 0),
-                d_shift_two,
-                jnp.sum(grad_top, 0),
-            ]
-        )
-        d_up_bias = jnp.sum(grad_hidden.astype(jnp.float32), 0)
+        vectors = jnp.stack([d_gain_one, sums[0], d_shift_one, sums[2], sums[1], sums[3]])
+        d_up_bias = up_sums.reshape(-1)
         return grad_in, share, qkv_piece, joined_sums, vectors, d_up_bias
 
     forward_pairs = [(i, i + 1) for i in range(sections - 1)]
     entering = fresh
     for _ in range(sections - 1):
-        result = forward(entering, False)
+        result, _ = forward(entering)
         received = lax.ppermute(result, "section", forward_pairs)
         entering = jnp.where(section_id == 0, fresh, received)
-    layer_out, saved = forward(entering, True)
+    layer_out, saved = forward(entering)
 
     back_pairs = [(i + 1, i) for i in range(sections - 1)]
     grad_low = top_grad
     for _ in range(sections - 1):
-        result = backward(grad_low, saved, False)
+        result, kept = backward(grad_low, saved, None)
         received = lax.ppermute(result, "section", back_pairs)
         grad_low = jnp.where(section_id == sections - 1, top_grad, received)
-    input_grad, share, qkv_piece, joined_sums, vectors, d_up_bias = backward(grad_low, saved, True)
+    input_grad, share, qkv_piece, joined_sums, vectors, d_up_bias = backward(grad_low, saved, kept)
 
     ours = jnp.arange(fsdp_count)[:, None] == group_id
     vector_parts = jnp.concatenate(
@@ -729,7 +749,6 @@
     vector_share = jnp.pad(vector_share, ((0, 12), (0, 0)))
     qkv_piece = jnp.concatenate([qkv_piece, vector_share], 0)
     qkv_piece = jnp.pad(qkv_piece, ((0, 0), (0, model_width - 3 * WIDTH)))
-    share, qkv_piece = lax.optimization_barrier((share, qkv_piece))
     joint_piece = sum_low(exchange(share.reshape(8, -1, model_width), ("x", "yh")))
     joint_piece, layer_out = lax.optimization_barrier((joint_piece, layer_out))
     both = spread(jnp.concatenate([joint_piece, qkv_piece], 0), ("x", "yh"))

time: 455 us -> 443 us (0.974)
  matrix products: 33.1 us -> 0 us
  Pallas kernels: 69.7 us -> 101 us
  blocking collectives: 108 us -> 131 us
  local copies, waits for them, and re-layouts: 45.7 us -> 26.4 us
  other arithmetic: 22.8 us -> 11.7 us
  starting transfers between devices: 62 us -> 54.6 us
  waiting for transfers between devices: 83.7 us -> 89.9 us
    dot_general x8 -> x0, matrix products: 33.1 us -> none  [cross(): jnp.einsum(pattern, left_side, right_side, preferred_element_type=jnp.flo...]
    pallas_call x0 -> x2, Pallas kernels: none -> 23.7 us  [feed_back(): pl.pallas_call(feed_back_body, in_specs=[pl.BlockSpec(memory_space=pltpu....]
    all_to_all x5 -> x7, blocking collectives: 108 us -> 131 us  [exchange(): return lax.all_to_all(value, axes, 0, 0, tiled=True)]
    all_to_all x7 -> x5, waiting for transfers between devices: 33.1 us -> 21.4 us  [exchange(): return lax.all_to_all(value, axes, 0, 0, tiled=True)]
    slice x4 -> x3, local copies, waits for them, and re-layouts: 11.6 us -> 0.84 us  [the longest x1 0.76 us: shards(): up_rows = small_all[:, 8:].reshape(-1, model_width)]
    ppermute x11, waiting for transfers between devices: 3.22 us -> 12.8 us  [swap(): return lax.ppermute(value, 'core', [(0, 1), (1, 0)])]
    pallas_call x1 -> x2, Pallas kernels: 8.5 us -> 17.7 us  [feed_forward(): pl.pallas_call(feed_forward_body, in_specs=[pl.BlockSpec(memory_space=plt...]
    reduce_scatter x1, waiting for transfers between devices: 0.02 us -> 8.16 us  [backward(): lax.psum_scatter(joint.reshape(-1, model_width), 'fsdp', scatter_dimensio...]
  transfers between devices with their start and end apart: 31 -> 29, of which waited for: 14 -> 16; matrix products, arithmetic and copies ran while one was open for 13% -> 4% of each run, Pallas kernels for 8% -> 12%
where the time goes in v1:
time: 443 us; the launch traced here: 437 us
  blocking collectives  131 us (30%)
  Pallas kernels  101 us (23%)
  waiting for transfers between devices  89.9 us (20%)
  starting transfers between devices  54.6 us (12%)
  local copies, waits for them, and re-layouts  26.4 us (6%)
  between operations  23 us (5%)
  other arithmetic  11.7 us (3%)
    all_to_all x7, blocking collectives, exchange(): return lax.all_to_all(value, axes, 0, 0, tiled=True)  131 us
    all_to_all x5, starting transfers between devices, exchange(): return lax.all_to_all(value, axes, 0, 0, tiled=True)  26.5 us
    pallas_call x2, Pallas kernels, attend_back(): pl.pallas_call(attend_back_body, grid_spec=pltpu.PrefetchScalarGridSpec(n...  24.2 us
    pallas_call x2, Pallas kernels, feed_back(): pl.pallas_call(feed_back_body, in_specs=[pl.BlockSpec(memory_space=pltpu....  23.7 us
    all_to_all x5, waiting for transfers between devices, exchange(): return lax.all_to_all(value, axes, 0, 0, tiled=True)  21.4 us
    ppermute x3, waiting for transfers between devices, gather_ring(): lax.ppermute(value, axis, ring_pairs(axis, -shift))  19.7 us
    pallas_call x2, Pallas kernels, attend(): pl.pallas_call(attend_body, grid_spec=pltpu.PrefetchScalarGridSpec(num_sc...  19.4 us
    pallas_call x2, Pallas kernels, feed_forward(): pl.pallas_call(feed_forward_body, in_specs=[pl.BlockSpec(memory_space=plt...  17.7 us
  transfers between devices with their start and end apart: 29, of which 16 were waited for; matrix products, arithmetic and copies ran while one was open for 4% of the time, Pallas kernels for 12%

profile of v1, /device:TPU:1, one launch (start us, length us, event | category | flops | bytes accessed | tf_op | source)
XLA Modules:
  0.0 436.7 jit_solution(6287809992135624899)
XLA Ops:
  11.7 5.9 %all-to-all-start = ((bf16[4,4,576]{2,1,0:T(4,128)(2,1)}), bf16[4,4,576]{2,1,0:T(4,128)(2,1)S(1)}, u32[]{:S(2)}, u32[]{:S(2)}) async-start(bf16[4,4,576]{2,1,0:T(4,128)(2,1)} %broadcast_in_dim.98), calls=%async_computation | async-start | bytes 40960 | tf_op jit(solution)/shard_map/all_to_all | solution.py:552
  28.2 22.4 %all_to_all.60 = bf16[16,64,384]{2,1,0:T(8,128)(2,1)S(1)} all-to-all(bf16[16,64,384]{2,1,0:T(8,128)(2,1)S(1)} %bitcast.116), channel_id=1, replica_groups=mesh['section'=2,'x'=4,'yh'=2,'core'=2,'fsdp'=4] {'x','yh','core'}, dimensions={0} | all-to-all | bytes 1572864 | tf_op jit(solution)/shard_map/all_to_all | solution.py:552
  50.9 2.1 reshape_squeeze.3
  53.0 1.9 constant_dynamic-slice_fusion.5
  56.0 1.9 collective-permute-start.3
  57.8 2.4 collective-permute-start.2
  62.5 8.3 %collective-permute-done.3.w3 = bf16[192,576]{1,0:T(8,128)(2,1)S(1)} collective-permute-done((bf16[192,576]{1,0:T(8,128)(2,1)S(1)}, bf16[192,576]{1,0:T(8,128)(2,1)S(1)}, u32[]{:S(2)}, u32[]{:S(2)}) %collective-permute-start.3) | collective-permute-done | bytes 221216 | tf_op jit(solution)/shard_map/ppermute | solution.py:585
  70.8 11.5 %collective-permute-done.2.w2 = bf16[192,576]{1,0:T(8,128)(2,1)S(1)} collective-permute-done((bf16[192,576]{1,0:T(8,128)(2,1)S(1)}, bf16[192,576]{1,0:T(8,128)(2,1)S(1)}, u32[]{:S(2)}, u32[]{:S(2)}) %collective-permute-start.2) | collective-permute-done | bytes 221216 | tf_op jit(solution)/shard_map/ppermute | solution.py:585
  82.3 10.3 %shard_map.178 = (bf16[1024,576]{1,0:T(8,128)(2,1)}, bf16[1024,192]{1,0:T(8,128)(2,1)}, f32[8,1024]{1,0:T(8,128)}) custom-call(s32[32]{0:T(128)S(1)} %copy-done.27, s32[2]{0:T(128)S(1)} %pad_add_fusion.ids, bf16[1024,384]{1,0:T(8,128)(2,1)S(1)} %bitcast.104, bf16[1024,384]{1,0:T(8,128)(2,1)S(1)} %collective-permute-done.other, ...), custom_call_target="tpu_custom_call" | custom-call | flops 805306368 | bytes 1572864 | tf_op jit(solution)/shard_map/pallas_call | solution.py:109
  92.6 4.1 all-to-all-start.2
  97.7 10.2 %all-to-all-done.2.mixed = bf16[16,64,192]{2,1,0:T(8,128)(2,1)S(1)} async-done(((bf16[16,64,192]{2,1,0:T(8,128)(2,1)}), bf16[16,64,192]{2,1,0:T(8,128)(2,1)S(1)}, u32[]{:S(2)}, u32[]{:S(2)}) %all-to-all-start.2) | async-done | bytes 393248 | tf_op jit(solution)/shard_map/all_to_all | solution.py:552
  107.9 8.5 %shard_map.179 = bf16[256,768]{1,0:T(8,128)(2,1)S(1)} custom-call(bf16[16,64,192]{2,1,0:T(8,128)(2,1)S(1)} %all-to-all-done.2.mixed, bf16[256,768]{1,0:T(8,128)(2,1)S(1)} %bitcast.99, bf16[8,864,768]{2,1,0:T(8,128)(2,1)} %bitcast.107, f32[8,768]{1,0:T(8,128)S(1)} %reshape.368.vectors, f32[4,768]{1,0:T(4,128)S(1)} %reshape.369.up_bias), custom_call_target="tpu_custom_call" | custom-call | flops 2717908992 | bytes 10616832 | tf_op jit(solution)/shard_map/pallas_call | solution.py:342
  116.4 2.6 collective-permute-start.4
  119.2 6.9 %collective-permute-done.4 = bf16[256,768]{1,0:T(8,128)(2,1)S(1)} collective-permute-done((bf16[256,768]{1,0:T(8,128)(2,1)S(1)}, bf16[256,768]{1,0:T(8,128)(2,1)S(1)}, u32[]{:S(2)}, u32[]{:S(2)}) %collective-permute-start.4) | collective-permute-done | bytes 393248 | tf_op jit(solution)/shard_map/ppermute | solution.py:725
  127.1 20.6 %all_to_all.61 = bf16[16,64,384]{2,1,0:T(8,128)(2,1)S(1)} all-to-all(bf16[16,64,384]{2,1,0:T(8,128)(2,1)S(1)} %bitcast.117), channel_id=1, replica_groups=mesh['section'=2,'x'=4,'yh'=2,'core'=2,'fsdp'=4] {'x','yh','core'}, dimensions={0} | all-to-all | bytes 1572864 | tf_op jit(solution)/shard_map/all_to_all | solution.py:552
  148.3 1.9 collective-permute-done.5.other
  150.2 9.0 %shard_map.180 = (bf16[1024,576]{1,0:T(8,128)(2,1)S(1)}, bf16[1024,192]{1,0:T(8,128)(2,1)S(1)}, f32[8,1024]{1,0:T(8,128)S(1)}) custom-call(s32[32]{0:T(128)S(1)} %copy-done.27, s32[2]{0:T(128)S(1)} %pad_add_fusion.ids, bf16[1024,384]{1,0:T(8,128)(2,1)S(1)} %bitcast.101, bf16[1024,384]{1,0:T(8,128)(2,1)S(1)} %collective-permute-done.5.other, ...), custom_call_target="tpu_custom_call" | custom-call | flops 805306368 | bytes 1572864 | tf_op jit(solution)/shard_map/pallas_call | solution.py:109
  159.3 14.7 %all_to_all.62.mixed = bf16[16,64,192]{2,1,0:T(8,128)(2,1)} all-to-all(bf16[16,64,192]{2,1,0:T(8,128)(2,1)S(1)} %bitcast.106), channel_id=1, replica_groups=mesh['section'=2,'x'=4,'yh'=2,'core'=2,'fsdp'=4] {'x','yh','core'}, dimensions={0} | all-to-all | bytes 786432 | tf_op jit(solution)/shard_map/all_to_all | solution.py:552
  173.9 11.9 %shard_map.181 = (bf16[16,64,192]{2,1,0:T(8,128)(2,1)}, f32[256,768]{1,0:T(8,128)}, bf16[256,3072]{1,0:T(8,128)(2,1)}, bf16[768,256]{1,0:T(8,128)(2,1)}, bf16[768,256]{1,0:T(8,128)(2,1)}) custom-call(bf16[16,64,192]{2,1,0:T(8,128)(2,1)} %all_to_all.62.mixed, bf16[256,768]{1,0:T(8,128)(2,1)} %copy-done.2, bf16[8,864,768]{2,1,0:T(8,128)(2,1)} %bitcast.108, ...), custom_call_target="tpu_custom_call" | custom-call | flops 4227858432 | bytes 14155776 | tf_op jit(solution)/shard_map/pallas_call | solution.py:428
  185.9 16.3 %all_to_all.63 = bf16[16,64,192]{2,1,0:T(8,128)(2,1)S(1)} all-to-all(bf16[16,64,192]{2,1,0:T(8,128)(2,1)} %get-tuple-element.47), channel_id=1, replica_groups=mesh['section'=2,'x'=4,'yh'=2,'core'=2,'fsdp'=4] {'x','yh','core'}, dimensions={0} | all-to-all | bytes 786432 | tf_op jit(solution)/shard_map/all_to_all | solution.py:552
  202.2 12.1 %shard_map.182 = (bf16[1024,576]{1,0:T(8,128)(2,1)}, bf16[1024,384]{1,0:T(8,128)(2,1)S(1)}, bf16[1024,384]{1,0:T(8,128)(2,1)S(1)}) custom-call(s32[32]{0:T(128)S(1)} %copy-done.27, s32[2]{0:T(128)S(1)} %pad_add_fusion.ids, bf16[1024,576]{1,0:T(8,128)(2,1)S(1)} %get-tuple-element.46.joined, bf16[1024,192]{1,0:T(8,128)(2,1)S(1)} %bitcast.105, ...), custom_call_target="tpu_custom_call" | custom-call | flops 2013265920 | bytes 3145728 | tf_op jit(solution)/shard_map/pallas_call | solution.py:202
  215.7 1.9 collective-permute-done.6
  217.8 17.4 %all_to_all.64 = bf16[16,64,384]{2,1,0:T(8,128)(2,1)S(1)} all-to-all(bf16[16,64,384]{2,1,0:T(8,128)(2,1)S(1)} %bitcast.120), channel_id=1, replica_groups=mesh['section'=2,'x'=4,'yh'=2,'core'=2,'fsdp'=4] {'x','yh','core'}, dimensions={0} | all-to-all | bytes 1572864 | tf_op jit(solution)/shard_map/all_to_all | solution.py:552
  241.6 10.2 %collective-permute-done.7 = bf16[256,768]{1,0:T(8,128)(2,1)S(1)} collective-permute-done((bf16[256,768]{1,0:T(8,128)(2,1)S(1)}, bf16[256,768]{1,0:T(8,128)(2,1)S(1)}, u32[]{:S(2)}, u32[]{:S(2)}) %collective-permute-start.7) | collective-permute-done | bytes 393248 | tf_op jit(solution)/shard_map/ppermute | solution.py:733
  252.6 11.8 %shard_map.183 = (bf16[16,64,192]{2,1,0:T(8,128)(2,1)}, f32[256,768]{1,0:T(8,128)}, bf16[256,3072]{1,0:T(8,128)(2,1)}, bf16[256,768]{1,0:T(8,128)(2,1)}, f32[4,768]{1,0:T(4,128)}, /*index=5*/f32[4,768]{1,0:T(4,128)}) custom-call(bf16[16,64,192]{2,1,0:T(8,128)(2,1)} %all_to_all.62.mixed, bf16[256,768]{1,0:T(8,128)(2,1)} %copy-done.2, ...), custom_call_target="tpu_custom_call" | custom-call | flops 4227858432 | bytes 14155776 | tf_op jit(solution)/shard_map/pallas_call | solution.py:428
  266.2 4.0 collective-permute-done.10.normed_two_other
  271.1 4.3 all-to-all-start.7
  277.7 8.0 %shard_map.184 = bf16[4,896,768]{2,1,0:T(8,128)(2,1)} custom-call(s32[1]{0:T(128)} %bitcast.core_id, bf16[256,3072]{1,0:T(8,128)(2,1)S(1)} %copy-done.6, bf16[256,3072]{1,0:T(8,128)(2,1)} %collective-permute-done.8.active_other, bf16[256,768]{1,0:T(8,128)(2,1)S(1)} %copy-done.7, bf16[256,768]{1,0:T(8,128)(2,1)} %collective-permute-done.9.grad_low_other, ...), custom_call_target="tpu_custom_call" | custom-call | flops 2717908992 | bytes 5505024 | tf_op jit(solution)/shard_map/pallas_call | solution.py:282
  288.5 12.1 %shard_map.186 = (bf16[1024,576]{1,0:T(8,128)(2,1)S(1)}, bf16[1024,384]{1,0:T(8,128)(2,1)S(1)}, bf16[1024,384]{1,0:T(8,128)(2,1)S(1)}) custom-call(s32[32]{0:T(128)S(1)} %copy-done.27, s32[2]{0:T(128)S(1)} %copy-done.29, bf16[1024,576]{1,0:T(8,128)(2,1)S(1)} %copy-done.33, bf16[1024,192]{1,0:T(8,128)(2,1)} %bitcast.35.grad_mixed, f32[8,1024]{1,0:T(8,128)S(1)} %copy-done.35, ...), custom_call_target="tpu_custom_call" | custom-call | flops 2013265920 | bytes 3145728 | tf_op jit(solution)/shard_map/pallas_call | solution.py:202
  302.1 1.9 collective-permute-done.14
  305.1 5.8 %all-to-all-start.9 = ((bf16[16,64,384]{2,1,0:T(8,128)(2,1)}), bf16[16,64,384]{2,1,0:T(8,128)(2,1)}, u32[]{:S(2)}, u32[]{:S(2)}) async-start(bf16[16,64,384]{2,1,0:T(8,128)(2,1)} %bitcast.40), calls=%async_computation.10 | async-start | bytes 1572864 | tf_op jit(solution)/shard_map/all_to_all | solution.py:552
  312.7 2.1 shard_map.187
  314.8 10.2 %all-to-all-done.9 = bf16[16,64,384]{2,1,0:T(8,128)(2,1)} async-done(((bf16[16,64,384]{2,1,0:T(8,128)(2,1)}), bf16[16,64,384]{2,1,0:T(8,128)(2,1)}, u32[]{:S(2)}, u32[]{:S(2)}) %all-to-all-start.9) | async-done | bytes 786464 | tf_op jit(solution)/shard_map/all_to_all | solution.py:552
  328.5 8.0 %all_to_all.65 = bf16[4,4,576]{2,1,0:T(4,128)(2,1)S(1)} all-to-all(bf16[4,4,576]{2,1,0:T(4,128)(2,1)S(1)} %convert_element_type.157), channel_id=1, replica_groups=mesh['section'=2,'x'=4,'yh'=2,'core'=2,'fsdp'=4] {'fsdp'}, dimensions={0} | all-to-all | bytes 36864 | tf_op jit(solution)/shard_map/all_to_all | solution.py:552
  336.4 8.2 %reduce-scatter.2.cloned.1.call-done = bf16[896,768]{1,0:T(8,128)(2,1)} async-done(((bf16[3584,768]{1,0:T(8,128)(2,1)}), bf16[896,768]{1,0:T(8,128)(2,1)}) %reduce-scatter.2.cloned.1.call-update) | async-done | bytes 1376272 | tf_op jit(solution)/shard_map/reduce_scatter | solution.py:684
  344.6 6.4 %all-to-all-start.8 = ((bf16[8,112,768]{2,1,0:T(8,128)(2,1)}), bf16[8,112,768]{2,1,0:T(8,128)(2,1)}, u32[]{:S(2)}, u32[]{:S(2)}) async-start(bf16[8,112,768]{2,1,0:T(8,128)(2,1)} %bitcast.122), calls=%async_computation.9 | async-start | bytes 2752512 | tf_op jit(solution)/shard_map/all_to_all | solution.py:552
  351.1 1.7 collective-permute-start.16
  352.8 1.6 collective-permute-start.17
  354.4 5.6 %collective-permute-done.15 = bf16[192,576]{1,0:T(8,128)(2,1)S(1)} collective-permute-done((bf16[192,576]{1,0:T(8,128)(2,1)S(1)}, bf16[192,576]{1,0:T(8,128)(2,1)S(1)}, u32[]{:S(2)}, u32[]{:S(2)}) %collective-permute-start.15) | collective-permute-done | bytes 221216 | tf_op jit(solution)/shard_map/ppermute | solution.py:593
  359.9 3.4 collective-permute-done.16
  363.3 1.7 collective-permute-done.17
  369.7 1.7 collective-permute-start.19
  371.4 9.2 %shard_map.185 = bf16[256,768]{1,0:T(8,128)(2,1)} custom-call(bf16[16,64,192]{2,1,0:T(8,128)(2,1)S(1)} %copy-done.5, bf16[256,768]{1,0:T(8,128)(2,1)S(1)} %copy-done.4, bf16[8,864,768]{2,1,0:T(8,128)(2,1)} %bitcast.110, f32[8,768]{1,0:T(8,128)S(1)} %copy-done.16, f32[4,768]{1,0:T(4,128)S(1)} %copy-done.18), custom_call_target="tpu_custom_call" | custom-call | flops 2717908992 | bytes 10616832 | tf_op jit(solution)/shard_map/pallas_call | solution.py:342
  380.8 1.5 reduce_sum.120
  382.5 31.3 %all_to_all.66.own = bf16[8,176,768]{2,1,0:T(8,128)(2,1)} all-to-all(bf16[8,176,768]{2,1,0:T(8,128)(2,1)S(1)} %broadcast_in_dim.111), channel_id=1, replica_groups=mesh['section'=2,'x'=4,'yh'=2,'core'=2,'fsdp'=4] {'x','yh'}, dimensions={0} | all-to-all | bytes 4325376 | tf_op jit(solution)/shard_map/all_to_all | solution.py:552
  413.8 4.1 collective-permute-start.21
  419.0 3.1 collective-permute-done.21.other
  422.0 5.5 %shard_map.188 = (f32[192,2304]{1,0:T(8,128)}, f32[192,768]{1,0:T(8,128)}, f32[192,3072]{1,0:T(8,128)}, f32[768,768]{1,0:T(8,128)}, f32[4,768]{1,0:T(4,128)S(1)}) custom-call(s32[1]{0:T(128)} %bitcast.core_id, bf16[8,176,768]{2,1,0:T(8,128)(2,1)} %all_to_all.66.own, bf16[8,176,768]{2,1,0:T(8,128)(2,1)} %collective-permute-done.21.other), custom_call_target="tpu_custom_call" | custom-call | bytes 12582912 | tf_op jit(solution)/shard_map/pallas_call | solution.py:517
  (262 shorter events, 45.8 us)
Async XLA Ops:
  7.2 100.7 %all-gather.3.cloned.1.call-start = ((), (), s32[]{:S(2)}) async-start(), calls=%async_computation.14 | async-start | bytes 11943936 | tf_op jit(solution)/shard_map/all_gather | solution.py:575
  8.9 17.0 %copy-start.40 = (bf16[4,1,64,768]{3,2,1,0:T(8,128)(2,1)S(1)}, bf16[4,1,64,768]{3,2,1,0:T(8,128)(2,1)}, u32[]{:S(2)}) copy-start(bf16[4,1,64,768]{3,2,1,0:T(8,128)(2,1)} %param.11) | copy-start | bytes 1179652
  11.7 15.1 %all-to-all-start = ((bf16[4,4,576]{2,1,0:T(4,128)(2,1)}), bf16[4,4,576]{2,1,0:T(4,128)(2,1)S(1)}, u32[]{:S(2)}, u32[]{:S(2)}) async-start(bf16[4,4,576]{2,1,0:T(4,128)(2,1)} %broadcast_in_dim.98), calls=%async_computation | async-start | bytes 40960 | tf_op jit(solution)/shard_map/all_to_all | solution.py:552
  28.0 22.9 %copy-start.37 = (bf16[1,192,2304]{2,1,0:T(8,128)(2,1)S(1)}, bf16[1,192,2304]{2,1,0:T(8,128)(2,1)}, u32[]{:S(2)}) copy-start(bf16[1,192,2304]{2,1,0:T(8,128)(2,1)} %param.15) | copy-start | bytes 2654212
  50.5 31.8 %collective-permute-start = (bf16[1024,384]{1,0:T(8,128)(2,1)S(1)}, bf16[1024,384]{1,0:T(8,128)(2,1)S(1)}, u32[]{:S(2)}, u32[]{:S(2)}) collective-permute-start(bf16[1024,384]{1,0:T(8,128)(2,1)S(1)} %bitcast.103), channel_id=1, source_target_pairs={{0,4},{4,0},{1,5},{5,1},{2,6},{6,2},{3,7},{7,3},{8,12},{12,8},{9,1... | collective-permute-start | bytes 2359304 | tf_op jit(solution)/shard_map/ppermute | solution.py:556
  53.0 29.3 %copy-start.27 = (s32[32]{0:T(128)S(1)}, s32[32]{0:T(128)}, u32[]{:S(2)}) copy-start(s32[32]{0:T(128)} %table.7) | copy-start | bytes 388
  56.0 146.2 %copy-start.13 = (bf16[192,576]{1,0:T(8,128)(2,1)}, bf16[192,576]{1,0:T(8,128)(2,1)S(1)}, u32[]{:S(2)}) copy-start(bf16[192,576]{1,0:T(8,128)(2,1)S(1)} %copy.52.w0) | copy-start | bytes 663556
  56.0 14.8 %collective-permute-start.3 = (bf16[192,576]{1,0:T(8,128)(2,1)S(1)}, bf16[192,576]{1,0:T(8,128)(2,1)S(1)}, u32[]{:S(2)}, u32[]{:S(2)}) collective-permute-start(bf16[192,576]{1,0:T(8,128)(2,1)S(1)} %copy.52.w0), channel_id=1, source_target_pairs={{0,1},{1,2},{2,3},{3,0},{4,5},{5,6},{6,7},{7,4},{8,9},{9,10},{10,1... | collective-permute-start | bytes 663560 | tf_op jit(solution)/shard_map/ppermute | solution.py:585
  57.8 24.4 %collective-permute-start.2 = (bf16[192,576]{1,0:T(8,128)(2,1)S(1)}, bf16[192,576]{1,0:T(8,128)(2,1)S(1)}, u32[]{:S(2)}, u32[]{:S(2)}) collective-permute-start(bf16[192,576]{1,0:T(8,128)(2,1)S(1)} %copy.52.w0), channel_id=1, source_target_pairs={{0,2},{1,3},{2,0},{3,1},{4,6},{5,7},{6,4},{7,5},{8,10},{9,11},{10,... | collective-permute-start | bytes 663560 | tf_op jit(solution)/shard_map/ppermute | solution.py:585
  60.2 22.0 %collective-permute-start.1 = (bf16[192,576]{1,0:T(8,128)(2,1)S(1)}, bf16[192,576]{1,0:T(8,128)(2,1)S(1)}, u32[]{:S(2)}, u32[]{:S(2)}) collective-permute-start(bf16[192,576]{1,0:T(8,128)(2,1)S(1)} %copy.52.w0), channel_id=1, source_target_pairs={{0,3},{1,0},{2,1},{3,2},{4,7},{5,4},{6,5},{7,6},{8,11},{9,8},{10,9... | collective-permute-start | bytes 663560 | tf_op jit(solution)/shard_map/ppermute | solution.py:585
  61.7 140.5 %copy-start.28 = (s32[2]{0:T(128)}, s32[2]{0:T(128)S(1)}, u32[]{:S(2)}) copy-start(s32[2]{0:T(128)S(1)} %pad_add_fusion.ids) | copy-start | bytes 28
  70.8 131.4 %copy-start.21 = (bf16[192,576]{1,0:T(8,128)(2,1)}, bf16[192,576]{1,0:T(8,128)(2,1)S(1)}, u32[]{:S(2)}) copy-start(bf16[192,576]{1,0:T(8,128)(2,1)S(1)} %collective-permute-done.3.w3) | copy-start | bytes 663556
  82.3 119.9 %copy-start.23 = (bf16[192,576]{1,0:T(8,128)(2,1)}, bf16[192,576]{1,0:T(8,128)(2,1)S(1)}, u32[]{:S(2)}) copy-start(bf16[192,576]{1,0:T(8,128)(2,1)S(1)} %collective-permute-done.2.w2) | copy-start | bytes 663556
  82.3 119.9 %copy-start.25 = (bf16[192,576]{1,0:T(8,128)(2,1)}, bf16[192,576]{1,0:T(8,128)(2,1)S(1)}, u32[]{:S(2)}) copy-start(bf16[192,576]{1,0:T(8,128)(2,1)S(1)} %collective-permute-done.1.w1) | copy-start | bytes 663556
  92.6 15.3 %all-to-all-start.2 = ((bf16[16,64,192]{2,1,0:T(8,128)(2,1)}), bf16[16,64,192]{2,1,0:T(8,128)(2,1)S(1)}, u32[]{:S(2)}, u32[]{:S(2)}) async-start(bf16[16,64,192]{2,1,0:T(8,128)(2,1)} %bitcast.17), calls=%async_computation.2 | async-start | bytes 1048576 | tf_op jit(solution)/shard_map/all_to_all | solution.py:552
  97.6 18.8 %copy-start.17 = (f32[4,768]{1,0:T(4,128)}, f32[4,768]{1,0:T(4,128)S(1)}, u32[]{:S(2)}) copy-start(f32[4,768]{1,0:T(4,128)S(1)} %reshape.369.up_bias) | copy-start | bytes 36868
  97.7 18.8 %copy-start.15 = (f32[8,768]{1,0:T(8,128)}, f32[8,768]{1,0:T(8,128)S(1)}, u32[]{:S(2)}) copy-start(f32[8,768]{1,0:T(8,128)S(1)} %reshape.368.vectors) | copy-start | bytes 73732
  116.4 9.6 %collective-permute-start.4 = (bf16[256,768]{1,0:T(8,128)(2,1)S(1)}, bf16[256,768]{1,0:T(8,128)(2,1)S(1)}, u32[]{:S(2)}, u32[]{:S(2)}) collective-permute-start(bf16[256,768]{1,0:T(8,128)(2,1)S(1)} %shard_map.179), channel_id=1, source_target_pairs={{0,64},{1,65},{2,66},{3,67},{4,68},{5,69},{6,70},{7,71},{8,72},{9,... | collective-permute-start | bytes 1179656 | tf_op jit(solution)/shard_map/ppermute | solution.py:725
  126.5 110.9 %copy-start.52 = (f32[256]{0:T(256)}, f32[256]{0:T(256)S(1)}, u32[]{:S(2)}) copy-start(f32[256]{0:T(256)S(1)} %add_rsqrt_fusion.1) | copy-start | bytes 3076
  147.7 2.5 collective-permute-start.5
  159.3 43.0 %copy-start.32 = (bf16[1024,576]{1,0:T(8,128)(2,1)}, bf16[1024,576]{1,0:T(8,128)(2,1)S(1)}, u32[]{:S(2)}) copy-start(bf16[1024,576]{1,0:T(8,128)(2,1)S(1)} %get-tuple-element.46.joined) | copy-start | bytes 3538948
  159.3 42.9 %copy-start.34 = (f32[8,1024]{1,0:T(8,128)}, f32[8,1024]{1,0:T(8,128)S(1)}, u32[]{:S(2)}) copy-start(f32[8,1024]{1,0:T(8,128)S(1)} %get-tuple-element.48.log_total) | copy-start | bytes 98308
  214.4 3.3 collective-permute-start.6
  238.0 13.7 %copy-start.41 = (bf16[4,1,64,768]{3,2,1,0:T(8,128)(2,1)S(1)}, bf16[4,1,64,768]{3,2,1,0:T(8,128)(2,1)}, u32[]{:S(2)}) copy-start(bf16[4,1,64,768]{3,2,1,0:T(8,128)(2,1)} %param.12) | copy-start | bytes 1179652
  239.6 12.2 %collective-permute-start.7 = (bf16[256,768]{1,0:T(8,128)(2,1)S(1)}, bf16[256,768]{1,0:T(8,128)(2,1)S(1)}, u32[]{:S(2)}, u32[]{:S(2)}) collective-permute-start(bf16[256,768]{1,0:T(8,128)(2,1)S(1)} %fusion.14), channel_id=1, source_target_pairs={{64,0},{65,1},{66,2},{67,3},{68,4},{69,5},{70,6},{71,7},{72,8},{73... | collective-permute-start | bytes 1179656 | tf_op jit(solution)/shard_map/ppermute | solution.py:733
  240.9 34.8 %collective-permute-start.8 = (bf16[256,3072]{1,0:T(8,128)(2,1)S(1)}, bf16[256,3072]{1,0:T(8,128)(2,1)}, u32[]{:S(2)}, u32[]{:S(2)}) collective-permute-start(bf16[256,3072]{1,0:T(8,128)(2,1)S(1)} %copy-done.6), channel_id=1, source_target_pairs={{0,4},{4,0},{1,5},{5,1},{2,6},{6,2},{3,7},{7,3},{8,12},{12,8},{9,1... | collective-permute-start | bytes 4718600 | tf_op jit(solution)/shard_map/ppermute | solution.py:556
  252.6 18.4 %copy-start.7 = (bf16[256,768]{1,0:T(8,128)(2,1)S(1)}, bf16[256,768]{1,0:T(8,128)(2,1)}, u32[]{:S(2)}) copy-start(bf16[256,768]{1,0:T(8,128)(2,1)} %broadcast_select_fusion.grad_low) | copy-start | bytes 1179652
  264.3 11.4 %collective-permute-start.11 = (bf16[256,3072]{1,0:T(8,128)(2,1)}, bf16[256,3072]{1,0:T(8,128)(2,1)}, u32[]{:S(2)}, u32[]{:S(2)}) collective-permute-start(bf16[256,3072]{1,0:T(8,128)(2,1)} %get-tuple-element.54.grad_hidden), channel_id=1, source_target_pairs={{0,4},{4,0},{1,5},{5,1},{2,6},{6,2},{3,7},{7,3},{8,12},{12,8},{9,1... | collective-permute-start | bytes 4718600 | tf_op jit(solution)/shard_map/ppermute | solution.py:556
  265.6 4.6 %collective-permute-start.10 = (bf16[768,256]{1,0:T(8,128)(2,1)S(1)}, bf16[768,256]{1,0:T(8,128)(2,1)S(1)}, u32[]{:S(2)}, u32[]{:S(2)}) collective-permute-start(bf16[768,256]{1,0:T(8,128)(2,1)S(1)} %copy-done.8), channel_id=1, source_target_pairs={{0,4},{4,0},{1,5},{5,1},{2,6},{6,2},{3,7},{7,3},{8,12},{12,8},{9,1... | collective-permute-start | bytes 1179656 | tf_op jit(solution)/shard_map/ppermute | solution.py:556
  265.7 10.0 %collective-permute-start.12 = (bf16[768,256]{1,0:T(8,128)(2,1)S(1)}, bf16[768,256]{1,0:T(8,128)(2,1)}, u32[]{:S(2)}, u32[]{:S(2)}) collective-permute-start(bf16[768,256]{1,0:T(8,128)(2,1)S(1)} %copy-done.9), channel_id=1, source_target_pairs={{0,4},{4,0},{1,5},{5,1},{2,6},{6,2},{3,7},{7,3},{8,12},{12,8},{9,1... | collective-permute-start | bytes 1179656 | tf_op jit(solution)/shard_map/ppermute | solution.py:556
  266.1 9.6 %collective-permute-start.13 = (bf16[256,768]{1,0:T(8,128)(2,1)}, bf16[256,768]{1,0:T(8,128)(2,1)}, u32[]{:S(2)}, u32[]{:S(2)}) collective-permute-start(bf16[256,768]{1,0:T(8,128)(2,1)} %get-tuple-element.56.grad_attn), channel_id=1, source_target_pairs={{0,4},{4,0},{1,5},{5,1},{2,6},{6,2},{3,7},{7,3},{8,12},{12,8},{9,1... | collective-permute-start | bytes 1179656 | tf_op jit(solution)/shard_map/ppermute | solution.py:556
  270.9 4.8 %collective-permute-start.9 = (bf16[256,768]{1,0:T(8,128)(2,1)S(1)}, bf16[256,768]{1,0:T(8,128)(2,1)}, u32[]{:S(2)}, u32[]{:S(2)}) collective-permute-start(bf16[256,768]{1,0:T(8,128)(2,1)S(1)} %copy-done.7), channel_id=1, source_target_pairs={{0,4},{4,0},{1,5},{5,1},{2,6},{6,2},{3,7},{7,3},{8,12},{12,8},{9,1... | collective-permute-start | bytes 1179656 | tf_op jit(solution)/shard_map/ppermute | solution.py:556
  271.1 15.6 %all-to-all-start.7 = ((bf16[16,64,192]{2,1,0:T(8,128)(2,1)}), bf16[16,64,192]{2,1,0:T(8,128)(2,1)}, u32[]{:S(2)}, u32[]{:S(2)}) async-start(bf16[16,64,192]{2,1,0:T(8,128)(2,1)} %get-tuple-element.51), calls=%async_computation.7 | async-start | bytes 1048576 | tf_op jit(solution)/shard_map/all_to_all | solution.py:552
  275.4 69.2 %reduce-scatter.2.cloned.1.call-start = ((), (), s32[]{:S(2)}) async-start(), calls=%async_computation.13 | async-start | bytes 6881280 | tf_op jit(solution)/shard_map/reduce_scatter | solution.py:684
  300.6 3.3 collective-permute-start.14
  305.1 19.9 %all-to-all-start.9 = ((bf16[16,64,384]{2,1,0:T(8,128)(2,1)}), bf16[16,64,384]{2,1,0:T(8,128)(2,1)}, u32[]{:S(2)}, u32[]{:S(2)}) async-start(bf16[16,64,384]{2,1,0:T(8,128)(2,1)} %bitcast.40), calls=%async_computation.10 | async-start | bytes 1572864 | tf_op jit(solution)/shard_map/all_to_all | solution.py:552
  344.6 36.2 %all-to-all-start.8 = ((bf16[8,112,768]{2,1,0:T(8,128)(2,1)}), bf16[8,112,768]{2,1,0:T(8,128)(2,1)}, u32[]{:S(2)}, u32[]{:S(2)}) async-start(bf16[8,112,768]{2,1,0:T(8,128)(2,1)} %bitcast.122), calls=%async_computation.9 | async-start | bytes 2752512 | tf_op jit(solution)/shard_map/all_to_all | solution.py:552
  351.0 20.4 %copy-start.5 = (bf16[16,64,192]{2,1,0:T(8,128)(2,1)S(1)}, bf16[16,64,192]{2,1,0:T(8,128)(2,1)}, u32[]{:S(2)}) copy-start(bf16[16,64,192]{2,1,0:T(8,128)(2,1)} %all_to_all.62.mixed) | copy-start | bytes 1179652
  351.0 20.4 %copy-start.16 = (f32[8,768]{1,0:T(8,128)S(1)}, f32[8,768]{1,0:T(8,128)}, u32[]{:S(2)}) copy-start(f32[8,768]{1,0:T(8,128)} %copy-done.15) | copy-start | bytes 73732
  351.0 20.4 %copy-start.18 = (f32[4,768]{1,0:T(4,128)S(1)}, f32[4,768]{1,0:T(4,128)}, u32[]{:S(2)}) copy-start(f32[4,768]{1,0:T(4,128)} %copy-done.17) | copy-start | bytes 36868
  351.0 8.9 %collective-permute-start.15 = (bf16[192,576]{1,0:T(8,128)(2,1)S(1)}, bf16[192,576]{1,0:T(8,128)(2,1)S(1)}, u32[]{:S(2)}, u32[]{:S(2)}) collective-permute-start(bf16[192,576]{1,0:T(8,128)(2,1)S(1)} %get-tuple-element.66), channel_id=1, source_target_pairs={{0,1},{1,2},{2,3},{3,0},{4,5},{5,6},{6,7},{7,4},{8,9},{9,10},{10,1... | collective-permute-start | bytes 663560 | tf_op jit(solution)/shard_map/ppermute | solution.py:593
  351.1 12.2 %collective-permute-start.16 = (bf16[192,576]{1,0:T(8,128)(2,1)S(1)}, bf16[192,576]{1,0:T(8,128)(2,1)}, u32[]{:S(2)}, u32[]{:S(2)}) collective-permute-start(bf16[192,576]{1,0:T(8,128)(2,1)S(1)} %get-tuple-element.67), channel_id=1, source_target_pairs={{0,2},{1,3},{2,0},{3,1},{4,6},{5,7},{6,4},{7,5},{8,10},{9,11},{10,... | collective-permute-start | bytes 663560 | tf_op jit(solution)/shard_map/ppermute | solution.py:593
  352.8 12.2 %collective-permute-start.17 = (bf16[192,576]{1,0:T(8,128)(2,1)S(1)}, bf16[192,576]{1,0:T(8,128)(2,1)S(1)}, u32[]{:S(2)}, u32[]{:S(2)}) collective-permute-start(bf16[192,576]{1,0:T(8,128)(2,1)S(1)} %get-tuple-element.68), channel_id=1, source_target_pairs={{0,3},{1,0},{2,1},{3,2},{4,7},{5,4},{6,5},{7,6},{8,11},{9,8},{10,9... | collective-permute-start | bytes 663560 | tf_op jit(solution)/shard_map/ppermute | solution.py:593
  366.9 13.7 %collective-permute-start.18 = (bf16[48,576]{1,0:T(8,128)(2,1)S(1)}, bf16[48,576]{1,0:T(8,128)(2,1)S(1)}, u32[]{:S(2)}, u32[]{:S(2)}) collective-permute-start(bf16[48,576]{1,0:T(8,128)(2,1)S(1)} %get-tuple-element.125), channel_id=1, source_target_pairs={{0,16},{16,32},{32,48},{48,0},{1,17},{17,33},{33,49},{49,1},{2,18}... | collective-permute-start | bytes 165896 | tf_op jit(solution)/shard_map/ppermute | solution.py:593
  368.4 12.2 %collective-permute-start.20 = (bf16[48,576]{1,0:T(8,128)(2,1)S(1)}, bf16[48,576]{1,0:T(8,128)(2,1)S(1)}, u32[]{:S(2)}, u32[]{:S(2)}) collective-permute-start(bf16[48,576]{1,0:T(8,128)(2,1)S(1)} %get-tuple-element.126), channel_id=1, source_target_pairs={{0,48},{16,0},{32,16},{48,32},{1,49},{17,1},{33,17},{49,33},{2,50}... | collective-permute-start | bytes 165896 | tf_op jit(solution)/shard_map/ppermute | solution.py:593
  369.7 10.9 %collective-permute-start.19 = (bf16[48,576]{1,0:T(8,128)(2,1)S(1)}, bf16[48,576]{1,0:T(8,128)(2,1)S(1)}, u32[]{:S(2)}, u32[]{:S(2)}) collective-permute-start(bf16[48,576]{1,0:T(8,128)(2,1)S(1)} %get-tuple-element.127), channel_id=1, source_target_pairs={{0,32},{16,48},{32,0},{48,16},{1,33},{17,49},{33,1},{49,17},{2,34}... | collective-permute-start | bytes 165896 | tf_op jit(solution)/shard_map/ppermute | solution.py:593
  382.5 35.4 %copy-start.38 = (f32[256,768]{1,0:T(8,128)S(1)}, f32[256,768]{1,0:T(8,128)}, u32[]{:S(2)}) copy-start(f32[256,768]{1,0:T(8,128)} %get-tuple-element.59) | copy-start | bytes 2359300
  413.8 8.3 %collective-permute-start.21 = (bf16[8,176,768]{2,1,0:T(8,128)(2,1)}, bf16[8,176,768]{2,1,0:T(8,128)(2,1)}, u32[]{:S(2)}, u32[]{:S(2)}) collective-permute-start(bf16[8,176,768]{2,1,0:T(8,128)(2,1)} %all_to_all.66.own), channel_id=1, source_target_pairs={{0,4},{4,0},{1,5},{5,1},{2,6},{6,2},{3,7},{7,3},{8,12},{12,8},{9,1... | collective-permute-start | bytes 6488072 | tf_op jit(solution)/shard_map/ppermute | solution.py:556
  (42 other events, 140.0 us)
Sparse Core Ops, SparseCore 0:
  11.0 73.1 all-gather.2
  286.9 57.6 reduce-scatter.1

commit v2 on v1

--- a/solution.py
+++ b/solution.py
@@ -561,7 +561,7 @@
     return jnp.where(first, own, other), jnp.where(first, other, own)
 
 
-def gather_weights(attn_out, mlp_in, mlp_out):
+def pack_weights(attn_out, mlp_in, mlp_out):
     core_id = lax.axis_index("core")
     width = attn_out.shape[2]
     out_half, up_half, down_half = (
@@ -571,8 +571,7 @@
         for weight in (attn_out, mlp_in, mlp_out)
     )
     panels = [up_half[:, start : start + width] for start in range(0, mlp_in.shape[2], width)]
-    packed = jnp.concatenate([down_half] + panels + [out_half], 0)
-    return lax.all_gather(packed, ("fsdp", "core"), axis=0)
+    return jnp.concatenate([down_half] + panels + [out_half], 0)
 
 
 def ring_pairs(axis, shift):
@@ -632,7 +631,10 @@
     ).reshape(shard, 3 * WIDTH)
     small_all = spread(small, "fsdp").reshape(fsdp_count, -1, shard).astype(jnp.float32)
     w_group = gather_ring(own_columns, "fsdp")
-    packed = gather_weights(attn_out, mlp_in, mlp_out)
+    packed, w_group, small_all = lax.optimization_barrier(
+        (pack_weights(attn_out, mlp_in, mlp_out), w_group, small_all)
+    )
+    packed = lax.all_gather(packed, ("fsdp", "core"), axis=0)
     model_width = attn_out.shape[2]
     half = model_width // 2
     vector_rows = small_all[:, :8].transpose(1, 0, 2).reshape(8, model_width)
@@ -675,10 +677,14 @@
         grad_heads = exchange(grad_mixed.reshape(-1, local_rows, WIDTH), CTX).reshape(-1, WIDTH)
         if last:
             grad_hidden, grad_attn, sums, up_sums = extra
-            active_low, normed_tall, mixed_tall = kept
-            members = (active_low, grad_low, normed_tall, grad_hidden, mixed_tall, grad_attn)
+            active_pair, normed_pair, mixed_pair = kept
+            low_pair, hidden_pair, attn_pair = (
+                (value, swap(value)) for value in (grad_low, grad_hidden, grad_attn)
+            )
             joint = weight_grads(
-                core_number, [(value, swap(value)) for value in members], fsdp_count
+                core_number,
+                [active_pair, low_pair, normed_pair, hidden_pair, mixed_pair, attn_pair],
+                fsdp_count,
             )
             grad_heads, joint = lax.optimization_barrier((grad_heads, joint))
             share = lax.psum_scatter(
@@ -693,6 +699,8 @@
         received = swap(grad_other)
         summed = (grad_own.astype(jnp.float32) + received.astype(jnp.float32)).astype(jnp.bfloat16)
         returned = exchange(summed.reshape(-1, local_rows, half), CTX)
+        if last:
+            returned, own = lax.optimization_barrier((returned, own))
         returned = returned.reshape(micro_count, 2, 2, local_rows, half).astype(jnp.float32)
         grad_normed = (returned[:, 0] + returned[:, 1]).transpose(0, 2, 1, 3)
         grad_normed = grad_normed.reshape(rows, model_width)
@@ -705,6 +713,7 @@
         *pieces, joined_sums = qkv_grads(numbers, own, other, grad_joined, fsdp_count)
         joined_sums = joined_sums[0]
         qkv_share = sum_pieces(pieces, "fsdp")
+        share, qkv_share = lax.optimization_barrier((share, qkv_share))
         x_count = lax.axis_size("x")
         piece_rows = shard // x_count
         x_pieces = [
@@ -732,6 +741,8 @@
         result, kept = backward(grad_low, saved, None)
         received = lax.ppermute(result, "section", back_pairs)
         grad_low = jnp.where(section_id == sections - 1, top_grad, received)
+        kept = [(value, swap(value)) for value in kept]
+        grad_low, kept = lax.optimization_barrier((grad_low, kept))
     input_grad, share, qkv_piece, joined_sums, vectors, d_up_bias = backward(grad_low, saved, kept)
 
     ours = jnp.arange(fsdp_count)[:, None] == group_id

time: 443 us -> 430 us (0.971)
  blocking collectives: 131 us -> 106 us
  starting transfers between devices: 54.6 us -> 61.5 us
    all_to_all x7 -> x5, blocking collectives: 131 us -> 106 us  [exchange(): return lax.all_to_all(value, axes, 0, 0, tiled=True)]
    all_to_all x5 -> x7, waiting for transfers between devices: 21.4 us -> 43.6 us  [exchange(): return lax.all_to_all(value, axes, 0, 0, tiled=True)]
    ppermute x3, waiting for transfers between devices: 19.7 us -> 0.01 us  [gather_ring(): lax.ppermute(value, axis, ring_pairs(axis, -shift))]
    ppermute x6, waiting for transfers between devices: 10.7 us -> 22.8 us  [sum_pieces(): received = lax.ppermute(pieces[shift], axis, ring_pairs(axis, shift))]
    reduce_scatter x1, waiting for transfers between devices: 8.16 us -> 0.55 us  [backward(): lax.psum_scatter(joint.reshape(-1, model_width), 'fsdp', scatter_dimensio...]
    unnamed x135 -> x115, local copies, waits for them, and re-layouts: 12.8 us -> 7.6 us
    all_to_all x5 -> x7, starting transfers between devices: 26.5 us -> 30.8 us  [exchange(): return lax.all_to_all(value, axes, 0, 0, tiled=True)]
  transfers between devices with their start and end apart: 29 -> 31, of which waited for: 16 -> 19; matrix products, arithmetic and copies ran while one was open for 4% -> 5% of each run, Pallas kernels for 12% -> 10%
where the time goes in v2:
time: 430 us; the launch traced here: 423 us
  blocking collectives  106 us (25%)
  Pallas kernels  101 us (23%)
  waiting for transfers between devices  93.4 us (22%)
  starting transfers between devices  61.5 us (14%)
  local copies, waits for them, and re-layouts  24.2 us (6%)
  between operations  23.2 us (5%)
  other arithmetic  14.3 us (3%)
    all_to_all x5, blocking collectives, exchange(): return lax.all_to_all(value, axes, 0, 0, tiled=True)  106 us
    all_to_all x7, waiting for transfers between devices, exchange(): return lax.all_to_all(value, axes, 0, 0, tiled=True)  43.6 us
    all_to_all x7, starting transfers between devices, exchange(): return lax.all_to_all(value, axes, 0, 0, tiled=True)  30.8 us
    pallas_call x2, Pallas kernels, attend_back(): pl.pallas_call(attend_back_body, grid_spec=pltpu.PrefetchScalarGridSpec(n...  24.2 us
    pallas_call x2, Pallas kernels, feed_back(): pl.pallas_call(feed_back_body, in_specs=[pl.BlockSpec(memory_space=pltpu....  23.8 us
    ppermute x6, waiting for transfers between devices, sum_pieces(): received = lax.ppermute(pieces[shift], axis, ring_pairs(axis, shift))  22.8 us
    pallas_call x2, Pallas kernels, attend(): pl.pallas_call(attend_body, grid_spec=pltpu.PrefetchScalarGridSpec(num_sc...  19.3 us
    pallas_call x2, Pallas kernels, feed_forward(): pl.pallas_call(feed_forward_body, in_specs=[pl.BlockSpec(memory_space=plt...  17.7 us
  transfers between devices with their start and end apart: 31, of which 19 were waited for; matrix products, arithmetic and copies ran while one was open for 5% of the time, Pallas kernels for 10%

profile of v2, /device:TPU:1, one launch (start us, length us, event | category | flops | bytes accessed | tf_op | source)
XLA Modules:
  0.0 423.4 jit_solution(9134761195347109479)
XLA Ops:
  7.2 3.0 reshape_squeeze.3
  12.6 2.5 collective-permute-start.2
  15.0 3.3 collective-permute-start.1
  19.9 3.3 all-to-all-start
  24.6 4.8 %all-to-all-done = bf16[4,4,576]{2,1,0:T(4,128)(2,1)S(1)} async-done(((bf16[4,4,576]{2,1,0:T(4,128)(2,1)}), bf16[4,4,576]{2,1,0:T(4,128)(2,1)S(1)}, u32[]{:S(2)}, u32[]{:S(2)}) %all-to-all-start) | async-done | bytes 18464 | tf_op jit(solution)/shard_map/all_to_all | solution.py:552
  40.0 22.9 %all_to_all.60 = bf16[16,64,384]{2,1,0:T(8,128)(2,1)S(1)} all-to-all(bf16[16,64,384]{2,1,0:T(8,128)(2,1)S(1)} %bitcast.116), channel_id=1, replica_groups=mesh['section'=2,'x'=4,'yh'=2,'core'=2,'fsdp'=4] {'x','yh','core'}, dimensions={0} | all-to-all | bytes 1572864 | tf_op jit(solution)/shard_map/all_to_all | solution.py:552
  65.4 10.3 %shard_map.178 = (bf16[1024,576]{1,0:T(8,128)(2,1)}, bf16[1024,192]{1,0:T(8,128)(2,1)}, f32[8,1024]{1,0:T(8,128)}) custom-call(s32[32]{0:T(128)S(1)} %copy-done.24, s32[2]{0:T(128)S(1)} %pad_add_fusion.ids, bf16[1024,384]{1,0:T(8,128)(2,1)S(1)} %bitcast.104, bf16[1024,384]{1,0:T(8,128)(2,1)S(1)} %collective-permute-done.3.other, ...), custom_call_target="tpu_custom_call" | custom-call | flops 805306368 | bytes 1572864 | tf_op jit(solution)/shard_map/pallas_call | solution.py:109
  75.7 3.7 all-to-all-start.2
  79.7 11.0 %all-to-all-done.2.mixed = bf16[16,64,192]{2,1,0:T(8,128)(2,1)S(1)} async-done(((bf16[16,64,192]{2,1,0:T(8,128)(2,1)}), bf16[16,64,192]{2,1,0:T(8,128)(2,1)S(1)}, u32[]{:S(2)}, u32[]{:S(2)}) %all-to-all-start.2) | async-done | bytes 393248 | tf_op jit(solution)/shard_map/all_to_all | solution.py:552
  90.9 8.5 %shard_map.179 = bf16[256,768]{1,0:T(8,128)(2,1)S(1)} custom-call(bf16[16,64,192]{2,1,0:T(8,128)(2,1)S(1)} %all-to-all-done.2.mixed, bf16[256,768]{1,0:T(8,128)(2,1)S(1)} %bitcast.99, bf16[8,864,768]{2,1,0:T(8,128)(2,1)} %bitcast.107, f32[8,768]{1,0:T(8,128)S(1)} %reshape.368.vectors, f32[4,768]{1,0:T(4,128)S(1)} %reshape.369.up_bias), custom_call_target="tpu_custom_call" | custom-call | flops 2717908992 | bytes 10616832 | tf_op jit(solution)/shard_map/pallas_call | solution.py:342
  99.4 3.1 collective-permute-start.4
  102.6 8.1 %collective-permute-done.4 = bf16[256,768]{1,0:T(8,128)(2,1)S(1)} collective-permute-done((bf16[256,768]{1,0:T(8,128)(2,1)S(1)}, bf16[256,768]{1,0:T(8,128)(2,1)S(1)}, u32[]{:S(2)}, u32[]{:S(2)}) %collective-permute-start.4) | collective-permute-done | bytes 393248 | tf_op jit(solution)/shard_map/ppermute | solution.py:734
  111.7 21.9 %all_to_all.61 = bf16[16,64,384]{2,1,0:T(8,128)(2,1)S(1)} all-to-all(bf16[16,64,384]{2,1,0:T(8,128)(2,1)S(1)} %bitcast.117), channel_id=1, replica_groups=mesh['section'=2,'x'=4,'yh'=2,'core'=2,'fsdp'=4] {'x','yh','core'}, dimensions={0} | all-to-all | bytes 1572864 | tf_op jit(solution)/shard_map/all_to_all | solution.py:552
  134.2 1.9 collective-permute-done.5.other
  136.1 9.0 %shard_map.180 = (bf16[1024,576]{1,0:T(8,128)(2,1)S(1)}, bf16[1024,192]{1,0:T(8,128)(2,1)S(1)}, f32[8,1024]{1,0:T(8,128)S(1)}) custom-call(s32[32]{0:T(128)S(1)} %copy-done.24, s32[2]{0:T(128)S(1)} %pad_add_fusion.ids, bf16[1024,384]{1,0:T(8,128)(2,1)S(1)} %bitcast.101, bf16[1024,384]{1,0:T(8,128)(2,1)S(1)} %collective-permute-done.5.other, ...), custom_call_target="tpu_custom_call" | custom-call | flops 805306368 | bytes 1572864 | tf_op jit(solution)/shard_map/pallas_call | solution.py:109
  145.2 14.7 %all_to_all.62.mixed = bf16[16,64,192]{2,1,0:T(8,128)(2,1)} all-to-all(bf16[16,64,192]{2,1,0:T(8,128)(2,1)S(1)} %bitcast.106), channel_id=1, replica_groups=mesh['section'=2,'x'=4,'yh'=2,'core'=2,'fsdp'=4] {'x','yh','core'}, dimensions={0} | all-to-all | bytes 786432 | tf_op jit(solution)/shard_map/all_to_all | solution.py:552
  159.9 12.0 %shard_map.181 = (bf16[16,64,192]{2,1,0:T(8,128)(2,1)}, f32[256,768]{1,0:T(8,128)}, bf16[256,3072]{1,0:T(8,128)(2,1)}, bf16[768,256]{1,0:T(8,128)(2,1)}, bf16[768,256]{1,0:T(8,128)(2,1)}) custom-call(bf16[16,64,192]{2,1,0:T(8,128)(2,1)} %all_to_all.62.mixed, bf16[256,768]{1,0:T(8,128)(2,1)} %copy-done.2, bf16[8,864,768]{2,1,0:T(8,128)(2,1)} %bitcast.108, ...), custom_call_target="tpu_custom_call" | custom-call | flops 4227858432 | bytes 14155776 | tf_op jit(solution)/shard_map/pallas_call | solution.py:428
  171.8 16.3 %all_to_all.63 = bf16[16,64,192]{2,1,0:T(8,128)(2,1)S(1)} all-to-all(bf16[16,64,192]{2,1,0:T(8,128)(2,1)} %get-tuple-element.70), channel_id=1, replica_groups=mesh['section'=2,'x'=4,'yh'=2,'core'=2,'fsdp'=4] {'x','yh','core'}, dimensions={0} | all-to-all | bytes 786432 | tf_op jit(solution)/shard_map/all_to_all | solution.py:552
  188.1 12.1 %shard_map.182 = (bf16[1024,576]{1,0:T(8,128)(2,1)}, bf16[1024,384]{1,0:T(8,128)(2,1)S(1)}, bf16[1024,384]{1,0:T(8,128)(2,1)S(1)}) custom-call(s32[32]{0:T(128)S(1)} %copy-done.24, s32[2]{0:T(128)S(1)} %pad_add_fusion.ids, bf16[1024,576]{1,0:T(8,128)(2,1)S(1)} %get-tuple-element.69.joined, bf16[1024,192]{1,0:T(8,128)(2,1)S(1)} %bitcast.105, ...), custom_call_target="tpu_custom_call" | custom-call | flops 2013265920 | bytes 3145728 | tf_op jit(solution)/shard_map/pallas_call | solution.py:202
  201.6 1.9 collective-permute-done.6
  204.6 4.5 %all-to-all-start.6 = ((bf16[16,64,384]{2,1,0:T(8,128)(2,1)}), bf16[16,64,384]{2,1,0:T(8,128)(2,1)}, u32[]{:S(2)}, u32[]{:S(2)}) async-start(bf16[16,64,384]{2,1,0:T(8,128)(2,1)} %bitcast.121), calls=%async_computation.6 | async-start | bytes 1572864 | tf_op jit(solution)/shard_map/all_to_all | solution.py:552
  209.5 14.0 %all-to-all-done.6 = bf16[16,64,384]{2,1,0:T(8,128)(2,1)} async-done(((bf16[16,64,384]{2,1,0:T(8,128)(2,1)}), bf16[16,64,384]{2,1,0:T(8,128)(2,1)}, u32[]{:S(2)}, u32[]{:S(2)}) %all-to-all-start.6) | async-done | bytes 786464 | tf_op jit(solution)/shard_map/all_to_all | solution.py:552
  226.5 1.8 copy.57
  232.4 8.8 %collective-permute-done.7 = bf16[256,768]{1,0:T(8,128)(2,1)} collective-permute-done((bf16[256,768]{1,0:T(8,128)(2,1)S(1)}, bf16[256,768]{1,0:T(8,128)(2,1)}, u32[]{:S(2)}, u32[]{:S(2)}) %collective-permute-start.7) | collective-permute-done | bytes 393248 | tf_op jit(solution)/shard_map/ppermute | solution.py:742
  241.2 1.9 broadcast_select_fusion.grad_low
  243.2 11.8 %shard_map.183 = (bf16[16,64,192]{2,1,0:T(8,128)(2,1)}, f32[256,768]{1,0:T(8,128)}, bf16[256,3072]{1,0:T(8,128)(2,1)}, bf16[256,768]{1,0:T(8,128)(2,1)}, f32[4,768]{1,0:T(4,128)}, /*index=5*/f32[4,768]{1,0:T(4,128)}) custom-call(bf16[16,64,192]{2,1,0:T(8,128)(2,1)} %all_to_all.62.mixed, bf16[256,768]{1,0:T(8,128)(2,1)} %copy-done.2, ...), custom_call_target="tpu_custom_call" | custom-call | flops 4227858432 | bytes 14155776 | tf_op jit(solution)/shard_map/pallas_call | solution.py:428
  255.0 2.0 collective-permute-start.12
  257.5 4.1 all-to-all-start.7
  262.9 8.1 %shard_map.184 = bf16[4,896,768]{2,1,0:T(8,128)(2,1)} custom-call(s32[1]{0:T(128)} %bitcast.core_id, bf16[256,3072]{1,0:T(8,128)(2,1)S(1)} %copy-done.6, bf16[256,3072]{1,0:T(8,128)(2,1)} %collective-permute-done.8.active_other, bf16[256,768]{1,0:T(8,128)(2,1)S(1)} %copy-done.7, bf16[256,768]{1,0:T(8,128)(2,1)} %collective-permute-done.11.grad_low_other, ...), custom_call_target="tpu_custom_call" | custom-call | flops 2717908992 | bytes 5505024 | tf_op jit(solution)/shard_map/pallas_call | solution.py:282
  271.0 1.8 all-to-all-done.7
  274.6 12.1 %shard_map.185 = (bf16[1024,576]{1,0:T(8,128)(2,1)S(1)}, bf16[1024,384]{1,0:T(8,128)(2,1)S(1)}, bf16[1024,384]{1,0:T(8,128)(2,1)S(1)}) custom-call(s32[32]{0:T(128)S(1)} %copy-done.24, s32[2]{0:T(128)S(1)} %copy-done.26, bf16[1024,576]{1,0:T(8,128)(2,1)S(1)} %copy-done.30, bf16[1024,192]{1,0:T(8,128)(2,1)} %bitcast.35.grad_mixed, f32[8,1024]{1,0:T(8,128)S(1)} %copy-done.32, ...), custom_call_target="tpu_custom_call" | custom-call | flops 2013265920 | bytes 3145728 | tf_op jit(solution)/shard_map/pallas_call | solution.py:202
  288.2 1.9 collective-permute-done.14
  291.2 4.9 %all-to-all-start.8 = ((bf16[16,64,384]{2,1,0:T(8,128)(2,1)}), bf16[16,64,384]{2,1,0:T(8,128)(2,1)S(1)}, u32[]{:S(2)}, u32[]{:S(2)}) async-start(bf16[16,64,384]{2,1,0:T(8,128)(2,1)} %bitcast.120), calls=%async_computation.9 | async-start | bytes 1572864 | tf_op jit(solution)/shard_map/all_to_all | solution.py:552
  298.1 12.0 %all-to-all-done.8 = bf16[16,64,384]{2,1,0:T(8,128)(2,1)S(1)} async-done(((bf16[16,64,384]{2,1,0:T(8,128)(2,1)}), bf16[16,64,384]{2,1,0:T(8,128)(2,1)S(1)}, u32[]{:S(2)}, u32[]{:S(2)}) %all-to-all-start.8) | async-done | bytes 786464 | tf_op jit(solution)/shard_map/all_to_all | solution.py:552
  311.5 2.1 shard_map.186
  315.4 2.0 collective-permute-start.17
  320.4 3.3 all-to-all-start.10
  323.6 4.5 %collective-permute-done.15 = bf16[192,576]{1,0:T(8,128)(2,1)} collective-permute-done((bf16[192,576]{1,0:T(8,128)(2,1)S(1)}, bf16[192,576]{1,0:T(8,128)(2,1)}, u32[]{:S(2)}, u32[]{:S(2)}) %collective-permute-start.15) | collective-permute-done | bytes 221216 | tf_op jit(solution)/shard_map/ppermute | solution.py:592
  328.1 9.2 %collective-permute-done.16 = bf16[192,576]{1,0:T(8,128)(2,1)} collective-permute-done((bf16[192,576]{1,0:T(8,128)(2,1)S(1)}, bf16[192,576]{1,0:T(8,128)(2,1)}, u32[]{:S(2)}, u32[]{:S(2)}) %collective-permute-start.16) | collective-permute-done | bytes 221216 | tf_op jit(solution)/shard_map/ppermute | solution.py:592
  339.2 7.0 %all-to-all-start.9 = ((bf16[8,112,768]{2,1,0:T(8,128)(2,1)}), bf16[8,112,768]{2,1,0:T(8,128)(2,1)}, u32[]{:S(2)}, u32[]{:S(2)}) async-start(bf16[8,112,768]{2,1,0:T(8,128)(2,1)} %bitcast.125), calls=%async_computation.10 | async-start | bytes 2752512 | tf_op jit(solution)/shard_map/all_to_all | solution.py:552
  350.8 9.2 %shard_map.187 = bf16[256,768]{1,0:T(8,128)(2,1)} custom-call(bf16[16,64,192]{2,1,0:T(8,128)(2,1)S(1)} %copy-done.5, bf16[256,768]{1,0:T(8,128)(2,1)S(1)} %copy-done.4, bf16[8,864,768]{2,1,0:T(8,128)(2,1)} %bitcast.110, f32[8,768]{1,0:T(8,128)S(1)} %copy-done.13, f32[4,768]{1,0:T(4,128)S(1)} %copy-done.15), custom_call_target="tpu_custom_call" | custom-call | flops 2717908992 | bytes 10616832 | tf_op jit(solution)/shard_map/pallas_call | solution.py:342
  360.0 2.5 collective-permute-done.18
  362.5 2.3 collective-permute-done.20
  364.8 4.3 %collective-permute-done.19 = bf16[48,576]{1,0:T(8,128)(2,1)S(1)} collective-permute-done((bf16[48,576]{1,0:T(8,128)(2,1)S(1)}, bf16[48,576]{1,0:T(8,128)(2,1)S(1)}, u32[]{:S(2)}, u32[]{:S(2)}) %collective-permute-start.19) | collective-permute-done | bytes 55328 | tf_op jit(solution)/shard_map/ppermute | solution.py:592
  370.9 30.5 %all_to_all.64.own = bf16[8,176,768]{2,1,0:T(8,128)(2,1)} all-to-all(bf16[8,176,768]{2,1,0:T(8,128)(2,1)S(1)} %broadcast_in_dim.111), channel_id=1, replica_groups=mesh['section'=2,'x'=4,'yh'=2,'core'=2,'fsdp'=4] {'x','yh'}, dimensions={0} | all-to-all | bytes 4325376 | tf_op jit(solution)/shard_map/all_to_all | solution.py:552
  401.4 3.0 collective-permute-start.21
  405.5 3.1 collective-permute-done.21.other
  408.6 5.5 %shard_map.188 = (f32[192,2304]{1,0:T(8,128)}, f32[192,768]{1,0:T(8,128)}, f32[192,3072]{1,0:T(8,128)}, f32[768,768]{1,0:T(8,128)}, f32[4,768]{1,0:T(4,128)S(1)}) custom-call(s32[1]{0:T(128)} %bitcast.core_id, bf16[8,176,768]{2,1,0:T(8,128)(2,1)} %all_to_all.64.own, bf16[8,176,768]{2,1,0:T(8,128)(2,1)} %collective-permute-done.21.other), custom_call_target="tpu_custom_call" | custom-call | bytes 12582912 | tf_op jit(solution)/shard_map/pallas_call | solution.py:517
  (245 shorter events, 48.0 us)
Async XLA Ops:
  7.2 16.1 %copy-start = (bf16[1,192,3072]{2,1,0:T(8,128)(2,1)S(1)}, bf16[1,192,3072]{2,1,0:T(8,128)(2,1)}, u32[]{:S(2)}) copy-start(bf16[1,192,3072]{2,1,0:T(8,128)(2,1)} %param.17) | copy-start | bytes 3538948
  12.6 16.9 %collective-permute-start.2 = (bf16[192,576]{1,0:T(8,128)(2,1)}, bf16[192,576]{1,0:T(8,128)(2,1)S(1)}, u32[]{:S(2)}, u32[]{:S(2)}) collective-permute-start(bf16[192,576]{1,0:T(8,128)(2,1)} %copy.48), channel_id=1, source_target_pairs={{0,1},{1,2},{2,3},{3,0},{4,5},{5,6},{6,7},{7,4},{8,9},{9,10},{10,1... | collective-permute-start | bytes 663560 | tf_op jit(solution)/shard_map/ppermute | solution.py:584
  15.0 14.5 %collective-permute-start.1 = (bf16[192,576]{1,0:T(8,128)(2,1)}, bf16[192,576]{1,0:T(8,128)(2,1)S(1)}, u32[]{:S(2)}, u32[]{:S(2)}) collective-permute-start(bf16[192,576]{1,0:T(8,128)(2,1)} %copy.48), channel_id=1, source_target_pairs={{0,2},{1,3},{2,0},{3,1},{4,6},{5,7},{6,4},{7,5},{8,10},{9,11},{10,... | collective-permute-start | bytes 663560 | tf_op jit(solution)/shard_map/ppermute | solution.py:584
  18.3 11.2 %collective-permute-start = (bf16[192,576]{1,0:T(8,128)(2,1)}, bf16[192,576]{1,0:T(8,128)(2,1)S(1)}, u32[]{:S(2)}, u32[]{:S(2)}) collective-permute-start(bf16[192,576]{1,0:T(8,128)(2,1)} %copy.48), channel_id=1, source_target_pairs={{0,3},{1,0},{2,1},{3,2},{4,7},{5,4},{6,5},{7,6},{8,11},{9,8},{10,9... | collective-permute-start | bytes 663560 | tf_op jit(solution)/shard_map/ppermute | solution.py:584
  19.9 9.5 %all-to-all-start = ((bf16[4,4,576]{2,1,0:T(4,128)(2,1)}), bf16[4,4,576]{2,1,0:T(4,128)(2,1)S(1)}, u32[]{:S(2)}, u32[]{:S(2)}) async-start(bf16[4,4,576]{2,1,0:T(4,128)(2,1)} %broadcast_in_dim.98), calls=%async_computation | async-start | bytes 40960 | tf_op jit(solution)/shard_map/all_to_all | solution.py:552
  23.2 67.7 %all-gather.3.cloned.1.call-start = ((), (), s32[]{:S(2)}) async-start(), calls=%async_computation.14 | async-start | bytes 11943936 | tf_op jit(solution)/shard_map/all_gather | solution.py:637
  24.5 13.5 %copy-start.37 = (bf16[4,1,64,768]{3,2,1,0:T(8,128)(2,1)S(1)}, bf16[4,1,64,768]{3,2,1,0:T(8,128)(2,1)}, u32[]{:S(2)}) copy-start(bf16[4,1,64,768]{3,2,1,0:T(8,128)(2,1)} %param.11) | copy-start | bytes 1179652
  29.5 158.6 %copy-start.18 = (bf16[192,576]{1,0:T(8,128)(2,1)}, bf16[192,576]{1,0:T(8,128)(2,1)S(1)}, u32[]{:S(2)}) copy-start(bf16[192,576]{1,0:T(8,128)(2,1)S(1)} %collective-permute-done.2.w3) | copy-start | bytes 663556
  29.5 158.6 %copy-start.20 = (bf16[192,576]{1,0:T(8,128)(2,1)}, bf16[192,576]{1,0:T(8,128)(2,1)S(1)}, u32[]{:S(2)}) copy-start(bf16[192,576]{1,0:T(8,128)(2,1)S(1)} %collective-permute-done.1.w2) | copy-start | bytes 663556
  29.5 158.6 %copy-start.22 = (bf16[192,576]{1,0:T(8,128)(2,1)}, bf16[192,576]{1,0:T(8,128)(2,1)S(1)}, u32[]{:S(2)}) copy-start(bf16[192,576]{1,0:T(8,128)(2,1)S(1)} %collective-permute-done.w1) | copy-start | bytes 663556
  39.0 185.8 %copy-start.39 = (f32[2,384]{1,0:T(2,128)}, f32[2,384]{1,0:T(2,128)S(1)}, u32[]{:S(2)}) copy-start(f32[2,384]{1,0:T(2,128)S(1)} %mul.148) | copy-start | bytes 9220
  40.0 25.4 %copy-start.24 = (s32[32]{0:T(128)S(1)}, s32[32]{0:T(128)}, u32[]{:S(2)}) copy-start(s32[32]{0:T(128)} %table.7) | copy-start | bytes 388
  63.0 2.5 collective-permute-start.3
  63.6 124.5 %copy-start.25 = (s32[2]{0:T(128)}, s32[2]{0:T(128)S(1)}, u32[]{:S(2)}) copy-start(s32[2]{0:T(128)S(1)} %pad_add_fusion.ids) | copy-start | bytes 28
  64.8 123.4 %copy-start.10 = (bf16[192,576]{1,0:T(8,128)(2,1)}, bf16[192,576]{1,0:T(8,128)(2,1)S(1)}, u32[]{:S(2)}) copy-start(bf16[192,576]{1,0:T(8,128)(2,1)S(1)} %copy.52.w0) | copy-start | bytes 663556
  75.7 14.9 %all-to-all-start.2 = ((bf16[16,64,192]{2,1,0:T(8,128)(2,1)}), bf16[16,64,192]{2,1,0:T(8,128)(2,1)S(1)}, u32[]{:S(2)}, u32[]{:S(2)}) async-start(bf16[16,64,192]{2,1,0:T(8,128)(2,1)} %bitcast.20), calls=%async_computation.2 | async-start | bytes 1048576 | tf_op jit(solution)/shard_map/all_to_all | solution.py:552
  79.6 19.7 %copy-start.14 = (f32[4,768]{1,0:T(4,128)}, f32[4,768]{1,0:T(4,128)S(1)}, u32[]{:S(2)}) copy-start(f32[4,768]{1,0:T(4,128)S(1)} %reshape.369.up_bias) | copy-start | bytes 36868
  79.7 19.7 %copy-start.12 = (f32[8,768]{1,0:T(8,128)}, f32[8,768]{1,0:T(8,128)S(1)}, u32[]{:S(2)}) copy-start(f32[8,768]{1,0:T(8,128)S(1)} %reshape.368.vectors) | copy-start | bytes 73732
  99.4 11.3 %collective-permute-start.4 = (bf16[256,768]{1,0:T(8,128)(2,1)S(1)}, bf16[256,768]{1,0:T(8,128)(2,1)S(1)}, u32[]{:S(2)}, u32[]{:S(2)}) collective-permute-start(bf16[256,768]{1,0:T(8,128)(2,1)S(1)} %shard_map.179), channel_id=1, source_target_pairs={{0,64},{1,65},{2,66},{3,67},{4,68},{5,69},{6,70},{7,71},{8,72},{9,... | collective-permute-start | bytes 1179656 | tf_op jit(solution)/shard_map/ppermute | solution.py:734
  133.6 2.5 collective-permute-start.5
  145.2 43.0 %copy-start.29 = (bf16[1024,576]{1,0:T(8,128)(2,1)}, bf16[1024,576]{1,0:T(8,128)(2,1)S(1)}, u32[]{:S(2)}) copy-start(bf16[1024,576]{1,0:T(8,128)(2,1)S(1)} %get-tuple-element.69.joined) | copy-start | bytes 3538948
  145.2 43.0 %copy-start.31 = (f32[8,1024]{1,0:T(8,128)}, f32[8,1024]{1,0:T(8,128)S(1)}, u32[]{:S(2)}) copy-start(f32[8,1024]{1,0:T(8,128)S(1)} %get-tuple-element.71.log_total) | copy-start | bytes 98308
  200.3 3.3 collective-permute-start.6
  204.6 18.9 %all-to-all-start.6 = ((bf16[16,64,384]{2,1,0:T(8,128)(2,1)}), bf16[16,64,384]{2,1,0:T(8,128)(2,1)}, u32[]{:S(2)}, u32[]{:S(2)}) async-start(bf16[16,64,384]{2,1,0:T(8,128)(2,1)} %bitcast.121), calls=%async_computation.6 | async-start | bytes 1572864 | tf_op jit(solution)/shard_map/all_to_all | solution.py:552
  209.2 34.0 %collective-permute-start.8 = (bf16[256,3072]{1,0:T(8,128)(2,1)S(1)}, bf16[256,3072]{1,0:T(8,128)(2,1)}, u32[]{:S(2)}, u32[]{:S(2)}) collective-permute-start(bf16[256,3072]{1,0:T(8,128)(2,1)S(1)} %copy-done.6), channel_id=1, source_target_pairs={{0,4},{4,0},{1,5},{5,1},{2,6},{6,2},{3,7},{7,3},{8,12},{12,8},{9,1... | collective-permute-start | bytes 4718600 | tf_op jit(solution)/shard_map/ppermute | solution.py:556
  229.7 11.5 %collective-permute-start.7 = (bf16[256,768]{1,0:T(8,128)(2,1)S(1)}, bf16[256,768]{1,0:T(8,128)(2,1)}, u32[]{:S(2)}, u32[]{:S(2)}) collective-permute-start(bf16[256,768]{1,0:T(8,128)(2,1)S(1)} %fusion.14), channel_id=1, source_target_pairs={{64,0},{65,1},{66,2},{67,3},{68,4},{69,5},{70,6},{71,7},{72,8},{73... | collective-permute-start | bytes 1179656 | tf_op jit(solution)/shard_map/ppermute | solution.py:742
  231.0 12.1 %collective-permute-start.9 = (bf16[768,256]{1,0:T(8,128)(2,1)S(1)}, bf16[768,256]{1,0:T(8,128)(2,1)S(1)}, u32[]{:S(2)}, u32[]{:S(2)}) collective-permute-start(bf16[768,256]{1,0:T(8,128)(2,1)S(1)} %copy-done.8), channel_id=1, source_target_pairs={{0,4},{4,0},{1,5},{5,1},{2,6},{6,2},{3,7},{7,3},{8,12},{12,8},{9,1... | collective-permute-start | bytes 1179656 | tf_op jit(solution)/shard_map/ppermute | solution.py:556
  232.4 10.8 %collective-permute-start.10 = (bf16[768,256]{1,0:T(8,128)(2,1)}, bf16[768,256]{1,0:T(8,128)(2,1)}, u32[]{:S(2)}, u32[]{:S(2)}) collective-permute-start(bf16[768,256]{1,0:T(8,128)(2,1)} %get-tuple-element.84.mixed), channel_id=1, source_target_pairs={{0,4},{4,0},{1,5},{5,1},{2,6},{6,2},{3,7},{7,3},{8,12},{12,8},{9,1... | collective-permute-start | bytes 1179656 | tf_op jit(solution)/shard_map/ppermute | solution.py:556
  243.1 13.9 %copy-start.7 = (bf16[256,768]{1,0:T(8,128)(2,1)S(1)}, bf16[256,768]{1,0:T(8,128)(2,1)}, u32[]{:S(2)}) copy-start(bf16[256,768]{1,0:T(8,128)(2,1)} %broadcast_select_fusion.grad_low) | copy-start | bytes 1179652
  255.0 7.0 %collective-permute-start.12 = (bf16[256,3072]{1,0:T(8,128)(2,1)}, bf16[256,3072]{1,0:T(8,128)(2,1)}, u32[]{:S(2)}, u32[]{:S(2)}) collective-permute-start(bf16[256,3072]{1,0:T(8,128)(2,1)} %get-tuple-element.83.grad_hidden), channel_id=1, source_target_pairs={{0,4},{4,0},{1,5},{5,1},{2,6},{6,2},{3,7},{7,3},{8,12},{12,8},{9,1... | collective-permute-start | bytes 4718600 | tf_op jit(solution)/shard_map/ppermute | solution.py:556
  257.0 4.9 %collective-permute-start.13 = (bf16[256,768]{1,0:T(8,128)(2,1)}, bf16[256,768]{1,0:T(8,128)(2,1)}, u32[]{:S(2)}, u32[]{:S(2)}) collective-permute-start(bf16[256,768]{1,0:T(8,128)(2,1)} %get-tuple-element.86.grad_attn), channel_id=1, source_target_pairs={{0,4},{4,0},{1,5},{5,1},{2,6},{6,2},{3,7},{7,3},{8,12},{12,8},{9,1... | collective-permute-start | bytes 1179656 | tf_op jit(solution)/shard_map/ppermute | solution.py:556
  257.1 4.8 %collective-permute-start.11 = (bf16[256,768]{1,0:T(8,128)(2,1)S(1)}, bf16[256,768]{1,0:T(8,128)(2,1)}, u32[]{:S(2)}, u32[]{:S(2)}) collective-permute-start(bf16[256,768]{1,0:T(8,128)(2,1)S(1)} %copy-done.7), channel_id=1, source_target_pairs={{0,4},{4,0},{1,5},{5,1},{2,6},{6,2},{3,7},{7,3},{8,12},{12,8},{9,1... | collective-permute-start | bytes 1179656 | tf_op jit(solution)/shard_map/ppermute | solution.py:556
  257.5 15.3 %all-to-all-start.7 = ((bf16[16,64,192]{2,1,0:T(8,128)(2,1)}), bf16[16,64,192]{2,1,0:T(8,128)(2,1)}, u32[]{:S(2)}, u32[]{:S(2)}) async-start(bf16[16,64,192]{2,1,0:T(8,128)(2,1)} %get-tuple-element.78), calls=%async_computation.7 | async-start | bytes 1048576 | tf_op jit(solution)/shard_map/all_to_all | solution.py:552
  261.6 77.6 %reduce-scatter.2.cloned.1.call-start = ((), (), s32[]{:S(2)}) async-start(), calls=%async_computation.13 | async-start | bytes 6881280 | tf_op jit(solution)/shard_map/reduce_scatter | solution.py:690
  286.8 3.3 collective-permute-start.14
  291.2 18.9 %copy-start.17 = (bf16[1024,384]{1,0:T(8,128)(2,1)S(1)}, bf16[1024,384]{1,0:T(8,128)(2,1)}, u32[]{:S(2)}) copy-start(bf16[1024,384]{1,0:T(8,128)(2,1)} %copy-done.16) | copy-start | bytes 2359300
  291.2 18.9 %all-to-all-start.8 = ((bf16[16,64,384]{2,1,0:T(8,128)(2,1)}), bf16[16,64,384]{2,1,0:T(8,128)(2,1)S(1)}, u32[]{:S(2)}, u32[]{:S(2)}) async-start(bf16[16,64,384]{2,1,0:T(8,128)(2,1)} %bitcast.120), calls=%async_computation.9 | async-start | bytes 1572864 | tf_op jit(solution)/shard_map/all_to_all | solution.py:552
  313.6 14.6 %collective-permute-start.15 = (bf16[192,576]{1,0:T(8,128)(2,1)S(1)}, bf16[192,576]{1,0:T(8,128)(2,1)}, u32[]{:S(2)}, u32[]{:S(2)}) collective-permute-start(bf16[192,576]{1,0:T(8,128)(2,1)S(1)} %get-tuple-element.94), channel_id=1, source_target_pairs={{0,1},{1,2},{2,3},{3,0},{4,5},{5,6},{6,7},{7,4},{8,9},{9,10},{10,1... | collective-permute-start | bytes 663560 | tf_op jit(solution)/shard_map/ppermute | solution.py:592
  314.0 23.4 %collective-permute-start.16 = (bf16[192,576]{1,0:T(8,128)(2,1)S(1)}, bf16[192,576]{1,0:T(8,128)(2,1)}, u32[]{:S(2)}, u32[]{:S(2)}) collective-permute-start(bf16[192,576]{1,0:T(8,128)(2,1)S(1)} %get-tuple-element.95), channel_id=1, source_target_pairs={{0,2},{1,3},{2,0},{3,1},{4,6},{5,7},{6,4},{7,5},{8,10},{9,11},{10,... | collective-permute-start | bytes 663560 | tf_op jit(solution)/shard_map/ppermute | solution.py:592
  315.4 22.0 %collective-permute-start.17 = (bf16[192,576]{1,0:T(8,128)(2,1)S(1)}, bf16[192,576]{1,0:T(8,128)(2,1)}, u32[]{:S(2)}, u32[]{:S(2)}) collective-permute-start(bf16[192,576]{1,0:T(8,128)(2,1)S(1)} %get-tuple-element.96), channel_id=1, source_target_pairs={{0,3},{1,0},{2,1},{3,2},{4,7},{5,4},{6,5},{7,6},{8,11},{9,8},{10,9... | collective-permute-start | bytes 663560 | tf_op jit(solution)/shard_map/ppermute | solution.py:592
  320.4 18.9 %all-to-all-start.10 = ((bf16[4,4,576]{2,1,0:T(4,128)(2,1)}), bf16[4,4,576]{2,1,0:T(4,128)(2,1)S(1)}, u32[]{:S(2)}, u32[]{:S(2)}) async-start(bf16[4,4,576]{2,1,0:T(4,128)(2,1)} %convert_element_type.157), calls=%async_computation.11 | async-start | bytes 40960 | tf_op jit(solution)/shard_map/all_to_all | solution.py:552
  339.2 29.9 %all-to-all-start.9 = ((bf16[8,112,768]{2,1,0:T(8,128)(2,1)}), bf16[8,112,768]{2,1,0:T(8,128)(2,1)}, u32[]{:S(2)}, u32[]{:S(2)}) async-start(bf16[8,112,768]{2,1,0:T(8,128)(2,1)} %bitcast.125), calls=%async_computation.10 | async-start | bytes 2752512 | tf_op jit(solution)/shard_map/all_to_all | solution.py:552
  346.3 16.2 %collective-permute-start.18 = (bf16[48,576]{1,0:T(8,128)(2,1)S(1)}, bf16[48,576]{1,0:T(8,128)(2,1)S(1)}, u32[]{:S(2)}, u32[]{:S(2)}) collective-permute-start(bf16[48,576]{1,0:T(8,128)(2,1)S(1)} %get-tuple-element.159), channel_id=1, source_target_pairs={{0,16},{16,32},{32,48},{48,0},{1,17},{17,33},{33,49},{49,1},{2,18}... | collective-permute-start | bytes 165896 | tf_op jit(solution)/shard_map/ppermute | solution.py:592
  347.8 17.0 %collective-permute-start.20 = (bf16[48,576]{1,0:T(8,128)(2,1)S(1)}, bf16[48,576]{1,0:T(8,128)(2,1)S(1)}, u32[]{:S(2)}, u32[]{:S(2)}) collective-permute-start(bf16[48,576]{1,0:T(8,128)(2,1)S(1)} %get-tuple-element.160), channel_id=1, source_target_pairs={{0,48},{16,0},{32,16},{48,32},{1,49},{17,1},{33,17},{49,33},{2,50}... | collective-permute-start | bytes 165896 | tf_op jit(solution)/shard_map/ppermute | solution.py:592
  349.1 20.0 %collective-permute-start.19 = (bf16[48,576]{1,0:T(8,128)(2,1)S(1)}, bf16[48,576]{1,0:T(8,128)(2,1)S(1)}, u32[]{:S(2)}, u32[]{:S(2)}) collective-permute-start(bf16[48,576]{1,0:T(8,128)(2,1)S(1)} %get-tuple-element.161), channel_id=1, source_target_pairs={{0,32},{16,48},{32,0},{48,16},{1,33},{17,49},{33,1},{49,17},{2,34}... | collective-permute-start | bytes 165896 | tf_op jit(solution)/shard_map/ppermute | solution.py:592
  370.9 33.6 %copy-start.35 = (f32[256,768]{1,0:T(8,128)S(1)}, f32[256,768]{1,0:T(8,128)}, u32[]{:S(2)}) copy-start(f32[256,768]{1,0:T(8,128)} %get-tuple-element.99) | copy-start | bytes 2359300
  401.4 7.2 %collective-permute-start.21 = (bf16[8,176,768]{2,1,0:T(8,128)(2,1)}, bf16[8,176,768]{2,1,0:T(8,128)(2,1)}, u32[]{:S(2)}, u32[]{:S(2)}) collective-permute-start(bf16[8,176,768]{2,1,0:T(8,128)(2,1)} %all_to_all.64.own), channel_id=1, source_target_pairs={{0,4},{4,0},{1,5},{5,1},{2,6},{6,2},{3,7},{7,3},{8,12},{12,8},{9,1... | collective-permute-start | bytes 6488072 | tf_op jit(solution)/shard_map/ppermute | solution.py:556
  404.5 11.7 %copy-start.1 = (bf16[1,192,3072]{2,1,0:T(8,128)(2,1)S(1)}, bf16[1,192,3072]{2,1,0:T(8,128)(2,1)}, u32[]{:S(2)}) copy-start(bf16[1,192,3072]{2,1,0:T(8,128)(2,1)} %param.17) | copy-start | bytes 3538948
  (34 other events, 141.4 us)
Sparse Core Ops, SparseCore 0:
  29.7 61.1 all-gather.2
  273.0 66.1 reduce-scatter.1

commit v3 on v2

--- a/solution.py
+++ b/solution.py
@@ -1,3 +1,5 @@
+import functools
+
 import jax
 import jax.numpy as jnp
 from jax import lax
@@ -439,7 +441,7 @@
     )(mixed, entering, packed, vectors, up_bias, grad_low)
 
 
-def qkv_grads_body(ids, own, other, grad_joined, *outs):
+def qkv_grads_body(owners, ids, own, other, grad_joined, *outs):
     pieces, sums, both = outs[:-2], outs[-2], outs[-1]
     first_core = ids[0] == 0
     grads = grad_joined[...]
@@ -448,19 +450,22 @@
     other_grads = dot(other[...], grads, 0, 0).astype(jnp.bfloat16)
     both[:half, :] = jnp.where(first_core, own_grads, other_grads)
     both[half:, :] = jnp.where(first_core, other_grads, own_grads)
-    count, piece_rows = len(pieces), pieces[0].shape[0]
+    count = len(pieces)
+    rows = pieces[0].shape[0] // owners
     for shift in range(count):
-        start = lax.rem(ids[1] + shift, count) * piece_rows
-        pieces[shift][...] = both[pl.ds(pl.multiple_of(start, piece_rows), piece_rows), :]
+        place = lax.rem(ids[2] + shift, count) * rows
+        for owner in range(owners):
+            start = pl.multiple_of(owner * rows * count + place, rows)
+            pieces[shift][owner * rows : (owner + 1) * rows, :] = both[pl.ds(start, rows), :]
     sums[...] = jnp.sum(grads.astype(jnp.float32), 0, keepdims=True)
 
 
-def qkv_grads(ids, own, other, grad_joined, count):
+def qkv_grads(ids, own, other, grad_joined, count, owners):
     rows, half = own.shape
     width = grad_joined.shape[1]
     piece = jax.ShapeDtypeStruct((2 * half // count, width), jnp.bfloat16)
     return pl.pallas_call(
-        qkv_grads_body,
+        functools.partial(qkv_grads_body, owners),
         in_specs=[pl.BlockSpec(memory_space=pltpu.SMEM)]
         + [pl.BlockSpec(memory_space=pltpu.VMEM)] * 3,
         out_specs=[pl.BlockSpec(memory_space=pltpu.VMEM)] * (count + 1),
@@ -631,9 +636,7 @@
     ).reshape(shard, 3 * WIDTH)
     small_all = spread(small, "fsdp").reshape(fsdp_count, -1, shard).astype(jnp.float32)
     w_group = gather_ring(own_columns, "fsdp")
-    packed, w_group, small_all = lax.optimization_barrier(
-        (pack_weights(attn_out, mlp_in, mlp_out), w_group, small_all)
-    )
+    packed = pack_weights(attn_out, mlp_in, mlp_out)
     packed = lax.all_gather(packed, ("fsdp", "core"), axis=0)
     model_width = attn_out.shape[2]
     half = model_width // 2
@@ -650,7 +653,7 @@
     ).reshape(rows, model_width)
     top_grad = cotangent.reshape(rows, model_width)
     core_number = core_id.astype(jnp.int32)[None]
-    numbers = jnp.stack([core_id, fsdp_id]).astype(jnp.int32)
+    numbers = jnp.stack([core_id, fsdp_id, lax.axis_index("x")]).astype(jnp.int32)
 
     def forward(entering):
         stream = entering.astype(jnp.float32)
@@ -660,9 +663,10 @@
             halves.transpose(0, 1, 3, 2, 4), (micro_count, 2, 2, local_rows, half)
         )
         own = exchange(halves.reshape(-1, local_rows, half), CTX).reshape(-1, half)
+        own, weights = lax.optimization_barrier((own, w_group))
         other = swap(own)
         joined, mixed_heads, log_total = attend(
-            block_table, numbers, own, other, w_group, group_bias
+            block_table, numbers, own, other, weights, group_bias
         )
         mixed = exchange(mixed_heads.reshape(-1, local_rows, WIDTH), CTX)
         result = feed_forward(mixed, entering, packed, vector_rows, up_rows)
@@ -699,8 +703,6 @@
         received = swap(grad_other)
         summed = (grad_own.astype(jnp.float32) + received.astype(jnp.float32)).astype(jnp.bfloat16)
         returned = exchange(summed.reshape(-1, local_rows, half), CTX)
-        if last:
-            returned, own = lax.optimization_barrier((returned, own))
         returned = returned.reshape(micro_count, 2, 2, local_rows, half).astype(jnp.float32)
         grad_normed = (returned[:, 0] + returned[:, 1]).transpose(0, 2, 1, 3)
         grad_normed = grad_normed.reshape(rows, model_width)
@@ -710,19 +712,19 @@
         grad_in = (grad_middle + grad_norm_one).astype(jnp.bfloat16)
         if not last:
             return grad_in, extra
-        *pieces, joined_sums = qkv_grads(numbers, own, other, grad_joined, fsdp_count)
+        x_count = lax.axis_size("x")
+        *pieces, joined_sums = qkv_grads(numbers, own, other, grad_joined, x_count, fsdp_count)
         joined_sums = joined_sums[0]
-        qkv_share = sum_pieces(pieces, "fsdp")
+        qkv_share = sum_pieces(pieces, "x")
         share, qkv_share = lax.optimization_barrier((share, qkv_share))
-        x_count = lax.axis_size("x")
         piece_rows = shard // x_count
-        x_pieces = [
+        owner_pieces = [
             lax.dynamic_slice_in_dim(
-                qkv_share, (lax.axis_index("x") + shift) % x_count * piece_rows, piece_rows, 0
+                qkv_share, (fsdp_id + shift) % fsdp_count * piece_rows, piece_rows, 0
             )
-            for shift in range(x_count)
+            for shift in range(fsdp_count)
         ]
-        qkv_piece = sum_pieces(x_pieces, "x")
+        qkv_piece = sum_pieces(owner_pieces, "fsdp")
         vectors = jnp.stack([d_gain_one, sums[0], d_shift_one, sums[2], sums[1], sums[3]])
         d_up_bias = up_sums.reshape(-1)
         return grad_in, share, qkv_piece, joined_sums, vectors, d_up_bias

time: 430 us -> 422 us (0.981)
  blocking collectives: 106 us -> 82.2 us
  starting transfers between devices: 61.5 us -> 73.9 us
    all_to_all x5 -> x4, blocking collectives: 106 us -> 82.2 us  [exchange(): return lax.all_to_all(value, axes, 0, 0, tiled=True)]
    ppermute x3, waiting for transfers between devices: 0.01 us -> 20.9 us  [gather_ring(): lax.ppermute(value, axis, ring_pairs(axis, -shift))]
    ppermute x6, waiting for transfers between devices: 22.8 us -> 2.27 us  [sum_pieces(): received = lax.ppermute(pieces[shift], axis, ring_pairs(axis, shift))]
    all_to_all x7 -> x8, starting transfers between devices: 30.8 us -> 45 us  [exchange(): return lax.all_to_all(value, axes, 0, 0, tiled=True)]
    reduce_scatter x1, waiting for transfers between devices: 0.55 us -> 8.75 us  [backward(): lax.psum_scatter(joint.reshape(-1, model_width), 'fsdp', scatter_dimensio...]
    all_to_all x7 -> x8, waiting for transfers between devices: 43.6 us -> 39.1 us  [exchange(): return lax.all_to_all(value, axes, 0, 0, tiled=True)]
    unnamed x115 -> x125, local copies, waits for them, and re-layouts: 7.6 us -> 10.6 us
  transfers between devices with their start and end apart: 31 -> 32, of which waited for: 19 -> 16; matrix products, arithmetic and copies ran while one was open for 5% -> 6% of each run, Pallas kernels for 10% -> 10%
where the time goes in v3:
time: 422 us; the launch traced here: 415 us
  Pallas kernels  101 us (24%)
  waiting for transfers between devices  96 us (23%)
  blocking collectives  82.2 us (19%)
  starting transfers between devices  73.9 us (18%)
  local copies, waits for them, and re-layouts  25.6 us (6%)
  between operations  23.1 us (5%)
  other arithmetic  13.7 us (3%)
    all_to_all x4, blocking collectives, exchange(): return lax.all_to_all(value, axes, 0, 0, tiled=True)  82.2 us
    all_to_all x8, starting transfers between devices, exchange(): return lax.all_to_all(value, axes, 0, 0, tiled=True)  45 us
    all_to_all x8, waiting for transfers between devices, exchange(): return lax.all_to_all(value, axes, 0, 0, tiled=True)  39.1 us
    pallas_call x2, Pallas kernels, attend_back(): pl.pallas_call(attend_back_body, grid_spec=pltpu.PrefetchScalarGridSpec(n...  24.2 us
    pallas_call x2, Pallas kernels, feed_back(): pl.pallas_call(feed_back_body, in_specs=[pl.BlockSpec(memory_space=pltpu....  23.8 us
    ppermute x3, waiting for transfers between devices, gather_ring(): lax.ppermute(value, axis, ring_pairs(axis, -shift))  20.9 us
    pallas_call x2, Pallas kernels, attend(): pl.pallas_call(attend_body, grid_spec=pltpu.PrefetchScalarGridSpec(num_sc...  19.3 us
    pallas_call x2, Pallas kernels, feed_forward(): pl.pallas_call(feed_forward_body, in_specs=[pl.BlockSpec(memory_space=plt...  17.7 us
  transfers between devices with their start and end apart: 32, of which 16 were waited for; matrix products, arithmetic and copies ran while one was open for 6% of the time, Pallas kernels for 10%

profile of v3, /device:TPU:1, one launch (start us, length us, event | category | flops | bytes accessed | tf_op | source)
XLA Modules:
  0.0 415.1 jit_solution(10466496584784124080)
XLA Ops:
  11.7 5.9 %all-to-all-start = ((bf16[4,4,576]{2,1,0:T(4,128)(2,1)}), bf16[4,4,576]{2,1,0:T(4,128)(2,1)S(1)}, u32[]{:S(2)}, u32[]{:S(2)}) async-start(bf16[4,4,576]{2,1,0:T(4,128)(2,1)} %broadcast_in_dim.98), calls=%async_computation | async-start | bytes 40960 | tf_op jit(solution)/shard_map/all_to_all | solution.py:557
  29.0 7.9 %all-to-all-start.1 = ((bf16[16,64,384]{2,1,0:T(8,128)(2,1)}), bf16[16,64,384]{2,1,0:T(8,128)(2,1)S(1)}, u32[]{:S(2)}, u32[]{:S(2)}) async-start(bf16[16,64,384]{2,1,0:T(8,128)(2,1)} %bitcast.13), calls=%async_computation.1 | async-start | bytes 1572864 | tf_op jit(solution)/shard_map/all_to_all | solution.py:557
  39.7 1.8 collective-permute-start.2
  41.5 2.4 collective-permute-start.1
  45.1 9.4 %collective-permute-done.2.w3 = bf16[192,576]{1,0:T(8,128)(2,1)S(1)} collective-permute-done((bf16[192,576]{1,0:T(8,128)(2,1)S(1)}, bf16[192,576]{1,0:T(8,128)(2,1)S(1)}, u32[]{:S(2)}, u32[]{:S(2)}) %collective-permute-start.2) | collective-permute-done | bytes 221216 | tf_op jit(solution)/shard_map/ppermute | solution.py:589
  54.5 11.6 %collective-permute-done.1.w2 = bf16[192,576]{1,0:T(8,128)(2,1)S(1)} collective-permute-done((bf16[192,576]{1,0:T(8,128)(2,1)S(1)}, bf16[192,576]{1,0:T(8,128)(2,1)S(1)}, u32[]{:S(2)}, u32[]{:S(2)}) %collective-permute-start.1) | collective-permute-done | bytes 221216 | tf_op jit(solution)/shard_map/ppermute | solution.py:589
  69.1 10.3 %shard_map.178 = (bf16[1024,576]{1,0:T(8,128)(2,1)}, bf16[1024,192]{1,0:T(8,128)(2,1)}, f32[8,1024]{1,0:T(8,128)}) custom-call(s32[32]{0:T(128)S(1)} %copy-done.24, s32[3]{0:T(128)S(1)} %pad_add_fusion.ids, bf16[1024,384]{1,0:T(8,128)(2,1)S(1)} %bitcast.105, bf16[1024,384]{1,0:T(8,128)(2,1)S(1)} %collective-permute-done.3.other, ...), custom_call_target="tpu_custom_call" | custom-call | flops 805306368 | bytes 1572864 | tf_op jit(solution)/shard_map/pallas_call | solution.py:111
  79.4 7.4 %all-to-all-start.2 = ((bf16[16,64,192]{2,1,0:T(8,128)(2,1)}), bf16[16,64,192]{2,1,0:T(8,128)(2,1)S(1)}, u32[]{:S(2)}, u32[]{:S(2)}) async-start(bf16[16,64,192]{2,1,0:T(8,128)(2,1)} %bitcast.18), calls=%async_computation.2 | async-start | bytes 1048576 | tf_op jit(solution)/shard_map/all_to_all | solution.py:557
  87.0 10.9 %all-to-all-done.2.mixed = bf16[16,64,192]{2,1,0:T(8,128)(2,1)S(1)} async-done(((bf16[16,64,192]{2,1,0:T(8,128)(2,1)}), bf16[16,64,192]{2,1,0:T(8,128)(2,1)S(1)}, u32[]{:S(2)}, u32[]{:S(2)}) %all-to-all-start.2) | async-done | bytes 393248 | tf_op jit(solution)/shard_map/all_to_all | solution.py:557
  98.0 8.5 %shard_map.179 = bf16[256,768]{1,0:T(8,128)(2,1)S(1)} custom-call(bf16[16,64,192]{2,1,0:T(8,128)(2,1)S(1)} %all-to-all-done.2.mixed, bf16[256,768]{1,0:T(8,128)(2,1)S(1)} %bitcast.100, bf16[8,864,768]{2,1,0:T(8,128)(2,1)} %bitcast.108, f32[8,768]{1,0:T(8,128)S(1)} %reshape.368.vectors, f32[4,768]{1,0:T(4,128)S(1)} %reshape.369.up_bias), custom_call_target="tpu_custom_call" | custom-call | flops 2717908992 | bytes 10616832 | tf_op jit(solution)/shard_map/pallas_call | solution.py:344
  106.5 2.3 collective-permute-start.4
  109.0 6.9 %collective-permute-done.4 = bf16[256,768]{1,0:T(8,128)(2,1)S(1)} collective-permute-done((bf16[256,768]{1,0:T(8,128)(2,1)S(1)}, bf16[256,768]{1,0:T(8,128)(2,1)S(1)}, u32[]{:S(2)}, u32[]{:S(2)}) %collective-permute-start.4) | collective-permute-done | bytes 393248 | tf_op jit(solution)/shard_map/ppermute | solution.py:736
  116.9 20.8 %all_to_all.60 = bf16[16,64,384]{2,1,0:T(8,128)(2,1)S(1)} all-to-all(bf16[16,64,384]{2,1,0:T(8,128)(2,1)S(1)} %bitcast.120), channel_id=1, replica_groups=mesh['section'=2,'x'=4,'yh'=2,'core'=2,'fsdp'=4] {'x','yh','core'}, dimensions={0} | all-to-all | bytes 1572864 | tf_op jit(solution)/shard_map/all_to_all | solution.py:557
  138.5 1.7 collective-permute-done.5.other
  140.2 9.0 %shard_map.180 = (bf16[1024,576]{1,0:T(8,128)(2,1)S(1)}, bf16[1024,192]{1,0:T(8,128)(2,1)S(1)}, f32[8,1024]{1,0:T(8,128)S(1)}) custom-call(s32[32]{0:T(128)S(1)} %copy-done.24, s32[3]{0:T(128)S(1)} %pad_add_fusion.ids, bf16[1024,384]{1,0:T(8,128)(2,1)S(1)} %bitcast.102, bf16[1024,384]{1,0:T(8,128)(2,1)S(1)} %collective-permute-done.5.other, ...), custom_call_target="tpu_custom_call" | custom-call | flops 805306368 | bytes 1572864 | tf_op jit(solution)/shard_map/pallas_call | solution.py:111
  149.3 14.7 %all_to_all.61.mixed = bf16[16,64,192]{2,1,0:T(8,128)(2,1)} all-to-all(bf16[16,64,192]{2,1,0:T(8,128)(2,1)S(1)} %bitcast.106), channel_id=1, replica_groups=mesh['section'=2,'x'=4,'yh'=2,'core'=2,'fsdp'=4] {'x','yh','core'}, dimensions={0} | all-to-all | bytes 786432 | tf_op jit(solution)/shard_map/all_to_all | solution.py:557
  164.0 12.0 %shard_map.181 = (bf16[16,64,192]{2,1,0:T(8,128)(2,1)}, f32[256,768]{1,0:T(8,128)}, bf16[256,3072]{1,0:T(8,128)(2,1)}, bf16[768,256]{1,0:T(8,128)(2,1)}, bf16[768,256]{1,0:T(8,128)(2,1)}) custom-call(bf16[16,64,192]{2,1,0:T(8,128)(2,1)} %all_to_all.61.mixed, bf16[256,768]{1,0:T(8,128)(2,1)} %copy-done.2, bf16[8,864,768]{2,1,0:T(8,128)(2,1)} %bitcast.109, ...), custom_call_target="tpu_custom_call" | custom-call | flops 4227858432 | bytes 14155776 | tf_op jit(solution)/shard_map/pallas_call | solution.py:430
  175.9 16.3 %all_to_all.62 = bf16[16,64,192]{2,1,0:T(8,128)(2,1)S(1)} all-to-all(bf16[16,64,192]{2,1,0:T(8,128)(2,1)} %get-tuple-element.76), channel_id=1, replica_groups=mesh['section'=2,'x'=4,'yh'=2,'core'=2,'fsdp'=4] {'x','yh','core'}, dimensions={0} | all-to-all | bytes 786432 | tf_op jit(solution)/shard_map/all_to_all | solution.py:557
  192.2 12.1 %shard_map.182 = (bf16[1024,576]{1,0:T(8,128)(2,1)}, bf16[1024,384]{1,0:T(8,128)(2,1)S(1)}, bf16[1024,384]{1,0:T(8,128)(2,1)S(1)}) custom-call(s32[32]{0:T(128)S(1)} %copy-done.24, s32[3]{0:T(128)S(1)} %pad_add_fusion.ids, bf16[1024,576]{1,0:T(8,128)(2,1)S(1)} %get-tuple-element.75.joined, bf16[1024,192]{1,0:T(8,128)(2,1)S(1)} %bitcast.107, ...), custom_call_target="tpu_custom_call" | custom-call | flops 2013265920 | bytes 3145728 | tf_op jit(solution)/shard_map/pallas_call | solution.py:204
  205.7 1.9 collective-permute-done.6
  208.7 4.5 %all-to-all-start.6 = ((bf16[16,64,384]{2,1,0:T(8,128)(2,1)}), bf16[16,64,384]{2,1,0:T(8,128)(2,1)}, u32[]{:S(2)}, u32[]{:S(2)}) async-start(bf16[16,64,384]{2,1,0:T(8,128)(2,1)} %bitcast.124), calls=%async_computation.6 | async-start | bytes 1572864 | tf_op jit(solution)/shard_map/all_to_all | solution.py:557
  213.6 14.0 %all-to-all-done.6 = bf16[16,64,384]{2,1,0:T(8,128)(2,1)} async-done(((bf16[16,64,384]{2,1,0:T(8,128)(2,1)}), bf16[16,64,384]{2,1,0:T(8,128)(2,1)}, u32[]{:S(2)}, u32[]{:S(2)}) %all-to-all-start.6) | async-done | bytes 786464 | tf_op jit(solution)/shard_map/all_to_all | solution.py:557
  230.6 1.8 copy.57
  236.5 8.8 %collective-permute-done.7 = bf16[256,768]{1,0:T(8,128)(2,1)} collective-permute-done((bf16[256,768]{1,0:T(8,128)(2,1)S(1)}, bf16[256,768]{1,0:T(8,128)(2,1)}, u32[]{:S(2)}, u32[]{:S(2)}) %collective-permute-start.7) | collective-permute-done | bytes 393248 | tf_op jit(solution)/shard_map/ppermute | solution.py:744
  245.3 1.9 broadcast_select_fusion.grad_low
  247.3 11.8 %shard_map.183 = (bf16[16,64,192]{2,1,0:T(8,128)(2,1)}, f32[256,768]{1,0:T(8,128)}, bf16[256,3072]{1,0:T(8,128)(2,1)}, bf16[256,768]{1,0:T(8,128)(2,1)}, f32[4,768]{1,0:T(4,128)}, /*index=5*/f32[4,768]{1,0:T(4,128)}) custom-call(bf16[16,64,192]{2,1,0:T(8,128)(2,1)} %all_to_all.61.mixed, bf16[256,768]{1,0:T(8,128)(2,1)} %copy-done.2, ...), custom_call_target="tpu_custom_call" | custom-call | flops 4227858432 | bytes 14155776 | tf_op jit(solution)/shard_map/pallas_call | solution.py:430
  259.1 2.0 collective-permute-start.12
  261.6 4.1 all-to-all-start.7
  267.1 8.1 %shard_map.184 = bf16[4,896,768]{2,1,0:T(8,128)(2,1)} custom-call(s32[1]{0:T(128)} %bitcast.core_id, bf16[256,3072]{1,0:T(8,128)(2,1)S(1)} %copy-done.6, bf16[256,3072]{1,0:T(8,128)(2,1)} %collective-permute-done.8.active_other, bf16[256,768]{1,0:T(8,128)(2,1)S(1)} %copy-done.7, bf16[256,768]{1,0:T(8,128)(2,1)} %collective-permute-done.11.grad_low_other, ...), custom_call_target="tpu_custom_call" | custom-call | flops 2717908992 | bytes 5505024 | tf_op jit(solution)/shard_map/pallas_call | solution.py:284
  275.1 1.9 all-to-all-done.7
  279.6 12.1 %shard_map.185 = (bf16[1024,576]{1,0:T(8,128)(2,1)S(1)}, bf16[1024,384]{1,0:T(8,128)(2,1)S(1)}, bf16[1024,384]{1,0:T(8,128)(2,1)S(1)}) custom-call(s32[32]{0:T(128)S(1)} %copy-done.25, s32[3]{0:T(128)S(1)} %pad_add_fusion.ids, bf16[1024,576]{1,0:T(8,128)(2,1)S(1)} %copy-done.29, bf16[1024,192]{1,0:T(8,128)(2,1)} %bitcast.36.grad_mixed, ...), custom_call_target="tpu_custom_call" | custom-call | flops 2013265920 | bytes 3145728 | tf_op jit(solution)/shard_map/pallas_call | solution.py:204
  293.2 1.9 collective-permute-done.17
  296.2 4.8 %all-to-all-start.9 = ((bf16[16,64,384]{2,1,0:T(8,128)(2,1)}), bf16[16,64,384]{2,1,0:T(8,128)(2,1)S(1)}, u32[]{:S(2)}, u32[]{:S(2)}) async-start(bf16[16,64,384]{2,1,0:T(8,128)(2,1)} %bitcast.123), calls=%async_computation.10 | async-start | bytes 1572864 | tf_op jit(solution)/shard_map/all_to_all | solution.py:557
  304.0 2.0 shard_map.186
  307.5 2.4 collective-permute-start.15
  311.1 3.9 all-to-all-done.9
  318.0 3.7 all-to-all-start.10
  321.7 2.3 collective-permute-done.15
  325.3 8.8 %reduce-scatter.2.cloned.1.call-done = bf16[896,768]{1,0:T(8,128)(2,1)} async-done(((bf16[3584,768]{1,0:T(8,128)(2,1)}), bf16[896,768]{1,0:T(8,128)(2,1)}) %reduce-scatter.2.cloned.1.call-update) | async-done | bytes 1376272 | tf_op jit(solution)/shard_map/reduce_scatter | solution.py:694
  334.0 6.6 %all-to-all-start.8 = ((bf16[8,112,768]{2,1,0:T(8,128)(2,1)}), bf16[8,112,768]{2,1,0:T(8,128)(2,1)}, u32[]{:S(2)}, u32[]{:S(2)}) async-start(bf16[8,112,768]{2,1,0:T(8,128)(2,1)} %bitcast.126), calls=%async_computation.9 | async-start | bytes 2752512 | tf_op jit(solution)/shard_map/all_to_all | solution.py:557
  340.7 2.7 collective-permute-start.20
  343.4 9.2 %shard_map.187 = bf16[256,768]{1,0:T(8,128)(2,1)} custom-call(bf16[16,64,192]{2,1,0:T(8,128)(2,1)S(1)} %copy-done.5, bf16[256,768]{1,0:T(8,128)(2,1)S(1)} %copy-done.4, bf16[8,864,768]{2,1,0:T(8,128)(2,1)} %bitcast.111, f32[8,768]{1,0:T(8,128)S(1)} %copy-done.13, f32[4,768]{1,0:T(4,128)S(1)} %copy-done.15), custom_call_target="tpu_custom_call" | custom-call | flops 2717908992 | bytes 10616832 | tf_op jit(solution)/shard_map/pallas_call | solution.py:344
  352.7 8.3 %all-to-all-done.8 = bf16[8,112,768]{2,1,0:T(8,128)(2,1)} async-done(((bf16[8,112,768]{2,1,0:T(8,128)(2,1)}), bf16[8,112,768]{2,1,0:T(8,128)(2,1)}, u32[]{:S(2)}, u32[]{:S(2)}) %all-to-all-start.8) | async-done | bytes 1376288 | tf_op jit(solution)/shard_map/all_to_all | solution.py:557
  361.1 1.5 reduce_sum.120
  362.8 30.5 %all_to_all.63.own = bf16[8,176,768]{2,1,0:T(8,128)(2,1)} all-to-all(bf16[8,176,768]{2,1,0:T(8,128)(2,1)S(1)} %broadcast_in_dim.111), channel_id=1, replica_groups=mesh['section'=2,'x'=4,'yh'=2,'core'=2,'fsdp'=4] {'x','yh'}, dimensions={0} | all-to-all | bytes 4325376 | tf_op jit(solution)/shard_map/all_to_all | solution.py:557
  393.3 2.9 collective-permute-start.21
  397.4 3.1 collective-permute-done.21.other
  400.4 5.5 %shard_map.188 = (f32[192,2304]{1,0:T(8,128)}, f32[192,768]{1,0:T(8,128)}, f32[192,3072]{1,0:T(8,128)}, f32[768,768]{1,0:T(8,128)}, f32[4,768]{1,0:T(4,128)S(1)}) custom-call(s32[1]{0:T(128)} %bitcast.core_id, bf16[8,176,768]{2,1,0:T(8,128)(2,1)} %all_to_all.63.own, bf16[8,176,768]{2,1,0:T(8,128)(2,1)} %collective-permute-done.21.other), custom_call_target="tpu_custom_call" | custom-call | bytes 12582912 | tf_op jit(solution)/shard_map/pallas_call | solution.py:522
  (257 shorter events, 47.1 us)
Async XLA Ops:
  7.2 90.8 %all-gather.3.cloned.1.call-start = ((), (), s32[]{:S(2)}) async-start(), calls=%async_computation.14 | async-start | bytes 11943936 | tf_op jit(solution)/shard_map/all_gather | solution.py:640
  8.9 17.0 %copy-start.38 = (bf16[4,1,64,768]{3,2,1,0:T(8,128)(2,1)S(1)}, bf16[4,1,64,768]{3,2,1,0:T(8,128)(2,1)}, u32[]{:S(2)}) copy-start(bf16[4,1,64,768]{3,2,1,0:T(8,128)(2,1)} %param.11) | copy-start | bytes 1179652
  11.7 15.1 %all-to-all-start = ((bf16[4,4,576]{2,1,0:T(4,128)(2,1)}), bf16[4,4,576]{2,1,0:T(4,128)(2,1)S(1)}, u32[]{:S(2)}, u32[]{:S(2)}) async-start(bf16[4,4,576]{2,1,0:T(4,128)(2,1)} %broadcast_in_dim.98), calls=%async_computation | async-start | bytes 40960 | tf_op jit(solution)/shard_map/all_to_all | solution.py:557
  27.1 201.8 %copy-start.43 = (f32[2,384]{1,0:T(2,128)}, f32[2,384]{1,0:T(2,128)S(1)}, u32[]{:S(2)}) copy-start(f32[2,384]{1,0:T(2,128)S(1)} %mul.145) | copy-start | bytes 9220
  29.0 37.1 %all-to-all-start.1 = ((bf16[16,64,384]{2,1,0:T(8,128)(2,1)}), bf16[16,64,384]{2,1,0:T(8,128)(2,1)S(1)}, u32[]{:S(2)}, u32[]{:S(2)}) async-start(bf16[16,64,384]{2,1,0:T(8,128)(2,1)} %bitcast.13), calls=%async_computation.1 | async-start | bytes 1572864 | tf_op jit(solution)/shard_map/all_to_all | solution.py:557
  38.0 31.1 %copy-start.24 = (s32[32]{0:T(128)S(1)}, s32[32]{0:T(128)}, u32[]{:S(2)}) copy-start(s32[32]{0:T(128)} %table.7) | copy-start | bytes 388
  39.5 27.9 %copy-start.32 = (bf16[192,3,1,192]{0,3,1,2:T(8,128)(2,1)}, bf16[192,3,1,192]{0,3,1,2:T(8,128)(2,1)S(1)}, u32[]{:S(2)}) copy-start(bf16[192,3,1,192]{0,3,1,2:T(8,128)(2,1)S(1)} %copy.65) | copy-start | bytes 663556
  39.7 152.5 %copy-start.10 = (bf16[192,576]{1,0:T(8,128)(2,1)}, bf16[192,576]{1,0:T(8,128)(2,1)S(1)}, u32[]{:S(2)}) copy-start(bf16[192,576]{1,0:T(8,128)(2,1)S(1)} %copy.49.w0) | copy-start | bytes 663556
  39.7 14.8 %collective-permute-start.2 = (bf16[192,576]{1,0:T(8,128)(2,1)S(1)}, bf16[192,576]{1,0:T(8,128)(2,1)S(1)}, u32[]{:S(2)}, u32[]{:S(2)}) collective-permute-start(bf16[192,576]{1,0:T(8,128)(2,1)S(1)} %copy.49.w0), channel_id=1, source_target_pairs={{0,1},{1,2},{2,3},{3,0},{4,5},{5,6},{6,7},{7,4},{8,9},{9,10},{10,1... | collective-permute-start | bytes 663560 | tf_op jit(solution)/shard_map/ppermute | solution.py:589
  41.5 24.5 %collective-permute-start.1 = (bf16[192,576]{1,0:T(8,128)(2,1)S(1)}, bf16[192,576]{1,0:T(8,128)(2,1)S(1)}, u32[]{:S(2)}, u32[]{:S(2)}) collective-permute-start(bf16[192,576]{1,0:T(8,128)(2,1)S(1)} %copy.49.w0), channel_id=1, source_target_pairs={{0,2},{1,3},{2,0},{3,1},{4,6},{5,7},{6,4},{7,5},{8,10},{9,11},{10,... | collective-permute-start | bytes 663560 | tf_op jit(solution)/shard_map/ppermute | solution.py:589
  43.9 22.1 %collective-permute-start = (bf16[192,576]{1,0:T(8,128)(2,1)S(1)}, bf16[192,576]{1,0:T(8,128)(2,1)S(1)}, u32[]{:S(2)}, u32[]{:S(2)}) collective-permute-start(bf16[192,576]{1,0:T(8,128)(2,1)S(1)} %copy.49.w0), channel_id=1, source_target_pairs={{0,3},{1,0},{2,1},{3,2},{4,7},{5,4},{6,5},{7,6},{8,11},{9,8},{10,9... | collective-permute-start | bytes 663560 | tf_op jit(solution)/shard_map/ppermute | solution.py:589
  54.5 137.7 %copy-start.18 = (bf16[192,576]{1,0:T(8,128)(2,1)}, bf16[192,576]{1,0:T(8,128)(2,1)S(1)}, u32[]{:S(2)}) copy-start(bf16[192,576]{1,0:T(8,128)(2,1)S(1)} %collective-permute-done.2.w3) | copy-start | bytes 663556
  66.0 126.2 %copy-start.20 = (bf16[192,576]{1,0:T(8,128)(2,1)}, bf16[192,576]{1,0:T(8,128)(2,1)S(1)}, u32[]{:S(2)}) copy-start(bf16[192,576]{1,0:T(8,128)(2,1)S(1)} %collective-permute-done.1.w2) | copy-start | bytes 663556
  66.0 126.2 %copy-start.22 = (bf16[192,576]{1,0:T(8,128)(2,1)}, bf16[192,576]{1,0:T(8,128)(2,1)S(1)}, u32[]{:S(2)}) copy-start(bf16[192,576]{1,0:T(8,128)(2,1)S(1)} %collective-permute-done.w1) | copy-start | bytes 663556
  66.0 3.1 collective-permute-start.3
  79.4 18.5 %all-to-all-start.2 = ((bf16[16,64,192]{2,1,0:T(8,128)(2,1)}), bf16[16,64,192]{2,1,0:T(8,128)(2,1)S(1)}, u32[]{:S(2)}, u32[]{:S(2)}) async-start(bf16[16,64,192]{2,1,0:T(8,128)(2,1)} %bitcast.18), calls=%async_computation.2 | async-start | bytes 1048576 | tf_op jit(solution)/shard_map/all_to_all | solution.py:557
  86.9 19.5 %copy-start.14 = (f32[4,768]{1,0:T(4,128)}, f32[4,768]{1,0:T(4,128)S(1)}, u32[]{:S(2)}) copy-start(f32[4,768]{1,0:T(4,128)S(1)} %reshape.369.up_bias) | copy-start | bytes 36868
  87.0 19.4 %copy-start.12 = (f32[8,768]{1,0:T(8,128)}, f32[8,768]{1,0:T(8,128)S(1)}, u32[]{:S(2)}) copy-start(f32[8,768]{1,0:T(8,128)S(1)} %reshape.368.vectors) | copy-start | bytes 73732
  106.5 9.4 %collective-permute-start.4 = (bf16[256,768]{1,0:T(8,128)(2,1)S(1)}, bf16[256,768]{1,0:T(8,128)(2,1)S(1)}, u32[]{:S(2)}, u32[]{:S(2)}) collective-permute-start(bf16[256,768]{1,0:T(8,128)(2,1)S(1)} %shard_map.179), channel_id=1, source_target_pairs={{0,64},{1,65},{2,66},{3,67},{4,68},{5,69},{6,70},{7,71},{8,72},{9,... | collective-permute-start | bytes 1179656 | tf_op jit(solution)/shard_map/ppermute | solution.py:736
  116.1 116.7 %copy-start.41 = (f32[256]{0:T(256)}, f32[256]{0:T(256)S(1)}, u32[]{:S(2)}) copy-start(f32[256]{0:T(256)S(1)} %broadcast_multiply_fusion.5) | copy-start | bytes 3076
  116.4 116.4 %copy-start.45 = (f32[256]{0:T(256)}, f32[256]{0:T(256)S(1)}, u32[]{:S(2)}) copy-start(f32[256]{0:T(256)S(1)} %add_rsqrt_fusion.1) | copy-start | bytes 3076
  116.9 21.4 %copy-start.33 = (bf16[192,3,1,192]{0,3,1,2:T(8,128)(2,1)S(1)}, bf16[192,3,1,192]{0,3,1,2:T(8,128)(2,1)}, u32[]{:S(2)}) copy-start(bf16[192,3,1,192]{0,3,1,2:T(8,128)(2,1)} %copy-done.32) | copy-start | bytes 663556
  137.7 2.5 collective-permute-start.5
  149.3 43.0 %copy-start.28 = (bf16[1024,576]{1,0:T(8,128)(2,1)}, bf16[1024,576]{1,0:T(8,128)(2,1)S(1)}, u32[]{:S(2)}) copy-start(bf16[1024,576]{1,0:T(8,128)(2,1)S(1)} %get-tuple-element.75.joined) | copy-start | bytes 3538948
  149.3 43.0 %copy-start.30 = (f32[8,1024]{1,0:T(8,128)}, f32[8,1024]{1,0:T(8,128)S(1)}, u32[]{:S(2)}) copy-start(f32[8,1024]{1,0:T(8,128)S(1)} %get-tuple-element.77.log_total) | copy-start | bytes 98308
  204.4 3.3 collective-permute-start.6
  208.7 18.9 %all-to-all-start.6 = ((bf16[16,64,384]{2,1,0:T(8,128)(2,1)}), bf16[16,64,384]{2,1,0:T(8,128)(2,1)}, u32[]{:S(2)}, u32[]{:S(2)}) async-start(bf16[16,64,384]{2,1,0:T(8,128)(2,1)} %bitcast.124), calls=%async_computation.6 | async-start | bytes 1572864 | tf_op jit(solution)/shard_map/all_to_all | solution.py:557
  213.3 34.0 %collective-permute-start.8 = (bf16[256,3072]{1,0:T(8,128)(2,1)S(1)}, bf16[256,3072]{1,0:T(8,128)(2,1)}, u32[]{:S(2)}, u32[]{:S(2)}) collective-permute-start(bf16[256,3072]{1,0:T(8,128)(2,1)S(1)} %copy-done.6), channel_id=1, source_target_pairs={{0,4},{4,0},{1,5},{5,1},{2,6},{6,2},{3,7},{7,3},{8,12},{12,8},{9,1... | collective-permute-start | bytes 4718600 | tf_op jit(solution)/shard_map/ppermute | solution.py:561
  233.8 11.5 %collective-permute-start.7 = (bf16[256,768]{1,0:T(8,128)(2,1)S(1)}, bf16[256,768]{1,0:T(8,128)(2,1)}, u32[]{:S(2)}, u32[]{:S(2)}) collective-permute-start(bf16[256,768]{1,0:T(8,128)(2,1)S(1)} %fusion.14), channel_id=1, source_target_pairs={{64,0},{65,1},{66,2},{67,3},{68,4},{69,5},{70,6},{71,7},{72,8},{73... | collective-permute-start | bytes 1179656 | tf_op jit(solution)/shard_map/ppermute | solution.py:744
  235.1 12.1 %collective-permute-start.9 = (bf16[768,256]{1,0:T(8,128)(2,1)S(1)}, bf16[768,256]{1,0:T(8,128)(2,1)S(1)}, u32[]{:S(2)}, u32[]{:S(2)}) collective-permute-start(bf16[768,256]{1,0:T(8,128)(2,1)S(1)} %copy-done.8), channel_id=1, source_target_pairs={{0,4},{4,0},{1,5},{5,1},{2,6},{6,2},{3,7},{7,3},{8,12},{12,8},{9,1... | collective-permute-start | bytes 1179656 | tf_op jit(solution)/shard_map/ppermute | solution.py:561
  236.5 10.8 %collective-permute-start.10 = (bf16[768,256]{1,0:T(8,128)(2,1)}, bf16[768,256]{1,0:T(8,128)(2,1)}, u32[]{:S(2)}, u32[]{:S(2)}) collective-permute-start(bf16[768,256]{1,0:T(8,128)(2,1)} %get-tuple-element.90.mixed), channel_id=1, source_target_pairs={{0,4},{4,0},{1,5},{5,1},{2,6},{6,2},{3,7},{7,3},{8,12},{12,8},{9,1... | collective-permute-start | bytes 1179656 | tf_op jit(solution)/shard_map/ppermute | solution.py:561
  259.1 7.0 %collective-permute-start.12 = (bf16[256,3072]{1,0:T(8,128)(2,1)}, bf16[256,3072]{1,0:T(8,128)(2,1)}, u32[]{:S(2)}, u32[]{:S(2)}) collective-permute-start(bf16[256,3072]{1,0:T(8,128)(2,1)} %get-tuple-element.89.grad_hidden), channel_id=1, source_target_pairs={{0,4},{4,0},{1,5},{5,1},{2,6},{6,2},{3,7},{7,3},{8,12},{12,8},{9,1... | collective-permute-start | bytes 4718600 | tf_op jit(solution)/shard_map/ppermute | solution.py:561
  261.1 4.9 %collective-permute-start.13 = (bf16[256,768]{1,0:T(8,128)(2,1)}, bf16[256,768]{1,0:T(8,128)(2,1)}, u32[]{:S(2)}, u32[]{:S(2)}) collective-permute-start(bf16[256,768]{1,0:T(8,128)(2,1)} %get-tuple-element.92.grad_attn), channel_id=1, source_target_pairs={{0,4},{4,0},{1,5},{5,1},{2,6},{6,2},{3,7},{7,3},{8,12},{12,8},{9,1... | collective-permute-start | bytes 1179656 | tf_op jit(solution)/shard_map/ppermute | solution.py:561
  261.2 4.9 %collective-permute-start.11 = (bf16[256,768]{1,0:T(8,128)(2,1)S(1)}, bf16[256,768]{1,0:T(8,128)(2,1)}, u32[]{:S(2)}, u32[]{:S(2)}) collective-permute-start(bf16[256,768]{1,0:T(8,128)(2,1)S(1)} %copy-done.7), channel_id=1, source_target_pairs={{0,4},{4,0},{1,5},{5,1},{2,6},{6,2},{3,7},{7,3},{8,12},{12,8},{9,1... | collective-permute-start | bytes 1179656 | tf_op jit(solution)/shard_map/ppermute | solution.py:561
  261.6 15.4 %all-to-all-start.7 = ((bf16[16,64,192]{2,1,0:T(8,128)(2,1)}), bf16[16,64,192]{2,1,0:T(8,128)(2,1)}, u32[]{:S(2)}, u32[]{:S(2)}) async-start(bf16[16,64,192]{2,1,0:T(8,128)(2,1)} %get-tuple-element.84), calls=%async_computation.7 | async-start | bytes 1048576 | tf_op jit(solution)/shard_map/all_to_all | solution.py:557
  265.8 68.2 %reduce-scatter.2.cloned.1.call-start = ((), (), s32[]{:S(2)}) async-start(), calls=%async_computation.13 | async-start | bytes 6881280 | tf_op jit(solution)/shard_map/reduce_scatter | solution.py:694
  291.7 3.3 collective-permute-start.17
  296.2 18.9 %all-to-all-start.9 = ((bf16[16,64,384]{2,1,0:T(8,128)(2,1)}), bf16[16,64,384]{2,1,0:T(8,128)(2,1)S(1)}, u32[]{:S(2)}, u32[]{:S(2)}) async-start(bf16[16,64,384]{2,1,0:T(8,128)(2,1)} %bitcast.123), calls=%async_computation.10 | async-start | bytes 1572864 | tf_op jit(solution)/shard_map/all_to_all | solution.py:557
  306.0 15.7 %collective-permute-start.14 = (bf16[192,576]{1,0:T(8,128)(2,1)S(1)}, bf16[192,576]{1,0:T(8,128)(2,1)}, u32[]{:S(2)}, u32[]{:S(2)}) collective-permute-start(bf16[192,576]{1,0:T(8,128)(2,1)S(1)} %get-tuple-element.97), channel_id=1, source_target_pairs={{0,16},{16,32},{32,48},{48,0},{1,17},{17,33},{33,49},{49,1},{2,18}... | collective-permute-start | bytes 663560 | tf_op jit(solution)/shard_map/ppermute | solution.py:597
  307.5 16.5 %collective-permute-start.15 = (bf16[192,576]{1,0:T(8,128)(2,1)S(1)}, bf16[192,576]{1,0:T(8,128)(2,1)}, u32[]{:S(2)}, u32[]{:S(2)}) collective-permute-start(bf16[192,576]{1,0:T(8,128)(2,1)S(1)} %get-tuple-element.98), channel_id=1, source_target_pairs={{0,32},{16,48},{32,0},{48,16},{1,33},{17,49},{33,1},{49,17},{2,34}... | collective-permute-start | bytes 663560 | tf_op jit(solution)/shard_map/ppermute | solution.py:597
  309.9 14.1 %collective-permute-start.16 = (bf16[192,576]{1,0:T(8,128)(2,1)S(1)}, bf16[192,576]{1,0:T(8,128)(2,1)}, u32[]{:S(2)}, u32[]{:S(2)}) collective-permute-start(bf16[192,576]{1,0:T(8,128)(2,1)S(1)} %get-tuple-element.99), channel_id=1, source_target_pairs={{0,48},{16,0},{32,16},{48,32},{1,49},{17,1},{33,17},{49,33},{2,50}... | collective-permute-start | bytes 663560 | tf_op jit(solution)/shard_map/ppermute | solution.py:597
  318.0 16.0 %all-to-all-start.10 = ((bf16[4,4,576]{2,1,0:T(4,128)(2,1)}), bf16[4,4,576]{2,1,0:T(4,128)(2,1)S(1)}, u32[]{:S(2)}, u32[]{:S(2)}) async-start(bf16[4,4,576]{2,1,0:T(4,128)(2,1)} %convert_element_type.157), calls=%async_computation.11 | async-start | bytes 40960 | tf_op jit(solution)/shard_map/all_to_all | solution.py:557
  334.0 27.0 %all-to-all-start.8 = ((bf16[8,112,768]{2,1,0:T(8,128)(2,1)}), bf16[8,112,768]{2,1,0:T(8,128)(2,1)}, u32[]{:S(2)}, u32[]{:S(2)}) async-start(bf16[8,112,768]{2,1,0:T(8,128)(2,1)} %bitcast.126), calls=%async_computation.9 | async-start | bytes 2752512 | tf_op jit(solution)/shard_map/all_to_all | solution.py:557
  340.6 12.0 %collective-permute-start.18 = (bf16[48,576]{1,0:T(8,128)(2,1)S(1)}, bf16[48,576]{1,0:T(8,128)(2,1)S(1)}, u32[]{:S(2)}, u32[]{:S(2)}) collective-permute-start(bf16[48,576]{1,0:T(8,128)(2,1)S(1)} %get-tuple-element.163), channel_id=1, source_target_pairs={{0,1},{1,2},{2,3},{3,0},{4,5},{5,6},{6,7},{7,4},{8,9},{9,10},{10,1... | collective-permute-start | bytes 165896 | tf_op jit(solution)/shard_map/ppermute | solution.py:597
  340.7 11.9 %collective-permute-start.20 = (bf16[48,576]{1,0:T(8,128)(2,1)S(1)}, bf16[48,576]{1,0:T(8,128)(2,1)S(1)}, u32[]{:S(2)}, u32[]{:S(2)}) collective-permute-start(bf16[48,576]{1,0:T(8,128)(2,1)S(1)} %get-tuple-element.164), channel_id=1, source_target_pairs={{0,3},{1,0},{2,1},{3,2},{4,7},{5,4},{6,5},{7,6},{8,11},{9,8},{10,9... | collective-permute-start | bytes 165896 | tf_op jit(solution)/shard_map/ppermute | solution.py:597
  343.4 9.3 %collective-permute-start.19 = (bf16[48,576]{1,0:T(8,128)(2,1)S(1)}, bf16[48,576]{1,0:T(8,128)(2,1)S(1)}, u32[]{:S(2)}, u32[]{:S(2)}) collective-permute-start(bf16[48,576]{1,0:T(8,128)(2,1)S(1)} %get-tuple-element.165), channel_id=1, source_target_pairs={{0,2},{1,3},{2,0},{3,1},{4,6},{5,7},{6,4},{7,5},{8,10},{9,11},{10,... | collective-permute-start | bytes 165896 | tf_op jit(solution)/shard_map/ppermute | solution.py:597
  362.8 33.5 %copy-start.36 = (f32[256,768]{1,0:T(8,128)S(1)}, f32[256,768]{1,0:T(8,128)}, u32[]{:S(2)}) copy-start(f32[256,768]{1,0:T(8,128)} %get-tuple-element.102) | copy-start | bytes 2359300
  393.3 7.1 %collective-permute-start.21 = (bf16[8,176,768]{2,1,0:T(8,128)(2,1)}, bf16[8,176,768]{2,1,0:T(8,128)(2,1)}, u32[]{:S(2)}, u32[]{:S(2)}) collective-permute-start(bf16[8,176,768]{2,1,0:T(8,128)(2,1)} %all_to_all.63.own), channel_id=1, source_target_pairs={{0,4},{4,0},{1,5},{5,1},{2,6},{6,2},{3,7},{7,3},{8,12},{12,8},{9,1... | collective-permute-start | bytes 6488072 | tf_op jit(solution)/shard_map/ppermute | solution.py:561
  (40 other events, 150.1 us)
Sparse Core Ops, SparseCore 0:
  11.0 73.4 all-gather.2
  277.2 56.7 reduce-scatter.1

commit v4 on v3

--- a/solution.py
+++ b/solution.py
@@ -318,33 +318,74 @@
     return middle
 
 
-def feed_forward_body(mixed, entering, packed, vectors, up_bias, result):
+def start_copies(stored, packed, landed, panels):
+    members, width = packed.shape[0], packed.shape[2]
+    up_rows = width // members
+    down_rows = panels * up_rows
+    per_panel = members // panels
+
+    def copy(index, rows, sources):
+        here = (slice(None) if sources is None else sources, rows)
+        return pltpu.make_async_copy(stored.at[here], packed.at[here], landed.at[index])
+
+    out = copy(0, pl.ds(2 * down_rows, up_rows), None)
+    ups, downs = [], []
+    for panel in range(panels):
+        ups.append(copy(1 + panel, pl.ds(down_rows + panel * up_rows, up_rows), None))
+        downs.append(
+            copy(1 + panels + panel, pl.ds(0, down_rows), pl.ds(panel * per_panel, per_panel))
+        )
+    return out, ups, downs
+
+
+def feed_forward_body(mixed, entering, stored, vectors, up_bias, result, packed, landed):
     members, width = packed.shape[0], packed.shape[2]
     panels = up_bias.shape[0]
     up_rows = width // members
     down_rows = panels * up_rows
+    out, ups, downs = start_copies(stored, packed, landed, panels)
+    for copy in [out] + ups + downs:
+        copy.start()
+    out.wait()
     middle = attend_out(mixed, entering, packed, vectors, weight_panel(packed, 2 * down_rows))
     normed, _, _ = normalize(middle, vectors[1:2, :], vectors[6:7, :])
     normed = normed.astype(jnp.bfloat16)
     parts = []
     for panel in range(panels):
+        ups[panel].wait()
         hidden = dot(normed, weight_panel(packed, down_rows + panel * up_rows), 1, 0)
         hidden = hidden + up_bias[panel : panel + 1, :]
         parts.append(jax.nn.gelu(hidden).astype(jnp.bfloat16))
     active = jnp.concatenate(parts, 1)
     total = middle + vectors[7:8, :]
     for member in range(members):
+        if member % (members // panels) == 0:
+            downs[member // (members // panels)].wait()
         columns = slice(member * down_rows, (member + 1) * down_rows)
         total += dot(active[:, columns], packed[member, :down_rows, :], 1, 0)
     result[...] = total.astype(jnp.bfloat16)
+
+
+def feed_specs(count):
+    specs = [pl.BlockSpec(memory_space=pltpu.VMEM) for _ in range(count)]
+    specs[2] = pl.BlockSpec(memory_space=pl.ANY)
+    return specs
+
+
+def feed_scratch(packed, up_bias):
+    return [
+        pltpu.VMEM(packed.shape, packed.dtype),
+        pltpu.SemaphoreType.DMA((1 + 2 * up_bias.shape[0],)),
+    ]
 
 
 def feed_forward(mixed, entering, packed, vectors, up_bias):
     rows, width = entering.shape
     return pl.pallas_call(
         feed_forward_body,
-        in_specs=[pl.BlockSpec(memory_space=pltpu.VMEM)] * 5,
+        in_specs=feed_specs(5),
         out_specs=pl.BlockSpec(memory_space=pltpu.VMEM),
+        scratch_shapes=feed_scratch(packed, up_bias),
         out_shape=jax.ShapeDtypeStruct((rows, width), jnp.bfloat16),
         compiler_params=pltpu.CompilerParams(vmem_limit_bytes=48 << 20),
         cost_estimate=pl.CostEstimate(
@@ -355,7 +396,9 @@
     )(mixed, entering, packed, vectors, up_bias)
 
 
-def feed_back_body(mixed, entering, packed, vectors, up_bias, grad_low, *outs):
+def feed_back_body(mixed, entering, stored, vectors, up_bias, grad_low, *outs):
+    packed, landed = outs[-2:]
+    outs = outs[:-2]
     last = len(outs) == 6
     grad_mixed, grad_middle = outs[:2]
     members, width = packed.shape[0], packed.shape[2]
@@ -364,6 +407,12 @@
     down_rows = panels * up_rows
     micro_count = mixed.shape[0] // GROUPS
     local_rows = mixed.shape[1]
+    out, ups, downs = start_copies(stored, packed, landed, panels)
+    out.start()
+    for panel in range(panels):
+        ups[panel].start()
+        downs[panel].start()
+    out.wait()
     w_out = weight_panel(packed, 2 * down_rows)
     middle = attend_out(mixed, entering, packed, vectors, w_out)
     normed, unit, spread_two = normalize(middle, vectors[1:2, :], vectors[6:7, :])
@@ -373,6 +422,7 @@
     per_panel = members // panels
     for panel in range(panels):
         columns = slice(panel * width, (panel + 1) * width)
+        ups[panel].wait()
         w_up = weight_panel(packed, down_rows + panel * up_rows)
         hidden = dot(normed, w_up, 1, 0) + up_bias[panel : panel + 1, :]
         square = hidden * hidden
@@ -380,6 +430,7 @@
         slope = 0.5 * (1.0 + bend) + 0.5 * hidden * (1.0 - bend * bend) * (
             GELU_SCALE * (1.0 + 3.0 * GELU_CUBE * square)
         )
+        downs[panel].wait()
         w_down = jnp.concatenate(
             [packed[i, :down_rows, :] for i in range(panel * per_panel, (panel + 1) * per_panel)],
             0,
@@ -429,7 +480,8 @@
         shapes += [((width, rows), jnp.bfloat16)] * 2
     return pl.pallas_call(
         feed_back_body,
-        in_specs=[pl.BlockSpec(memory_space=pltpu.VMEM)] * 6,
+        in_specs=feed_specs(6),
+        scratch_shapes=feed_scratch(packed, up_bias),
         out_specs=[pl.BlockSpec(memory_space=pltpu.VMEM)] * len(shapes),
         out_shape=[jax.ShapeDtypeStruct(*shape) for shape in shapes],
         compiler_params=pltpu.CompilerParams(vmem_limit_bytes=56 << 20),
@@ -636,6 +688,9 @@
     ).reshape(shard, 3 * WIDTH)
     small_all = spread(small, "fsdp").reshape(fsdp_count, -1, shard).astype(jnp.float32)
     w_group = gather_ring(own_columns, "fsdp")
+    small_all, w_group[1], w_group[3] = lax.optimization_barrier(
+        (small_all, w_group[1], w_group[3])
+    )
     packed = pack_weights(attn_out, mlp_in, mlp_out)
     packed = lax.all_gather(packed, ("fsdp", "core"), axis=0)
     model_width = attn_out.shape[2]

time: 422 us -> 413 us (0.979)
  waiting for transfers between devices: 96 us -> 87.6 us
    ppermute x3, waiting for transfers between devices: 20.9 us -> 11.6 us  [gather_ring(): lax.ppermute(value, axis, ring_pairs(axis, -shift))]
  transfers between devices with their start and end apart: 32 -> 32, of which waited for: 16 -> 15; matrix products, arithmetic and copies ran while one was open for 6% -> 6% of each run, Pallas kernels for 10% -> 10%
where the time goes in v4:
time: 413 us; the launch traced here: 407 us
  Pallas kernels  100 us (24%)
  waiting for transfers between devices  87.6 us (21%)
  blocking collectives  82 us (20%)
  starting transfers between devices  74.5 us (18%)
  local copies, waits for them, and re-layouts  25.6 us (6%)
  between operations  23.1 us (6%)
  other arithmetic  13.7 us (3%)
    all_to_all x4, blocking collectives, exchange(): return lax.all_to_all(value, axes, 0, 0, tiled=True)  82 us
    all_to_all x8, starting transfers between devices, exchange(): return lax.all_to_all(value, axes, 0, 0, tiled=True)  43.3 us
    all_to_all x8, waiting for transfers between devices, exchange(): return lax.all_to_all(value, axes, 0, 0, tiled=True)  40 us
    pallas_call x2, Pallas kernels, feed_back(): pl.pallas_call(feed_back_body, in_specs=feed_specs(6), scratch_shapes=fee...  25.5 us
    pallas_call x2, Pallas kernels, attend_back(): pl.pallas_call(attend_back_body, grid_spec=pltpu.PrefetchScalarGridSpec(n...  24.2 us
    pallas_call x2, Pallas kernels, attend(): pl.pallas_call(attend_body, grid_spec=pltpu.PrefetchScalarGridSpec(num_sc...  19.3 us
    pallas_call x2, Pallas kernels, feed_forward(): pl.pallas_call(feed_forward_body, in_specs=feed_specs(5), out_specs=pl.Bl...  15.5 us
    ppermute x3, waiting for transfers between devices, gather_ring(): lax.ppermute(value, axis, ring_pairs(axis, -shift))  11.6 us
  transfers between devices with their start and end apart: 32, of which 15 were waited for; matrix products, arithmetic and copies ran while one was open for 6% of the time, Pallas kernels for 10%

profile of v4, /device:TPU:1, one launch (start us, length us, event | category | flops | bytes accessed | tf_op | source)
XLA Modules:
  0.0 406.8 jit_solution(610231578052552660)
XLA Ops:
  13.7 2.5 collective-permute-start.1
  16.3 2.2 collective-permute-start
  19.3 3.3 all-to-all-start
  34.0 8.0 %all-to-all-start.1 = ((bf16[16,64,384]{2,1,0:T(8,128)(2,1)}), bf16[16,64,384]{2,1,0:T(8,128)(2,1)S(1)}, u32[]{:S(2)}, u32[]{:S(2)}) async-start(bf16[16,64,384]{2,1,0:T(8,128)(2,1)} %bitcast.14), calls=%async_computation.1 | async-start | bytes 1572864 | tf_op jit(solution)/shard_map/all_to_all | solution.py:609
  42.1 3.2 collective-permute-start.2
  45.3 11.6 %collective-permute-done.2.w2 = bf16[192,576]{1,0:T(8,128)(2,1)S(1)} collective-permute-done((bf16[192,576]{1,0:T(8,128)(2,1)S(1)}, bf16[192,576]{1,0:T(8,128)(2,1)S(1)}, u32[]{:S(2)}, u32[]{:S(2)}) %collective-permute-start.2) | collective-permute-done | bytes 221216 | tf_op jit(solution)/shard_map/ppermute | solution.py:641
  59.8 10.3 %shard_map.178 = (bf16[1024,576]{1,0:T(8,128)(2,1)}, bf16[1024,192]{1,0:T(8,128)(2,1)}, f32[8,1024]{1,0:T(8,128)}) custom-call(s32[32]{0:T(128)S(1)} %copy-done.24, s32[3]{0:T(128)S(1)} %pad_add_fusion.ids, bf16[1024,384]{1,0:T(8,128)(2,1)S(1)} %bitcast.105, bf16[1024,384]{1,0:T(8,128)(2,1)S(1)} %collective-permute-done.3.other, ...), custom_call_target="tpu_custom_call" | custom-call | flops 805306368 | bytes 1572864 | tf_op jit(solution)/shard_map/pallas_call | solution.py:111
  70.0 7.4 %all-to-all-start.2 = ((bf16[16,64,192]{2,1,0:T(8,128)(2,1)}), bf16[16,64,192]{2,1,0:T(8,128)(2,1)S(1)}, u32[]{:S(2)}, u32[]{:S(2)}) async-start(bf16[16,64,192]{2,1,0:T(8,128)(2,1)} %bitcast.18), calls=%async_computation.2 | async-start | bytes 1048576 | tf_op jit(solution)/shard_map/all_to_all | solution.py:609
  77.6 10.9 %all-to-all-done.2.mixed = bf16[16,64,192]{2,1,0:T(8,128)(2,1)S(1)} async-done(((bf16[16,64,192]{2,1,0:T(8,128)(2,1)}), bf16[16,64,192]{2,1,0:T(8,128)(2,1)S(1)}, u32[]{:S(2)}, u32[]{:S(2)}) %all-to-all-start.2) | async-done | bytes 393248 | tf_op jit(solution)/shard_map/all_to_all | solution.py:609
  88.6 7.4 %shard_map.179 = bf16[256,768]{1,0:T(8,128)(2,1)S(1)} custom-call(bf16[16,64,192]{2,1,0:T(8,128)(2,1)S(1)} %all-to-all-done.2.mixed, bf16[256,768]{1,0:T(8,128)(2,1)S(1)} %bitcast.100, bf16[8,864,768]{2,1,0:T(8,128)(2,1)} %bitcast.108, f32[8,768]{1,0:T(8,128)S(1)} %reshape.368.vectors, f32[4,768]{1,0:T(4,128)S(1)} %reshape.369.up_bias), custom_call_target="tpu_custom_call" | custom-call | flops 2717908992 | bytes 10616832 | tf_op jit(solution)/shard_map/pallas_call | solution.py:384
  96.0 2.3 collective-permute-start.4
  98.4 6.9 %collective-permute-done.4 = bf16[256,768]{1,0:T(8,128)(2,1)S(1)} collective-permute-done((bf16[256,768]{1,0:T(8,128)(2,1)S(1)}, bf16[256,768]{1,0:T(8,128)(2,1)S(1)}, u32[]{:S(2)}, u32[]{:S(2)}) %collective-permute-start.4) | collective-permute-done | bytes 393248 | tf_op jit(solution)/shard_map/ppermute | solution.py:791
  106.4 20.8 %all_to_all.60 = bf16[16,64,384]{2,1,0:T(8,128)(2,1)S(1)} all-to-all(bf16[16,64,384]{2,1,0:T(8,128)(2,1)S(1)} %bitcast.120), channel_id=1, replica_groups=mesh['section'=2,'x'=4,'yh'=2,'core'=2,'fsdp'=4] {'x','yh','core'}, dimensions={0} | all-to-all | bytes 1572864 | tf_op jit(solution)/shard_map/all_to_all | solution.py:609
  127.7 1.7 collective-permute-done.5.other
  129.5 9.0 %shard_map.180 = (bf16[1024,576]{1,0:T(8,128)(2,1)S(1)}, bf16[1024,192]{1,0:T(8,128)(2,1)S(1)}, f32[8,1024]{1,0:T(8,128)S(1)}) custom-call(s32[32]{0:T(128)S(1)} %copy-done.24, s32[3]{0:T(128)S(1)} %pad_add_fusion.ids, bf16[1024,384]{1,0:T(8,128)(2,1)S(1)} %bitcast.102, bf16[1024,384]{1,0:T(8,128)(2,1)S(1)} %collective-permute-done.5.other, ...), custom_call_target="tpu_custom_call" | custom-call | flops 805306368 | bytes 1572864 | tf_op jit(solution)/shard_map/pallas_call | solution.py:111
  138.6 14.7 %all_to_all.61.mixed = bf16[16,64,192]{2,1,0:T(8,128)(2,1)} all-to-all(bf16[16,64,192]{2,1,0:T(8,128)(2,1)S(1)} %bitcast.106), channel_id=1, replica_groups=mesh['section'=2,'x'=4,'yh'=2,'core'=2,'fsdp'=4] {'x','yh','core'}, dimensions={0} | all-to-all | bytes 786432 | tf_op jit(solution)/shard_map/all_to_all | solution.py:609
  153.2 13.0 %shard_map.181 = (bf16[16,64,192]{2,1,0:T(8,128)(2,1)}, f32[256,768]{1,0:T(8,128)}, bf16[256,3072]{1,0:T(8,128)(2,1)}, bf16[768,256]{1,0:T(8,128)(2,1)}, bf16[768,256]{1,0:T(8,128)(2,1)}) custom-call(bf16[16,64,192]{2,1,0:T(8,128)(2,1)} %all_to_all.61.mixed, bf16[256,768]{1,0:T(8,128)(2,1)} %copy-done.2, bf16[8,864,768]{2,1,0:T(8,128)(2,1)} %bitcast.109, ...), custom_call_target="tpu_custom_call" | custom-call | flops 4227858432 | bytes 14155776 | tf_op jit(solution)/shard_map/pallas_call | solution.py:481
  166.2 16.0 %all_to_all.62 = bf16[16,64,192]{2,1,0:T(8,128)(2,1)S(1)} all-to-all(bf16[16,64,192]{2,1,0:T(8,128)(2,1)} %get-tuple-element.82), channel_id=1, replica_groups=mesh['section'=2,'x'=4,'yh'=2,'core'=2,'fsdp'=4] {'x','yh','core'}, dimensions={0} | all-to-all | bytes 786432 | tf_op jit(solution)/shard_map/all_to_all | solution.py:609
  182.3 12.1 %shard_map.182 = (bf16[1024,576]{1,0:T(8,128)(2,1)}, bf16[1024,384]{1,0:T(8,128)(2,1)S(1)}, bf16[1024,384]{1,0:T(8,128)(2,1)S(1)}) custom-call(s32[32]{0:T(128)S(1)} %copy-done.24, s32[3]{0:T(128)S(1)} %pad_add_fusion.ids, bf16[1024,576]{1,0:T(8,128)(2,1)S(1)} %get-tuple-element.81.joined, bf16[1024,192]{1,0:T(8,128)(2,1)S(1)} %bitcast.107, ...), custom_call_target="tpu_custom_call" | custom-call | flops 2013265920 | bytes 3145728 | tf_op jit(solution)/shard_map/pallas_call | solution.py:204
  195.8 1.9 collective-permute-done.6
  198.8 4.5 %all-to-all-start.6 = ((bf16[16,64,384]{2,1,0:T(8,128)(2,1)}), bf16[16,64,384]{2,1,0:T(8,128)(2,1)}, u32[]{:S(2)}, u32[]{:S(2)}) async-start(bf16[16,64,384]{2,1,0:T(8,128)(2,1)} %bitcast.124), calls=%async_computation.6 | async-start | bytes 1572864 | tf_op jit(solution)/shard_map/all_to_all | solution.py:609
  203.7 14.0 %all-to-all-done.6 = bf16[16,64,384]{2,1,0:T(8,128)(2,1)} async-done(((bf16[16,64,384]{2,1,0:T(8,128)(2,1)}), bf16[16,64,384]{2,1,0:T(8,128)(2,1)}, u32[]{:S(2)}, u32[]{:S(2)}) %all-to-all-start.6) | async-done | bytes 786464 | tf_op jit(solution)/shard_map/all_to_all | solution.py:609
  220.6 1.8 copy.57
  226.6 8.7 %collective-permute-done.7 = bf16[256,768]{1,0:T(8,128)(2,1)} collective-permute-done((bf16[256,768]{1,0:T(8,128)(2,1)S(1)}, bf16[256,768]{1,0:T(8,128)(2,1)}, u32[]{:S(2)}, u32[]{:S(2)}) %collective-permute-start.7) | collective-permute-done | bytes 393248 | tf_op jit(solution)/shard_map/ppermute | solution.py:799
  235.4 1.9 broadcast_select_fusion.grad_low
  237.3 12.5 %shard_map.183 = (bf16[16,64,192]{2,1,0:T(8,128)(2,1)}, f32[256,768]{1,0:T(8,128)}, bf16[256,3072]{1,0:T(8,128)(2,1)}, bf16[256,768]{1,0:T(8,128)(2,1)}, f32[4,768]{1,0:T(4,128)}, /*index=5*/f32[4,768]{1,0:T(4,128)}) custom-call(bf16[16,64,192]{2,1,0:T(8,128)(2,1)} %all_to_all.61.mixed, bf16[256,768]{1,0:T(8,128)(2,1)} %copy-done.2, ...), custom_call_target="tpu_custom_call" | custom-call | flops 4227858432 | bytes 14155776 | tf_op jit(solution)/shard_map/pallas_call | solution.py:481
  249.8 2.1 collective-permute-start.12
  252.5 4.1 %all-to-all-start.7 = ((bf16[16,64,192]{2,1,0:T(8,128)(2,1)}), bf16[16,64,192]{2,1,0:T(8,128)(2,1)}, u32[]{:S(2)}, u32[]{:S(2)}) async-start(bf16[16,64,192]{2,1,0:T(8,128)(2,1)} %get-tuple-element.90), calls=%async_computation.7 | async-start | bytes 1048576 | tf_op jit(solution)/shard_map/all_to_all | solution.py:609
  258.1 8.1 %shard_map.184 = bf16[4,896,768]{2,1,0:T(8,128)(2,1)} custom-call(s32[1]{0:T(128)} %bitcast.core_id, bf16[256,3072]{1,0:T(8,128)(2,1)S(1)} %copy-done.6, bf16[256,3072]{1,0:T(8,128)(2,1)} %collective-permute-done.8.active_other, bf16[256,768]{1,0:T(8,128)(2,1)S(1)} %copy-done.7, bf16[256,768]{1,0:T(8,128)(2,1)} %collective-permute-done.11.grad_low_other, ...), custom_call_target="tpu_custom_call" | custom-call | flops 2717908992 | bytes 5505024 | tf_op jit(solution)/shard_map/pallas_call | solution.py:284
  266.2 1.7 all-to-all-done.7
  270.5 12.1 %shard_map.185 = (bf16[1024,576]{1,0:T(8,128)(2,1)S(1)}, bf16[1024,384]{1,0:T(8,128)(2,1)S(1)}, bf16[1024,384]{1,0:T(8,128)(2,1)S(1)}) custom-call(s32[32]{0:T(128)S(1)} %copy-done.25, s32[3]{0:T(128)S(1)} %pad_add_fusion.ids, bf16[1024,576]{1,0:T(8,128)(2,1)S(1)} %copy-done.29, bf16[1024,192]{1,0:T(8,128)(2,1)} %bitcast.36.grad_mixed, ...), custom_call_target="tpu_custom_call" | custom-call | flops 2013265920 | bytes 3145728 | tf_op jit(solution)/shard_map/pallas_call | solution.py:204
  284.0 1.9 collective-permute-done.17
  287.0 5.0 %all-to-all-start.9 = ((bf16[16,64,384]{2,1,0:T(8,128)(2,1)}), bf16[16,64,384]{2,1,0:T(8,128)(2,1)S(1)}, u32[]{:S(2)}, u32[]{:S(2)}) async-start(bf16[16,64,384]{2,1,0:T(8,128)(2,1)} %bitcast.123), calls=%async_computation.10 | async-start | bytes 1572864 | tf_op jit(solution)/shard_map/all_to_all | solution.py:609
  294.9 2.0 shard_map.186
  298.4 2.4 collective-permute-start.15
  302.1 3.9 all-to-all-done.9
  309.0 4.4 %all-to-all-start.10 = ((bf16[4,4,576]{2,1,0:T(4,128)(2,1)}), bf16[4,4,576]{2,1,0:T(4,128)(2,1)S(1)}, u32[]{:S(2)}, u32[]{:S(2)}) async-start(bf16[4,4,576]{2,1,0:T(4,128)(2,1)} %convert_element_type.157), calls=%async_computation.11 | async-start | bytes 40960 | tf_op jit(solution)/shard_map/all_to_all | solution.py:609
  313.4 1.5 collective-permute-done.15
  316.2 9.6 %reduce-scatter.2.cloned.1.call-done = bf16[896,768]{1,0:T(8,128)(2,1)} async-done(((bf16[3584,768]{1,0:T(8,128)(2,1)}), bf16[896,768]{1,0:T(8,128)(2,1)}) %reduce-scatter.2.cloned.1.call-update) | async-done | bytes 1376272 | tf_op jit(solution)/shard_map/reduce_scatter | solution.py:749
  325.8 6.6 %all-to-all-start.8 = ((bf16[8,112,768]{2,1,0:T(8,128)(2,1)}), bf16[8,112,768]{2,1,0:T(8,128)(2,1)}, u32[]{:S(2)}, u32[]{:S(2)}) async-start(bf16[8,112,768]{2,1,0:T(8,128)(2,1)} %bitcast.126), calls=%async_computation.9 | async-start | bytes 2752512 | tf_op jit(solution)/shard_map/all_to_all | solution.py:609
  332.5 2.7 collective-permute-start.20
  335.1 8.1 %shard_map.187 = bf16[256,768]{1,0:T(8,128)(2,1)} custom-call(bf16[16,64,192]{2,1,0:T(8,128)(2,1)S(1)} %copy-done.5, bf16[256,768]{1,0:T(8,128)(2,1)S(1)} %copy-done.4, bf16[8,864,768]{2,1,0:T(8,128)(2,1)} %bitcast.111, f32[8,768]{1,0:T(8,128)S(1)} %copy-done.13, f32[4,768]{1,0:T(4,128)S(1)} %copy-done.15), custom_call_target="tpu_custom_call" | custom-call | flops 2717908992 | bytes 10616832 | tf_op jit(solution)/shard_map/pallas_call | solution.py:384
  343.4 9.4 %all-to-all-done.8 = bf16[8,112,768]{2,1,0:T(8,128)(2,1)} async-done(((bf16[8,112,768]{2,1,0:T(8,128)(2,1)}), bf16[8,112,768]{2,1,0:T(8,128)(2,1)}, u32[]{:S(2)}, u32[]{:S(2)}) %all-to-all-start.8) | async-done | bytes 1376288 | tf_op jit(solution)/shard_map/all_to_all | solution.py:609
  352.8 1.5 reduce_sum.120
  354.5 30.5 %all_to_all.63.own = bf16[8,176,768]{2,1,0:T(8,128)(2,1)} all-to-all(bf16[8,176,768]{2,1,0:T(8,128)(2,1)S(1)} %broadcast_in_dim.111), channel_id=1, replica_groups=mesh['section'=2,'x'=4,'yh'=2,'core'=2,'fsdp'=4] {'x','yh'}, dimensions={0} | all-to-all | bytes 4325376 | tf_op jit(solution)/shard_map/all_to_all | solution.py:609
  385.1 2.9 collective-permute-start.21
  389.1 3.1 collective-permute-done.21.other
  392.2 5.5 %shard_map.188 = (f32[192,2304]{1,0:T(8,128)}, f32[192,768]{1,0:T(8,128)}, f32[192,3072]{1,0:T(8,128)}, f32[768,768]{1,0:T(8,128)}, f32[4,768]{1,0:T(4,128)S(1)}) custom-call(s32[1]{0:T(128)} %bitcast.core_id, bf16[8,176,768]{2,1,0:T(8,128)(2,1)} %all_to_all.63.own, bf16[8,176,768]{2,1,0:T(8,128)(2,1)} %collective-permute-done.21.other), custom_call_target="tpu_custom_call" | custom-call | bytes 12582912 | tf_op jit(solution)/shard_map/pallas_call | solution.py:574
  (257 shorter events, 45.7 us)
Async XLA Ops:
  7.2 81.3 %all-gather.3.cloned.1.call-start = ((), (), s32[]{:S(2)}) async-start(), calls=%async_computation.14 | async-start | bytes 11943936 | tf_op jit(solution)/shard_map/all_gather | solution.py:695
  12.0 18.9 %copy-start.38 = (bf16[4,1,64,768]{3,2,1,0:T(8,128)(2,1)S(1)}, bf16[4,1,64,768]{3,2,1,0:T(8,128)(2,1)}, u32[]{:S(2)}) copy-start(bf16[4,1,64,768]{3,2,1,0:T(8,128)(2,1)} %param.11) | copy-start | bytes 1179652
  13.5 17.5 %copy-start.32 = (bf16[192,3,1,192]{0,3,1,2:T(8,128)(2,1)}, bf16[192,3,1,192]{0,3,1,2:T(8,128)(2,1)S(1)}, u32[]{:S(2)}) copy-start(bf16[192,3,1,192]{0,3,1,2:T(8,128)(2,1)S(1)} %copy.65) | copy-start | bytes 663556
  13.7 168.5 %copy-start.10 = (bf16[192,576]{1,0:T(8,128)(2,1)}, bf16[192,576]{1,0:T(8,128)(2,1)S(1)}, u32[]{:S(2)}) copy-start(bf16[192,576]{1,0:T(8,128)(2,1)S(1)} %copy.48.w0) | copy-start | bytes 663556
  13.7 18.2 %collective-permute-start.1 = (bf16[192,576]{1,0:T(8,128)(2,1)S(1)}, bf16[192,576]{1,0:T(8,128)(2,1)S(1)}, u32[]{:S(2)}, u32[]{:S(2)}) collective-permute-start(bf16[192,576]{1,0:T(8,128)(2,1)S(1)} %copy.48.w0), channel_id=1, source_target_pairs={{0,1},{1,2},{2,3},{3,0},{4,5},{5,6},{6,7},{7,4},{8,9},{9,10},{10,1... | collective-permute-start | bytes 663560 | tf_op jit(solution)/shard_map/ppermute | solution.py:641
  16.3 15.7 %collective-permute-start = (bf16[192,576]{1,0:T(8,128)(2,1)S(1)}, bf16[192,576]{1,0:T(8,128)(2,1)S(1)}, u32[]{:S(2)}, u32[]{:S(2)}) collective-permute-start(bf16[192,576]{1,0:T(8,128)(2,1)S(1)} %copy.48.w0), channel_id=1, source_target_pairs={{0,3},{1,0},{2,1},{3,2},{4,7},{5,4},{6,5},{7,6},{8,11},{9,8},{10,9... | collective-permute-start | bytes 663560 | tf_op jit(solution)/shard_map/ppermute | solution.py:641
  19.3 12.6 %all-to-all-start = ((bf16[4,4,576]{2,1,0:T(4,128)(2,1)}), bf16[4,4,576]{2,1,0:T(4,128)(2,1)S(1)}, u32[]{:S(2)}, u32[]{:S(2)}) async-start(bf16[4,4,576]{2,1,0:T(4,128)(2,1)} %broadcast_in_dim.98), calls=%async_computation | async-start | bytes 40960 | tf_op jit(solution)/shard_map/all_to_all | solution.py:609
  32.0 150.3 %copy-start.18 = (bf16[192,576]{1,0:T(8,128)(2,1)}, bf16[192,576]{1,0:T(8,128)(2,1)S(1)}, u32[]{:S(2)}) copy-start(bf16[192,576]{1,0:T(8,128)(2,1)S(1)} %collective-permute-done.1.w3) | copy-start | bytes 663556
  32.0 150.3 %copy-start.20 = (bf16[192,576]{1,0:T(8,128)(2,1)}, bf16[192,576]{1,0:T(8,128)(2,1)S(1)}, u32[]{:S(2)}) copy-start(bf16[192,576]{1,0:T(8,128)(2,1)S(1)} %collective-permute-done.w1) | copy-start | bytes 663556
  32.1 186.8 %copy-start.43 = (f32[2,384]{1,0:T(2,128)}, f32[2,384]{1,0:T(2,128)S(1)}, u32[]{:S(2)}) copy-start(f32[2,384]{1,0:T(2,128)S(1)} %mul.146) | copy-start | bytes 9220
  34.0 25.7 %copy-start.24 = (s32[32]{0:T(128)S(1)}, s32[32]{0:T(128)}, u32[]{:S(2)}) copy-start(s32[32]{0:T(128)} %table.7) | copy-start | bytes 388
  34.0 22.9 %all-to-all-start.1 = ((bf16[16,64,384]{2,1,0:T(8,128)(2,1)}), bf16[16,64,384]{2,1,0:T(8,128)(2,1)S(1)}, u32[]{:S(2)}, u32[]{:S(2)}) async-start(bf16[16,64,384]{2,1,0:T(8,128)(2,1)} %bitcast.14), calls=%async_computation.1 | async-start | bytes 1572864 | tf_op jit(solution)/shard_map/all_to_all | solution.py:609
  42.1 14.8 %collective-permute-start.2 = (bf16[192,576]{1,0:T(8,128)(2,1)S(1)}, bf16[192,576]{1,0:T(8,128)(2,1)S(1)}, u32[]{:S(2)}, u32[]{:S(2)}) collective-permute-start(bf16[192,576]{1,0:T(8,128)(2,1)S(1)} %copy.48.w0), channel_id=1, source_target_pairs={{0,2},{1,3},{2,0},{3,1},{4,6},{5,7},{6,4},{7,5},{8,10},{9,11},{10,... | collective-permute-start | bytes 663560 | tf_op jit(solution)/shard_map/ppermute | solution.py:641
  56.9 125.4 %copy-start.22 = (bf16[192,576]{1,0:T(8,128)(2,1)}, bf16[192,576]{1,0:T(8,128)(2,1)S(1)}, u32[]{:S(2)}) copy-start(bf16[192,576]{1,0:T(8,128)(2,1)S(1)} %collective-permute-done.2.w2) | copy-start | bytes 663556
  56.9 2.8 collective-permute-start.3
  70.0 18.5 %all-to-all-start.2 = ((bf16[16,64,192]{2,1,0:T(8,128)(2,1)}), bf16[16,64,192]{2,1,0:T(8,128)(2,1)S(1)}, u32[]{:S(2)}, u32[]{:S(2)}) async-start(bf16[16,64,192]{2,1,0:T(8,128)(2,1)} %bitcast.18), calls=%async_computation.2 | async-start | bytes 1048576 | tf_op jit(solution)/shard_map/all_to_all | solution.py:609
  77.5 18.4 %copy-start.14 = (f32[4,768]{1,0:T(4,128)}, f32[4,768]{1,0:T(4,128)S(1)}, u32[]{:S(2)}) copy-start(f32[4,768]{1,0:T(4,128)S(1)} %reshape.369.up_bias) | copy-start | bytes 36868
  77.6 18.3 %copy-start.12 = (f32[8,768]{1,0:T(8,128)}, f32[8,768]{1,0:T(8,128)S(1)}, u32[]{:S(2)}) copy-start(f32[8,768]{1,0:T(8,128)S(1)} %reshape.368.vectors) | copy-start | bytes 73732
  96.0 9.4 %collective-permute-start.4 = (bf16[256,768]{1,0:T(8,128)(2,1)S(1)}, bf16[256,768]{1,0:T(8,128)(2,1)S(1)}, u32[]{:S(2)}, u32[]{:S(2)}) collective-permute-start(bf16[256,768]{1,0:T(8,128)(2,1)S(1)} %shard_map.179), channel_id=1, source_target_pairs={{0,64},{1,65},{2,66},{3,67},{4,68},{5,69},{6,70},{7,71},{8,72},{9,... | collective-permute-start | bytes 1179656 | tf_op jit(solution)/shard_map/ppermute | solution.py:791
  105.5 117.3 %copy-start.41 = (f32[256]{0:T(256)}, f32[256]{0:T(256)S(1)}, u32[]{:S(2)}) copy-start(f32[256]{0:T(256)S(1)} %broadcast_multiply_fusion.5) | copy-start | bytes 3076
  105.8 117.0 %copy-start.45 = (f32[256]{0:T(256)}, f32[256]{0:T(256)S(1)}, u32[]{:S(2)}) copy-start(f32[256]{0:T(256)S(1)} %add_rsqrt_fusion.1) | copy-start | bytes 3076
  106.4 21.2 %copy-start.33 = (bf16[192,3,1,192]{0,3,1,2:T(8,128)(2,1)S(1)}, bf16[192,3,1,192]{0,3,1,2:T(8,128)(2,1)}, u32[]{:S(2)}) copy-start(bf16[192,3,1,192]{0,3,1,2:T(8,128)(2,1)} %copy-done.32) | copy-start | bytes 663556
  127.2 2.3 collective-permute-start.5
  138.5 43.8 %copy-start.28 = (bf16[1024,576]{1,0:T(8,128)(2,1)}, bf16[1024,576]{1,0:T(8,128)(2,1)S(1)}, u32[]{:S(2)}) copy-start(bf16[1024,576]{1,0:T(8,128)(2,1)S(1)} %get-tuple-element.81.joined) | copy-start | bytes 3538948
  138.5 43.7 %copy-start.30 = (f32[8,1024]{1,0:T(8,128)}, f32[8,1024]{1,0:T(8,128)S(1)}, u32[]{:S(2)}) copy-start(f32[8,1024]{1,0:T(8,128)S(1)} %get-tuple-element.83.log_total) | copy-start | bytes 98308
  194.4 3.3 collective-permute-start.6
  198.8 18.9 %all-to-all-start.6 = ((bf16[16,64,384]{2,1,0:T(8,128)(2,1)}), bf16[16,64,384]{2,1,0:T(8,128)(2,1)}, u32[]{:S(2)}, u32[]{:S(2)}) async-start(bf16[16,64,384]{2,1,0:T(8,128)(2,1)} %bitcast.124), calls=%async_computation.6 | async-start | bytes 1572864 | tf_op jit(solution)/shard_map/all_to_all | solution.py:609
  203.3 34.0 %collective-permute-start.8 = (bf16[256,3072]{1,0:T(8,128)(2,1)S(1)}, bf16[256,3072]{1,0:T(8,128)(2,1)}, u32[]{:S(2)}, u32[]{:S(2)}) collective-permute-start(bf16[256,3072]{1,0:T(8,128)(2,1)S(1)} %copy-done.6), channel_id=1, source_target_pairs={{0,4},{4,0},{1,5},{5,1},{2,6},{6,2},{3,7},{7,3},{8,12},{12,8},{9,1... | collective-permute-start | bytes 4718600 | tf_op jit(solution)/shard_map/ppermute | solution.py:613
  223.9 11.5 %collective-permute-start.7 = (bf16[256,768]{1,0:T(8,128)(2,1)S(1)}, bf16[256,768]{1,0:T(8,128)(2,1)}, u32[]{:S(2)}, u32[]{:S(2)}) collective-permute-start(bf16[256,768]{1,0:T(8,128)(2,1)S(1)} %fusion.14), channel_id=1, source_target_pairs={{64,0},{65,1},{66,2},{67,3},{68,4},{69,5},{70,6},{71,7},{72,8},{73... | collective-permute-start | bytes 1179656 | tf_op jit(solution)/shard_map/ppermute | solution.py:799
  225.2 12.1 %collective-permute-start.9 = (bf16[768,256]{1,0:T(8,128)(2,1)S(1)}, bf16[768,256]{1,0:T(8,128)(2,1)S(1)}, u32[]{:S(2)}, u32[]{:S(2)}) collective-permute-start(bf16[768,256]{1,0:T(8,128)(2,1)S(1)} %copy-done.8), channel_id=1, source_target_pairs={{0,4},{4,0},{1,5},{5,1},{2,6},{6,2},{3,7},{7,3},{8,12},{12,8},{9,1... | collective-permute-start | bytes 1179656 | tf_op jit(solution)/shard_map/ppermute | solution.py:613
  226.6 10.7 %collective-permute-start.10 = (bf16[768,256]{1,0:T(8,128)(2,1)}, bf16[768,256]{1,0:T(8,128)(2,1)}, u32[]{:S(2)}, u32[]{:S(2)}) collective-permute-start(bf16[768,256]{1,0:T(8,128)(2,1)} %get-tuple-element.96.mixed), channel_id=1, source_target_pairs={{0,4},{4,0},{1,5},{5,1},{2,6},{6,2},{3,7},{7,3},{8,12},{12,8},{9,1... | collective-permute-start | bytes 1179656 | tf_op jit(solution)/shard_map/ppermute | solution.py:613
  249.8 7.2 %collective-permute-start.12 = (bf16[256,3072]{1,0:T(8,128)(2,1)}, bf16[256,3072]{1,0:T(8,128)(2,1)}, u32[]{:S(2)}, u32[]{:S(2)}) collective-permute-start(bf16[256,3072]{1,0:T(8,128)(2,1)} %get-tuple-element.95.grad_hidden), channel_id=1, source_target_pairs={{0,4},{4,0},{1,5},{5,1},{2,6},{6,2},{3,7},{7,3},{8,12},{12,8},{9,1... | collective-permute-start | bytes 4718600 | tf_op jit(solution)/shard_map/ppermute | solution.py:613
  251.9 5.1 %collective-permute-start.13 = (bf16[256,768]{1,0:T(8,128)(2,1)}, bf16[256,768]{1,0:T(8,128)(2,1)}, u32[]{:S(2)}, u32[]{:S(2)}) collective-permute-start(bf16[256,768]{1,0:T(8,128)(2,1)} %get-tuple-element.98.grad_attn), channel_id=1, source_target_pairs={{0,4},{4,0},{1,5},{5,1},{2,6},{6,2},{3,7},{7,3},{8,12},{12,8},{9,1... | collective-permute-start | bytes 1179656 | tf_op jit(solution)/shard_map/ppermute | solution.py:613
  252.0 5.0 %collective-permute-start.11 = (bf16[256,768]{1,0:T(8,128)(2,1)S(1)}, bf16[256,768]{1,0:T(8,128)(2,1)}, u32[]{:S(2)}, u32[]{:S(2)}) collective-permute-start(bf16[256,768]{1,0:T(8,128)(2,1)S(1)} %copy-done.7), channel_id=1, source_target_pairs={{0,4},{4,0},{1,5},{5,1},{2,6},{6,2},{3,7},{7,3},{8,12},{12,8},{9,1... | collective-permute-start | bytes 1179656 | tf_op jit(solution)/shard_map/ppermute | solution.py:613
  252.5 15.4 %all-to-all-start.7 = ((bf16[16,64,192]{2,1,0:T(8,128)(2,1)}), bf16[16,64,192]{2,1,0:T(8,128)(2,1)}, u32[]{:S(2)}, u32[]{:S(2)}) async-start(bf16[16,64,192]{2,1,0:T(8,128)(2,1)} %get-tuple-element.90), calls=%async_computation.7 | async-start | bytes 1048576 | tf_op jit(solution)/shard_map/all_to_all | solution.py:609
  256.6 69.2 %reduce-scatter.2.cloned.1.call-start = ((), (), s32[]{:S(2)}) async-start(), calls=%async_computation.13 | async-start | bytes 6881280 | tf_op jit(solution)/shard_map/reduce_scatter | solution.py:749
  282.6 3.3 collective-permute-start.17
  287.0 19.0 %all-to-all-start.9 = ((bf16[16,64,384]{2,1,0:T(8,128)(2,1)}), bf16[16,64,384]{2,1,0:T(8,128)(2,1)S(1)}, u32[]{:S(2)}, u32[]{:S(2)}) async-start(bf16[16,64,384]{2,1,0:T(8,128)(2,1)} %bitcast.123), calls=%async_computation.10 | async-start | bytes 1572864 | tf_op jit(solution)/shard_map/all_to_all | solution.py:609
  297.0 16.4 %collective-permute-start.14 = (bf16[192,576]{1,0:T(8,128)(2,1)S(1)}, bf16[192,576]{1,0:T(8,128)(2,1)}, u32[]{:S(2)}, u32[]{:S(2)}) collective-permute-start(bf16[192,576]{1,0:T(8,128)(2,1)S(1)} %get-tuple-element.103), channel_id=1, source_target_pairs={{0,16},{16,32},{32,48},{48,0},{1,17},{17,33},{33,49},{49,1},{2,18}... | collective-permute-start | bytes 663560 | tf_op jit(solution)/shard_map/ppermute | solution.py:649
  298.4 16.5 %collective-permute-start.15 = (bf16[192,576]{1,0:T(8,128)(2,1)S(1)}, bf16[192,576]{1,0:T(8,128)(2,1)}, u32[]{:S(2)}, u32[]{:S(2)}) collective-permute-start(bf16[192,576]{1,0:T(8,128)(2,1)S(1)} %get-tuple-element.104), channel_id=1, source_target_pairs={{0,32},{16,48},{32,0},{48,16},{1,33},{17,49},{33,1},{49,17},{2,34}... | collective-permute-start | bytes 663560 | tf_op jit(solution)/shard_map/ppermute | solution.py:649
  300.8 14.1 %collective-permute-start.16 = (bf16[192,576]{1,0:T(8,128)(2,1)S(1)}, bf16[192,576]{1,0:T(8,128)(2,1)}, u32[]{:S(2)}, u32[]{:S(2)}) collective-permute-start(bf16[192,576]{1,0:T(8,128)(2,1)S(1)} %get-tuple-element.105), channel_id=1, source_target_pairs={{0,48},{16,0},{32,16},{48,32},{1,49},{17,1},{33,17},{49,33},{2,50}... | collective-permute-start | bytes 663560 | tf_op jit(solution)/shard_map/ppermute | solution.py:649
  309.0 16.8 %all-to-all-start.10 = ((bf16[4,4,576]{2,1,0:T(4,128)(2,1)}), bf16[4,4,576]{2,1,0:T(4,128)(2,1)S(1)}, u32[]{:S(2)}, u32[]{:S(2)}) async-start(bf16[4,4,576]{2,1,0:T(4,128)(2,1)} %convert_element_type.157), calls=%async_computation.11 | async-start | bytes 40960 | tf_op jit(solution)/shard_map/all_to_all | solution.py:609
  325.8 27.0 %all-to-all-start.8 = ((bf16[8,112,768]{2,1,0:T(8,128)(2,1)}), bf16[8,112,768]{2,1,0:T(8,128)(2,1)}, u32[]{:S(2)}, u32[]{:S(2)}) async-start(bf16[8,112,768]{2,1,0:T(8,128)(2,1)} %bitcast.126), calls=%async_computation.9 | async-start | bytes 2752512 | tf_op jit(solution)/shard_map/all_to_all | solution.py:609
  332.4 10.9 %collective-permute-start.18 = (bf16[48,576]{1,0:T(8,128)(2,1)S(1)}, bf16[48,576]{1,0:T(8,128)(2,1)S(1)}, u32[]{:S(2)}, u32[]{:S(2)}) collective-permute-start(bf16[48,576]{1,0:T(8,128)(2,1)S(1)} %get-tuple-element.169), channel_id=1, source_target_pairs={{0,1},{1,2},{2,3},{3,0},{4,5},{5,6},{6,7},{7,4},{8,9},{9,10},{10,1... | collective-permute-start | bytes 165896 | tf_op jit(solution)/shard_map/ppermute | solution.py:649
  332.5 10.9 %collective-permute-start.20 = (bf16[48,576]{1,0:T(8,128)(2,1)S(1)}, bf16[48,576]{1,0:T(8,128)(2,1)S(1)}, u32[]{:S(2)}, u32[]{:S(2)}) collective-permute-start(bf16[48,576]{1,0:T(8,128)(2,1)S(1)} %get-tuple-element.170), channel_id=1, source_target_pairs={{0,3},{1,0},{2,1},{3,2},{4,7},{5,4},{6,5},{7,6},{8,11},{9,8},{10,9... | collective-permute-start | bytes 165896 | tf_op jit(solution)/shard_map/ppermute | solution.py:649
  335.1 8.2 %collective-permute-start.19 = (bf16[48,576]{1,0:T(8,128)(2,1)S(1)}, bf16[48,576]{1,0:T(8,128)(2,1)S(1)}, u32[]{:S(2)}, u32[]{:S(2)}) collective-permute-start(bf16[48,576]{1,0:T(8,128)(2,1)S(1)} %get-tuple-element.171), channel_id=1, source_target_pairs={{0,2},{1,3},{2,0},{3,1},{4,6},{5,7},{6,4},{7,5},{8,10},{9,11},{10,... | collective-permute-start | bytes 165896 | tf_op jit(solution)/shard_map/ppermute | solution.py:649
  354.5 33.5 %copy-start.36 = (f32[256,768]{1,0:T(8,128)S(1)}, f32[256,768]{1,0:T(8,128)}, u32[]{:S(2)}) copy-start(f32[256,768]{1,0:T(8,128)} %get-tuple-element.108) | copy-start | bytes 2359300
  385.1 7.1 %collective-permute-start.21 = (bf16[8,176,768]{2,1,0:T(8,128)(2,1)}, bf16[8,176,768]{2,1,0:T(8,128)(2,1)}, u32[]{:S(2)}, u32[]{:S(2)}) collective-permute-start(bf16[8,176,768]{2,1,0:T(8,128)(2,1)} %all_to_all.63.own), channel_id=1, source_target_pairs={{0,4},{4,0},{1,5},{5,1},{2,6},{6,2},{3,7},{7,3},{8,12},{12,8},{9,1... | collective-permute-start | bytes 6488072 | tf_op jit(solution)/shard_map/ppermute | solution.py:613
  (40 other events, 159.7 us)
Sparse Core Ops, SparseCore 0:
  11.0 68.1 all-gather.2
  268.0 57.7 reduce-scatter.1

commit v5 on v4

--- a/solution.py
+++ b/solution.py
@@ -396,54 +396,8 @@
     )(mixed, entering, packed, vectors, up_bias)
 
 
-def feed_back_body(mixed, entering, stored, vectors, up_bias, grad_low, *outs):
-    packed, landed = outs[-2:]
-    outs = outs[:-2]
-    last = len(outs) == 6
-    grad_mixed, grad_middle = outs[:2]
-    members, width = packed.shape[0], packed.shape[2]
-    panels = up_bias.shape[0]
-    up_rows = width // members
-    down_rows = panels * up_rows
-    micro_count = mixed.shape[0] // GROUPS
-    local_rows = mixed.shape[1]
-    out, ups, downs = start_copies(stored, packed, landed, panels)
-    out.start()
-    for panel in range(panels):
-        ups[panel].start()
-        downs[panel].start()
-    out.wait()
-    w_out = weight_panel(packed, 2 * down_rows)
-    middle = attend_out(mixed, entering, packed, vectors, w_out)
-    normed, unit, spread_two = normalize(middle, vectors[1:2, :], vectors[6:7, :])
-    normed = normed.astype(jnp.bfloat16)
-    grads = grad_low[...]
-    grad_normed = jnp.zeros(middle.shape, jnp.float32)
-    per_panel = members // panels
-    for panel in range(panels):
-        columns = slice(panel * width, (panel + 1) * width)
-        ups[panel].wait()
-        w_up = weight_panel(packed, down_rows + panel * up_rows)
-        hidden = dot(normed, w_up, 1, 0) + up_bias[panel : panel + 1, :]
-        square = hidden * hidden
-        bend = jnp.tanh(GELU_SCALE * (hidden + GELU_CUBE * (square * hidden)))
-        slope = 0.5 * (1.0 + bend) + 0.5 * hidden * (1.0 - bend * bend) * (
-            GELU_SCALE * (1.0 + 3.0 * GELU_CUBE * square)
-        )
-        downs[panel].wait()
-        w_down = jnp.concatenate(
-            [packed[i, :down_rows, :] for i in range(panel * per_panel, (panel + 1) * per_panel)],
-            0,
-        )
-        grad_hidden = (dot(grads, w_down, 1, 1) * slope).astype(jnp.bfloat16)
-        grad_normed += dot(grad_hidden, w_up, 1, 1)
-        if last:
-            outs[2][:, columns] = grad_hidden
-            outs[5][panel : panel + 1, :] = jnp.sum(
-                grad_hidden.astype(jnp.float32), 0, keepdims=True
-            )
-        else:
-            outs[2][:, columns] = (0.5 * hidden * (1.0 + bend)).astype(jnp.bfloat16)
+def feed_back_end(grads, grad_normed, unit, spread_two, vectors, w_out, grad_mixed, grad_middle):
+    local_rows = grad_mixed.shape[1]
     grad_top = grads.astype(jnp.float32)
     grad_norm, d_gain, d_shift = normalize_back(grad_normed, unit, spread_two, vectors[1:2, :])
     grad_sum = grad_top + grad_norm
@@ -452,36 +406,113 @@
     for group in range(GROUPS):
         part = dot(grad_attn, w_out[group * WIDTH : (group + 1) * WIDTH, :], 1, 1)
         part = part.astype(jnp.bfloat16)
-        for m in range(micro_count):
+        for m in range(grad_mixed.shape[0] // GROUPS):
             grad_mixed[m * GROUPS + group] = part[m * local_rows : (m + 1) * local_rows]
-    if last:
-        outs[3][...] = grad_attn
-        sums = outs[4]
-        sums[0:1, :] = d_gain[None]
-        sums[1:2, :] = d_shift[None]
-        sums[2:3, :] = jnp.sum(grad_attn.astype(jnp.float32), 0, keepdims=True)
-        sums[3:4, :] = jnp.sum(grad_top, 0, keepdims=True)
-    else:
-        outs[3][...] = normed.astype(jnp.float32).T.astype(jnp.bfloat16)
-        for group in range(GROUPS):
-            part = join_groups(mixed, group).astype(jnp.float32).T.astype(jnp.bfloat16)
-            outs[4][group * WIDTH : (group + 1) * WIDTH, :] = part
-
-
-def feed_back(mixed, entering, packed, vectors, up_bias, grad_low, last):
-    rows, width = entering.shape
-    hidden_width = up_bias.size
-    shapes = [(mixed.shape, jnp.bfloat16), ((rows, width), jnp.float32)]
-    shapes.append(((rows, hidden_width), jnp.bfloat16))
-    if last:
-        shapes.append(((rows, width), jnp.bfloat16))
-        shapes += [((4, width), jnp.float32), (up_bias.shape, jnp.float32)]
-    else:
-        shapes += [((width, rows), jnp.bfloat16)] * 2
+    return grad_attn, d_gain, d_shift
+
+
+def down_panel(packed, panel, panels):
+    members, width = packed.shape[0], packed.shape[2]
+    each = members // panels
+    rows = panels * width // members
+    return jnp.concatenate(
+        [packed[i, :rows, :] for i in range(panel * each, (panel + 1) * each)], 0
+    )
+
+
+def feed_back_first_body(
+    mixed,
+    entering,
+    packed,
+    vectors,
+    up_bias,
+    grad_low,
+    grad_mixed,
+    grad_middle,
+    active,
+    normed_tall,
+    mixed_tall,
+    slopes,
+    units,
+    spreads,
+):
+    members, width = packed.shape[0], packed.shape[2]
+    panels = up_bias.shape[0]
+    up_rows = width // members
+    down_rows = panels * up_rows
+    w_out = weight_panel(packed, 2 * down_rows)
+    middle = attend_out(mixed, entering, packed, vectors, w_out)
+    normed, unit, spread_two = normalize(middle, vectors[1:2, :], vectors[6:7, :])
+    normed = normed.astype(jnp.bfloat16)
+    grads = grad_low[...]
+    grad_normed = jnp.zeros(middle.shape, jnp.float32)
+    for panel in range(panels):
+        columns = slice(panel * width, (panel + 1) * width)
+        w_up = weight_panel(packed, down_rows + panel * up_rows)
+        hidden = dot(normed, w_up, 1, 0) + up_bias[panel : panel + 1, :]
+        square = hidden * hidden
+        bend = jnp.tanh(GELU_SCALE * (hidden + GELU_CUBE * (square * hidden)))
+        slope = 0.5 * (1.0 + bend) + 0.5 * hidden * (1.0 - bend * bend) * (
+            GELU_SCALE * (1.0 + 3.0 * GELU_CUBE * square)
+        )
+        slopes[:, columns] = slope
+        active[:, columns] = (0.5 * hidden * (1.0 + bend)).astype(jnp.bfloat16)
+        w_down = down_panel(packed, panel, panels)
+        grad_hidden = (dot(grads, w_down, 1, 1) * slope).astype(jnp.bfloat16)
+        grad_normed += dot(grad_hidden, w_up, 1, 1)
+    feed_back_end(grads, grad_normed, unit, spread_two, vectors, w_out, grad_mixed, grad_middle)
+    units[...] = unit
+    spreads[...] = jnp.broadcast_to(spread_two, spreads.shape)
+    normed_tall[...] = normed.astype(jnp.float32).T.astype(jnp.bfloat16)
+    for group in range(GROUPS):
+        part = join_groups(mixed, group).astype(jnp.float32).T.astype(jnp.bfloat16)
+        mixed_tall[group * WIDTH : (group + 1) * WIDTH, :] = part
+
+
+def feed_back_last_body(
+    packed,
+    vectors,
+    grad_low,
+    slopes,
+    units,
+    spreads,
+    grad_mixed,
+    grad_middle,
+    grad_hidden,
+    grad_attn,
+    sums,
+    up_sums,
+):
+    members, width = packed.shape[0], packed.shape[2]
+    panels = up_sums.shape[0]
+    up_rows = width // members
+    down_rows = panels * up_rows
+    w_out = weight_panel(packed, 2 * down_rows)
+    grads = grad_low[...]
+    grad_normed = jnp.zeros(units.shape, jnp.float32)
+    for panel in range(panels):
+        columns = slice(panel * width, (panel + 1) * width)
+        w_up = weight_panel(packed, down_rows + panel * up_rows)
+        w_down = down_panel(packed, panel, panels)
+        part = (dot(grads, w_down, 1, 1) * slopes[:, columns]).astype(jnp.bfloat16)
+        grad_normed += dot(part, w_up, 1, 1)
+        grad_hidden[:, columns] = part
+        up_sums[panel : panel + 1, :] = jnp.sum(part.astype(jnp.float32), 0, keepdims=True)
+    attn, d_gain, d_shift = feed_back_end(
+        grads, grad_normed, units[...], spreads[:, :1], vectors, w_out, grad_mixed, grad_middle
+    )
+    grad_attn[...] = attn
+    sums[0:1, :] = d_gain[None]
+    sums[1:2, :] = d_shift[None]
+    sums[2:3, :] = jnp.sum(attn.astype(jnp.float32), 0, keepdims=True)
+    sums[3:4, :] = jnp.sum(grads.astype(jnp.float32), 0, keepdims=True)
+
+
+def feed_back(body, args, shapes):
+    rows, width = shapes[1][0]
     return pl.pallas_call(
-        feed_back_body,
-        in_specs=feed_specs(6),
-        scratch_shapes=feed_scratch(packed, up_bias),
+        body,
+        in_specs=[pl.BlockSpec(memory_space=pltpu.VMEM)] * len(args),
         out_specs=[pl.BlockSpec(memory_space=pltpu.VMEM)] * len(shapes),
         out_shape=[jax.ShapeDtypeStruct(*shape) for shape in shapes],
         compiler_params=pltpu.CompilerParams(vmem_limit_bytes=56 << 20),
@@ -490,7 +521,42 @@
             bytes_accessed=24 * width * width,
             transcendentals=4 * rows * width,
         ),
-    )(mixed, entering, packed, vectors, up_bias, grad_low)
+    )(*args)
+
+
+def norm_back_body(returned, entering, grad_middle, vectors, grad_in, sums):
+    parts = []
+    for m in range(returned.shape[0] // GROUPS):
+        halves = [
+            returned[m * GROUPS + core].astype(jnp.float32)
+            + returned[m * GROUPS + 2 + core].astype(jnp.float32)
+            for core in range(2)
+        ]
+        parts.append(jnp.concatenate(halves, 1))
+    grad_normed = jnp.concatenate(parts, 0)
+    gain = vectors[0:1, :]
+    _, unit, spread_one = normalize(entering[...].astype(jnp.float32), gain, vectors[2:3, :])
+    grad_norm, d_gain, d_shift = normalize_back(grad_normed, unit, spread_one, gain)
+    grad_in[...] = (grad_middle[...] + grad_norm).astype(jnp.bfloat16)
+    sums[0:1, :] = d_gain[None]
+    sums[1:2, :] = d_shift[None]
+
+
+def norm_back(returned, entering, grad_middle, vectors):
+    rows, width = entering.shape
+    return pl.pallas_call(
+        norm_back_body,
+        in_specs=[pl.BlockSpec(memory_space=pltpu.VMEM)] * 4,
+        out_specs=[pl.BlockSpec(memory_space=pltpu.VMEM)] * 2,
+        out_shape=[
+            jax.ShapeDtypeStruct((rows, width), jnp.bfloat16),
+            jax.ShapeDtypeStruct((2, width), jnp.float32),
+        ],
+        compiler_params=pltpu.CompilerParams(vmem_limit_bytes=32 << 20),
+        cost_estimate=pl.CostEstimate(
+            flops=20 * rows * width, bytes_accessed=10 * rows * width, transcendentals=rows
+        ),
+    )(returned, entering, grad_middle, vectors)
 
 
 def qkv_grads_body(owners, ids, own, other, grad_joined, *outs):
@@ -694,6 +760,7 @@
     packed = pack_weights(attn_out, mlp_in, mlp_out)
     packed = lax.all_gather(packed, ("fsdp", "core"), axis=0)
     model_width = attn_out.shape[2]
+    hidden_width = mlp_in.shape[2]
     half = model_width // 2
     vector_rows = small_all[:, :8].transpose(1, 0, 2).reshape(8, model_width)
     gain_rows, bias_rows = vector_rows[:2], vector_rows[2:]
@@ -712,7 +779,7 @@
 
     def forward(entering):
         stream = entering.astype(jnp.float32)
-        normed, unit_one, spread_one = normalize(stream, gain_rows[0], bias_rows[0])
+        normed, _, _ = normalize(stream, gain_rows[0], bias_rows[0])
         halves = normed.astype(jnp.bfloat16).reshape(micro_count, 1, local_rows, 2, half)
         halves = jnp.broadcast_to(
             halves.transpose(0, 1, 3, 2, 4), (micro_count, 2, 2, local_rows, half)
@@ -725,18 +792,31 @@
         )
         mixed = exchange(mixed_heads.reshape(-1, local_rows, WIDTH), CTX)
         result = feed_forward(mixed, entering, packed, vector_rows, up_rows)
-        return result, (entering, unit_one, spread_one, own, other, joined, log_total, mixed)
+        return result, (entering, own, other, joined, log_total, mixed)
 
     def backward(grad_low, saved, kept):
-        entering, unit_one, spread_one, own, other, joined, log_total, mixed = saved
+        entering, own, other, joined, log_total, mixed = saved
         last = kept is not None
-        grad_mixed, grad_middle, *extra = feed_back(
-            mixed, entering, packed, vector_rows, up_rows, grad_low, last
-        )
+        low, full = jnp.bfloat16, jnp.float32
+        shapes = [(mixed.shape, low), ((rows, model_width), full), ((rows, hidden_width), low)]
+        if last:
+            pairs, plain = kept
+            shapes += [((rows, model_width), low), ((4, model_width), full), (up_rows.shape, full)]
+            grad_mixed, grad_middle, *extra = feed_back(
+                feed_back_last_body, (packed, vector_rows, grad_low, *plain), shapes
+            )
+        else:
+            shapes += [((model_width, rows), low)] * 2
+            shapes += [((rows, hidden_width), full), ((rows, model_width), full), ((rows, 128), full)]
+            grad_mixed, grad_middle, *extra = feed_back(
+                feed_back_first_body,
+                (mixed, entering, packed, vector_rows, up_rows, grad_low),
+                shapes,
+            )
         grad_heads = exchange(grad_mixed.reshape(-1, local_rows, WIDTH), CTX).reshape(-1, WIDTH)
         if last:
             grad_hidden, grad_attn, sums, up_sums = extra
-            active_pair, normed_pair, mixed_pair = kept
+            active_pair, normed_pair, mixed_pair = pairs
             low_pair, hidden_pair, attn_pair = (
                 (value, swap(value)) for value in (grad_low, grad_hidden, grad_attn)
             )
@@ -758,13 +838,7 @@
         received = swap(grad_other)
         summed = (grad_own.astype(jnp.float32) + received.astype(jnp.float32)).astype(jnp.bfloat16)
         returned = exchange(summed.reshape(-1, local_rows, half), CTX)
-        returned = returned.reshape(micro_count, 2, 2, local_rows, half).astype(jnp.float32)
-        grad_normed = (returned[:, 0] + returned[:, 1]).transpose(0, 2, 1, 3)
-        grad_normed = grad_normed.reshape(rows, model_width)
-        grad_norm_one, d_gain_one, d_shift_one = normalize_back(
-            grad_normed, unit_one, spread_one, gain_rows[0]
-        )
-        grad_in = (grad_middle + grad_norm_one).astype(jnp.bfloat16)
+        grad_in, norm_sums = norm_back(returned, entering, grad_middle, vector_rows)
         if not last:
             return grad_in, extra
         x_count = lax.axis_size("x")
@@ -780,7 +854,9 @@
             for shift in range(fsdp_count)
         ]
         qkv_piece = sum_pieces(owner_pieces, "fsdp")
-        vectors = jnp.stack([d_gain_one, sums[0], d_shift_one, sums[2], sums[1], sums[3]])
+        vectors = jnp.stack(
+            [norm_sums[0], sums[0], norm_sums[1], sums[2], sums[1], sums[3]]
+        )
         d_up_bias = up_sums.reshape(-1)
         return grad_in, share, qkv_piece, joined_sums, vectors, d_up_bias
 
@@ -798,8 +874,9 @@
         result, kept = backward(grad_low, saved, None)
         received = lax.ppermute(result, "section", back_pairs)
         grad_low = jnp.where(section_id == sections - 1, top_grad, received)
-        kept = [(value, swap(value)) for value in kept]
-        grad_low, kept = lax.optimization_barrier((grad_low, kept))
+        pairs = [(value, swap(value)) for value in kept[:3]]
+        grad_low, pairs = lax.optimization_barrier((grad_low, pairs))
+        kept = (pairs, kept[3:])
     input_grad, share, qkv_piece, joined_sums, vectors, d_up_bias = backward(grad_low, saved, kept)
 
     ours = jnp.arange(fsdp_count)[:, None] == group_id

time: 413 us -> 404 us (0.978)
  blocking collectives: 82 us -> 99.9 us
  waiting for transfers between devices: 87.6 us -> 77.6 us
  other arithmetic: 13.7 us -> 5.73 us
  starting transfers between devices: 74.5 us -> 67.9 us
    all_to_all x4 -> x5, blocking collectives: 82 us -> 99.9 us  [exchange(): return lax.all_to_all(value, axes, 0, 0, tiled=True)]
    all_to_all x8 -> x7, waiting for transfers between devices: 40 us -> 24.9 us  [exchange(): return lax.all_to_all(value, axes, 0, 0, tiled=True)]
    all_to_all x8 -> x7, starting transfers between devices: 43.3 us -> 39.3 us  [exchange(): return lax.all_to_all(value, axes, 0, 0, tiled=True)]
    unnamed x125 -> x114, local copies, waits for them, and re-layouts: 10.7 us -> 14 us
    pallas_call x2 -> x4, Pallas kernels: 25.5 us -> 25.7 us  [the longest x2 22.9 us: feed_back(): pl.pallas_call(body, in_specs=[pl.BlockSpec(memory_space=pltpu.VMEM)] * l...]
  transfers between devices with their start and end apart: 32 -> 31, of which waited for: 15 -> 14; matrix products, arithmetic and copies ran while one was open for 6% -> 3% of each run, Pallas kernels for 10% -> 11%
where the time goes in v5:
time: 404 us; the launch traced here: 397 us
  blocking collectives  99.9 us (25%)
  Pallas kernels  98.9 us (24%)
  waiting for transfers between devices  77.6 us (19%)
  starting transfers between devices  67.9 us (17%)
  local copies, waits for them, and re-layouts  24.3 us (6%)
  between operations  22.9 us (6%)
  other arithmetic  5.73 us (1%)
    all_to_all x5, blocking collectives, exchange(): return lax.all_to_all(value, axes, 0, 0, tiled=True)  99.9 us
    all_to_all x7, starting transfers between devices, exchange(): return lax.all_to_all(value, axes, 0, 0, tiled=True)  39.3 us
    all_to_all x7, waiting for transfers between devices, exchange(): return lax.all_to_all(value, axes, 0, 0, tiled=True)  24.9 us
    pallas_call x2, Pallas kernels, attend_back(): pl.pallas_call(attend_back_body, grid_spec=pltpu.PrefetchScalarGridSpec(n...  24.3 us
    pallas_call x2, Pallas kernels, feed_back(): pl.pallas_call(body, in_specs=[pl.BlockSpec(memory_space=pltpu.VMEM)] * l...  22.9 us
    pallas_call x2, Pallas kernels, attend(): pl.pallas_call(attend_body, grid_spec=pltpu.PrefetchScalarGridSpec(num_sc...  19.3 us
    pallas_call x2, Pallas kernels, feed_forward(): pl.pallas_call(feed_forward_body, in_specs=feed_specs(5), out_specs=pl.Bl...  15.5 us
    unnamed x114, local copies, waits for them, and re-layouts  14 us
  transfers between devices with their start and end apart: 31, of which 14 were waited for; matrix products, arithmetic and copies ran while one was open for 3% of the time, Pallas kernels for 11%

profile of v5, /device:TPU:1, one launch (start us, length us, event | category | flops | bytes accessed | tf_op | source)
XLA Modules:
  0.0 397.3 jit_solution(11982558228341253812)
XLA Ops:
  13.7 2.5 collective-permute-start.1
  16.3 2.2 collective-permute-start
  19.3 3.3 all-to-all-start
  34.0 8.0 %all-to-all-start.1 = ((bf16[16,64,384]{2,1,0:T(8,128)(2,1)}), bf16[16,64,384]{2,1,0:T(8,128)(2,1)S(1)}, u32[]{:S(2)}, u32[]{:S(2)}) async-start(bf16[16,64,384]{2,1,0:T(8,128)(2,1)} %bitcast.19), calls=%async_computation.1 | async-start | bytes 1572864 | tf_op jit(solution)/shard_map/all_to_all | solution.py:675
  42.1 3.2 collective-permute-start.2
  45.3 11.6 %collective-permute-done.2.w2 = bf16[192,576]{1,0:T(8,128)(2,1)S(1)} collective-permute-done((bf16[192,576]{1,0:T(8,128)(2,1)S(1)}, bf16[192,576]{1,0:T(8,128)(2,1)S(1)}, u32[]{:S(2)}, u32[]{:S(2)}) %collective-permute-start.2) | collective-permute-done | bytes 221216 | tf_op jit(solution)/shard_map/ppermute | solution.py:707
  61.4 10.3 %shard_map.178 = (bf16[1024,576]{1,0:T(8,128)(2,1)}, bf16[1024,192]{1,0:T(8,128)(2,1)}, f32[8,1024]{1,0:T(8,128)}) custom-call(s32[32]{0:T(128)S(1)} %copy-done.33, s32[3]{0:T(128)S(1)} %pad_add_fusion.ids, bf16[1024,384]{1,0:T(8,128)(2,1)S(1)} %bitcast.73, bf16[1024,384]{1,0:T(8,128)(2,1)S(1)} %collective-permute-done.3.other, ...), custom_call_target="tpu_custom_call" | custom-call | flops 805306368 | bytes 1572864 | tf_op jit(solution)/shard_map/pallas_call | solution.py:111
  71.7 7.4 %all-to-all-start.2 = ((bf16[16,64,192]{2,1,0:T(8,128)(2,1)}), bf16[16,64,192]{2,1,0:T(8,128)(2,1)S(1)}, u32[]{:S(2)}, u32[]{:S(2)}) async-start(bf16[16,64,192]{2,1,0:T(8,128)(2,1)} %bitcast.23), calls=%async_computation.2 | async-start | bytes 1048576 | tf_op jit(solution)/shard_map/all_to_all | solution.py:675
  79.3 10.9 %all-to-all-done.2.mixed = bf16[16,64,192]{2,1,0:T(8,128)(2,1)S(1)} async-done(((bf16[16,64,192]{2,1,0:T(8,128)(2,1)}), bf16[16,64,192]{2,1,0:T(8,128)(2,1)S(1)}, u32[]{:S(2)}, u32[]{:S(2)}) %all-to-all-start.2) | async-done | bytes 393248 | tf_op jit(solution)/shard_map/all_to_all | solution.py:675
  90.2 7.4 %shard_map.179 = bf16[256,768]{1,0:T(8,128)(2,1)S(1)} custom-call(bf16[16,64,192]{2,1,0:T(8,128)(2,1)S(1)} %all-to-all-done.2.mixed, bf16[256,768]{1,0:T(8,128)(2,1)S(1)} %bitcast.68, bf16[8,864,768]{2,1,0:T(8,128)(2,1)} %bitcast.76, f32[8,768]{1,0:T(8,128)S(1)} %reshape.299.vectors, f32[4,768]{1,0:T(4,128)S(1)} %reshape.305.up_bias), custom_call_target="tpu_custom_call" | custom-call | flops 2717908992 | bytes 10616832 | tf_op jit(solution)/shard_map/pallas_call | solution.py:384
  97.6 2.3 collective-permute-start.4
  100.1 6.9 %collective-permute-done.4 = bf16[256,768]{1,0:T(8,128)(2,1)S(1)} collective-permute-done((bf16[256,768]{1,0:T(8,128)(2,1)S(1)}, bf16[256,768]{1,0:T(8,128)(2,1)S(1)}, u32[]{:S(2)}, u32[]{:S(2)}) %collective-permute-start.4) | collective-permute-done | bytes 393248 | tf_op jit(solution)/shard_map/ppermute | solution.py:867
  108.0 20.8 %all_to_all.60 = bf16[16,64,384]{2,1,0:T(8,128)(2,1)S(1)} all-to-all(bf16[16,64,384]{2,1,0:T(8,128)(2,1)S(1)} %bitcast.84), channel_id=1, replica_groups=mesh['section'=2,'x'=4,'yh'=2,'core'=2,'fsdp'=4] {'x','yh','core'}, dimensions={0} | all-to-all | bytes 1572864 | tf_op jit(solution)/shard_map/all_to_all | solution.py:675
  129.4 1.7 collective-permute-done.5.other
  131.1 9.0 %shard_map.180 = (bf16[1024,576]{1,0:T(8,128)(2,1)S(1)}, bf16[1024,192]{1,0:T(8,128)(2,1)S(1)}, f32[8,1024]{1,0:T(8,128)S(1)}) custom-call(s32[32]{0:T(128)S(1)} %copy-done.33, s32[3]{0:T(128)S(1)} %pad_add_fusion.ids, bf16[1024,384]{1,0:T(8,128)(2,1)S(1)} %bitcast.70, bf16[1024,384]{1,0:T(8,128)(2,1)S(1)} %collective-permute-done.5.other, ...), custom_call_target="tpu_custom_call" | custom-call | flops 805306368 | bytes 1572864 | tf_op jit(solution)/shard_map/pallas_call | solution.py:111
  140.2 14.7 %all_to_all.61.mixed = bf16[16,64,192]{2,1,0:T(8,128)(2,1)} all-to-all(bf16[16,64,192]{2,1,0:T(8,128)(2,1)S(1)} %bitcast.74), channel_id=1, replica_groups=mesh['section'=2,'x'=4,'yh'=2,'core'=2,'fsdp'=4] {'x','yh','core'}, dimensions={0} | all-to-all | bytes 786432 | tf_op jit(solution)/shard_map/all_to_all | solution.py:675
  154.9 12.6 %shard_map.181 = (bf16[16,64,192]{2,1,0:T(8,128)(2,1)}, f32[256,768]{1,0:T(8,128)}, bf16[256,3072]{1,0:T(8,128)(2,1)}, bf16[768,256]{1,0:T(8,128)(2,1)}, bf16[76...) custom-call(bf16[16,64,192]{2,1,0:T(8,128)(2,1)} %all_to_all.61.mixed, ...), custom_call_target="tpu_custom_call" | custom-call | flops 4227858432 | bytes 14155776 | tf_op jit(solution)/shard_map/pallas_call | solution.py:513
  167.5 16.3 %all_to_all.62 = bf16[16,64,192]{2,1,0:T(8,128)(2,1)S(1)} all-to-all(bf16[16,64,192]{2,1,0:T(8,128)(2,1)} %get-tuple-element.87), channel_id=1, replica_groups=mesh['section'=2,'x'=4,'yh'=2,'core'=2,'fsdp'=4] {'x','yh','core'}, dimensions={0} | all-to-all | bytes 786432 | tf_op jit(solution)/shard_map/all_to_all | solution.py:675
  183.9 12.1 %shard_map.182 = (bf16[1024,576]{1,0:T(8,128)(2,1)}, bf16[1024,384]{1,0:T(8,128)(2,1)S(1)}, bf16[1024,384]{1,0:T(8,128)(2,1)S(1)}) custom-call(s32[32]{0:T(128)S(1)} %copy-done.33, s32[3]{0:T(128)S(1)} %pad_add_fusion.ids, bf16[1024,576]{1,0:T(8,128)(2,1)S(1)} %get-tuple-element.85.joined, bf16[1024,192]{1,0:T(8,128)(2,1)S(1)} %bitcast.75, ...), custom_call_target="tpu_custom_call" | custom-call | flops 2013265920 | bytes 3145728 | tf_op jit(solution)/shard_map/pallas_call | solution.py:204
  196.0 1.4 collective-permute-start.6
  197.4 3.0 collective-permute-done.6
  200.6 17.5 %all_to_all.63.returned = bf16[16,64,384]{2,1,0:T(8,128)(2,1)S(1)} all-to-all(bf16[16,64,384]{2,1,0:T(8,128)(2,1)S(1)} %bitcast.85), channel_id=1, replica_groups=mesh['section'=2,'x'=4,'yh'=2,'core'=2,'fsdp'=4] {'x','yh','core'}, dimensions={0} | all-to-all | bytes 1572864 | tf_op jit(solution)/shard_map/all_to_all | solution.py:675
  218.1 1.4 shard_map.183
  221.6 10.4 %collective-permute-done.7 = bf16[256,768]{1,0:T(8,128)(2,1)} collective-permute-done((bf16[256,768]{1,0:T(8,128)(2,1)}, bf16[256,768]{1,0:T(8,128)(2,1)}, u32[]{:S(2)}, u32[]{:S(2)}) %collective-permute-start.7) | collective-permute-done | bytes 393248 | tf_op jit(solution)/shard_map/ppermute | solution.py:875
  232.0 1.9 broadcast_select_fusion.1.grad_low
  234.7 10.2 %shard_map.184 = (bf16[16,64,192]{2,1,0:T(8,128)(2,1)}, f32[256,768]{1,0:T(8,128)}, bf16[256,3072]{1,0:T(8,128)(2,1)}, bf16[256,768]{1,0:T(8,128)(2,1)}, f32[4,768]{1,0:T(4,128)}, /*index=5*/f32[4,768]{1,0:T(4,128)}) custom-call(bf16[8,864,768]{2,1,0:T(8,128)(2,1)} %bitcast.78, f32[8,768]{1,0:T(8,128)} %copy-done.9, ...), custom_call_target="tpu_custom_call" | custom-call | flops 4227858432 | bytes 14155776 | tf_op jit(solution)/shard_map/pallas_call | solution.py:513
  246.7 4.1 %all-to-all-start.7 = ((bf16[16,64,192]{2,1,0:T(8,128)(2,1)}), bf16[16,64,192]{2,1,0:T(8,128)(2,1)}, u32[]{:S(2)}, u32[]{:S(2)}) async-start(bf16[16,64,192]{2,1,0:T(8,128)(2,1)} %get-tuple-element.100), calls=%async_computation.7 | async-start | bytes 1048576 | tf_op jit(solution)/shard_map/all_to_all | solution.py:675
  253.0 8.1 %shard_map.185 = bf16[4,896,768]{2,1,0:T(8,128)(2,1)} custom-call(s32[1]{0:T(128)} %bitcast.9.core_id, bf16[256,3072]{1,0:T(8,128)(2,1)S(1)} %copy-done.5, bf16[256,3072]{1,0:T(8,128)(2,1)} %collective-permute-done.8.active_other, bf16[256,768]{1,0:T(8,128)(2,1)S(1)} %copy-done.6, bf16[256,768]{1,0:T(8,128)(2,1)} %collective-permute-done.11.grad_low_other, ...), custom_call_target="tpu_custom_call" | custom-call | flops 2717908992 | bytes 5505024 | tf_op jit(solution)/shard_map/pallas_call | solution.py:284
  264.7 12.1 %shard_map.186 = (bf16[1024,576]{1,0:T(8,128)(2,1)S(1)}, bf16[1024,384]{1,0:T(8,128)(2,1)S(1)}, bf16[1024,384]{1,0:T(8,128)(2,1)S(1)}) custom-call(s32[32]{0:T(128)S(1)} %copy-done.34, s32[3]{0:T(128)S(1)} %pad_add_fusion.ids, bf16[1024,576]{1,0:T(8,128)(2,1)S(1)} %copy-done.38, bf16[1024,192]{1,0:T(8,128)(2,1)} %bitcast.31.grad_mixed, ...), custom_call_target="tpu_custom_call" | custom-call | flops 2013265920 | bytes 3145728 | tf_op jit(solution)/shard_map/pallas_call | solution.py:204
  276.9 1.4 collective-permute-start.17
  278.3 1.9 collective-permute-done.17
  281.3 5.6 %all-to-all-start.9 = ((bf16[16,64,384]{2,1,0:T(8,128)(2,1)}), bf16[16,64,384]{2,1,0:T(8,128)(2,1)S(1)}, u32[]{:S(2)}, u32[]{:S(2)}) async-start(bf16[16,64,384]{2,1,0:T(8,128)(2,1)} %bitcast.36), calls=%async_computation.10 | async-start | bytes 1572864 | tf_op jit(solution)/shard_map/all_to_all | solution.py:675
  289.4 2.8 shard_map.187
  292.2 1.4 collective-permute-start.14
  293.6 2.4 collective-permute-start.15
  297.3 3.6 all-to-all-done.9.returned
  300.9 1.4 shard_map.189
  303.4 4.4 %all-to-all-start.10 = ((bf16[4,4,576]{2,1,0:T(4,128)(2,1)}), bf16[4,4,576]{2,1,0:T(4,128)(2,1)S(1)}, u32[]{:S(2)}, u32[]{:S(2)}) async-start(bf16[4,4,576]{2,1,0:T(4,128)(2,1)} %convert_element_type.133), calls=%async_computation.11 | async-start | bytes 40960 | tf_op jit(solution)/shard_map/all_to_all | solution.py:675
  307.8 1.9 collective-permute-done.15
  309.8 10.8 %reduce-scatter.2.cloned.1.call-done = bf16[896,768]{1,0:T(8,128)(2,1)} async-done(((bf16[3584,768]{1,0:T(8,128)(2,1)}), bf16[896,768]{1,0:T(8,128)(2,1)}) %reduce-scatter.2.cloned.1.call-update) | async-done | bytes 1376272 | tf_op jit(solution)/shard_map/reduce_scatter | solution.py:829
  320.6 6.6 %all-to-all-start.8 = ((bf16[8,112,768]{2,1,0:T(8,128)(2,1)}), bf16[8,112,768]{2,1,0:T(8,128)(2,1)S(1)}, u32[]{:S(2)}, u32[]{:S(2)}) async-start(bf16[8,112,768]{2,1,0:T(8,128)(2,1)} %bitcast.87), calls=%async_computation.9 | async-start | bytes 2752512 | tf_op jit(solution)/shard_map/all_to_all | solution.py:675
  327.3 2.7 collective-permute-start.20
  330.0 8.1 %shard_map.188 = bf16[256,768]{1,0:T(8,128)(2,1)} custom-call(bf16[16,64,192]{2,1,0:T(8,128)(2,1)S(1)} %copy-done.4, bf16[256,768]{1,0:T(8,128)(2,1)S(1)} %copy-done.3, bf16[8,864,768]{2,1,0:T(8,128)(2,1)} %bitcast.79, f32[8,768]{1,0:T(8,128)S(1)} %copy-done.11, f32[4,768]{1,0:T(4,128)S(1)} %copy-done.20), custom_call_target="tpu_custom_call" | custom-call | flops 2717908992 | bytes 10616832 | tf_op jit(solution)/shard_map/pallas_call | solution.py:384
  338.2 9.3 %all-to-all-done.8 = bf16[8,112,768]{2,1,0:T(8,128)(2,1)S(1)} async-done(((bf16[8,112,768]{2,1,0:T(8,128)(2,1)}), bf16[8,112,768]{2,1,0:T(8,128)(2,1)S(1)}, u32[]{:S(2)}, u32[]{:S(2)}) %all-to-all-start.8) | async-done | bytes 1376288 | tf_op jit(solution)/shard_map/all_to_all | solution.py:675
  347.9 30.6 %all_to_all.64.own = bf16[8,176,768]{2,1,0:T(8,128)(2,1)S(1)} all-to-all(bf16[8,176,768]{2,1,0:T(8,128)(2,1)S(1)} %broadcast_in_dim.107), channel_id=1, replica_groups=mesh['section'=2,'x'=4,'yh'=2,'core'=2,'fsdp'=4] {'x','yh'}, dimensions={0} | all-to-all | bytes 4325376 | tf_op jit(solution)/shard_map/all_to_all | solution.py:675
  378.5 2.6 collective-permute-start.21
  381.1 3.9 collective-permute-done.21.other
  385.0 3.3 shard_map.190
  (227 shorter events, 36.4 us)
Async XLA Ops:
  7.2 83.0 %all-gather.3.cloned.1.call-start = ((), (), s32[]{:S(2)}) async-start(), calls=%async_computation.14 | async-start | bytes 11943936 | tf_op jit(solution)/shard_map/all_gather | solution.py:761
  12.0 18.9 %copy-start.45 = (bf16[4,1,64,768]{3,2,1,0:T(8,128)(2,1)S(1)}, bf16[4,1,64,768]{3,2,1,0:T(8,128)(2,1)}, u32[]{:S(2)}) copy-start(bf16[4,1,64,768]{3,2,1,0:T(8,128)(2,1)} %param.11) | copy-start | bytes 1179652
  13.5 20.5 %copy-start.41 = (bf16[192,3,1,192]{0,3,1,2:T(8,128)(2,1)}, bf16[192,3,1,192]{0,3,1,2:T(8,128)(2,1)S(1)}, u32[]{:S(2)}) copy-start(bf16[192,3,1,192]{0,3,1,2:T(8,128)(2,1)S(1)} %copy.40) | copy-start | bytes 663556
  13.7 170.1 %copy-start.17 = (bf16[192,576]{1,0:T(8,128)(2,1)}, bf16[192,576]{1,0:T(8,128)(2,1)S(1)}, u32[]{:S(2)}) copy-start(bf16[192,576]{1,0:T(8,128)(2,1)S(1)} %copy.27.w0) | copy-start | bytes 663556
  13.7 18.2 %collective-permute-start.1 = (bf16[192,576]{1,0:T(8,128)(2,1)S(1)}, bf16[192,576]{1,0:T(8,128)(2,1)S(1)}, u32[]{:S(2)}, u32[]{:S(2)}) collective-permute-start(bf16[192,576]{1,0:T(8,128)(2,1)S(1)} %copy.27.w0), channel_id=1, source_target_pairs={{0,1},{1,2},{2,3},{3,0},{4,5},{5,6},{6,7},{7,4},{8,9},{9,10},{10,1... | collective-permute-start | bytes 663560 | tf_op jit(solution)/shard_map/ppermute | solution.py:707
  16.3 15.7 %collective-permute-start = (bf16[192,576]{1,0:T(8,128)(2,1)S(1)}, bf16[192,576]{1,0:T(8,128)(2,1)S(1)}, u32[]{:S(2)}, u32[]{:S(2)}) collective-permute-start(bf16[192,576]{1,0:T(8,128)(2,1)S(1)} %copy.27.w0), channel_id=1, source_target_pairs={{0,3},{1,0},{2,1},{3,2},{4,7},{5,4},{6,5},{7,6},{8,11},{9,8},{10,9... | collective-permute-start | bytes 663560 | tf_op jit(solution)/shard_map/ppermute | solution.py:707
  19.3 12.6 %all-to-all-start = ((bf16[4,4,576]{2,1,0:T(4,128)(2,1)}), bf16[4,4,576]{2,1,0:T(4,128)(2,1)S(1)}, u32[]{:S(2)}, u32[]{:S(2)}) async-start(bf16[4,4,576]{2,1,0:T(4,128)(2,1)} %broadcast_in_dim.94), calls=%async_computation | async-start | bytes 40960 | tf_op jit(solution)/shard_map/all_to_all | solution.py:675
  32.0 151.9 %copy-start.23 = (bf16[192,576]{1,0:T(8,128)(2,1)}, bf16[192,576]{1,0:T(8,128)(2,1)S(1)}, u32[]{:S(2)}) copy-start(bf16[192,576]{1,0:T(8,128)(2,1)S(1)} %collective-permute-done.1.w3) | copy-start | bytes 663556
  32.0 99.1 %copy-start.25 = (bf16[192,576]{1,0:T(8,128)(2,1)}, bf16[192,576]{1,0:T(8,128)(2,1)S(1)}, u32[]{:S(2)}) copy-start(bf16[192,576]{1,0:T(8,128)(2,1)S(1)} %collective-permute-done.w1) | copy-start | bytes 663556
  34.0 26.4 %copy-start.33 = (s32[32]{0:T(128)S(1)}, s32[32]{0:T(128)}, u32[]{:S(2)}) copy-start(s32[32]{0:T(128)} %table.7) | copy-start | bytes 388
  34.0 23.6 %all-to-all-start.1 = ((bf16[16,64,384]{2,1,0:T(8,128)(2,1)}), bf16[16,64,384]{2,1,0:T(8,128)(2,1)S(1)}, u32[]{:S(2)}, u32[]{:S(2)}) async-start(bf16[16,64,384]{2,1,0:T(8,128)(2,1)} %bitcast.19), calls=%async_computation.1 | async-start | bytes 1572864 | tf_op jit(solution)/shard_map/all_to_all | solution.py:675
  42.1 14.8 %collective-permute-start.2 = (bf16[192,576]{1,0:T(8,128)(2,1)S(1)}, bf16[192,576]{1,0:T(8,128)(2,1)S(1)}, u32[]{:S(2)}, u32[]{:S(2)}) collective-permute-start(bf16[192,576]{1,0:T(8,128)(2,1)S(1)} %copy.27.w0), channel_id=1, source_target_pairs={{0,2},{1,3},{2,0},{3,1},{4,6},{5,7},{6,4},{7,5},{8,10},{9,11},{10,... | collective-permute-start | bytes 663560 | tf_op jit(solution)/shard_map/ppermute | solution.py:707
  57.6 2.8 collective-permute-start.3
  71.7 18.5 %all-to-all-start.2 = ((bf16[16,64,192]{2,1,0:T(8,128)(2,1)}), bf16[16,64,192]{2,1,0:T(8,128)(2,1)S(1)}, u32[]{:S(2)}, u32[]{:S(2)}) async-start(bf16[16,64,192]{2,1,0:T(8,128)(2,1)} %bitcast.23), calls=%async_computation.2 | async-start | bytes 1048576 | tf_op jit(solution)/shard_map/all_to_all | solution.py:675
  79.2 18.4 %copy-start.19 = (f32[4,768]{1,0:T(4,128)}, f32[4,768]{1,0:T(4,128)S(1)}, u32[]{:S(2)}) copy-start(f32[4,768]{1,0:T(4,128)S(1)} %reshape.305.up_bias) | copy-start | bytes 36868
  79.3 18.3 %copy-start.9 = (f32[8,768]{1,0:T(8,128)}, f32[8,768]{1,0:T(8,128)S(1)}, u32[]{:S(2)}) copy-start(f32[8,768]{1,0:T(8,128)S(1)} %reshape.299.vectors) | copy-start | bytes 73732
  97.6 9.4 %collective-permute-start.4 = (bf16[256,768]{1,0:T(8,128)(2,1)S(1)}, bf16[256,768]{1,0:T(8,128)(2,1)S(1)}, u32[]{:S(2)}, u32[]{:S(2)}) collective-permute-start(bf16[256,768]{1,0:T(8,128)(2,1)S(1)} %shard_map.179), channel_id=1, source_target_pairs={{0,64},{1,65},{2,66},{3,67},{4,68},{5,69},{6,70},{7,71},{8,72},{9,... | collective-permute-start | bytes 1179656 | tf_op jit(solution)/shard_map/ppermute | solution.py:867
  107.9 21.3 %copy-start.42 = (bf16[192,3,1,192]{0,3,1,2:T(8,128)(2,1)S(1)}, bf16[192,3,1,192]{0,3,1,2:T(8,128)(2,1)}, u32[]{:S(2)}) copy-start(bf16[192,3,1,192]{0,3,1,2:T(8,128)(2,1)} %copy-done.41) | copy-start | bytes 663556
  108.0 23.1 %copy-start.30 = (bf16[192,576]{1,0:T(8,128)(2,1)S(1)}, bf16[192,576]{1,0:T(8,128)(2,1)}, u32[]{:S(2)}) copy-start(bf16[192,576]{1,0:T(8,128)(2,1)} %copy-done.28) | copy-start | bytes 663556
  128.8 2.3 collective-permute-start.5
  140.2 43.7 %copy-start.37 = (bf16[1024,576]{1,0:T(8,128)(2,1)}, bf16[1024,576]{1,0:T(8,128)(2,1)S(1)}, u32[]{:S(2)}) copy-start(bf16[1024,576]{1,0:T(8,128)(2,1)S(1)} %get-tuple-element.85.joined) | copy-start | bytes 3538948
  140.2 43.7 %copy-start.39 = (f32[8,1024]{1,0:T(8,128)}, f32[8,1024]{1,0:T(8,128)S(1)}, u32[]{:S(2)}) copy-start(f32[8,1024]{1,0:T(8,128)S(1)} %get-tuple-element.88.log_total) | copy-start | bytes 98308
  154.9 29.0 %copy-start.26 = (bf16[192,576]{1,0:T(8,128)(2,1)S(1)}, bf16[192,576]{1,0:T(8,128)(2,1)}, u32[]{:S(2)}) copy-start(bf16[192,576]{1,0:T(8,128)(2,1)} %copy-done.25) | copy-start | bytes 663556
  154.9 29.0 %copy-start.31 = (bf16[192,576]{1,0:T(8,128)(2,1)S(1)}, bf16[192,576]{1,0:T(8,128)(2,1)}, u32[]{:S(2)}) copy-start(bf16[192,576]{1,0:T(8,128)(2,1)} %copy-done.28) | copy-start | bytes 663556
  196.0 4.3 %collective-permute-start.6 = (bf16[1024,384]{1,0:T(8,128)(2,1)S(1)}, bf16[1024,384]{1,0:T(8,128)(2,1)S(1)}, u32[]{:S(2)}, u32[]{:S(2)}) collective-permute-start(bf16[1024,384]{1,0:T(8,128)(2,1)S(1)} %get-tuple-element.90), channel_id=1, source_target_pairs={{0,4},{4,0},{1,5},{5,1},{2,6},{6,2},{3,7},{7,3},{8,12},{12,8},{9,1... | collective-permute-start | bytes 2359304 | tf_op jit(solution)/shard_map/ppermute | solution.py:679
  197.4 37.3 %collective-permute-start.8 = (bf16[256,3072]{1,0:T(8,128)(2,1)S(1)}, bf16[256,3072]{1,0:T(8,128)(2,1)}, u32[]{:S(2)}, u32[]{:S(2)}) collective-permute-start(bf16[256,3072]{1,0:T(8,128)(2,1)S(1)} %copy-done.5), channel_id=1, source_target_pairs={{0,4},{4,0},{1,5},{5,1},{2,6},{6,2},{3,7},{7,3},{8,12},{12,8},{9,1... | collective-permute-start | bytes 4718600 | tf_op jit(solution)/shard_map/ppermute | solution.py:679
  200.6 17.5 %copy-start.3 = (bf16[256,768]{1,0:T(8,128)(2,1)S(1)}, bf16[256,768]{1,0:T(8,128)(2,1)}, u32[]{:S(2)}) copy-start(bf16[256,768]{1,0:T(8,128)(2,1)} %copy-done.2) | copy-start | bytes 1179652
  200.6 17.5 %copy-start.8 = (f32[256,768]{1,0:T(8,128)S(1)}, f32[256,768]{1,0:T(8,128)}, u32[]{:S(2)}) copy-start(f32[256,768]{1,0:T(8,128)} %get-tuple-element.91.grad_middle) | copy-start | bytes 2359300
  219.6 12.5 %collective-permute-start.7 = (bf16[256,768]{1,0:T(8,128)(2,1)}, bf16[256,768]{1,0:T(8,128)(2,1)}, u32[]{:S(2)}, u32[]{:S(2)}) collective-permute-start(bf16[256,768]{1,0:T(8,128)(2,1)} %get-tuple-element.92), channel_id=1, source_target_pairs={{64,0},{65,1},{66,2},{67,3},{68,4},{69,5},{70,6},{71,7},{72,8},{73... | collective-permute-start | bytes 1179656 | tf_op jit(solution)/shard_map/ppermute | solution.py:875
  220.8 13.1 %collective-permute-start.9 = (bf16[768,256]{1,0:T(8,128)(2,1)S(1)}, bf16[768,256]{1,0:T(8,128)(2,1)S(1)}, u32[]{:S(2)}, u32[]{:S(2)}) collective-permute-start(bf16[768,256]{1,0:T(8,128)(2,1)S(1)} %copy-done.12), channel_id=1, source_target_pairs={{0,4},{4,0},{1,5},{5,1},{2,6},{6,2},{3,7},{7,3},{8,12},{12,8},{9,1... | collective-permute-start | bytes 1179656 | tf_op jit(solution)/shard_map/ppermute | solution.py:679
  221.4 13.4 %collective-permute-start.10 = (bf16[768,256]{1,0:T(8,128)(2,1)}, bf16[768,256]{1,0:T(8,128)(2,1)}, u32[]{:S(2)}, u32[]{:S(2)}) collective-permute-start(bf16[768,256]{1,0:T(8,128)(2,1)} %get-tuple-element.106.mixed), channel_id=1, source_target_pairs={{0,4},{4,0},{1,5},{5,1},{2,6},{6,2},{3,7},{7,3},{8,12},{12,8},{9,1... | collective-permute-start | bytes 1179656 | tf_op jit(solution)/shard_map/ppermute | solution.py:679
  245.0 6.0 %collective-permute-start.12 = (bf16[256,3072]{1,0:T(8,128)(2,1)}, bf16[256,3072]{1,0:T(8,128)(2,1)}, u32[]{:S(2)}, u32[]{:S(2)}) collective-permute-start(bf16[256,3072]{1,0:T(8,128)(2,1)} %get-tuple-element.105.grad_hidden), channel_id=1, source_target_pairs={{0,4},{4,0},{1,5},{5,1},{2,6},{6,2},{3,7},{7,3},{8,12},{12,8},{9,1... | collective-permute-start | bytes 4718600 | tf_op jit(solution)/shard_map/ppermute | solution.py:679
  246.2 4.7 %collective-permute-start.13 = (bf16[256,768]{1,0:T(8,128)(2,1)}, bf16[256,768]{1,0:T(8,128)(2,1)}, u32[]{:S(2)}, u32[]{:S(2)}) collective-permute-start(bf16[256,768]{1,0:T(8,128)(2,1)} %get-tuple-element.108.grad_attn), channel_id=1, source_target_pairs={{0,4},{4,0},{1,5},{5,1},{2,6},{6,2},{3,7},{7,3},{8,12},{12,8},{9,1... | collective-permute-start | bytes 1179656 | tf_op jit(solution)/shard_map/ppermute | solution.py:679
  246.3 4.6 %collective-permute-start.11 = (bf16[256,768]{1,0:T(8,128)(2,1)S(1)}, bf16[256,768]{1,0:T(8,128)(2,1)}, u32[]{:S(2)}, u32[]{:S(2)}) collective-permute-start(bf16[256,768]{1,0:T(8,128)(2,1)S(1)} %copy-done.6), channel_id=1, source_target_pairs={{0,4},{4,0},{1,5},{5,1},{2,6},{6,2},{3,7},{7,3},{8,12},{12,8},{9,1... | collective-permute-start | bytes 1179656 | tf_op jit(solution)/shard_map/ppermute | solution.py:679
  246.7 15.3 %all-to-all-start.7 = ((bf16[16,64,192]{2,1,0:T(8,128)(2,1)}), bf16[16,64,192]{2,1,0:T(8,128)(2,1)}, u32[]{:S(2)}, u32[]{:S(2)}) async-start(bf16[16,64,192]{2,1,0:T(8,128)(2,1)} %get-tuple-element.100), calls=%async_computation.7 | async-start | bytes 1048576 | tf_op jit(solution)/shard_map/all_to_all | solution.py:675
  250.9 69.7 %reduce-scatter.2.cloned.1.call-start = ((), (), s32[]{:S(2)}) async-start(), calls=%async_computation.13 | async-start | bytes 6881280 | tf_op jit(solution)/shard_map/reduce_scatter | solution.py:829
  276.9 3.3 collective-permute-start.17
  281.3 19.6 %all-to-all-start.9 = ((bf16[16,64,384]{2,1,0:T(8,128)(2,1)}), bf16[16,64,384]{2,1,0:T(8,128)(2,1)S(1)}, u32[]{:S(2)}, u32[]{:S(2)}) async-start(bf16[16,64,384]{2,1,0:T(8,128)(2,1)} %bitcast.36), calls=%async_computation.10 | async-start | bytes 1572864 | tf_op jit(solution)/shard_map/all_to_all | solution.py:675
  292.2 15.5 %collective-permute-start.14 = (bf16[192,576]{1,0:T(8,128)(2,1)}, bf16[192,576]{1,0:T(8,128)(2,1)S(1)}, u32[]{:S(2)}, u32[]{:S(2)}) collective-permute-start(bf16[192,576]{1,0:T(8,128)(2,1)} %get-tuple-element.113), channel_id=1, source_target_pairs={{0,16},{16,32},{32,48},{48,0},{1,17},{17,33},{33,49},{49,1},{2,18}... | collective-permute-start | bytes 663560 | tf_op jit(solution)/shard_map/ppermute | solution.py:715
  293.6 16.1 %collective-permute-start.15 = (bf16[192,576]{1,0:T(8,128)(2,1)}, bf16[192,576]{1,0:T(8,128)(2,1)S(1)}, u32[]{:S(2)}, u32[]{:S(2)}) collective-permute-start(bf16[192,576]{1,0:T(8,128)(2,1)} %get-tuple-element.114), channel_id=1, source_target_pairs={{0,32},{16,48},{32,0},{48,16},{1,33},{17,49},{33,1},{49,17},{2,34}... | collective-permute-start | bytes 663560 | tf_op jit(solution)/shard_map/ppermute | solution.py:715
  296.0 13.7 %collective-permute-start.16 = (bf16[192,576]{1,0:T(8,128)(2,1)S(1)}, bf16[192,576]{1,0:T(8,128)(2,1)S(1)}, u32[]{:S(2)}, u32[]{:S(2)}) collective-permute-start(bf16[192,576]{1,0:T(8,128)(2,1)S(1)} %get-tuple-element.115), channel_id=1, source_target_pairs={{0,48},{16,0},{32,16},{48,32},{1,49},{17,1},{33,17},{49,33},{2,50}... | collective-permute-start | bytes 663560 | tf_op jit(solution)/shard_map/ppermute | solution.py:715
  303.4 17.2 %all-to-all-start.10 = ((bf16[4,4,576]{2,1,0:T(4,128)(2,1)}), bf16[4,4,576]{2,1,0:T(4,128)(2,1)S(1)}, u32[]{:S(2)}, u32[]{:S(2)}) async-start(bf16[4,4,576]{2,1,0:T(4,128)(2,1)} %convert_element_type.133), calls=%async_computation.11 | async-start | bytes 40960 | tf_op jit(solution)/shard_map/all_to_all | solution.py:675
  320.6 26.9 %all-to-all-start.8 = ((bf16[8,112,768]{2,1,0:T(8,128)(2,1)}), bf16[8,112,768]{2,1,0:T(8,128)(2,1)S(1)}, u32[]{:S(2)}, u32[]{:S(2)}) async-start(bf16[8,112,768]{2,1,0:T(8,128)(2,1)} %bitcast.87), calls=%async_computation.9 | async-start | bytes 2752512 | tf_op jit(solution)/shard_map/all_to_all | solution.py:675
  327.2 10.9 %collective-permute-start.18 = (bf16[48,576]{1,0:T(8,128)(2,1)S(1)}, bf16[48,576]{1,0:T(8,128)(2,1)S(1)}, u32[]{:S(2)}, u32[]{:S(2)}) collective-permute-start(bf16[48,576]{1,0:T(8,128)(2,1)S(1)} %get-tuple-element.161), channel_id=1, source_target_pairs={{0,1},{1,2},{2,3},{3,0},{4,5},{5,6},{6,7},{7,4},{8,9},{9,10},{10,1... | collective-permute-start | bytes 165896 | tf_op jit(solution)/shard_map/ppermute | solution.py:715
  327.3 10.8 %collective-permute-start.20 = (bf16[48,576]{1,0:T(8,128)(2,1)S(1)}, bf16[48,576]{1,0:T(8,128)(2,1)S(1)}, u32[]{:S(2)}, u32[]{:S(2)}) collective-permute-start(bf16[48,576]{1,0:T(8,128)(2,1)S(1)} %get-tuple-element.162), channel_id=1, source_target_pairs={{0,3},{1,0},{2,1},{3,2},{4,7},{5,4},{6,5},{7,6},{8,11},{9,8},{10,9... | collective-permute-start | bytes 165896 | tf_op jit(solution)/shard_map/ppermute | solution.py:715
  329.9 8.2 %collective-permute-start.19 = (bf16[48,576]{1,0:T(8,128)(2,1)S(1)}, bf16[48,576]{1,0:T(8,128)(2,1)S(1)}, u32[]{:S(2)}, u32[]{:S(2)}) collective-permute-start(bf16[48,576]{1,0:T(8,128)(2,1)S(1)} %get-tuple-element.163), channel_id=1, source_target_pairs={{0,2},{1,3},{2,0},{3,1},{4,6},{5,7},{6,4},{7,5},{8,10},{9,11},{10,... | collective-permute-start | bytes 165896 | tf_op jit(solution)/shard_map/ppermute | solution.py:715
  347.9 42.4 %copy-start.1 = (bf16[1,192,3072]{2,1,0:T(8,128)(2,1)S(1)}, bf16[1,192,3072]{2,1,0:T(8,128)(2,1)}, u32[]{:S(2)}) copy-start(bf16[1,192,3072]{2,1,0:T(8,128)(2,1)} %param.17) | copy-start | bytes 3538948
  378.5 6.5 %collective-permute-start.21 = (bf16[8,176,768]{2,1,0:T(8,128)(2,1)S(1)}, bf16[8,176,768]{2,1,0:T(8,128)(2,1)S(1)}, u32[]{:S(2)}, u32[]{:S(2)}) collective-permute-start(bf16[8,176,768]{2,1,0:T(8,128)(2,1)S(1)} %all_to_all.64.own), channel_id=1, source_target_pairs={{0,4},{4,0},{1,5},{5,1},{2,6},{6,2},{3,7},{7,3},{8,12},{12,8},{9,1... | collective-permute-start | bytes 6488072 | tf_op jit(solution)/shard_map/ppermute | solution.py:679
  (37 other events, 181.3 us)
Sparse Core Ops, SparseCore 0:
  11.0 68.1 all-gather.2
  262.3 58.2 reduce-scatter.1

commit v6 on v5

--- a/solution.py
+++ b/solution.py
@@ -14,8 +14,7 @@
 GROUP_HEADS = HEADS // GROUPS
 WIDTH = GROUP_HEADS * HDIM
 QUERY_BLOCK = 256
-EXTRA = 32
-JOINT_ROWS = 112
+VECTOR_ROWS = 4
 CTX = ("x", "yh", "core")
 
 epsilon = 1e-05
@@ -262,15 +261,13 @@
     product = dot(mixed[...], grad_attn[...], 1, 0)
     product += dot(mixed_other[...], grad_attn_other[...], 1, 0)
     joint[0, place : place + up_rows, :] = product.astype(jnp.bfloat16)
-    place += up_rows
-    joint[0, place:, :] = jnp.zeros_like(joint[0, place:, :])
 
 
 def weight_grads(core_id, pairs, members):
     rows, hidden_width = pairs[0][0].shape
     width = pairs[1][0].shape[1]
     down_rows, up_rows = hidden_width // members // 2, width // members // 2
-    out_rows = 2 * down_rows + up_rows + EXTRA
+    out_rows = 2 * down_rows + up_rows
     flat = pl.BlockSpec((rows, width), lambda i, core: (0, 0))
     tall = pl.BlockSpec((up_rows, rows), lambda i, core: (2 * i + core[0], 0))
     specs = [
@@ -600,20 +597,15 @@
     first_core = core_id[0] == 0
     count = own.shape[0]
     width = own.shape[2]
-    joint_rows = JOINT_ROWS
-    piece_rows = own.shape[1] - joint_rows - 16
+    piece_rows = g_qkv.shape[0] // (count // 2)
+    joint_end = own.shape[1] - VECTOR_ROWS
     up_rows = g_up.shape[0] // 2
     down_rows = g_down.shape[0] // 2
     sums = jnp.zeros(vectors.shape, jnp.float32)
     for core in range(2):
         pick = first_core if core == 0 else jnp.logical_not(first_core)
-        joint = jnp.concatenate(
-            [
-                jnp.where(pick, own[i, :joint_rows, :], other[i, :joint_rows, :])
-                for i in range(count)
-            ],
-            0,
-        ).astype(jnp.float32)
+        blocks = [jnp.where(pick, own[i], other[i]).astype(jnp.float32) for i in range(count)]
+        joint = jnp.concatenate([block[piece_rows:joint_end] for block in blocks], 0)
         g_down[core * down_rows : (core + 1) * down_rows, :] = joint[:down_rows]
         place = down_rows
         for panel in range(g_up.shape[1] // width):
@@ -622,16 +614,14 @@
             )
             place += up_rows
         g_out[core * up_rows : (core + 1) * up_rows, :] = joint[place : place + up_rows]
-        for i in range(count):
+        for i, block in enumerate(blocks):
             x_id, group = i // 2, (i % 2) * 2 + core
-            piece = jnp.where(pick, own[i, joint_rows:, :], other[i, joint_rows:, :])
-            piece = piece.astype(jnp.float32)
             for part in range(3):
                 start = part * width + group * WIDTH
-                g_qkv[x_id * piece_rows : (x_id + 1) * piece_rows, start : start + WIDTH] = piece[
+                g_qkv[x_id * piece_rows : (x_id + 1) * piece_rows, start : start + WIDTH] = block[
                     :piece_rows, part * WIDTH : (part + 1) * WIDTH
                 ]
-            sums += piece[piece_rows : piece_rows + 4, :]
+            sums += block[joint_end:]
     vectors[...] = sums
 
 
@@ -891,12 +881,11 @@
     )
     vector_parts = vector_parts.astype(jnp.bfloat16).reshape(fsdp_count, 4, 3 * WIDTH)
     vector_share = sum_low(exchange(vector_parts, "fsdp"))
-    vector_share = jnp.pad(vector_share, ((0, 12), (0, 0)))
-    qkv_piece = jnp.concatenate([qkv_piece, vector_share], 0)
-    qkv_piece = jnp.pad(qkv_piece, ((0, 0), (0, model_width - 3 * WIDTH)))
+    wide = ((0, 0), (0, model_width - 3 * WIDTH))
+    qkv_piece, vector_share = jnp.pad(qkv_piece, wide), jnp.pad(vector_share, wide)
     joint_piece = sum_low(exchange(share.reshape(8, -1, model_width), ("x", "yh")))
     joint_piece, layer_out = lax.optimization_barrier((joint_piece, layer_out))
-    both = spread(jnp.concatenate([joint_piece, qkv_piece], 0), ("x", "yh"))
+    both = spread(jnp.concatenate([qkv_piece, joint_piece, vector_share], 0), ("x", "yh"))
     g_qkv, g_out, g_up, g_down, vector_sum = unpack(
         core_number, both, swap(both), shard, mlp_in.shape[2], mlp_out.shape[1]
     )

time: 404 us -> 402 us (level)
  transfers between devices with their start and end apart: 31 -> 31, of which waited for: 14 -> 14; matrix products, arithmetic and copies ran while one was open for 3% -> 4% of each run, Pallas kernels for 11% -> 11%
where the time goes in v6:
time: 402 us; the launch traced here: 395 us
  Pallas kernels  98.8 us (25%)
  blocking collectives  97.5 us (24%)
  waiting for transfers between devices  75.8 us (19%)
  starting transfers between devices  68 us (17%)
  local copies, waits for them, and re-layouts  26.6 us (7%)
  between operations  22.9 us (6%)
  other arithmetic  5.73 us (1%)
    all_to_all x5, blocking collectives, exchange(): return lax.all_to_all(value, axes, 0, 0, tiled=True)  97.5 us
    all_to_all x7, starting transfers between devices, exchange(): return lax.all_to_all(value, axes, 0, 0, tiled=True)  39.4 us
    all_to_all x7, waiting for transfers between devices, exchange(): return lax.all_to_all(value, axes, 0, 0, tiled=True)  25 us
    pallas_call x2, Pallas kernels, attend_back(): pl.pallas_call(attend_back_body, grid_spec=pltpu.PrefetchScalarGridSpec(n...  24.3 us
    pallas_call x2, Pallas kernels, feed_back(): pl.pallas_call(body, in_specs=[pl.BlockSpec(memory_space=pltpu.VMEM)] * l...  22.8 us
    pallas_call x2, Pallas kernels, attend(): pl.pallas_call(attend_body, grid_spec=pltpu.PrefetchScalarGridSpec(num_sc...  19.3 us
    pallas_call x2, Pallas kernels, feed_forward(): pl.pallas_call(feed_forward_body, in_specs=feed_specs(5), out_specs=pl.Bl...  15.5 us
    unnamed x114, local copies, waits for them, and re-layouts  14 us
  transfers between devices with their start and end apart: 31, of which 14 were waited for; matrix products, arithmetic and copies ran while one was open for 4% of the time, Pallas kernels for 11%

profile of v6, /device:TPU:1, one launch (start us, length us, event | category | flops | bytes accessed | tf_op | source)
XLA Modules:
  0.0 395.4 jit_solution(11996807308142073152)
XLA Ops:
  13.7 2.5 collective-permute-start.1
  16.3 2.2 collective-permute-start
  19.3 3.3 all-to-all-start
  34.0 8.0 %all-to-all-start.1 = ((bf16[16,64,384]{2,1,0:T(8,128)(2,1)}), bf16[16,64,384]{2,1,0:T(8,128)(2,1)S(1)}, u32[]{:S(2)}, u32[]{:S(2)}) async-start(bf16[16,64,384]{2,1,0:T(8,128)(2,1)} %bitcast.19), calls=%async_computation.1 | async-start | bytes 1572864 | tf_op jit(solution)/shard_map/all_to_all | solution.py:665
  42.1 3.2 collective-permute-start.2
  45.3 11.6 %collective-permute-done.2.w2 = bf16[192,576]{1,0:T(8,128)(2,1)S(1)} collective-permute-done((bf16[192,576]{1,0:T(8,128)(2,1)S(1)}, bf16[192,576]{1,0:T(8,128)(2,1)S(1)}, u32[]{:S(2)}, u32[]{:S(2)}) %collective-permute-start.2) | collective-permute-done | bytes 221216 | tf_op jit(solution)/shard_map/ppermute | solution.py:697
  61.4 10.3 %shard_map.178 = (bf16[1024,576]{1,0:T(8,128)(2,1)}, bf16[1024,192]{1,0:T(8,128)(2,1)}, f32[8,1024]{1,0:T(8,128)}) custom-call(s32[32]{0:T(128)S(1)} %copy-done.33, s32[3]{0:T(128)S(1)} %pad_add_fusion.ids, bf16[1024,384]{1,0:T(8,128)(2,1)S(1)} %bitcast.72, bf16[1024,384]{1,0:T(8,128)(2,1)S(1)} %collective-permute-done.3.other, ...), custom_call_target="tpu_custom_call" | custom-call | flops 805306368 | bytes 1572864 | tf_op jit(solution)/shard_map/pallas_call | solution.py:110
  71.7 7.4 %all-to-all-start.2 = ((bf16[16,64,192]{2,1,0:T(8,128)(2,1)}), bf16[16,64,192]{2,1,0:T(8,128)(2,1)S(1)}, u32[]{:S(2)}, u32[]{:S(2)}) async-start(bf16[16,64,192]{2,1,0:T(8,128)(2,1)} %bitcast.23), calls=%async_computation.2 | async-start | bytes 1048576 | tf_op jit(solution)/shard_map/all_to_all | solution.py:665
  79.3 10.9 %all-to-all-done.2.mixed = bf16[16,64,192]{2,1,0:T(8,128)(2,1)S(1)} async-done(((bf16[16,64,192]{2,1,0:T(8,128)(2,1)}), bf16[16,64,192]{2,1,0:T(8,128)(2,1)S(1)}, u32[]{:S(2)}, u32[]{:S(2)}) %all-to-all-start.2) | async-done | bytes 393248 | tf_op jit(solution)/shard_map/all_to_all | solution.py:665
  90.2 7.4 %shard_map.179 = bf16[256,768]{1,0:T(8,128)(2,1)S(1)} custom-call(bf16[16,64,192]{2,1,0:T(8,128)(2,1)S(1)} %all-to-all-done.2.mixed, bf16[256,768]{1,0:T(8,128)(2,1)S(1)} %bitcast.67, bf16[8,864,768]{2,1,0:T(8,128)(2,1)} %bitcast.75, f32[8,768]{1,0:T(8,128)S(1)} %reshape.299.vectors, f32[4,768]{1,0:T(4,128)S(1)} %reshape.305.up_bias), custom_call_target="tpu_custom_call" | custom-call | flops 2717908992 | bytes 10616832 | tf_op jit(solution)/shard_map/pallas_call | solution.py:381
  97.6 2.3 collective-permute-start.4
  100.1 6.9 %collective-permute-done.4 = bf16[256,768]{1,0:T(8,128)(2,1)S(1)} collective-permute-done((bf16[256,768]{1,0:T(8,128)(2,1)S(1)}, bf16[256,768]{1,0:T(8,128)(2,1)S(1)}, u32[]{:S(2)}, u32[]{:S(2)}) %collective-permute-start.4) | collective-permute-done | bytes 393248 | tf_op jit(solution)/shard_map/ppermute | solution.py:857
  108.0 20.8 %all_to_all.60 = bf16[16,64,384]{2,1,0:T(8,128)(2,1)S(1)} all-to-all(bf16[16,64,384]{2,1,0:T(8,128)(2,1)S(1)} %bitcast.83), channel_id=1, replica_groups=mesh['section'=2,'x'=4,'yh'=2,'core'=2,'fsdp'=4] {'x','yh','core'}, dimensions={0} | all-to-all | bytes 1572864 | tf_op jit(solution)/shard_map/all_to_all | solution.py:665
  129.4 1.7 collective-permute-done.5.other
  131.1 9.0 %shard_map.180 = (bf16[1024,576]{1,0:T(8,128)(2,1)S(1)}, bf16[1024,192]{1,0:T(8,128)(2,1)S(1)}, f32[8,1024]{1,0:T(8,128)S(1)}) custom-call(s32[32]{0:T(128)S(1)} %copy-done.33, s32[3]{0:T(128)S(1)} %pad_add_fusion.ids, bf16[1024,384]{1,0:T(8,128)(2,1)S(1)} %bitcast.69, bf16[1024,384]{1,0:T(8,128)(2,1)S(1)} %collective-permute-done.5.other, ...), custom_call_target="tpu_custom_call" | custom-call | flops 805306368 | bytes 1572864 | tf_op jit(solution)/shard_map/pallas_call | solution.py:110
  140.2 14.7 %all_to_all.61.mixed = bf16[16,64,192]{2,1,0:T(8,128)(2,1)} all-to-all(bf16[16,64,192]{2,1,0:T(8,128)(2,1)S(1)} %bitcast.73), channel_id=1, replica_groups=mesh['section'=2,'x'=4,'yh'=2,'core'=2,'fsdp'=4] {'x','yh','core'}, dimensions={0} | all-to-all | bytes 786432 | tf_op jit(solution)/shard_map/all_to_all | solution.py:665
  154.9 12.6 %shard_map.181 = (bf16[16,64,192]{2,1,0:T(8,128)(2,1)}, f32[256,768]{1,0:T(8,128)}, bf16[256,3072]{1,0:T(8,128)(2,1)}, bf16[768,256]{1,0:T(8,128)(2,1)}, bf16[76...) custom-call(bf16[16,64,192]{2,1,0:T(8,128)(2,1)} %all_to_all.61.mixed, ...), custom_call_target="tpu_custom_call" | custom-call | flops 4227858432 | bytes 14155776 | tf_op jit(solution)/shard_map/pallas_call | solution.py:510
  167.4 16.3 %all_to_all.62 = bf16[16,64,192]{2,1,0:T(8,128)(2,1)S(1)} all-to-all(bf16[16,64,192]{2,1,0:T(8,128)(2,1)} %get-tuple-element.87), channel_id=1, replica_groups=mesh['section'=2,'x'=4,'yh'=2,'core'=2,'fsdp'=4] {'x','yh','core'}, dimensions={0} | all-to-all | bytes 786432 | tf_op jit(solution)/shard_map/all_to_all | solution.py:665
  183.8 12.1 %shard_map.182 = (bf16[1024,576]{1,0:T(8,128)(2,1)}, bf16[1024,384]{1,0:T(8,128)(2,1)S(1)}, bf16[1024,384]{1,0:T(8,128)(2,1)S(1)}) custom-call(s32[32]{0:T(128)S(1)} %copy-done.33, s32[3]{0:T(128)S(1)} %pad_add_fusion.ids, bf16[1024,576]{1,0:T(8,128)(2,1)S(1)} %get-tuple-element.85.joined, bf16[1024,192]{1,0:T(8,128)(2,1)S(1)} %bitcast.74, ...), custom_call_target="tpu_custom_call" | custom-call | flops 2013265920 | bytes 3145728 | tf_op jit(solution)/shard_map/pallas_call | solution.py:203
  197.3 3.0 collective-permute-done.6
  200.5 17.5 %all_to_all.63.returned = bf16[16,64,384]{2,1,0:T(8,128)(2,1)S(1)} all-to-all(bf16[16,64,384]{2,1,0:T(8,128)(2,1)S(1)} %bitcast.84), channel_id=1, replica_groups=mesh['section'=2,'x'=4,'yh'=2,'core'=2,'fsdp'=4] {'x','yh','core'}, dimensions={0} | all-to-all | bytes 1572864 | tf_op jit(solution)/shard_map/all_to_all | solution.py:665
  218.1 1.4 shard_map.183
  221.6 10.4 %collective-permute-done.7 = bf16[256,768]{1,0:T(8,128)(2,1)} collective-permute-done((bf16[256,768]{1,0:T(8,128)(2,1)}, bf16[256,768]{1,0:T(8,128)(2,1)}, u32[]{:S(2)}, u32[]{:S(2)}) %collective-permute-start.7) | collective-permute-done | bytes 393248 | tf_op jit(solution)/shard_map/ppermute | solution.py:865
  232.0 1.9 broadcast_select_fusion.1.grad_low
  234.7 10.2 %shard_map.184 = (bf16[16,64,192]{2,1,0:T(8,128)(2,1)}, f32[256,768]{1,0:T(8,128)}, bf16[256,3072]{1,0:T(8,128)(2,1)}, bf16[256,768]{1,0:T(8,128)(2,1)}, f32[4,768]{1,0:T(4,128)}, /*index=5*/f32[4,768]{1,0:T(4,128)}) custom-call(bf16[8,864,768]{2,1,0:T(8,128)(2,1)} %bitcast.77, f32[8,768]{1,0:T(8,128)} %copy-done.9, ...), custom_call_target="tpu_custom_call" | custom-call | flops 4227858432 | bytes 14155776 | tf_op jit(solution)/shard_map/pallas_call | solution.py:510
  246.7 4.1 %all-to-all-start.7 = ((bf16[16,64,192]{2,1,0:T(8,128)(2,1)}), bf16[16,64,192]{2,1,0:T(8,128)(2,1)}, u32[]{:S(2)}, u32[]{:S(2)}) async-start(bf16[16,64,192]{2,1,0:T(8,128)(2,1)} %get-tuple-element.100), calls=%async_computation.7 | async-start | bytes 1048576 | tf_op jit(solution)/shard_map/all_to_all | solution.py:665
  252.9 8.0 %shard_map.185 = bf16[4,864,768]{2,1,0:T(8,128)(2,1)} custom-call(s32[1]{0:T(128)} %bitcast.9.core_id, bf16[256,3072]{1,0:T(8,128)(2,1)S(1)} %copy-done.5, bf16[256,3072]{1,0:T(8,128)(2,1)} %collective-permute-done.8.active_other, bf16[256,768]{1,0:T(8,128)(2,1)S(1)} %copy-done.6, bf16[256,768]{1,0:T(8,128)(2,1)} %collective-permute-done.11.grad_low_other, ...), custom_call_target="tpu_custom_call" | custom-call | flops 2717908992 | bytes 5308416 | tf_op jit(solution)/shard_map/pallas_call | solution.py:281
  264.7 12.1 %shard_map.186 = (bf16[1024,576]{1,0:T(8,128)(2,1)S(1)}, bf16[1024,384]{1,0:T(8,128)(2,1)S(1)}, bf16[1024,384]{1,0:T(8,128)(2,1)S(1)}) custom-call(s32[32]{0:T(128)S(1)} %copy-done.34, s32[3]{0:T(128)S(1)} %pad_add_fusion.ids, bf16[1024,576]{1,0:T(8,128)(2,1)S(1)} %copy-done.38, bf16[1024,192]{1,0:T(8,128)(2,1)} %bitcast.31.grad_mixed, ...), custom_call_target="tpu_custom_call" | custom-call | flops 2013265920 | bytes 3145728 | tf_op jit(solution)/shard_map/pallas_call | solution.py:203
  276.8 1.4 collective-permute-start.17
  278.2 1.9 collective-permute-done.17
  281.2 5.6 %all-to-all-start.9 = ((bf16[16,64,384]{2,1,0:T(8,128)(2,1)}), bf16[16,64,384]{2,1,0:T(8,128)(2,1)S(1)}, u32[]{:S(2)}, u32[]{:S(2)}) async-start(bf16[16,64,384]{2,1,0:T(8,128)(2,1)} %bitcast.35), calls=%async_computation.10 | async-start | bytes 1572864 | tf_op jit(solution)/shard_map/all_to_all | solution.py:665
  289.3 2.8 shard_map.187
  292.1 1.4 collective-permute-start.14
  293.5 2.4 collective-permute-start.15
  297.2 3.7 all-to-all-done.9.returned
  300.8 1.4 shard_map.189
  303.3 4.4 %all-to-all-start.10 = ((bf16[4,4,576]{2,1,0:T(4,128)(2,1)}), bf16[4,4,576]{2,1,0:T(4,128)(2,1)S(1)}, u32[]{:S(2)}, u32[]{:S(2)}) async-start(bf16[4,4,576]{2,1,0:T(4,128)(2,1)} %convert_element_type.133), calls=%async_computation.11 | async-start | bytes 40960 | tf_op jit(solution)/shard_map/all_to_all | solution.py:665
  307.7 1.9 collective-permute-done.15
  309.7 9.2 %reduce-scatter.2.cloned.1.call-done = bf16[864,768]{1,0:T(8,128)(2,1)} async-done(((bf16[3456,768]{1,0:T(8,128)(2,1)}), bf16[864,768]{1,0:T(8,128)(2,1)}) %reduce-scatter.2.cloned.1.call-update) | async-done | bytes 1327120 | tf_op jit(solution)/shard_map/reduce_scatter | solution.py:819
  318.9 2.3 reshape.314
  321.2 6.6 %all-to-all-start.8 = ((bf16[8,108,768]{2,1,0:T(8,128)(2,1)}), bf16[8,108,768]{2,1,0:T(8,128)(2,1)S(1)}, u32[]{:S(2)}, u32[]{:S(2)}) async-start(bf16[8,108,768]{2,1,0:T(8,128)(2,1)} %reshape.314), calls=%async_computation.9 | async-start | bytes 2752512 | tf_op jit(solution)/shard_map/all_to_all | solution.py:665
  327.9 2.7 collective-permute-start.20
  330.6 8.1 %shard_map.188 = bf16[256,768]{1,0:T(8,128)(2,1)} custom-call(bf16[16,64,192]{2,1,0:T(8,128)(2,1)S(1)} %copy-done.4, bf16[256,768]{1,0:T(8,128)(2,1)S(1)} %copy-done.3, bf16[8,864,768]{2,1,0:T(8,128)(2,1)} %bitcast.78, f32[8,768]{1,0:T(8,128)S(1)} %copy-done.11, f32[4,768]{1,0:T(4,128)S(1)} %copy-done.20), custom_call_target="tpu_custom_call" | custom-call | flops 2717908992 | bytes 10616832 | tf_op jit(solution)/shard_map/pallas_call | solution.py:381
  338.8 9.3 %all-to-all-done.8 = bf16[8,108,768]{2,1,0:T(8,128)(2,1)S(1)} async-done(((bf16[8,108,768]{2,1,0:T(8,128)(2,1)}), bf16[8,108,768]{2,1,0:T(8,128)(2,1)S(1)}, u32[]{:S(2)}, u32[]{:S(2)}) %all-to-all-start.8) | async-done | bytes 1327136 | tf_op jit(solution)/shard_map/all_to_all | solution.py:665
  348.5 28.2 %all_to_all.64.own = bf16[8,160,768]{2,1,0:T(8,128)(2,1)S(1)} all-to-all(bf16[8,160,768]{2,1,0:T(8,128)(2,1)S(1)} %broadcast_in_dim.107), channel_id=1, replica_groups=mesh['section'=2,'x'=4,'yh'=2,'core'=2,'fsdp'=4] {'x','yh'}, dimensions={0} | all-to-all | bytes 3932160 | tf_op jit(solution)/shard_map/all_to_all | solution.py:665
  376.8 2.7 collective-permute-start.21
  379.4 3.6 collective-permute-done.21.other
  383.0 3.3 shard_map.190
  (227 shorter events, 37.7 us)
Async XLA Ops:
  7.2 83.0 %all-gather.3.cloned.1.call-start = ((), (), s32[]{:S(2)}) async-start(), calls=%async_computation.14 | async-start | bytes 11943936 | tf_op jit(solution)/shard_map/all_gather | solution.py:751
  12.0 18.9 %copy-start.45 = (bf16[4,1,64,768]{3,2,1,0:T(8,128)(2,1)S(1)}, bf16[4,1,64,768]{3,2,1,0:T(8,128)(2,1)}, u32[]{:S(2)}) copy-start(bf16[4,1,64,768]{3,2,1,0:T(8,128)(2,1)} %param.11) | copy-start | bytes 1179652
  13.5 20.5 %copy-start.41 = (bf16[192,3,1,192]{0,3,1,2:T(8,128)(2,1)}, bf16[192,3,1,192]{0,3,1,2:T(8,128)(2,1)S(1)}, u32[]{:S(2)}) copy-start(bf16[192,3,1,192]{0,3,1,2:T(8,128)(2,1)S(1)} %copy.40) | copy-start | bytes 663556
  13.7 170.0 %copy-start.17 = (bf16[192,576]{1,0:T(8,128)(2,1)}, bf16[192,576]{1,0:T(8,128)(2,1)S(1)}, u32[]{:S(2)}) copy-start(bf16[192,576]{1,0:T(8,128)(2,1)S(1)} %copy.27.w0) | copy-start | bytes 663556
  13.7 18.2 %collective-permute-start.1 = (bf16[192,576]{1,0:T(8,128)(2,1)S(1)}, bf16[192,576]{1,0:T(8,128)(2,1)S(1)}, u32[]{:S(2)}, u32[]{:S(2)}) collective-permute-start(bf16[192,576]{1,0:T(8,128)(2,1)S(1)} %copy.27.w0), channel_id=1, source_target_pairs={{0,1},{1,2},{2,3},{3,0},{4,5},{5,6},{6,7},{7,4},{8,9},{9,10},{10,1... | collective-permute-start | bytes 663560 | tf_op jit(solution)/shard_map/ppermute | solution.py:697
  16.3 15.7 %collective-permute-start = (bf16[192,576]{1,0:T(8,128)(2,1)S(1)}, bf16[192,576]{1,0:T(8,128)(2,1)S(1)}, u32[]{:S(2)}, u32[]{:S(2)}) collective-permute-start(bf16[192,576]{1,0:T(8,128)(2,1)S(1)} %copy.27.w0), channel_id=1, source_target_pairs={{0,3},{1,0},{2,1},{3,2},{4,7},{5,4},{6,5},{7,6},{8,11},{9,8},{10,9... | collective-permute-start | bytes 663560 | tf_op jit(solution)/shard_map/ppermute | solution.py:697
  19.3 12.6 %all-to-all-start = ((bf16[4,4,576]{2,1,0:T(4,128)(2,1)}), bf16[4,4,576]{2,1,0:T(4,128)(2,1)S(1)}, u32[]{:S(2)}, u32[]{:S(2)}) async-start(bf16[4,4,576]{2,1,0:T(4,128)(2,1)} %broadcast_in_dim.94), calls=%async_computation | async-start | bytes 40960 | tf_op jit(solution)/shard_map/all_to_all | solution.py:665
  32.0 151.8 %copy-start.23 = (bf16[192,576]{1,0:T(8,128)(2,1)}, bf16[192,576]{1,0:T(8,128)(2,1)S(1)}, u32[]{:S(2)}) copy-start(bf16[192,576]{1,0:T(8,128)(2,1)S(1)} %collective-permute-done.1.w3) | copy-start | bytes 663556
  32.0 99.1 %copy-start.25 = (bf16[192,576]{1,0:T(8,128)(2,1)}, bf16[192,576]{1,0:T(8,128)(2,1)S(1)}, u32[]{:S(2)}) copy-start(bf16[192,576]{1,0:T(8,128)(2,1)S(1)} %collective-permute-done.w1) | copy-start | bytes 663556
  34.0 26.4 %copy-start.33 = (s32[32]{0:T(128)S(1)}, s32[32]{0:T(128)}, u32[]{:S(2)}) copy-start(s32[32]{0:T(128)} %table.7) | copy-start | bytes 388
  34.0 23.6 %all-to-all-start.1 = ((bf16[16,64,384]{2,1,0:T(8,128)(2,1)}), bf16[16,64,384]{2,1,0:T(8,128)(2,1)S(1)}, u32[]{:S(2)}, u32[]{:S(2)}) async-start(bf16[16,64,384]{2,1,0:T(8,128)(2,1)} %bitcast.19), calls=%async_computation.1 | async-start | bytes 1572864 | tf_op jit(solution)/shard_map/all_to_all | solution.py:665
  42.1 14.8 %collective-permute-start.2 = (bf16[192,576]{1,0:T(8,128)(2,1)S(1)}, bf16[192,576]{1,0:T(8,128)(2,1)S(1)}, u32[]{:S(2)}, u32[]{:S(2)}) collective-permute-start(bf16[192,576]{1,0:T(8,128)(2,1)S(1)} %copy.27.w0), channel_id=1, source_target_pairs={{0,2},{1,3},{2,0},{3,1},{4,6},{5,7},{6,4},{7,5},{8,10},{9,11},{10,... | collective-permute-start | bytes 663560 | tf_op jit(solution)/shard_map/ppermute | solution.py:697
  57.6 2.8 collective-permute-start.3
  71.7 18.5 %all-to-all-start.2 = ((bf16[16,64,192]{2,1,0:T(8,128)(2,1)}), bf16[16,64,192]{2,1,0:T(8,128)(2,1)S(1)}, u32[]{:S(2)}, u32[]{:S(2)}) async-start(bf16[16,64,192]{2,1,0:T(8,128)(2,1)} %bitcast.23), calls=%async_computation.2 | async-start | bytes 1048576 | tf_op jit(solution)/shard_map/all_to_all | solution.py:665
  79.2 18.4 %copy-start.19 = (f32[4,768]{1,0:T(4,128)}, f32[4,768]{1,0:T(4,128)S(1)}, u32[]{:S(2)}) copy-start(f32[4,768]{1,0:T(4,128)S(1)} %reshape.305.up_bias) | copy-start | bytes 36868
  79.3 18.3 %copy-start.9 = (f32[8,768]{1,0:T(8,128)}, f32[8,768]{1,0:T(8,128)S(1)}, u32[]{:S(2)}) copy-start(f32[8,768]{1,0:T(8,128)S(1)} %reshape.299.vectors) | copy-start | bytes 73732
  97.6 9.4 %collective-permute-start.4 = (bf16[256,768]{1,0:T(8,128)(2,1)S(1)}, bf16[256,768]{1,0:T(8,128)(2,1)S(1)}, u32[]{:S(2)}, u32[]{:S(2)}) collective-permute-start(bf16[256,768]{1,0:T(8,128)(2,1)S(1)} %shard_map.179), channel_id=1, source_target_pairs={{0,64},{1,65},{2,66},{3,67},{4,68},{5,69},{6,70},{7,71},{8,72},{9,... | collective-permute-start | bytes 1179656 | tf_op jit(solution)/shard_map/ppermute | solution.py:857
  107.9 21.3 %copy-start.42 = (bf16[192,3,1,192]{0,3,1,2:T(8,128)(2,1)S(1)}, bf16[192,3,1,192]{0,3,1,2:T(8,128)(2,1)}, u32[]{:S(2)}) copy-start(bf16[192,3,1,192]{0,3,1,2:T(8,128)(2,1)} %copy-done.41) | copy-start | bytes 663556
  108.0 23.1 %copy-start.30 = (bf16[192,576]{1,0:T(8,128)(2,1)S(1)}, bf16[192,576]{1,0:T(8,128)(2,1)}, u32[]{:S(2)}) copy-start(bf16[192,576]{1,0:T(8,128)(2,1)} %copy-done.28) | copy-start | bytes 663556
  128.8 2.3 collective-permute-start.5
  140.2 43.6 %copy-start.37 = (bf16[1024,576]{1,0:T(8,128)(2,1)}, bf16[1024,576]{1,0:T(8,128)(2,1)S(1)}, u32[]{:S(2)}) copy-start(bf16[1024,576]{1,0:T(8,128)(2,1)S(1)} %get-tuple-element.85.joined) | copy-start | bytes 3538948
  140.2 43.6 %copy-start.39 = (f32[8,1024]{1,0:T(8,128)}, f32[8,1024]{1,0:T(8,128)S(1)}, u32[]{:S(2)}) copy-start(f32[8,1024]{1,0:T(8,128)S(1)} %get-tuple-element.88.log_total) | copy-start | bytes 98308
  154.9 28.9 %copy-start.26 = (bf16[192,576]{1,0:T(8,128)(2,1)S(1)}, bf16[192,576]{1,0:T(8,128)(2,1)}, u32[]{:S(2)}) copy-start(bf16[192,576]{1,0:T(8,128)(2,1)} %copy-done.25) | copy-start | bytes 663556
  154.9 28.9 %copy-start.31 = (bf16[192,576]{1,0:T(8,128)(2,1)S(1)}, bf16[192,576]{1,0:T(8,128)(2,1)}, u32[]{:S(2)}) copy-start(bf16[192,576]{1,0:T(8,128)(2,1)} %copy-done.28) | copy-start | bytes 663556
  196.0 4.3 %collective-permute-start.6 = (bf16[1024,384]{1,0:T(8,128)(2,1)S(1)}, bf16[1024,384]{1,0:T(8,128)(2,1)S(1)}, u32[]{:S(2)}, u32[]{:S(2)}) collective-permute-start(bf16[1024,384]{1,0:T(8,128)(2,1)S(1)} %get-tuple-element.90), channel_id=1, source_target_pairs={{0,4},{4,0},{1,5},{5,1},{2,6},{6,2},{3,7},{7,3},{8,12},{12,8},{9,1... | collective-permute-start | bytes 2359304 | tf_op jit(solution)/shard_map/ppermute | solution.py:669
  197.3 37.3 %collective-permute-start.8 = (bf16[256,3072]{1,0:T(8,128)(2,1)S(1)}, bf16[256,3072]{1,0:T(8,128)(2,1)}, u32[]{:S(2)}, u32[]{:S(2)}) collective-permute-start(bf16[256,3072]{1,0:T(8,128)(2,1)S(1)} %copy-done.5), channel_id=1, source_target_pairs={{0,4},{4,0},{1,5},{5,1},{2,6},{6,2},{3,7},{7,3},{8,12},{12,8},{9,1... | collective-permute-start | bytes 4718600 | tf_op jit(solution)/shard_map/ppermute | solution.py:669
  200.5 17.5 %copy-start.3 = (bf16[256,768]{1,0:T(8,128)(2,1)S(1)}, bf16[256,768]{1,0:T(8,128)(2,1)}, u32[]{:S(2)}) copy-start(bf16[256,768]{1,0:T(8,128)(2,1)} %copy-done.2) | copy-start | bytes 1179652
  200.5 17.5 %copy-start.8 = (f32[256,768]{1,0:T(8,128)S(1)}, f32[256,768]{1,0:T(8,128)}, u32[]{:S(2)}) copy-start(f32[256,768]{1,0:T(8,128)} %get-tuple-element.91.grad_middle) | copy-start | bytes 2359300
  219.5 12.5 %collective-permute-start.7 = (bf16[256,768]{1,0:T(8,128)(2,1)}, bf16[256,768]{1,0:T(8,128)(2,1)}, u32[]{:S(2)}, u32[]{:S(2)}) collective-permute-start(bf16[256,768]{1,0:T(8,128)(2,1)} %get-tuple-element.92), channel_id=1, source_target_pairs={{64,0},{65,1},{66,2},{67,3},{68,4},{69,5},{70,6},{71,7},{72,8},{73... | collective-permute-start | bytes 1179656 | tf_op jit(solution)/shard_map/ppermute | solution.py:865
  220.8 13.1 %collective-permute-start.9 = (bf16[768,256]{1,0:T(8,128)(2,1)S(1)}, bf16[768,256]{1,0:T(8,128)(2,1)S(1)}, u32[]{:S(2)}, u32[]{:S(2)}) collective-permute-start(bf16[768,256]{1,0:T(8,128)(2,1)S(1)} %copy-done.12), channel_id=1, source_target_pairs={{0,4},{4,0},{1,5},{5,1},{2,6},{6,2},{3,7},{7,3},{8,12},{12,8},{9,1... | collective-permute-start | bytes 1179656 | tf_op jit(solution)/shard_map/ppermute | solution.py:669
  221.3 13.4 %collective-permute-start.10 = (bf16[768,256]{1,0:T(8,128)(2,1)}, bf16[768,256]{1,0:T(8,128)(2,1)}, u32[]{:S(2)}, u32[]{:S(2)}) collective-permute-start(bf16[768,256]{1,0:T(8,128)(2,1)} %get-tuple-element.106.mixed), channel_id=1, source_target_pairs={{0,4},{4,0},{1,5},{5,1},{2,6},{6,2},{3,7},{7,3},{8,12},{12,8},{9,1... | collective-permute-start | bytes 1179656 | tf_op jit(solution)/shard_map/ppermute | solution.py:669
  244.9 6.0 %collective-permute-start.12 = (bf16[256,3072]{1,0:T(8,128)(2,1)}, bf16[256,3072]{1,0:T(8,128)(2,1)}, u32[]{:S(2)}, u32[]{:S(2)}) collective-permute-start(bf16[256,3072]{1,0:T(8,128)(2,1)} %get-tuple-element.105.grad_hidden), channel_id=1, source_target_pairs={{0,4},{4,0},{1,5},{5,1},{2,6},{6,2},{3,7},{7,3},{8,12},{12,8},{9,1... | collective-permute-start | bytes 4718600 | tf_op jit(solution)/shard_map/ppermute | solution.py:669
  246.2 4.7 %collective-permute-start.13 = (bf16[256,768]{1,0:T(8,128)(2,1)}, bf16[256,768]{1,0:T(8,128)(2,1)}, u32[]{:S(2)}, u32[]{:S(2)}) collective-permute-start(bf16[256,768]{1,0:T(8,128)(2,1)} %get-tuple-element.108.grad_attn), channel_id=1, source_target_pairs={{0,4},{4,0},{1,5},{5,1},{2,6},{6,2},{3,7},{7,3},{8,12},{12,8},{9,1... | collective-permute-start | bytes 1179656 | tf_op jit(solution)/shard_map/ppermute | solution.py:669
  246.3 4.6 %collective-permute-start.11 = (bf16[256,768]{1,0:T(8,128)(2,1)S(1)}, bf16[256,768]{1,0:T(8,128)(2,1)}, u32[]{:S(2)}, u32[]{:S(2)}) collective-permute-start(bf16[256,768]{1,0:T(8,128)(2,1)S(1)} %copy-done.6), channel_id=1, source_target_pairs={{0,4},{4,0},{1,5},{5,1},{2,6},{6,2},{3,7},{7,3},{8,12},{12,8},{9,1... | collective-permute-start | bytes 1179656 | tf_op jit(solution)/shard_map/ppermute | solution.py:669
  246.7 15.4 %all-to-all-start.7 = ((bf16[16,64,192]{2,1,0:T(8,128)(2,1)}), bf16[16,64,192]{2,1,0:T(8,128)(2,1)}, u32[]{:S(2)}, u32[]{:S(2)}) async-start(bf16[16,64,192]{2,1,0:T(8,128)(2,1)} %get-tuple-element.100), calls=%async_computation.7 | async-start | bytes 1048576 | tf_op jit(solution)/shard_map/all_to_all | solution.py:665
  250.8 68.1 %reduce-scatter.2.cloned.1.call-start = ((), (), s32[]{:S(2)}) async-start(), calls=%async_computation.13 | async-start | bytes 6635520 | tf_op jit(solution)/shard_map/reduce_scatter | solution.py:819
  276.8 3.3 collective-permute-start.17
  281.2 19.6 %all-to-all-start.9 = ((bf16[16,64,384]{2,1,0:T(8,128)(2,1)}), bf16[16,64,384]{2,1,0:T(8,128)(2,1)S(1)}, u32[]{:S(2)}, u32[]{:S(2)}) async-start(bf16[16,64,384]{2,1,0:T(8,128)(2,1)} %bitcast.35), calls=%async_computation.10 | async-start | bytes 1572864 | tf_op jit(solution)/shard_map/all_to_all | solution.py:665
  292.1 15.6 %collective-permute-start.14 = (bf16[192,576]{1,0:T(8,128)(2,1)}, bf16[192,576]{1,0:T(8,128)(2,1)S(1)}, u32[]{:S(2)}, u32[]{:S(2)}) collective-permute-start(bf16[192,576]{1,0:T(8,128)(2,1)} %get-tuple-element.113), channel_id=1, source_target_pairs={{0,16},{16,32},{32,48},{48,0},{1,17},{17,33},{33,49},{49,1},{2,18}... | collective-permute-start | bytes 663560 | tf_op jit(solution)/shard_map/ppermute | solution.py:705
  293.5 16.1 %collective-permute-start.15 = (bf16[192,576]{1,0:T(8,128)(2,1)}, bf16[192,576]{1,0:T(8,128)(2,1)S(1)}, u32[]{:S(2)}, u32[]{:S(2)}) collective-permute-start(bf16[192,576]{1,0:T(8,128)(2,1)} %get-tuple-element.114), channel_id=1, source_target_pairs={{0,32},{16,48},{32,0},{48,16},{1,33},{17,49},{33,1},{49,17},{2,34}... | collective-permute-start | bytes 663560 | tf_op jit(solution)/shard_map/ppermute | solution.py:705
  295.9 13.7 %collective-permute-start.16 = (bf16[192,576]{1,0:T(8,128)(2,1)S(1)}, bf16[192,576]{1,0:T(8,128)(2,1)S(1)}, u32[]{:S(2)}, u32[]{:S(2)}) collective-permute-start(bf16[192,576]{1,0:T(8,128)(2,1)S(1)} %get-tuple-element.115), channel_id=1, source_target_pairs={{0,48},{16,0},{32,16},{48,32},{1,49},{17,1},{33,17},{49,33},{2,50}... | collective-permute-start | bytes 663560 | tf_op jit(solution)/shard_map/ppermute | solution.py:705
  303.3 17.9 %all-to-all-start.10 = ((bf16[4,4,576]{2,1,0:T(4,128)(2,1)}), bf16[4,4,576]{2,1,0:T(4,128)(2,1)S(1)}, u32[]{:S(2)}, u32[]{:S(2)}) async-start(bf16[4,4,576]{2,1,0:T(4,128)(2,1)} %convert_element_type.133), calls=%async_computation.11 | async-start | bytes 40960 | tf_op jit(solution)/shard_map/all_to_all | solution.py:665
  321.2 27.0 %all-to-all-start.8 = ((bf16[8,108,768]{2,1,0:T(8,128)(2,1)}), bf16[8,108,768]{2,1,0:T(8,128)(2,1)S(1)}, u32[]{:S(2)}, u32[]{:S(2)}) async-start(bf16[8,108,768]{2,1,0:T(8,128)(2,1)} %reshape.314), calls=%async_computation.9 | async-start | bytes 2752512 | tf_op jit(solution)/shard_map/all_to_all | solution.py:665
  327.8 10.9 %collective-permute-start.18 = (bf16[48,576]{1,0:T(8,128)(2,1)S(1)}, bf16[48,576]{1,0:T(8,128)(2,1)S(1)}, u32[]{:S(2)}, u32[]{:S(2)}) collective-permute-start(bf16[48,576]{1,0:T(8,128)(2,1)S(1)} %get-tuple-element.161), channel_id=1, source_target_pairs={{0,1},{1,2},{2,3},{3,0},{4,5},{5,6},{6,7},{7,4},{8,9},{9,10},{10,1... | collective-permute-start | bytes 165896 | tf_op jit(solution)/shard_map/ppermute | solution.py:705
  327.9 10.8 %collective-permute-start.20 = (bf16[48,576]{1,0:T(8,128)(2,1)S(1)}, bf16[48,576]{1,0:T(8,128)(2,1)S(1)}, u32[]{:S(2)}, u32[]{:S(2)}) collective-permute-start(bf16[48,576]{1,0:T(8,128)(2,1)S(1)} %get-tuple-element.162), channel_id=1, source_target_pairs={{0,3},{1,0},{2,1},{3,2},{4,7},{5,4},{6,5},{7,6},{8,11},{9,8},{10,9... | collective-permute-start | bytes 165896 | tf_op jit(solution)/shard_map/ppermute | solution.py:705
  330.6 8.2 %collective-permute-start.19 = (bf16[48,576]{1,0:T(8,128)(2,1)S(1)}, bf16[48,576]{1,0:T(8,128)(2,1)S(1)}, u32[]{:S(2)}, u32[]{:S(2)}) collective-permute-start(bf16[48,576]{1,0:T(8,128)(2,1)S(1)} %get-tuple-element.163), channel_id=1, source_target_pairs={{0,2},{1,3},{2,0},{3,1},{4,6},{5,7},{6,4},{7,5},{8,10},{9,11},{10,... | collective-permute-start | bytes 165896 | tf_op jit(solution)/shard_map/ppermute | solution.py:705
  348.5 39.8 %copy-start.1 = (bf16[1,192,3072]{2,1,0:T(8,128)(2,1)S(1)}, bf16[1,192,3072]{2,1,0:T(8,128)(2,1)}, u32[]{:S(2)}) copy-start(bf16[1,192,3072]{2,1,0:T(8,128)(2,1)} %param.17) | copy-start | bytes 3538948
  376.8 6.3 %collective-permute-start.21 = (bf16[8,160,768]{2,1,0:T(8,128)(2,1)S(1)}, bf16[8,160,768]{2,1,0:T(8,128)(2,1)S(1)}, u32[]{:S(2)}, u32[]{:S(2)}) collective-permute-start(bf16[8,160,768]{2,1,0:T(8,128)(2,1)S(1)} %all_to_all.64.own), channel_id=1, source_target_pairs={{0,4},{4,0},{1,5},{5,1},{2,6},{6,2},{3,7},{7,3},{8,12},{12,8},{9,1... | collective-permute-start | bytes 5898248 | tf_op jit(solution)/shard_map/ppermute | solution.py:669
  (37 other events, 181.4 us)
Sparse Core Ops, SparseCore 0:
  11.0 68.1 all-gather.2
  262.2 56.6 reduce-scatter.1

commit v7 on v6

--- a/solution.py
+++ b/solution.py
@@ -744,9 +744,7 @@
     ).reshape(shard, 3 * WIDTH)
     small_all = spread(small, "fsdp").reshape(fsdp_count, -1, shard).astype(jnp.float32)
     w_group = gather_ring(own_columns, "fsdp")
-    small_all, w_group[1], w_group[3] = lax.optimization_barrier(
-        (small_all, w_group[1], w_group[3])
-    )
+    small_all, w_group[2] = lax.optimization_barrier((small_all, w_group[2]))
     packed = pack_weights(attn_out, mlp_in, mlp_out)
     packed = lax.all_gather(packed, ("fsdp", "core"), axis=0)
     model_width = attn_out.shape[2]

time: 402 us -> 403 us (level)
  transfers between devices with their start and end apart: 31 -> 31, of which waited for: 14 -> 15; matrix products, arithmetic and copies ran while one was open for 4% -> 4% of each run, Pallas kernels for 11% -> 11%
where the time goes in v7:
time: 403 us; the launch traced here: 397 us
  Pallas kernels  98.8 us (25%)
  blocking collectives  97.5 us (24%)
  waiting for transfers between devices  76.7 us (19%)
  starting transfers between devices  68.4 us (17%)
  local copies, waits for them, and re-layouts  26.6 us (7%)
  between operations  22.9 us (6%)
  other arithmetic  5.73 us (1%)
    all_to_all x5, blocking collectives, exchange(): return lax.all_to_all(value, axes, 0, 0, tiled=True)  97.5 us
    all_to_all x7, starting transfers between devices, exchange(): return lax.all_to_all(value, axes, 0, 0, tiled=True)  41.8 us
    all_to_all x7, waiting for transfers between devices, exchange(): return lax.all_to_all(value, axes, 0, 0, tiled=True)  25 us
    pallas_call x2, Pallas kernels, attend_back(): pl.pallas_call(attend_back_body, grid_spec=pltpu.PrefetchScalarGridSpec(n...  24.3 us
    pallas_call x2, Pallas kernels, feed_back(): pl.pallas_call(body, in_specs=[pl.BlockSpec(memory_space=pltpu.VMEM)] * l...  22.8 us
    pallas_call x2, Pallas kernels, attend(): pl.pallas_call(attend_body, grid_spec=pltpu.PrefetchScalarGridSpec(num_sc...  19.3 us
    pallas_call x2, Pallas kernels, feed_forward(): pl.pallas_call(feed_forward_body, in_specs=feed_specs(5), out_specs=pl.Bl...  15.5 us
    unnamed x114, local copies, waits for them, and re-layouts  14 us
  transfers between devices with their start and end apart: 31, of which 15 were waited for; matrix products, arithmetic and copies ran while one was open for 4% of the time, Pallas kernels for 11%

profile of v7, /device:TPU:1, one launch (start us, length us, event | category | flops | bytes accessed | tf_op | source)
XLA Modules:
  0.0 396.6 jit_solution(16584451791568992261)
XLA Ops:
  11.7 5.9 %all-to-all-start = ((bf16[4,4,576]{2,1,0:T(4,128)(2,1)}), bf16[4,4,576]{2,1,0:T(4,128)(2,1)S(1)}, u32[]{:S(2)}, u32[]{:S(2)}) async-start(bf16[4,4,576]{2,1,0:T(4,128)(2,1)} %broadcast_in_dim.94), calls=%async_computation | async-start | bytes 40960 | tf_op jit(solution)/shard_map/all_to_all | solution.py:665
  20.4 3.0 collective-permute-start
  34.9 9.1 %all-to-all-start.1 = ((bf16[16,64,384]{2,1,0:T(8,128)(2,1)}), bf16[16,64,384]{2,1,0:T(8,128)(2,1)S(1)}, u32[]{:S(2)}, u32[]{:S(2)}) async-start(bf16[16,64,384]{2,1,0:T(8,128)(2,1)} %bitcast.19), calls=%async_computation.1 | async-start | bytes 1572864 | tf_op jit(solution)/shard_map/all_to_all | solution.py:665
  44.0 2.7 collective-permute-start.1
  46.6 11.6 %collective-permute-done.2.w3 = bf16[192,576]{1,0:T(8,128)(2,1)S(1)} collective-permute-done((bf16[192,576]{1,0:T(8,128)(2,1)S(1)}, bf16[192,576]{1,0:T(8,128)(2,1)S(1)}, u32[]{:S(2)}, u32[]{:S(2)}) %collective-permute-start.2) | collective-permute-done | bytes 221216 | tf_op jit(solution)/shard_map/ppermute | solution.py:697
  63.8 10.3 %shard_map.178 = (bf16[1024,576]{1,0:T(8,128)(2,1)}, bf16[1024,192]{1,0:T(8,128)(2,1)}, f32[8,1024]{1,0:T(8,128)}) custom-call(s32[32]{0:T(128)S(1)} %copy-done.33, s32[3]{0:T(128)S(1)} %pad_add_fusion.ids, bf16[1024,384]{1,0:T(8,128)(2,1)S(1)} %bitcast.72, bf16[1024,384]{1,0:T(8,128)(2,1)S(1)} %collective-permute-done.3.other, ...), custom_call_target="tpu_custom_call" | custom-call | flops 805306368 | bytes 1572864 | tf_op jit(solution)/shard_map/pallas_call | solution.py:110
  74.1 7.3 %all-to-all-start.2 = ((bf16[16,64,192]{2,1,0:T(8,128)(2,1)}), bf16[16,64,192]{2,1,0:T(8,128)(2,1)S(1)}, u32[]{:S(2)}, u32[]{:S(2)}) async-start(bf16[16,64,192]{2,1,0:T(8,128)(2,1)} %bitcast.23), calls=%async_computation.2 | async-start | bytes 1048576 | tf_op jit(solution)/shard_map/all_to_all | solution.py:665
  81.7 10.9 %all-to-all-done.2.mixed = bf16[16,64,192]{2,1,0:T(8,128)(2,1)S(1)} async-done(((bf16[16,64,192]{2,1,0:T(8,128)(2,1)}), bf16[16,64,192]{2,1,0:T(8,128)(2,1)S(1)}, u32[]{:S(2)}, u32[]{:S(2)}) %all-to-all-start.2) | async-done | bytes 393248 | tf_op jit(solution)/shard_map/all_to_all | solution.py:665
  92.6 7.4 %shard_map.179 = bf16[256,768]{1,0:T(8,128)(2,1)S(1)} custom-call(bf16[16,64,192]{2,1,0:T(8,128)(2,1)S(1)} %all-to-all-done.2.mixed, bf16[256,768]{1,0:T(8,128)(2,1)S(1)} %bitcast.67, bf16[8,864,768]{2,1,0:T(8,128)(2,1)} %bitcast.75, f32[8,768]{1,0:T(8,128)S(1)} %reshape.299.vectors, f32[4,768]{1,0:T(4,128)S(1)} %reshape.305.up_bias), custom_call_target="tpu_custom_call" | custom-call | flops 2717908992 | bytes 10616832 | tf_op jit(solution)/shard_map/pallas_call | solution.py:381
  100.0 2.3 collective-permute-start.4
  102.5 6.9 %collective-permute-done.4 = bf16[256,768]{1,0:T(8,128)(2,1)S(1)} collective-permute-done((bf16[256,768]{1,0:T(8,128)(2,1)S(1)}, bf16[256,768]{1,0:T(8,128)(2,1)S(1)}, u32[]{:S(2)}, u32[]{:S(2)}) %collective-permute-start.4) | collective-permute-done | bytes 393248 | tf_op jit(solution)/shard_map/ppermute | solution.py:855
  110.4 20.8 %all_to_all.60 = bf16[16,64,384]{2,1,0:T(8,128)(2,1)S(1)} all-to-all(bf16[16,64,384]{2,1,0:T(8,128)(2,1)S(1)} %bitcast.83), channel_id=1, replica_groups=mesh['section'=2,'x'=4,'yh'=2,'core'=2,'fsdp'=4] {'x','yh','core'}, dimensions={0} | all-to-all | bytes 1572864 | tf_op jit(solution)/shard_map/all_to_all | solution.py:665
  131.8 1.7 collective-permute-done.5.other
  133.5 9.0 %shard_map.180 = (bf16[1024,576]{1,0:T(8,128)(2,1)S(1)}, bf16[1024,192]{1,0:T(8,128)(2,1)S(1)}, f32[8,1024]{1,0:T(8,128)S(1)}) custom-call(s32[32]{0:T(128)S(1)} %copy-done.33, s32[3]{0:T(128)S(1)} %pad_add_fusion.ids, bf16[1024,384]{1,0:T(8,128)(2,1)S(1)} %bitcast.69, bf16[1024,384]{1,0:T(8,128)(2,1)S(1)} %collective-permute-done.5.other, ...), custom_call_target="tpu_custom_call" | custom-call | flops 805306368 | bytes 1572864 | tf_op jit(solution)/shard_map/pallas_call | solution.py:110
  142.6 14.7 %all_to_all.61.mixed = bf16[16,64,192]{2,1,0:T(8,128)(2,1)} all-to-all(bf16[16,64,192]{2,1,0:T(8,128)(2,1)S(1)} %bitcast.73), channel_id=1, replica_groups=mesh['section'=2,'x'=4,'yh'=2,'core'=2,'fsdp'=4] {'x','yh','core'}, dimensions={0} | all-to-all | bytes 786432 | tf_op jit(solution)/shard_map/all_to_all | solution.py:665
  157.3 12.6 %shard_map.181 = (bf16[16,64,192]{2,1,0:T(8,128)(2,1)}, f32[256,768]{1,0:T(8,128)}, bf16[256,3072]{1,0:T(8,128)(2,1)}, bf16[768,256]{1,0:T(8,128)(2,1)}, bf16[76...) custom-call(bf16[16,64,192]{2,1,0:T(8,128)(2,1)} %all_to_all.61.mixed, ...), custom_call_target="tpu_custom_call" | custom-call | flops 4227858432 | bytes 14155776 | tf_op jit(solution)/shard_map/pallas_call | solution.py:510
  169.8 16.3 %all_to_all.62 = bf16[16,64,192]{2,1,0:T(8,128)(2,1)S(1)} all-to-all(bf16[16,64,192]{2,1,0:T(8,128)(2,1)} %get-tuple-element.85), channel_id=1, replica_groups=mesh['section'=2,'x'=4,'yh'=2,'core'=2,'fsdp'=4] {'x','yh','core'}, dimensions={0} | all-to-all | bytes 786432 | tf_op jit(solution)/shard_map/all_to_all | solution.py:665
  186.2 12.1 %shard_map.182 = (bf16[1024,576]{1,0:T(8,128)(2,1)}, bf16[1024,384]{1,0:T(8,128)(2,1)S(1)}, bf16[1024,384]{1,0:T(8,128)(2,1)S(1)}) custom-call(s32[32]{0:T(128)S(1)} %copy-done.33, s32[3]{0:T(128)S(1)} %pad_add_fusion.ids, bf16[1024,576]{1,0:T(8,128)(2,1)S(1)} %get-tuple-element.83.joined, bf16[1024,192]{1,0:T(8,128)(2,1)S(1)} %bitcast.74, ...), custom_call_target="tpu_custom_call" | custom-call | flops 2013265920 | bytes 3145728 | tf_op jit(solution)/shard_map/pallas_call | solution.py:203
  198.4 1.3 collective-permute-start.6
  199.7 3.0 collective-permute-done.6
  202.9 17.5 %all_to_all.63.returned = bf16[16,64,384]{2,1,0:T(8,128)(2,1)S(1)} all-to-all(bf16[16,64,384]{2,1,0:T(8,128)(2,1)S(1)} %bitcast.84), channel_id=1, replica_groups=mesh['section'=2,'x'=4,'yh'=2,'core'=2,'fsdp'=4] {'x','yh','core'}, dimensions={0} | all-to-all | bytes 1572864 | tf_op jit(solution)/shard_map/all_to_all | solution.py:665
  220.5 1.4 shard_map.183
  224.0 10.4 %collective-permute-done.7 = bf16[256,768]{1,0:T(8,128)(2,1)} collective-permute-done((bf16[256,768]{1,0:T(8,128)(2,1)}, bf16[256,768]{1,0:T(8,128)(2,1)}, u32[]{:S(2)}, u32[]{:S(2)}) %collective-permute-start.7) | collective-permute-done | bytes 393248 | tf_op jit(solution)/shard_map/ppermute | solution.py:863
  234.4 1.9 broadcast_select_fusion.1.grad_low
  237.1 10.2 %shard_map.184 = (bf16[16,64,192]{2,1,0:T(8,128)(2,1)}, f32[256,768]{1,0:T(8,128)}, bf16[256,3072]{1,0:T(8,128)(2,1)}, bf16[256,768]{1,0:T(8,128)(2,1)}, f32[4,768]{1,0:T(4,128)}, /*index=5*/f32[4,768]{1,0:T(4,128)}) custom-call(bf16[8,864,768]{2,1,0:T(8,128)(2,1)} %bitcast.77, f32[8,768]{1,0:T(8,128)} %copy-done.9, ...), custom_call_target="tpu_custom_call" | custom-call | flops 4227858432 | bytes 14155776 | tf_op jit(solution)/shard_map/pallas_call | solution.py:510
  249.1 4.1 %all-to-all-start.7 = ((bf16[16,64,192]{2,1,0:T(8,128)(2,1)}), bf16[16,64,192]{2,1,0:T(8,128)(2,1)}, u32[]{:S(2)}, u32[]{:S(2)}) async-start(bf16[16,64,192]{2,1,0:T(8,128)(2,1)} %get-tuple-element.98), calls=%async_computation.7 | async-start | bytes 1048576 | tf_op jit(solution)/shard_map/all_to_all | solution.py:665
  255.3 8.0 %shard_map.185 = bf16[4,864,768]{2,1,0:T(8,128)(2,1)} custom-call(s32[1]{0:T(128)} %bitcast.9.core_id, bf16[256,3072]{1,0:T(8,128)(2,1)S(1)} %copy-done.5, bf16[256,3072]{1,0:T(8,128)(2,1)} %collective-permute-done.8.active_other, bf16[256,768]{1,0:T(8,128)(2,1)S(1)} %copy-done.6, bf16[256,768]{1,0:T(8,128)(2,1)} %collective-permute-done.11.grad_low_other, ...), custom_call_target="tpu_custom_call" | custom-call | flops 2717908992 | bytes 5308416 | tf_op jit(solution)/shard_map/pallas_call | solution.py:281
  267.1 12.1 %shard_map.186 = (bf16[1024,576]{1,0:T(8,128)(2,1)S(1)}, bf16[1024,384]{1,0:T(8,128)(2,1)S(1)}, bf16[1024,384]{1,0:T(8,128)(2,1)S(1)}) custom-call(s32[32]{0:T(128)S(1)} %copy-done.34, s32[3]{0:T(128)S(1)} %pad_add_fusion.ids, bf16[1024,576]{1,0:T(8,128)(2,1)S(1)} %copy-done.38, bf16[1024,192]{1,0:T(8,128)(2,1)} %bitcast.31.grad_mixed, ...), custom_call_target="tpu_custom_call" | custom-call | flops 2013265920 | bytes 3145728 | tf_op jit(solution)/shard_map/pallas_call | solution.py:203
  279.2 1.4 collective-permute-start.17
  280.6 1.9 collective-permute-done.17
  283.6 5.6 %all-to-all-start.9 = ((bf16[16,64,384]{2,1,0:T(8,128)(2,1)}), bf16[16,64,384]{2,1,0:T(8,128)(2,1)S(1)}, u32[]{:S(2)}, u32[]{:S(2)}) async-start(bf16[16,64,384]{2,1,0:T(8,128)(2,1)} %bitcast.35), calls=%async_computation.10 | async-start | bytes 1572864 | tf_op jit(solution)/shard_map/all_to_all | solution.py:665
  291.7 2.8 shard_map.187
  294.6 1.4 collective-permute-start.14
  296.0 2.4 collective-permute-start.15
  299.6 3.6 all-to-all-done.9.returned
  303.3 1.4 shard_map.189
  305.7 3.3 all-to-all-start.10
  309.0 3.0 collective-permute-done.15
  312.2 8.0 %reduce-scatter.2.cloned.1.call-done = bf16[864,768]{1,0:T(8,128)(2,1)} async-done(((bf16[3456,768]{1,0:T(8,128)(2,1)}), bf16[864,768]{1,0:T(8,128)(2,1)}) %reduce-scatter.2.cloned.1.call-update) | async-done | bytes 1327120 | tf_op jit(solution)/shard_map/reduce_scatter | solution.py:817
  320.2 2.3 reshape.314
  322.5 6.6 %all-to-all-start.8 = ((bf16[8,108,768]{2,1,0:T(8,128)(2,1)}), bf16[8,108,768]{2,1,0:T(8,128)(2,1)S(1)}, u32[]{:S(2)}, u32[]{:S(2)}) async-start(bf16[8,108,768]{2,1,0:T(8,128)(2,1)} %reshape.314), calls=%async_computation.9 | async-start | bytes 2752512 | tf_op jit(solution)/shard_map/all_to_all | solution.py:665
  329.1 2.7 collective-permute-start.20
  331.8 8.1 %shard_map.188 = bf16[256,768]{1,0:T(8,128)(2,1)} custom-call(bf16[16,64,192]{2,1,0:T(8,128)(2,1)S(1)} %copy-done.4, bf16[256,768]{1,0:T(8,128)(2,1)S(1)} %copy-done.3, bf16[8,864,768]{2,1,0:T(8,128)(2,1)} %bitcast.78, f32[8,768]{1,0:T(8,128)S(1)} %copy-done.11, f32[4,768]{1,0:T(4,128)S(1)} %copy-done.20), custom_call_target="tpu_custom_call" | custom-call | flops 2717908992 | bytes 10616832 | tf_op jit(solution)/shard_map/pallas_call | solution.py:381
  340.0 9.3 %all-to-all-done.8 = bf16[8,108,768]{2,1,0:T(8,128)(2,1)S(1)} async-done(((bf16[8,108,768]{2,1,0:T(8,128)(2,1)}), bf16[8,108,768]{2,1,0:T(8,128)(2,1)S(1)}, u32[]{:S(2)}, u32[]{:S(2)}) %all-to-all-start.8) | async-done | bytes 1327136 | tf_op jit(solution)/shard_map/all_to_all | solution.py:665
  349.8 28.2 %all_to_all.64.own = bf16[8,160,768]{2,1,0:T(8,128)(2,1)S(1)} all-to-all(bf16[8,160,768]{2,1,0:T(8,128)(2,1)S(1)} %broadcast_in_dim.107), channel_id=1, replica_groups=mesh['section'=2,'x'=4,'yh'=2,'core'=2,'fsdp'=4] {'x','yh'}, dimensions={0} | all-to-all | bytes 3932160 | tf_op jit(solution)/shard_map/all_to_all | solution.py:665
  378.0 2.7 collective-permute-start.21
  380.6 3.6 collective-permute-done.21.other
  384.2 3.3 shard_map.190
  (227 shorter events, 37.4 us)
Async XLA Ops:
  7.2 85.4 %all-gather.3.cloned.1.call-start = ((), (), s32[]{:S(2)}) async-start(), calls=%async_computation.14 | async-start | bytes 11943936 | tf_op jit(solution)/shard_map/all_gather | solution.py:749
  11.7 21.0 %all-to-all-start = ((bf16[4,4,576]{2,1,0:T(4,128)(2,1)}), bf16[4,4,576]{2,1,0:T(4,128)(2,1)S(1)}, u32[]{:S(2)}, u32[]{:S(2)}) async-start(bf16[4,4,576]{2,1,0:T(4,128)(2,1)} %broadcast_in_dim.94), calls=%async_computation | async-start | bytes 40960 | tf_op jit(solution)/shard_map/all_to_all | solution.py:665
  20.4 165.8 %copy-start.17 = (bf16[192,576]{1,0:T(8,128)(2,1)}, bf16[192,576]{1,0:T(8,128)(2,1)S(1)}, u32[]{:S(2)}) copy-start(bf16[192,576]{1,0:T(8,128)(2,1)S(1)} %copy.27.w0) | copy-start | bytes 663556
  20.4 12.5 %collective-permute-start = (bf16[192,576]{1,0:T(8,128)(2,1)S(1)}, bf16[192,576]{1,0:T(8,128)(2,1)S(1)}, u32[]{:S(2)}, u32[]{:S(2)}) collective-permute-start(bf16[192,576]{1,0:T(8,128)(2,1)S(1)} %copy.27.w0), channel_id=1, source_target_pairs={{0,2},{1,3},{2,0},{3,1},{4,6},{5,7},{6,4},{7,5},{8,10},{9,11},{10,... | collective-permute-start | bytes 663560 | tf_op jit(solution)/shard_map/ppermute | solution.py:697
  32.8 153.4 %copy-start.23 = (bf16[192,576]{1,0:T(8,128)(2,1)}, bf16[192,576]{1,0:T(8,128)(2,1)S(1)}, u32[]{:S(2)}) copy-start(bf16[192,576]{1,0:T(8,128)(2,1)S(1)} %collective-permute-done.w2) | copy-start | bytes 663556
  34.9 28.0 %copy-start.33 = (s32[32]{0:T(128)S(1)}, s32[32]{0:T(128)}, u32[]{:S(2)}) copy-start(s32[32]{0:T(128)} %table.7) | copy-start | bytes 388
  34.9 24.8 %all-to-all-start.1 = ((bf16[16,64,384]{2,1,0:T(8,128)(2,1)}), bf16[16,64,384]{2,1,0:T(8,128)(2,1)S(1)}, u32[]{:S(2)}, u32[]{:S(2)}) async-start(bf16[16,64,384]{2,1,0:T(8,128)(2,1)} %bitcast.19), calls=%async_computation.1 | async-start | bytes 1572864 | tf_op jit(solution)/shard_map/all_to_all | solution.py:665
  43.9 14.3 %collective-permute-start.2 = (bf16[192,576]{1,0:T(8,128)(2,1)S(1)}, bf16[192,576]{1,0:T(8,128)(2,1)S(1)}, u32[]{:S(2)}, u32[]{:S(2)}) collective-permute-start(bf16[192,576]{1,0:T(8,128)(2,1)S(1)} %copy.27.w0), channel_id=1, source_target_pairs={{0,1},{1,2},{2,3},{3,0},{4,5},{5,6},{6,7},{7,4},{8,9},{9,10},{10,1... | collective-permute-start | bytes 663560 | tf_op jit(solution)/shard_map/ppermute | solution.py:697
  44.0 15.0 %collective-permute-start.1 = (bf16[192,576]{1,0:T(8,128)(2,1)S(1)}, bf16[192,576]{1,0:T(8,128)(2,1)S(1)}, u32[]{:S(2)}, u32[]{:S(2)}) collective-permute-start(bf16[192,576]{1,0:T(8,128)(2,1)S(1)} %copy.27.w0), channel_id=1, source_target_pairs={{0,3},{1,0},{2,1},{3,2},{4,7},{5,4},{6,5},{7,6},{8,11},{9,8},{10,9... | collective-permute-start | bytes 663560 | tf_op jit(solution)/shard_map/ppermute | solution.py:697
  58.3 75.3 %copy-start.25 = (bf16[192,576]{1,0:T(8,128)(2,1)}, bf16[192,576]{1,0:T(8,128)(2,1)S(1)}, u32[]{:S(2)}) copy-start(bf16[192,576]{1,0:T(8,128)(2,1)S(1)} %collective-permute-done.2.w3) | copy-start | bytes 663556
  59.7 3.2 collective-permute-start.3
  74.1 18.4 %all-to-all-start.2 = ((bf16[16,64,192]{2,1,0:T(8,128)(2,1)}), bf16[16,64,192]{2,1,0:T(8,128)(2,1)S(1)}, u32[]{:S(2)}, u32[]{:S(2)}) async-start(bf16[16,64,192]{2,1,0:T(8,128)(2,1)} %bitcast.23), calls=%async_computation.2 | async-start | bytes 1048576 | tf_op jit(solution)/shard_map/all_to_all | solution.py:665
  81.6 18.4 %copy-start.19 = (f32[4,768]{1,0:T(4,128)}, f32[4,768]{1,0:T(4,128)S(1)}, u32[]{:S(2)}) copy-start(f32[4,768]{1,0:T(4,128)S(1)} %reshape.305.up_bias) | copy-start | bytes 36868
  81.7 18.3 %copy-start.9 = (f32[8,768]{1,0:T(8,128)}, f32[8,768]{1,0:T(8,128)S(1)}, u32[]{:S(2)}) copy-start(f32[8,768]{1,0:T(8,128)S(1)} %reshape.299.vectors) | copy-start | bytes 73732
  100.0 9.4 %collective-permute-start.4 = (bf16[256,768]{1,0:T(8,128)(2,1)S(1)}, bf16[256,768]{1,0:T(8,128)(2,1)S(1)}, u32[]{:S(2)}, u32[]{:S(2)}) collective-permute-start(bf16[256,768]{1,0:T(8,128)(2,1)S(1)} %shard_map.179), channel_id=1, source_target_pairs={{0,64},{1,65},{2,66},{3,67},{4,68},{5,69},{6,70},{7,71},{8,72},{9,... | collective-permute-start | bytes 1179656 | tf_op jit(solution)/shard_map/ppermute | solution.py:855
  110.3 21.3 %copy-start.42 = (bf16[192,3,1,192]{0,3,1,2:T(8,128)(2,1)S(1)}, bf16[192,3,1,192]{0,3,1,2:T(8,128)(2,1)}, u32[]{:S(2)}) copy-start(bf16[192,3,1,192]{0,3,1,2:T(8,128)(2,1)} %copy-done.41) | copy-start | bytes 663556
  110.4 23.1 %copy-start.30 = (bf16[192,576]{1,0:T(8,128)(2,1)S(1)}, bf16[192,576]{1,0:T(8,128)(2,1)}, u32[]{:S(2)}) copy-start(bf16[192,576]{1,0:T(8,128)(2,1)} %copy-done.28) | copy-start | bytes 663556
  131.2 2.3 collective-permute-start.5
  142.6 43.6 %copy-start.37 = (bf16[1024,576]{1,0:T(8,128)(2,1)}, bf16[1024,576]{1,0:T(8,128)(2,1)S(1)}, u32[]{:S(2)}) copy-start(bf16[1024,576]{1,0:T(8,128)(2,1)S(1)} %get-tuple-element.83.joined) | copy-start | bytes 3538948
  142.6 43.6 %copy-start.39 = (f32[8,1024]{1,0:T(8,128)}, f32[8,1024]{1,0:T(8,128)S(1)}, u32[]{:S(2)}) copy-start(f32[8,1024]{1,0:T(8,128)S(1)} %get-tuple-element.86.log_total) | copy-start | bytes 98308
  157.3 28.9 %copy-start.26 = (bf16[192,576]{1,0:T(8,128)(2,1)S(1)}, bf16[192,576]{1,0:T(8,128)(2,1)}, u32[]{:S(2)}) copy-start(bf16[192,576]{1,0:T(8,128)(2,1)} %copy-done.25) | copy-start | bytes 663556
  157.3 28.9 %copy-start.31 = (bf16[192,576]{1,0:T(8,128)(2,1)S(1)}, bf16[192,576]{1,0:T(8,128)(2,1)}, u32[]{:S(2)}) copy-start(bf16[192,576]{1,0:T(8,128)(2,1)} %copy-done.28) | copy-start | bytes 663556
  198.4 4.3 %collective-permute-start.6 = (bf16[1024,384]{1,0:T(8,128)(2,1)S(1)}, bf16[1024,384]{1,0:T(8,128)(2,1)S(1)}, u32[]{:S(2)}, u32[]{:S(2)}) collective-permute-start(bf16[1024,384]{1,0:T(8,128)(2,1)S(1)} %get-tuple-element.88), channel_id=1, source_target_pairs={{0,4},{4,0},{1,5},{5,1},{2,6},{6,2},{3,7},{7,3},{8,12},{12,8},{9,1... | collective-permute-start | bytes 2359304 | tf_op jit(solution)/shard_map/ppermute | solution.py:669
  199.7 37.3 %collective-permute-start.8 = (bf16[256,3072]{1,0:T(8,128)(2,1)S(1)}, bf16[256,3072]{1,0:T(8,128)(2,1)}, u32[]{:S(2)}, u32[]{:S(2)}) collective-permute-start(bf16[256,3072]{1,0:T(8,128)(2,1)S(1)} %copy-done.5), channel_id=1, source_target_pairs={{0,4},{4,0},{1,5},{5,1},{2,6},{6,2},{3,7},{7,3},{8,12},{12,8},{9,1... | collective-permute-start | bytes 4718600 | tf_op jit(solution)/shard_map/ppermute | solution.py:669
  202.9 17.5 %copy-start.3 = (bf16[256,768]{1,0:T(8,128)(2,1)S(1)}, bf16[256,768]{1,0:T(8,128)(2,1)}, u32[]{:S(2)}) copy-start(bf16[256,768]{1,0:T(8,128)(2,1)} %copy-done.2) | copy-start | bytes 1179652
  202.9 17.5 %copy-start.8 = (f32[256,768]{1,0:T(8,128)S(1)}, f32[256,768]{1,0:T(8,128)}, u32[]{:S(2)}) copy-start(f32[256,768]{1,0:T(8,128)} %get-tuple-element.89.grad_middle) | copy-start | bytes 2359300
  202.9 17.5 %copy-start.10 = (f32[8,768]{1,0:T(8,128)S(1)}, f32[8,768]{1,0:T(8,128)}, u32[]{:S(2)}) copy-start(f32[8,768]{1,0:T(8,128)} %copy-done.9) | copy-start | bytes 73732
  221.9 12.5 %collective-permute-start.7 = (bf16[256,768]{1,0:T(8,128)(2,1)}, bf16[256,768]{1,0:T(8,128)(2,1)}, u32[]{:S(2)}, u32[]{:S(2)}) collective-permute-start(bf16[256,768]{1,0:T(8,128)(2,1)} %get-tuple-element.90), channel_id=1, source_target_pairs={{64,0},{65,1},{66,2},{67,3},{68,4},{69,5},{70,6},{71,7},{72,8},{73... | collective-permute-start | bytes 1179656 | tf_op jit(solution)/shard_map/ppermute | solution.py:863
  223.2 13.1 %collective-permute-start.9 = (bf16[768,256]{1,0:T(8,128)(2,1)S(1)}, bf16[768,256]{1,0:T(8,128)(2,1)S(1)}, u32[]{:S(2)}, u32[]{:S(2)}) collective-permute-start(bf16[768,256]{1,0:T(8,128)(2,1)S(1)} %copy-done.12), channel_id=1, source_target_pairs={{0,4},{4,0},{1,5},{5,1},{2,6},{6,2},{3,7},{7,3},{8,12},{12,8},{9,1... | collective-permute-start | bytes 1179656 | tf_op jit(solution)/shard_map/ppermute | solution.py:669
  223.7 13.4 %collective-permute-start.10 = (bf16[768,256]{1,0:T(8,128)(2,1)}, bf16[768,256]{1,0:T(8,128)(2,1)}, u32[]{:S(2)}, u32[]{:S(2)}) collective-permute-start(bf16[768,256]{1,0:T(8,128)(2,1)} %get-tuple-element.104.mixed), channel_id=1, source_target_pairs={{0,4},{4,0},{1,5},{5,1},{2,6},{6,2},{3,7},{7,3},{8,12},{12,8},{9,1... | collective-permute-start | bytes 1179656 | tf_op jit(solution)/shard_map/ppermute | solution.py:669
  237.1 16.3 %copy-start.13 = (bf16[768,256]{1,0:T(8,128)(2,1)S(1)}, bf16[768,256]{1,0:T(8,128)(2,1)}, u32[]{:S(2)}) copy-start(bf16[768,256]{1,0:T(8,128)(2,1)} %get-tuple-element.101.normed_two) | copy-start | bytes 1179652
  247.3 6.0 %collective-permute-start.12 = (bf16[256,3072]{1,0:T(8,128)(2,1)}, bf16[256,3072]{1,0:T(8,128)(2,1)}, u32[]{:S(2)}, u32[]{:S(2)}) collective-permute-start(bf16[256,3072]{1,0:T(8,128)(2,1)} %get-tuple-element.103.grad_hidden), channel_id=1, source_target_pairs={{0,4},{4,0},{1,5},{5,1},{2,6},{6,2},{3,7},{7,3},{8,12},{12,8},{9,1... | collective-permute-start | bytes 4718600 | tf_op jit(solution)/shard_map/ppermute | solution.py:669
  248.6 4.7 %collective-permute-start.13 = (bf16[256,768]{1,0:T(8,128)(2,1)}, bf16[256,768]{1,0:T(8,128)(2,1)}, u32[]{:S(2)}, u32[]{:S(2)}) collective-permute-start(bf16[256,768]{1,0:T(8,128)(2,1)} %get-tuple-element.106.grad_attn), channel_id=1, source_target_pairs={{0,4},{4,0},{1,5},{5,1},{2,6},{6,2},{3,7},{7,3},{8,12},{12,8},{9,1... | collective-permute-start | bytes 1179656 | tf_op jit(solution)/shard_map/ppermute | solution.py:669
  248.7 4.6 %collective-permute-start.11 = (bf16[256,768]{1,0:T(8,128)(2,1)S(1)}, bf16[256,768]{1,0:T(8,128)(2,1)}, u32[]{:S(2)}, u32[]{:S(2)}) collective-permute-start(bf16[256,768]{1,0:T(8,128)(2,1)S(1)} %copy-done.6), channel_id=1, source_target_pairs={{0,4},{4,0},{1,5},{5,1},{2,6},{6,2},{3,7},{7,3},{8,12},{12,8},{9,1... | collective-permute-start | bytes 1179656 | tf_op jit(solution)/shard_map/ppermute | solution.py:669
  249.1 15.4 %all-to-all-start.7 = ((bf16[16,64,192]{2,1,0:T(8,128)(2,1)}), bf16[16,64,192]{2,1,0:T(8,128)(2,1)}, u32[]{:S(2)}, u32[]{:S(2)}) async-start(bf16[16,64,192]{2,1,0:T(8,128)(2,1)} %get-tuple-element.98), calls=%async_computation.7 | async-start | bytes 1048576 | tf_op jit(solution)/shard_map/all_to_all | solution.py:665
  253.2 66.9 %reduce-scatter.2.cloned.1.call-start = ((), (), s32[]{:S(2)}) async-start(), calls=%async_computation.13 | async-start | bytes 6635520 | tf_op jit(solution)/shard_map/reduce_scatter | solution.py:817
  279.2 3.3 collective-permute-start.17
  283.6 19.6 %all-to-all-start.9 = ((bf16[16,64,384]{2,1,0:T(8,128)(2,1)}), bf16[16,64,384]{2,1,0:T(8,128)(2,1)S(1)}, u32[]{:S(2)}, u32[]{:S(2)}) async-start(bf16[16,64,384]{2,1,0:T(8,128)(2,1)} %bitcast.35), calls=%async_computation.10 | async-start | bytes 1572864 | tf_op jit(solution)/shard_map/all_to_all | solution.py:665
  294.6 14.4 %collective-permute-start.14 = (bf16[192,576]{1,0:T(8,128)(2,1)}, bf16[192,576]{1,0:T(8,128)(2,1)S(1)}, u32[]{:S(2)}, u32[]{:S(2)}) collective-permute-start(bf16[192,576]{1,0:T(8,128)(2,1)} %get-tuple-element.111), channel_id=1, source_target_pairs={{0,16},{16,32},{32,48},{48,0},{1,17},{17,33},{33,49},{49,1},{2,18}... | collective-permute-start | bytes 663560 | tf_op jit(solution)/shard_map/ppermute | solution.py:705
  296.0 16.0 %collective-permute-start.15 = (bf16[192,576]{1,0:T(8,128)(2,1)}, bf16[192,576]{1,0:T(8,128)(2,1)S(1)}, u32[]{:S(2)}, u32[]{:S(2)}) collective-permute-start(bf16[192,576]{1,0:T(8,128)(2,1)} %get-tuple-element.112), channel_id=1, source_target_pairs={{0,32},{16,48},{32,0},{48,16},{1,33},{17,49},{33,1},{49,17},{2,34}... | collective-permute-start | bytes 663560 | tf_op jit(solution)/shard_map/ppermute | solution.py:705
  298.4 13.6 %collective-permute-start.16 = (bf16[192,576]{1,0:T(8,128)(2,1)S(1)}, bf16[192,576]{1,0:T(8,128)(2,1)S(1)}, u32[]{:S(2)}, u32[]{:S(2)}) collective-permute-start(bf16[192,576]{1,0:T(8,128)(2,1)S(1)} %get-tuple-element.113), channel_id=1, source_target_pairs={{0,48},{16,0},{32,16},{48,32},{1,49},{17,1},{33,17},{49,33},{2,50}... | collective-permute-start | bytes 663560 | tf_op jit(solution)/shard_map/ppermute | solution.py:705
  305.7 16.7 %all-to-all-start.10 = ((bf16[4,4,576]{2,1,0:T(4,128)(2,1)}), bf16[4,4,576]{2,1,0:T(4,128)(2,1)S(1)}, u32[]{:S(2)}, u32[]{:S(2)}) async-start(bf16[4,4,576]{2,1,0:T(4,128)(2,1)} %convert_element_type.133), calls=%async_computation.11 | async-start | bytes 40960 | tf_op jit(solution)/shard_map/all_to_all | solution.py:665
  322.5 26.9 %all-to-all-start.8 = ((bf16[8,108,768]{2,1,0:T(8,128)(2,1)}), bf16[8,108,768]{2,1,0:T(8,128)(2,1)S(1)}, u32[]{:S(2)}, u32[]{:S(2)}) async-start(bf16[8,108,768]{2,1,0:T(8,128)(2,1)} %reshape.314), calls=%async_computation.9 | async-start | bytes 2752512 | tf_op jit(solution)/shard_map/all_to_all | solution.py:665
  329.1 10.9 %collective-permute-start.18 = (bf16[48,576]{1,0:T(8,128)(2,1)S(1)}, bf16[48,576]{1,0:T(8,128)(2,1)S(1)}, u32[]{:S(2)}, u32[]{:S(2)}) collective-permute-start(bf16[48,576]{1,0:T(8,128)(2,1)S(1)} %get-tuple-element.159), channel_id=1, source_target_pairs={{0,1},{1,2},{2,3},{3,0},{4,5},{5,6},{6,7},{7,4},{8,9},{9,10},{10,1... | collective-permute-start | bytes 165896 | tf_op jit(solution)/shard_map/ppermute | solution.py:705
  329.1 10.8 %collective-permute-start.20 = (bf16[48,576]{1,0:T(8,128)(2,1)S(1)}, bf16[48,576]{1,0:T(8,128)(2,1)S(1)}, u32[]{:S(2)}, u32[]{:S(2)}) collective-permute-start(bf16[48,576]{1,0:T(8,128)(2,1)S(1)} %get-tuple-element.160), channel_id=1, source_target_pairs={{0,3},{1,0},{2,1},{3,2},{4,7},{5,4},{6,5},{7,6},{8,11},{9,8},{10,9... | collective-permute-start | bytes 165896 | tf_op jit(solution)/shard_map/ppermute | solution.py:705
  331.8 8.2 %collective-permute-start.19 = (bf16[48,576]{1,0:T(8,128)(2,1)S(1)}, bf16[48,576]{1,0:T(8,128)(2,1)S(1)}, u32[]{:S(2)}, u32[]{:S(2)}) collective-permute-start(bf16[48,576]{1,0:T(8,128)(2,1)S(1)} %get-tuple-element.161), channel_id=1, source_target_pairs={{0,2},{1,3},{2,0},{3,1},{4,6},{5,7},{6,4},{7,5},{8,10},{9,11},{10,... | collective-permute-start | bytes 165896 | tf_op jit(solution)/shard_map/ppermute | solution.py:705
  349.7 39.8 %copy-start.1 = (bf16[1,192,3072]{2,1,0:T(8,128)(2,1)S(1)}, bf16[1,192,3072]{2,1,0:T(8,128)(2,1)}, u32[]{:S(2)}) copy-start(bf16[1,192,3072]{2,1,0:T(8,128)(2,1)} %param.17) | copy-start | bytes 3538948
  378.0 6.3 %collective-permute-start.21 = (bf16[8,160,768]{2,1,0:T(8,128)(2,1)S(1)}, bf16[8,160,768]{2,1,0:T(8,128)(2,1)S(1)}, u32[]{:S(2)}, u32[]{:S(2)}) collective-permute-start(bf16[8,160,768]{2,1,0:T(8,128)(2,1)S(1)} %all_to_all.64.own), channel_id=1, source_target_pairs={{0,4},{4,0},{1,5},{5,1},{2,6},{6,2},{3,7},{7,3},{8,12},{12,8},{9,1... | collective-permute-start | bytes 5898248 | tf_op jit(solution)/shard_map/ppermute | solution.py:669
  (37 other events, 162.7 us)
Sparse Core Ops, SparseCore 0:
  11.0 68.9 all-gather.2
  264.6 55.5 reduce-scatter.1
